TPU v7x, 32 devices: a whole 2x2x4 slice. The times are simulated.
32 devices in a mesh: seq: 8 (over z, y), chan: 4 (over x, core).
Axes of the slice: x: 2, y: 2, z: 4, core: 2. Of those that a mesh axis runs over, the one named last changes fastest.
Arguments:
- q_proj: bfloat16 [1024, 8192], P('seq', 'chan'), may hold values from -6 to 6
- k_proj: bfloat16 [1024, 8192], P('seq', 'chan'), may hold values from -6 to 6
- v_proj: bfloat16 [1024, 8192], P('seq', 'chan'), may hold values from -6 to 6
- residues: float32 [8192, 16], P('chan'), may hold values from -1.5 to 1.5
- rates: float32 [8192, 16], P('chan'), may hold values from 0.5 to 32
- skip_gain: float32 [8192], P('chan'), may hold values from -4 to 4
- w_out: bfloat16 [8192, 8192], P('chan', 'seq'), may hold values from -0.0625 to 0.0625
Outputs:
- mixed: bfloat16 [1024, 8192], P('seq', 'chan')
All inputs are finite; a program needn't handle non-finite values.
Results may differ from a plain program's by a relative error of at most 0.0085.
Values may be sent and summed in bfloat16 or wider, within the bound.
No kernel may reach another device: no remote copies, remote signals or barrier semaphores. Data moves between devices by JAX's collectives and lax.ppermute only.
A program may use at most 128 MiB of HBM per device.

v0:
```python
import math

import jax
import jax.numpy as jnp
from jax import lax
from jax.sharding import PartitionSpec as P

TWO_PI = 2.0 * math.pi
HIGH = lax.Precision.HIGHEST


def cycle(first, second, period):
    turns = first[:, None] * second[None, :] % period
    angle = turns.astype(jnp.float32) * (TWO_PI / period)
    return (jnp.cos(angle), jnp.sin(angle))


def filter_time(residues, rates, start, count, total):
    places = (start + jnp.arange(count, dtype=jnp.int32)).astype(jnp.float32)
    weights = residues * jnp.sqrt(2.0 * rates / total)

    def add_mode(carry, mode):
        rate, weight = mode
        return (carry + weight[None, :] * jnp.exp(-(rate[None, :] * places[:, None]) / total), None)

    zeros = jnp.zeros((count, rates.shape[0]), jnp.float32)
    result, unused = lax.scan(add_mode, zeros, (rates.T, weights.T))
    return result


def forward(signal, index, parts, cos_b, sin_b):
    count, rows, width = signal.shape
    group = rows // parts
    coarse = 2 * parts
    length = 2 * rows * parts
    blocks = signal.reshape(count, parts, group, width)
    blocks = lax.all_to_all(blocks, "seq", split_axis=1, concat_axis=0, tiled=True)
    blocks = blocks.reshape(parts, count, group, width)
    cos_a, sin_a = cycle(
        jnp.arange(coarse, dtype=jnp.int32), jnp.arange(parts, dtype=jnp.int32), coarse
    )
    part_re = jnp.einsum("ka,afgc->fkgc", cos_a, blocks, precision=HIGH)
    part_im = -jnp.einsum("ka,afgc->fkgc", sin_a, blocks, precision=HIGH)
    offsets = index * group + jnp.arange(group, dtype=jnp.int32)
    twist_c, twist_s = cycle(jnp.arange(coarse, dtype=jnp.int32), offsets, length)
    twist_c = twist_c[None, :, :, None]
    twist_s = twist_s[None, :, :, None]
    rot_re = part_re * twist_c + part_im * twist_s
    rot_im = part_im * twist_c - part_re * twist_s
    stacked = lax.all_to_all(
        jnp.stack([rot_re, rot_im]), "seq", split_axis=2, concat_axis=3, tiled=True
    )
    real_in, imag_in = (stacked[0], stacked[1])
    spec_re = jnp.einsum("nb,fjbc->fjnc", cos_b, real_in, precision=HIGH) + jnp.einsum(
        "nb,fjbc->fjnc", sin_b, imag_in, precision=HIGH
    )
    spec_im = jnp.einsum("nb,fjbc->fjnc", cos_b, imag_in, precision=HIGH) - jnp.einsum(
        "nb,fjbc->fjnc", sin_b, real_in, precision=HIGH
    )
    return (spec_re, spec_im)


def inverse(spec_re, spec_im, index, parts, cos_b, sin_b):
    pair, rows, width = spec_re.shape
    group = rows // parts
    coarse = 2 * parts
    length = 2 * rows * parts
    val_re = jnp.einsum("bn,jnc->jbc", cos_b, spec_re, precision=HIGH) - jnp.einsum(
        "bn,jnc->jbc", sin_b, spec_im, precision=HIGH
    )
    val_im = jnp.einsum("bn,jnc->jbc", cos_b, spec_im, precision=HIGH) + jnp.einsum(
        "bn,jnc->jbc", sin_b, spec_re, precision=HIGH
    )
    freqs = 2 * index + jnp.arange(2, dtype=jnp.int32)
    twist_c, twist_s = cycle(freqs, jnp.arange(rows, dtype=jnp.int32), length)
    twist_c = twist_c[:, :, None]
    twist_s = twist_s[:, :, None]
    rot_re = val_re * twist_c - val_im * twist_s
    rot_im = val_im * twist_c + val_re * twist_s
    stacked = jnp.stack([rot_re, rot_im]).reshape(2, pair, parts, group, width)
    stacked = lax.all_to_all(
        stacked.astype(jnp.bfloat16), "seq", split_axis=2, concat_axis=1, tiled=True
    ).astype(stacked.dtype)
    stacked = stacked.reshape(2, coarse, group, width)
    cos_a, sin_a = cycle(
        jnp.arange(parts, dtype=jnp.int32), jnp.arange(coarse, dtype=jnp.int32), coarse
    )
    values = jnp.einsum("ak,kgc->agc", cos_a, stacked[0], precision=HIGH) - jnp.einsum(
        "ak,kgc->agc", sin_a, stacked[1], precision=HIGH
    )
    values = values * (1.0 / length)
    values = lax.all_to_all(
        values.reshape(parts, 1, group, width), "seq", split_axis=0, concat_axis=1, tiled=True
    )
    return values.reshape(rows, width)


def spectral(source, residues, rates, index, parts, total):
    rows = source.shape[0]
    cos_b, sin_b = cycle(jnp.arange(rows, dtype=jnp.int32), jnp.arange(rows, dtype=jnp.int32), rows)
    taps = filter_time(residues, rates, index * rows, rows, total)
    spec_re, spec_im = forward(jnp.stack([source, taps]), index, parts, cos_b, sin_b)
    sig_re, sig_im = (spec_re[0], spec_im[0])
    filt_re, filt_im = (spec_re[1], spec_im[1])
    prod_re = sig_re * filt_re - sig_im * filt_im
    prod_im = sig_re * filt_im + sig_im * filt_re
    return inverse(prod_re, prod_im, index, parts, cos_b, sin_b)


def local(q_proj, k_proj, v_proj, residues, rates, skip_gain, w_out):
    rows, width = q_proj.shape
    parts = lax.axis_size("seq")
    index = lax.axis_index("seq")
    total = rows * parts
    source = k_proj.astype(jnp.float32) * v_proj.astype(jnp.float32)
    conv = spectral(source, residues, rates, index, parts, total)
    hidden = (q_proj.astype(jnp.float32) * (conv + skip_gain[None, :] * source)).astype(
        jnp.bfloat16
    )
    spread = jnp.dot(
        lax.all_gather(hidden, "seq", axis=0, tiled=True), w_out, preferred_element_type=jnp.float32
    )
    partial_value = lax.all_to_all(spread, "seq", split_axis=0, concat_axis=1, tiled=True)
    summed = lax.psum_scatter(partial_value, "chan", scatter_dimension=1, tiled=True)
    return summed.astype(jnp.bfloat16)


def solution(mesh):
    return jax.shard_map(
        local,
        mesh=mesh,
        in_specs=(
            P("seq", "chan"),
            P("seq", "chan"),
            P("seq", "chan"),
            P("chan", None),
            P("chan", None),
            P("chan"),
            P("chan", "seq"),
        ),
        out_specs=P("seq", "chan"),
        check_vma=False,
    )
```

profile of v0, /device:TPU:10, one launch (start us, length us, event | category | flops | bytes accessed | tf_op | source)
XLA Modules:
  0.0 657.2 jit_solution(1251793951646729811)
XLA Ops:
  6.5 1.0 multiply_bitcast_fusion
  7.6 23.8 %while.11 = (s32[]{:T(128)}, f32[128,2048]{1,0:T(8,128)S(1)}, f32[16,2048]{1,0:T(8,128)S(1)}, f32[16,2048]{1,0:T(8,128)}, s32[]{:T(128)}, /*index=5*/s32[]{:T(128)}, s32[]{:T(128)}) while((s32[]{:T(128)}, f32[128,2048]{1,0:T(8,128)S(1)}, f32[16,2048]{1,0:T(8,128)S(1)}, f32[16,2048]{1,0:T(8,128)}, s32[]{:T(128)}, ...), condition=%wide.region_1.2_spmd.clone, body=%wide.region_0.1_spmd.clone.sunk | while | flops 1573123 | bytes 2147423 | solution.py:27
  7.6 0.9 constant_dynamic-slice_fusion.3
  9.1 0.9 constant_dynamic-slice_fusion.3
  10.6 0.9 constant_dynamic-slice_fusion.3
  12.1 0.9 constant_dynamic-slice_fusion.3
  13.6 0.9 constant_dynamic-slice_fusion.3
  15.1 0.9 constant_dynamic-slice_fusion.3
  16.6 0.9 constant_dynamic-slice_fusion.3
  18.0 0.9 constant_dynamic-slice_fusion.3
  19.5 0.9 constant_dynamic-slice_fusion.3
  21.0 0.9 constant_dynamic-slice_fusion.3
  22.5 0.9 constant_dynamic-slice_fusion.3
  24.0 0.9 constant_dynamic-slice_fusion.3
  25.4 0.9 constant_dynamic-slice_fusion.3
  26.9 0.9 constant_dynamic-slice_fusion.3
  28.4 0.9 constant_dynamic-slice_fusion.3
  29.9 0.9 constant_dynamic-slice_fusion.3
  31.7 1.5 copy.49
  33.2 6.3 all-to-all-start
  39.6 45.6 %all-to-all-done = f32[2,8,16,2048]{3,2,0,1:T(8,128)S(1)} async-done(((f32[2,8,16,2048]{3,2,0,1:T(8,128)}), f32[2,8,16,2048]{3,2,0,1:T(8,128)S(1)}, u32[]{:S(2)}, u32[]{:S(2)}) %all-to-all-start) | async-done | bytes 2097184 | tf_op jit(solution)/shard_map/all_to_all | solution.py:37
  85.3 5.8 fusion.14
  91.1 6.8 %fusion.3 = (f32[1,2,16,16,2048]{4,2,3,1,0:T(8,128)S(1)}, f32[1,2,16,16,2048]{4,2,3,1,0:T(8,128)S(1)}) fusion(f32[2,16,2048,16]{2,3,1,0:T(8,128)S(1)} %fusion.14, f32[16,16]{0,1:T(8,128)S(1)} %get-tuple-element.79, f32[16,16]{0,1:T(8,128)S(1)} %get-tuple-element.78, f32[2,8,16,2048]{3,2,0,1:T(8,128)S(1)} %all-to-all-done), kind=kOutput, calls=%fused_computation.9 | convolution fusion | flops 108005120 | bytes 14682112 | tf_op jit(solution)/shard_map/ka,afgc->fkgc/dot_general | solution.py:42
  97.9 1.1 pad_maximum_fusion
  99.0 8.4 %copy.51 = f32[2,2,16,16,2048]{4,3,1,0,2:T(8,128)} copy(f32[2,2,16,16,2048]{4,2,3,1,0:T(8,128)S(1)} %pad_maximum_fusion) | data formatting | bytes 16777216 | tf_op jit(solution)/shard_map/stack | solution.py:51
  107.4 7.3 %all-to-all-start.1 = ((f32[2,2,16,16,2048]{4,3,1,0,2:T(8,128)}), f32[2,2,16,16,2048]{4,3,1,0,2:T(8,128)}, u32[]{:S(2)}, u32[]{:S(2)}) async-start(f32[2,2,16,16,2048]{4,3,1,0,2:T(8,128)} %copy.51), calls=%async_computation.1 | async-start | bytes 16777216 | tf_op jit(solution)/shard_map/all_to_all | solution.py:50
  114.9 179.6 %all-to-all-done.1 = f32[2,2,16,16,2048]{4,3,1,0,2:T(8,128)} async-done(((f32[2,2,16,16,2048]{4,3,1,0,2:T(8,128)}), f32[2,2,16,16,2048]{4,3,1,0,2:T(8,128)}, u32[]{:S(2)}, u32[]{:S(2)}) %all-to-all-start.1) | async-done | bytes 8388640 | tf_op jit(solution)/shard_map/all_to_all | solution.py:50
  294.5 4.0 copy.52
  298.5 1.1 fusion.136
  300.1 6.8 %fusion.36 = f32[2,2,2048,128]{3,2,1,0:T(8,128)S(1)} fusion(f32[2,2,128,2048]{3,2,1,0:T(8,128)S(1)} %bitcast.138), kind=kOutput, calls=%fused_computation.61 | convolution fusion | flops 1610842112 | bytes 8388608 | tf_op jit(solution)/shard_map/nb,fjbc->fjnc/dot_general | solution.py:54
  307.4 7.0 %fusion.34 = f32[2,2,2048,128]{3,2,1,0:T(8,128)S(1)} fusion(f32[2,2,128,2048]{3,2,1,0:T(8,128)S(1)} %bitcast.140), kind=kOutput, calls=%fused_computation.59 | convolution fusion | flops 1610842112 | bytes 8388608 | tf_op jit(solution)/shard_map/nb,fjbc->fjnc/dot_general | solution.py:57
  314.4 6.8 %add_bitcast_fusion = f32[2,2,128,2048]{2,3,1,0:T(8,128)S(1)} fusion(f32[2,2,2048,128]{3,2,1,0:T(8,128)S(1)} %fusion.36, f32[2,2,128,2048]{3,2,1,0:T(8,128)S(1)} %bitcast.141), kind=kOutput, calls=%fused_computation.15 | convolution fusion | flops 1611890688 | bytes 12582912 | tf_op jit(solution)/shard_map/nb,fjbc->fjnc/dot_general | solution.py:54
  321.2 7.0 %subtract_bitcast_fusion = f32[2,2,128,2048]{2,3,1,0:T(8,128)S(1)} fusion(f32[2,2,2048,128]{3,2,1,0:T(8,128)S(1)} %fusion.34, f32[2,2,128,2048]{3,2,1,0:T(8,128)S(1)} %bitcast.139), kind=kOutput, calls=%fused_computation.14 | convolution fusion | flops 1611890688 | bytes 12582912 | tf_op jit(solution)/shard_map/nb,fjbc->fjnc/dot_general | solution.py:57
  328.7 2.2 fusion.12
  330.9 2.2 fusion.8
  333.1 2.5 convolution_subtract_fusion
  335.7 2.8 subtract_convert_fusion
  339.0 53.4 %all_to_all.73 = bf16[2,2,8,16,2048]{4,3,1,0,2:T(8,128)(2,1)S(1)} all-to-all(bf16[2,2,8,16,2048]{4,3,1,0,2:T(8,128)(2,1)S(1)} %copy.81), channel_id=1, replica_groups=mesh['seq'=8,'chan'=4] {'seq'}, dimensions={2} | all-to-all | bytes 4194304 | tf_op jit(solution)/shard_map/all_to_all | solution.py:81
  392.6 1.6 fusion.23
  394.2 1.6 fusion.7
  396.5 28.9 %all_to_all.74 = f32[8,1,16,2048]{3,2,1,0:T(8,128)S(1)} all-to-all(f32[8,1,16,2048]{3,2,1,0:T(8,128)S(1)} %copy.67), channel_id=1, replica_groups=mesh['seq'=8,'chan'=4] {'seq'}, dimensions={0} | all-to-all | bytes 2097152 | tf_op jit(solution)/shard_map/all_to_all | solution.py:92
  425.3 1.1 fusion.21
  426.5 72.2 %all-gather.2.cloned.1.call-done = bf16[1024,2048]{1,0:T(8,128)(2,1)} async-done(((bf16[128,2048]{1,0:T(8,128)(2,1)}), bf16[1024,2048]{1,0:T(8,128)(2,1)}) %all-gather.2.cloned.1.call-update) | async-done | bytes 4194320 | tf_op jit(solution)/shard_map/all_gather | solution.py:121
  498.7 7.5 %fusion.142 = f32[1024,1024]{1,0:T(8,128)S(1)} fusion(bf16[1024,2048]{1,0:T(8,128)(2,1)} %all-gather.2.cloned.1.call-done, bf16[2048,1024]{1,0:T(8,128)(2,1)} %param.15), kind=kOutput, calls=%fused_computation.165 | convolution fusion | flops 4294967296 | bytes 12582912 | tf_op jit(solution)/shard_map/dot_general | solution.py:120
  506.2 96.2 %all_to_all.75 = f32[8,128,1024]{2,1,0:T(8,128)S(1)} all-to-all(f32[8,128,1024]{2,1,0:T(8,128)S(1)} %bitcast.147), channel_id=1, replica_groups=mesh['seq'=8,'chan'=4] {'seq'}, dimensions={0} | all-to-all | bytes 8388608 | tf_op jit(solution)/shard_map/all_to_all | solution.py:123
  602.5 2.3 copy.84
  604.8 43.1 %reduce-scatter.2.cloned.1.call-done = f32[128,2048]{1,0:T(8,128)} async-done(((f32[128,8192]{1,0:T(8,128)}), f32[128,2048]{1,0:T(8,128)}) %reduce-scatter.2.cloned.1.call-update) | async-done | bytes 1048592 | tf_op jit(solution)/shard_map/reduce_scatter | solution.py:124
  647.9 2.1 convert_element_type.77
  (58 shorter events, 12.8 us)
Async XLA Ops:
  7.5 23.8 %copy-start = (bf16[128,2048]{1,0:T(8,128)(2,1)S(1)}, bf16[128,2048]{1,0:T(8,128)(2,1)}, u32[]{:S(2)}) copy-start(bf16[128,2048]{1,0:T(8,128)(2,1)} %param.11) | copy-start | bytes 1572868
  7.6 23.8 %copy-start.1 = (bf16[128,2048]{1,0:T(8,128)(2,1)S(1)}, bf16[128,2048]{1,0:T(8,128)(2,1)}, u32[]{:S(2)}) copy-start(bf16[128,2048]{1,0:T(8,128)(2,1)} %param.10) | copy-start | bytes 1572868
  33.2 52.1 %all-to-all-start = ((f32[2,8,16,2048]{3,2,0,1:T(8,128)}), f32[2,8,16,2048]{3,2,0,1:T(8,128)S(1)}, u32[]{:S(2)}, u32[]{:S(2)}) async-start(f32[2,8,16,2048]{3,2,0,1:T(8,128)} %copy.49), calls=%async_computation | async-start | bytes 4194304 | tf_op jit(solution)/shard_map/all_to_all | solution.py:37
  107.4 187.1 %all-to-all-start.1 = ((f32[2,2,16,16,2048]{4,3,1,0,2:T(8,128)}), f32[2,2,16,16,2048]{4,3,1,0,2:T(8,128)}, u32[]{:S(2)}, u32[]{:S(2)}) async-start(f32[2,2,16,16,2048]{4,3,1,0,2:T(8,128)} %copy.51), calls=%async_computation.1 | async-start | bytes 16777216 | tf_op jit(solution)/shard_map/all_to_all | solution.py:50
  114.8 384.0 %all-gather.2.cloned.1.call-start = ((), (), s32[]{:S(2)}) async-start(), calls=%async_computation.6 | async-start | bytes 4718592 | tf_op jit(solution)/shard_map/all_gather | solution.py:121
  394.2 31.1 %copy-start.2 = (bf16[128,2048]{1,0:T(8,128)(2,1)S(1)}, bf16[128,2048]{1,0:T(8,128)(2,1)}, u32[]{:S(2)}) copy-start(bf16[128,2048]{1,0:T(8,128)(2,1)} %param.9) | copy-start | bytes 1572868
  394.2 31.1 %copy-start.3 = (f32[2048]{0:T(1024)S(1)}, f32[2048]{0:T(1024)}, u32[]{:S(2)}) copy-start(f32[2048]{0:T(1024)} %param.14) | copy-start | bytes 24580
  426.5 221.4 %reduce-scatter.2.cloned.1.call-start = ((), (), s32[]{:S(2)}) async-start(), calls=%async_computation.7 | async-start | bytes 5242880 | tf_op jit(solution)/shard_map/reduce_scatter | solution.py:124
Sparse Core Ops, SparseCore 0:
  426.6 72.0 all-gather.1
  604.9 42.9 reduce-scatter.1
where the time goes:
time: 670 us; the launch traced here: 657 us
  waiting for transfers between devices  341 us (51%)
  blocking collectives  178 us (27%)
  matrix products  60.8 us (9%)
  local copies, waits for them, and re-layouts  33.1 us (5%)
  other arithmetic  15.9 us (2%)
  between operations  14.1 us (2%)
  starting transfers between devices  13.6 us (2%)
    all_to_all x1, waiting for transfers between devices, forward(): lax.all_to_all(jnp.stack([rot_re, rot_im]), 'seq', split_axis=2, concat_a...  180 us
    all_to_all x1, blocking collectives, local(): lax.all_to_all(spread, 'seq', split_axis=0, concat_axis=1, tiled=True)  96.2 us
    all_gather x1, waiting for transfers between devices, local(): lax.all_gather(hidden, 'seq', axis=0, tiled=True)  72.2 us
    all_to_all x1, blocking collectives, inverse(): lax.all_to_all(stacked.astype(jnp.bfloat16), 'seq', split_axis=2, concat_...  53.4 us
    all_to_all x1, waiting for transfers between devices, forward(): lax.all_to_all(blocks, 'seq', split_axis=1, concat_axis=0, tiled=True)  45.6 us
    reduce_scatter x1, waiting for transfers between devices, local(): lax.psum_scatter(partial_value, 'chan', scatter_dimension=1, tiled=True)  43.1 us
    all_to_all x1, blocking collectives, inverse(): lax.all_to_all(values.reshape(parts, 1, group, width), 'seq', split_axis=...  28.9 us
    dynamic_slice x16, local copies, waits for them, and re-layouts, filter_time(): result, unused = lax.scan(add_mode, zeros, (rates.T, weights.T))  13.8 us
  transfers between devices with their start and end apart: 4, of which 4 were waited for; matrix products, arithmetic and copies ran while one was open for 0% of the time, Pallas kernels for 0%

commit v1 on v0

v1 whole, which is shorter than its diff:
```python
import functools

import jax
import jax.numpy as jnp
from jax import lax
from jax.experimental import pallas as pl
from jax.experimental.pallas import tpu as pltpu
from jax.sharding import PartitionSpec as P

BF16 = jnp.bfloat16
F32 = jnp.float32
SUB = 8
LANES = 128
BOTH = ("seq", "chan")


def spread_rows(row):
    return jnp.broadcast_to(row, (SUB, row.shape[-1]))


def source_rows(k_ref, v_ref, x_ref, lanes):
    x_ref[...] = k_ref[:, lanes].astype(F32) * v_ref[:, lanes].astype(F32)
    length = x_ref.shape[0] // SUB
    return [x_ref[pl.ds(i, SUB, stride=length), :] for i in range(length)]


def state_kernel(total, k_ref, v_ref, rate_ref, state_ref, x_ref):
    modes, width = rate_ref.shape
    length = x_ref.shape[0] // SUB
    block = lax.broadcasted_iota(jnp.int32, (SUB, LANES), 0).astype(F32)

    @pl.loop(0, width // LANES)
    def _(chunk):
        lanes = pl.ds(pl.multiple_of(chunk * LANES, LANES), LANES)
        x = source_rows(k_ref, v_ref, x_ref, lanes)
        rate = rate_ref[:, lanes] * (-1.0 / total)
        decay = jnp.exp(rate)
        rows = []
        for m in range(modes):
            d = spread_rows(decay[m : m + 1])
            state = x[0]
            for i in range(1, length):
                state = state * d + x[i]
            weight = jnp.exp(spread_rows(rate[m : m + 1]) * ((SUB - 1.0 - block) * length))
            rows.append(jnp.sum(state * weight, axis=0, keepdims=True))
        state_ref[:, lanes] = jnp.concatenate(rows, axis=0)


def local_kernel(total, q_ref, k_ref, v_ref, res_ref, rate_ref, skip_ref, base_ref, x_ref, y_ref):
    modes, width = rate_ref.shape
    length = x_ref.shape[0] // SUB
    block = lax.broadcasted_iota(jnp.int32, (SUB, LANES), 0)

    @pl.loop(0, width // LANES)
    def _(chunk):
        lanes = pl.ds(pl.multiple_of(chunk * LANES, LANES), LANES)
        x = source_rows(k_ref, v_ref, x_ref, lanes)
        rate = rate_ref[:, lanes] * (-1.0 / total)
        gain = res_ref[:, lanes] * jnp.sqrt(rate_ref[:, lanes] * (2.0 / total))
        decay = jnp.exp(rate)
        y = [spread_rows(skip_ref[:, lanes]) * x[i] for i in range(length)]
        power = gain
        for j in range(length):
            tap = spread_rows(jnp.sum(power, axis=0, keepdims=True))
            for i in range(j, length):
                y[i] = y[i] + tap * x[i - j]
            power = power * decay
        for m in range(modes):
            d = spread_rows(decay[m : m + 1])
            state = x[0]
            for i in range(1, length):
                state = state * d + x[i]
            step = spread_rows(rate[m : m + 1]) * length
            state = jnp.where(block >= 1, pltpu.roll(state, 1, 0), 0.0)
            for shift in (1, 2, 4):
                moved = jnp.where(block >= shift, pltpu.roll(state, shift, 0), 0.0)
                state = state + jnp.exp(step * shift) * moved
            state = state * spread_rows(gain[m : m + 1])
            for i in range(length):
                state = state * d
                y[i] = y[i] + state
        for i in range(length):
            y_ref[pl.ds(i, SUB, stride=length), :] = y[i]
        base_ref[:, lanes] = y_ref[...] * q_ref[:, lanes].astype(F32)


def carry_kernel(total, q_ref, base_ref, state_ref, res_ref, rate_ref, out_ref, y_ref):
    modes, width = rate_ref.shape
    length = y_ref.shape[0] // SUB
    block = lax.broadcasted_iota(jnp.int32, (SUB, LANES), 0).astype(F32)

    @pl.loop(0, width // LANES)
    def _(chunk):
        lanes = pl.ds(pl.multiple_of(chunk * LANES, LANES), LANES)
        rate = rate_ref[:, lanes] * (-1.0 / total)
        start = state_ref[:, lanes] * res_ref[:, lanes] * jnp.sqrt(rate_ref[:, lanes] * (2.0 / total))
        decay = jnp.exp(rate)
        y = [jnp.zeros((SUB, LANES), F32) for i in range(length)]
        for m in range(modes):
            d = spread_rows(decay[m : m + 1])
            state = spread_rows(start[m : m + 1]) * jnp.exp(spread_rows(rate[m : m + 1]) * (block * length))
            for i in range(length):
                state = state * d
                y[i] = y[i] + state
        for i in range(length):
            y_ref[pl.ds(i, SUB, stride=length), :] = y[i]
        out_ref[:, lanes] = (base_ref[:, lanes] + y_ref[...] * q_ref[:, lanes].astype(F32)).astype(BF16)


def run(kernel, out, scratch, ops, *args):
    rows, width = args[0].shape
    return pl.pallas_call(
        kernel,
        out_shape=out,
        in_specs=[pl.BlockSpec(memory_space=pltpu.VMEM)] * len(args),
        out_specs=pl.BlockSpec(memory_space=pltpu.VMEM),
        scratch_shapes=[pltpu.VMEM((rows, LANES), F32)] * scratch,
        compiler_params=pltpu.CompilerParams(vmem_limit_bytes=32 * 1024 * 1024),
        cost_estimate=pl.CostEstimate(
            flops=ops * rows * width, bytes_accessed=6 * rows * width, transcendentals=0
        ),
    )(*args)


def matmul(x, w):
    return jnp.dot(x, w, preferred_element_type=F32)


def general(hidden_of, state, w_out, fade, rows, index, parts):
    states = lax.all_gather(state.astype(BF16), "seq", axis=0)
    entering = jnp.zeros(state.shape, F32)
    for b in range(parts):
        entering = jnp.where(b < index, entering * fade(rows) + states[b].astype(F32), entering)
    hidden = hidden_of(entering)
    spread = matmul(lax.all_gather(hidden, "seq", axis=0, tiled=True), w_out)
    partial_value = lax.all_to_all(spread, "seq", split_axis=0, concat_axis=1, tiled=True)
    summed = lax.psum_scatter(partial_value, "chan", scatter_dimension=1, tiled=True)
    return summed.astype(BF16)


def lined(hidden_of, state, w_out, fade, rows, index):
    depth = 4
    z, y = index // 2, index % 2

    def along(x, moves):
        return lax.ppermute(x, "seq", [(a * 2 + b, c * 2 + b) for a, c in moves for b in range(2)])

    def across(x, planes):
        return lax.ppermute(x, "seq", [(a * 2 + b, a * 2 + 1 - b) for a in planes for b in range(2)])

    def shift(by):
        return [(a, a + by) for a in range(depth) if 0 <= a + by < depth]

    every = range(depth)
    own = state.astype(BF16)
    other = across(own, every)
    first = jnp.where(y == 0, own, other).astype(F32)
    second = jnp.where(y == 0, other, own).astype(F32)
    plane = (first * fade(rows) + second).astype(BF16)
    entering = jnp.zeros(state.shape, F32)
    for by in range(1, depth):
        entering = entering + along(plane, shift(by)).astype(F32) * fade(2 * rows * (by - 1))
    entering = jnp.where(y == 0, entering, entering * fade(rows) + first)
    hidden = hidden_of(entering)

    up1 = along(hidden, shift(1))
    down1 = along(hidden, shift(-1))
    far2 = along(up1, [(1, 2), (2, 3)]) + along(down1, [(1, 0), (2, 1)])
    far3 = along(far2, [(1, 0), (2, 3)])
    swap = {0: 2, 1: 3, 2: 0, 3: 1}
    slots = [
        (hidden, [(a, a) for a in every]),
        (up1, shift(-1)),
        (down1, shift(1)),
        (far2, list(swap.items())),
        (far3, [(0, 3), (3, 0)]),
    ]
    gathered = []
    for block, moves in slots:
        gathered.append((block, moves, 0))
        gathered.append((across(block, [a for a, c in moves]), moves, 1))

    root = (lax.axis_index("chan") % 2) == (z % 2)
    sums = [0.0, 0.0]
    for block, moves, dy in gathered:
        part = matmul(block, w_out)
        pairs = [
            ((a * 2 + b) * 4 + x * 2 + 1 - a % 2, (a * 2 + b) * 4 + x * 2 + a % 2)
            for a, c in moves
            for b in range(2)
            for x in range(2)
        ]
        pair_sum = (part + lax.ppermute(part.astype(BF16), BOTH, pairs).astype(F32)).astype(BF16)
        for side in range(2):
            pairs = [
                (
                    (a * 2 + b) * 4 + ((a // 2) ^ side) * 2 + a % 2,
                    (c * 2 + (b ^ dy)) * 4 + a,
                )
                for a, c in moves
                for b in range(2)
            ]
            sums[dy] = sums[dy] + lax.ppermute(pair_sum, BOTH, pairs).astype(F32)
    low = jnp.where(y == 0, sums[0], sums[1])
    high = jnp.where(y == 0, sums[1], sums[0])
    return jnp.concatenate([low, high], axis=1).astype(BF16)


def local(q_proj, k_proj, v_proj, residues, rates, skip_gain, w_out):
    rows, width = q_proj.shape
    parts = lax.axis_size("seq")
    index = lax.axis_index("seq")
    total = rows * parts
    modes = rates.shape[1]
    res_t, rate_t = residues.T, rates.T
    state = run(
        functools.partial(state_kernel, total),
        jax.ShapeDtypeStruct((modes, width), F32),
        1,
        48,
        k_proj,
        v_proj,
        rate_t,
    )
    base = run(
        functools.partial(local_kernel, total),
        jax.ShapeDtypeStruct((rows, width), F32),
        2,
        100,
        q_proj,
        k_proj,
        v_proj,
        res_t,
        rate_t,
        skip_gain[None, :],
    )

    def hidden_of(entering):
        return run(
            functools.partial(carry_kernel, total),
            jax.ShapeDtypeStruct((rows, width), BF16),
            1,
            32,
            q_proj,
            base,
            entering,
            res_t,
            rate_t,
        )

    def fade(steps):
        return jnp.exp(rate_t * (-float(steps) / total))

    if parts == 8 and lax.axis_size("chan") == 4:
        return lined(hidden_of, state, w_out, fade, rows, index)
    return general(hidden_of, state, w_out, fade, rows, index, parts)


def solution(mesh):
    return jax.shard_map(
        local,
        mesh=mesh,
        in_specs=(
            P("seq", "chan"),
            P("seq", "chan"),
            P("seq", "chan"),
            P("chan", None),
            P("chan", None),
            P("chan"),
            P("chan", "seq"),
        ),
        out_specs=P("seq", "chan"),
        check_vma=False,
    )
```

time: 670 us -> 169 us (0.25)
  the two profiles are of different devices: /device:TPU:10 before, /device:TPU:7 now
where the time goes in v1:
time: 169 us; the launch traced here: 168 us
  starting transfers between devices  74.4 us (44%)
  waiting for transfers between devices  63.6 us (38%)
  Pallas kernels  9.25 us (5%)
  local copies, waits for them, and re-layouts  8.61 us (5%)
  matrix products  7.51 us (4%)
  other arithmetic  3.79 us (2%)
    ppermute x10, starting transfers between devices, lined(): lax.ppermute(part.astype(BF16), BOTH, pairs).astype(F32)  33.1 us
    ppermute x20, waiting for transfers between devices, lined(): sums[dy] = sums[dy] + lax.ppermute(pair_sum, BOTH, pairs).astype(F32)  28.7 us
    ppermute x8, waiting for transfers between devices, along(): lax.ppermute(x, 'seq', [(a * 2 + b, c * 2 + b) for a, c in moves for b in...  19.9 us
    ppermute x20, starting transfers between devices, lined(): sums[dy] = sums[dy] + lax.ppermute(pair_sum, BOTH, pairs).astype(F32)  16 us
    ppermute x6, waiting for transfers between devices, across(): lax.ppermute(x, 'seq', [(a * 2 + b, a * 2 + 1 - b) for a in planes for b...  15 us
    ppermute x8, starting transfers between devices, along(): lax.ppermute(x, 'seq', [(a * 2 + b, c * 2 + b) for a, c in moves for b in...  14.6 us
    ppermute x6, starting transfers between devices, across(): lax.ppermute(x, 'seq', [(a * 2 + b, a * 2 + 1 - b) for a in planes for b...  10.8 us
    pallas_call x3, Pallas kernels, run(): pl.pallas_call(kernel, out_shape=out, in_specs=[pl.BlockSpec(memory_space...  9.25 us
  transfers between devices with their start and end apart: 44, of which 11 were waited for; matrix products, arithmetic and copies ran while one was open for 5% of the time, Pallas kernels for 3%

profile of v1, /device:TPU:7, one launch (start us, length us, event | category | flops | bytes accessed | tf_op | source)
XLA Modules:
  0.0 168.1 jit_solution(10934836893068257236)
XLA Ops:
  0.0 0.9 copy-done
  0.9 1.0 copy-done.3
  1.9 1.0 copy-done.5
  3.0 2.2 %shard_map.74 = f32[16,2048]{1,0:T(8,128)S(1)} custom-call(bf16[128,2048]{1,0:T(8,128)(2,1)S(1)} %copy-done.3, bf16[128,2048]{1,0:T(8,128)(2,1)S(1)} %copy-done.5, f32[16,2048]{1,0:T(8,128)S(1)} %bitcast.25), custom_call_target="tpu_custom_call" | custom-call | flops 12582912 | bytes 1572864 | tf_op jit(solution)/shard_map/pallas_call | solution.py:112
  5.5 2.9 %collective-permute-done = bf16[16,2048]{1,0:T(8,128)(2,1)S(1)} collective-permute-done((bf16[16,2048]{1,0:T(8,128)(2,1)S(1)}, bf16[16,2048]{1,0:T(8,128)(2,1)S(1)}, u32[]{:S(2)}, u32[]{:S(2)}) %collective-permute-start) | collective-permute-done | bytes 65568 | tf_op jit(solution)/shard_map/ppermute | solution.py:149
  8.4 0.9 fusion.1
  9.4 3.2 %collective-permute-start.1 = (bf16[16,2048]{1,0:T(8,128)(2,1)S(1)}, bf16[16,2048]{1,0:T(8,128)(2,1)S(1)}, u32[]{:S(2)}, u32[]{:S(2)}) collective-permute-start(bf16[16,2048]{1,0:T(8,128)(2,1)S(1)} %fusion.1), channel_id=1, source_target_pairs={{0,8},{4,12},{8,16},{12,20},{16,24},{20,28},{1,9},{5,13},{9,17},{1... | collective-permute-start | bytes 196616 | tf_op jit(solution)/shard_map/ppermute | solution.py:146
  12.6 4.2 %collective-permute-start.2 = (bf16[16,2048]{1,0:T(8,128)(2,1)S(1)}, bf16[16,2048]{1,0:T(8,128)(2,1)S(1)}, u32[]{:S(2)}, u32[]{:S(2)}) collective-permute-start(bf16[16,2048]{1,0:T(8,128)(2,1)S(1)} %fusion.1), channel_id=1, source_target_pairs={{0,16},{4,20},{8,24},{12,28},{1,17},{5,21},{9,25},{13,29},{2,18},{... | collective-permute-start | bytes 196616 | tf_op jit(solution)/shard_map/ppermute | solution.py:146
  16.8 1.3 collective-permute-start.3
  18.1 0.9 copy-done.1
  19.0 1.0 copy-done.2
  20.0 1.0 copy-done.4
  21.1 1.0 copy-done.6
  22.1 0.9 copy-done.7
  23.7 5.2 %shard_map.73.base_ref = f32[128,2048]{1,0:T(8,128)S(1)} custom-call(bf16[128,2048]{1,0:T(8,128)(2,1)S(1)} %copy-done.2, bf16[128,2048]{1,0:T(8,128)(2,1)S(1)} %copy-done.4, bf16[128,2048]{1,0:T(8,128)(2,1)S(1)} %copy-done.6, f32[16,2048]{1,0:T(8,128)S(1)} %bitcast.28, f32[16,2048]{1,0:T(8,128)S(1)} %bitcast.26, f32[1,2048]{1,0:T(1,128)S(1)} %bitcast.30), custom_call_target="tpu_custom_call" | custom-call | flops 26214400 | bytes 1572864 | tf_op jit(solution)/shard_map/pallas_call | solution.py:112
  29.1 1.9 %shard_map.75 = bf16[128,2048]{1,0:T(8,128)(2,1)S(1)} custom-call(bf16[128,2048]{1,0:T(8,128)(2,1)S(1)} %copy-done.2, f32[128,2048]{1,0:T(8,128)S(1)} %shard_map.73.base_ref, f32[16,2048]{1,0:T(8,128)S(1)} %fusion.2.state_ref, f32[16,2048]{1,0:T(8,128)S(1)} %bitcast.29, f32[16,2048]{1,0:T(8,128)S(1)} %bitcast.27), custom_call_target="tpu_custom_call" | custom-call | flops 8388608 | bytes 1572864 | tf_op jit(solution)/shard_map/pallas_call | solution.py:112
  30.9 1.3 collective-permute-start.7
  33.0 4.3 %collective-permute-start.4 = (bf16[128,1024]{1,0:T(8,128)(2,1)S(1)}, bf16[128,1024]{1,0:T(8,128)(2,1)S(1)}, u32[]{:S(2)}, u32[]{:S(2)}) collective-permute-start(bf16[128,1024]{1,0:T(8,128)(2,1)S(1)} %get-tuple-element.16), channel_id=1, source_target_pairs={{1,0},{3,2},{5,4},{7,6},{8,9},{10,11},{12,13},{14,15},{17,16},{19,... | collective-permute-start | bytes 786440 | tf_op jit(solution)/shard_map/ppermute | solution.py:193
  37.3 1.3 collective-permute-start.11
  39.0 2.3 %collective-permute-done.7 = bf16[128,2048]{1,0:T(8,128)(2,1)S(1)} collective-permute-done((bf16[128,2048]{1,0:T(8,128)(2,1)S(1)}, bf16[128,2048]{1,0:T(8,128)(2,1)S(1)}, u32[]{:S(2)}, u32[]{:S(2)}) %collective-permute-start.7) | collective-permute-done | bytes 524320 | tf_op jit(solution)/shard_map/ppermute | solution.py:146
  42.8 10.1 %collective-permute-done.11 = bf16[128,2048]{1,0:T(8,128)(2,1)S(1)} collective-permute-done((bf16[128,2048]{1,0:T(8,128)(2,1)S(1)}, bf16[128,2048]{1,0:T(8,128)(2,1)S(1)}, u32[]{:S(2)}, u32[]{:S(2)}) %collective-permute-start.11) | collective-permute-done | bytes 524320 | tf_op jit(solution)/shard_map/ppermute | solution.py:146
  53.6 2.3 %collective-permute-start.12 = (bf16[128,1024]{1,0:T(8,128)(2,1)S(1)}, bf16[128,1024]{1,0:T(8,128)(2,1)S(1)}, u32[]{:S(2)}, u32[]{:S(2)}) collective-permute-start(bf16[128,1024]{1,0:T(8,128)(2,1)S(1)} %get-tuple-element.12), channel_id=1, source_target_pairs={{1,0},{3,2},{5,4},{7,6},{8,9},{10,11},{12,13},{14,15},{17,16},{19,... | collective-permute-start | bytes 786440 | tf_op jit(solution)/shard_map/ppermute | solution.py:193
  55.9 0.8 fusion.12
  56.7 1.3 collective-permute-start.25
  58.7 1.3 collective-permute-start.16
  60.0 5.5 %collective-permute-start.28 = (bf16[128,2048]{1,0:T(8,128)(2,1)S(1)}, bf16[128,2048]{1,0:T(8,128)(2,1)S(1)}, u32[]{:S(2)}, u32[]{:S(2)}) collective-permute-start(bf16[128,2048]{1,0:T(8,128)(2,1)S(1)} %collective-permute-done.7), channel_id=1, source_target_pairs={{8,12},{12,8},{16,20},{20,16},{24,28},{28,24},{9,13},{13,9},{17,21... | collective-permute-start | bytes 1572872 | tf_op jit(solution)/shard_map/ppermute | solution.py:149
  66.4 2.2 %collective-permute-start.32 = (bf16[128,2048]{1,0:T(8,128)(2,1)S(1)}, bf16[128,2048]{1,0:T(8,128)(2,1)S(1)}, u32[]{:S(2)}, u32[]{:S(2)}) collective-permute-start(bf16[128,2048]{1,0:T(8,128)(2,1)S(1)} %collective-permute-done.11), channel_id=1, source_target_pairs={{0,4},{4,0},{8,12},{12,8},{16,20},{20,16},{1,5},{5,1},{9,13},{13,9... | collective-permute-start | bytes 1572872 | tf_op jit(solution)/shard_map/ppermute | solution.py:149
  69.3 5.0 %collective-permute-done.16 = bf16[128,2048]{1,0:T(8,128)(2,1)S(1)} collective-permute-done((bf16[128,2048]{1,0:T(8,128)(2,1)S(1)}, bf16[128,2048]{1,0:T(8,128)(2,1)S(1)}, u32[]{:S(2)}, u32[]{:S(2)}) %collective-permute-start.16) | collective-permute-done | bytes 524320 | tf_op jit(solution)/shard_map/ppermute | solution.py:146
  74.5 1.3 collective-permute-start.20
  77.3 4.2 %collective-permute-done.32 = bf16[128,2048]{1,0:T(8,128)(2,1)S(1)} collective-permute-done((bf16[128,2048]{1,0:T(8,128)(2,1)S(1)}, bf16[128,2048]{1,0:T(8,128)(2,1)S(1)}, u32[]{:S(2)}, u32[]{:S(2)}) %collective-permute-start.32) | collective-permute-done | bytes 524320 | tf_op jit(solution)/shard_map/ppermute | solution.py:149
  82.2 3.1 %collective-permute-start.33 = (bf16[128,1024]{1,0:T(8,128)(2,1)S(1)}, bf16[128,1024]{1,0:T(8,128)(2,1)S(1)}, u32[]{:S(2)}, u32[]{:S(2)}) collective-permute-start(bf16[128,1024]{1,0:T(8,128)(2,1)S(1)} %get-tuple-element.22), channel_id=1, source_target_pairs={{1,0},{3,2},{5,4},{7,6},{8,9},{10,11},{12,13},{14,15},{17,16},{19,... | collective-permute-start | bytes 786440 | tf_op jit(solution)/shard_map/ppermute | solution.py:193
  87.2 2.5 %collective-permute-done.20 = bf16[128,2048]{1,0:T(8,128)(2,1)S(1)} collective-permute-done((bf16[128,2048]{1,0:T(8,128)(2,1)S(1)}, bf16[128,2048]{1,0:T(8,128)(2,1)S(1)}, u32[]{:S(2)}, u32[]{:S(2)}) %collective-permute-start.20) | collective-permute-done | bytes 524320 | tf_op jit(solution)/shard_map/ppermute | solution.py:146
  89.7 2.1 %collective-permute-start.40 = (bf16[128,2048]{1,0:T(8,128)(2,1)S(1)}, bf16[128,2048]{1,0:T(8,128)(2,1)S(1)}, u32[]{:S(2)}, u32[]{:S(2)}) collective-permute-start(bf16[128,2048]{1,0:T(8,128)(2,1)S(1)} %collective-permute-done.20), channel_id=1, source_target_pairs={{0,4},{4,0},{24,28},{28,24},{1,5},{5,1},{25,29},{29,25},{2,6},{6,2... | collective-permute-start | bytes 1572872 | tf_op jit(solution)/shard_map/ppermute | solution.py:149
  91.9 0.8 fusion.3
  92.6 8.0 %collective-permute-done.36 = bf16[128,2048]{1,0:T(8,128)(2,1)S(1)} collective-permute-done((bf16[128,2048]{1,0:T(8,128)(2,1)S(1)}, bf16[128,2048]{1,0:T(8,128)(2,1)S(1)}, u32[]{:S(2)}, u32[]{:S(2)}) %collective-permute-start.36) | collective-permute-done | bytes 524320 | tf_op jit(solution)/shard_map/ppermute | solution.py:149
  104.1 16.8 %collective-permute-start.17 = (bf16[128,1024]{1,0:T(8,128)(2,1)S(1)}, bf16[128,1024]{1,0:T(8,128)(2,1)S(1)}, u32[]{:S(2)}, u32[]{:S(2)}) collective-permute-start(bf16[128,1024]{1,0:T(8,128)(2,1)S(1)} %get-tuple-element.10), channel_id=1, source_target_pairs={{1,0},{3,2},{5,4},{7,6},{8,9},{10,11},{12,13},{14,15},{17,16},{19,... | collective-permute-start | bytes 786440 | tf_op jit(solution)/shard_map/ppermute | solution.py:193
  120.9 1.3 collective-permute-start.37
  125.0 1.3 collective-permute-start.21
  126.4 1.3 collective-permute-start.41
  132.1 1.3 collective-permute-start.22
  133.4 1.3 collective-permute-start.23
  134.7 1.3 collective-permute-start.42
  136.0 1.3 collective-permute-start.43
  137.4 11.4 %collective-permute-done.22 = bf16[128,1024]{1,0:T(8,128)(2,1)S(1)} collective-permute-done((bf16[128,1024]{1,0:T(8,128)(2,1)S(1)}, bf16[128,1024]{1,0:T(8,128)(2,1)S(1)}, u32[]{:S(2)}, u32[]{:S(2)}) %collective-permute-start.22) | collective-permute-done | bytes 262176 | tf_op jit(solution)/shard_map/ppermute | solution.py:203
  148.7 2.7 %collective-permute-done.23 = bf16[128,1024]{1,0:T(8,128)(2,1)S(1)} collective-permute-done((bf16[128,1024]{1,0:T(8,128)(2,1)S(1)}, bf16[128,1024]{1,0:T(8,128)(2,1)S(1)}, u32[]{:S(2)}, u32[]{:S(2)}) %collective-permute-start.23) | collective-permute-done | bytes 262176 | tf_op jit(solution)/shard_map/ppermute | solution.py:203
  151.7 14.2 %collective-permute-done.43 = bf16[128,1024]{1,0:T(8,128)(2,1)S(1)} collective-permute-done((bf16[128,1024]{1,0:T(8,128)(2,1)S(1)}, bf16[128,1024]{1,0:T(8,128)(2,1)S(1)}, u32[]{:S(2)}, u32[]{:S(2)}) %collective-permute-start.43) | collective-permute-done | bytes 262176 | tf_op jit(solution)/shard_map/ppermute | solution.py:203
  166.0 1.2 select_convert_fusion.1
  167.2 0.8 pad_maximum_fusion
  (90 shorter events, 21.7 us)
Async XLA Ops:
  0.9 1.0 copy-start.3
  5.2 3.2 %collective-permute-start = (bf16[16,2048]{1,0:T(8,128)(2,1)S(1)}, bf16[16,2048]{1,0:T(8,128)(2,1)S(1)}, u32[]{:S(2)}, u32[]{:S(2)}) collective-permute-start(bf16[16,2048]{1,0:T(8,128)(2,1)S(1)} %convert_element_type.172), channel_id=1, source_target_pairs={{0,4},{4,0},{8,12},{12,8},{16,20},{20,16},{24,28},{28,24},{1,5},{5... | collective-permute-start | bytes 196616 | tf_op jit(solution)/shard_map/ppermute | solution.py:149
  9.4 19.6 %collective-permute-start.1 = (bf16[16,2048]{1,0:T(8,128)(2,1)S(1)}, bf16[16,2048]{1,0:T(8,128)(2,1)S(1)}, u32[]{:S(2)}, u32[]{:S(2)}) collective-permute-start(bf16[16,2048]{1,0:T(8,128)(2,1)S(1)} %fusion.1), channel_id=1, source_target_pairs={{0,8},{4,12},{8,16},{12,20},{16,24},{20,28},{1,9},{5,13},{9,17},{1... | collective-permute-start | bytes 196616 | tf_op jit(solution)/shard_map/ppermute | solution.py:146
  12.6 16.4 %collective-permute-start.2 = (bf16[16,2048]{1,0:T(8,128)(2,1)S(1)}, bf16[16,2048]{1,0:T(8,128)(2,1)S(1)}, u32[]{:S(2)}, u32[]{:S(2)}) collective-permute-start(bf16[16,2048]{1,0:T(8,128)(2,1)S(1)} %fusion.1), channel_id=1, source_target_pairs={{0,16},{4,20},{8,24},{12,28},{1,17},{5,21},{9,25},{13,29},{2,18},{... | collective-permute-start | bytes 196616 | tf_op jit(solution)/shard_map/ppermute | solution.py:146
  16.8 12.2 %collective-permute-start.3 = (bf16[16,2048]{1,0:T(8,128)(2,1)S(1)}, bf16[16,2048]{1,0:T(8,128)(2,1)S(1)}, u32[]{:S(2)}, u32[]{:S(2)}) collective-permute-start(bf16[16,2048]{1,0:T(8,128)(2,1)S(1)} %fusion.1), channel_id=1, source_target_pairs={{0,24},{4,28},{1,25},{5,29},{2,26},{6,30},{3,27},{7,31}} | collective-permute-start | bytes 196616 | tf_op jit(solution)/shard_map/ppermute | solution.py:146
  19.0 1.0 copy-start.2
  20.0 1.0 copy-start.4
  23.7 8.5 %copy-start.9 = (bf16[2048,1024]{1,0:T(8,128)(2,1)S(1)}, bf16[2048,1024]{1,0:T(8,128)(2,1)}, u32[]{:S(2)}) copy-start(bf16[2048,1024]{1,0:T(8,128)(2,1)} %param.13) | copy-start | bytes 12582916
  30.9 10.4 %collective-permute-start.7 = (bf16[128,2048]{1,0:T(8,128)(2,1)S(1)}, bf16[128,2048]{1,0:T(8,128)(2,1)S(1)}, u32[]{:S(2)}, u32[]{:S(2)}) collective-permute-start(bf16[128,2048]{1,0:T(8,128)(2,1)S(1)} %shard_map.75), channel_id=1, source_target_pairs={{0,8},{4,12},{8,16},{12,20},{16,24},{20,28},{1,9},{5,13},{9,17},{1... | collective-permute-start | bytes 1572872 | tf_op jit(solution)/shard_map/ppermute | solution.py:146
  33.0 5.9 %collective-permute-start.4 = (bf16[128,1024]{1,0:T(8,128)(2,1)S(1)}, bf16[128,1024]{1,0:T(8,128)(2,1)S(1)}, u32[]{:S(2)}, u32[]{:S(2)}) collective-permute-start(bf16[128,1024]{1,0:T(8,128)(2,1)S(1)} %get-tuple-element.16), channel_id=1, source_target_pairs={{1,0},{3,2},{5,4},{7,6},{8,9},{10,11},{12,13},{14,15},{17,16},{19,... | collective-permute-start | bytes 786440 | tf_op jit(solution)/shard_map/ppermute | solution.py:193
  37.3 15.5 %collective-permute-start.11 = (bf16[128,2048]{1,0:T(8,128)(2,1)S(1)}, bf16[128,2048]{1,0:T(8,128)(2,1)S(1)}, u32[]{:S(2)}, u32[]{:S(2)}) collective-permute-start(bf16[128,2048]{1,0:T(8,128)(2,1)S(1)} %shard_map.75), channel_id=1, source_target_pairs={{8,0},{12,4},{16,8},{20,12},{24,16},{28,20},{9,1},{13,5},{17,9},{2... | collective-permute-start | bytes 1572872 | tf_op jit(solution)/shard_map/ppermute | solution.py:146
  38.6 17.3 %collective-permute-start.24 = (bf16[128,2048]{1,0:T(8,128)(2,1)S(1)}, bf16[128,2048]{1,0:T(8,128)(2,1)S(1)}, u32[]{:S(2)}, u32[]{:S(2)}) collective-permute-start(bf16[128,2048]{1,0:T(8,128)(2,1)S(1)} %shard_map.75), channel_id=1, source_target_pairs={{0,4},{4,0},{8,12},{12,8},{16,20},{20,16},{24,28},{28,24},{1,5},{5... | collective-permute-start | bytes 1572872 | tf_op jit(solution)/shard_map/ppermute | solution.py:149
  42.1 17.9 %collective-permute-start.8 = (bf16[128,1024]{1,0:T(8,128)(2,1)S(1)}, bf16[128,1024]{1,0:T(8,128)(2,1)S(1)}, u32[]{:S(2)}, u32[]{:S(2)}) collective-permute-start(bf16[128,1024]{1,0:T(8,128)(2,1)S(1)} %get-tuple-element.14), channel_id=1, source_target_pairs={{8,9},{10,11},{12,13},{14,15},{17,16},{19,18},{21,20},{23,22},{24,... | collective-permute-start | bytes 786440 | tf_op jit(solution)/shard_map/ppermute | solution.py:193
  53.6 12.0 %collective-permute-start.12 = (bf16[128,1024]{1,0:T(8,128)(2,1)S(1)}, bf16[128,1024]{1,0:T(8,128)(2,1)S(1)}, u32[]{:S(2)}, u32[]{:S(2)}) collective-permute-start(bf16[128,1024]{1,0:T(8,128)(2,1)S(1)} %get-tuple-element.12), channel_id=1, source_target_pairs={{1,0},{3,2},{5,4},{7,6},{8,9},{10,11},{12,13},{14,15},{17,16},{19,... | collective-permute-start | bytes 786440 | tf_op jit(solution)/shard_map/ppermute | solution.py:193
  56.7 9.7 %collective-permute-start.25 = (bf16[128,1024]{1,0:T(8,128)(2,1)S(1)}, bf16[128,1024]{1,0:T(8,128)(2,1)S(1)}, u32[]{:S(2)}, u32[]{:S(2)}) collective-permute-start(bf16[128,1024]{1,0:T(8,128)(2,1)S(1)} %get-tuple-element.26), channel_id=1, source_target_pairs={{1,0},{3,2},{5,4},{7,6},{8,9},{10,11},{12,13},{14,15},{17,16},{19,... | collective-permute-start | bytes 786440 | tf_op jit(solution)/shard_map/ppermute | solution.py:193
  58.0 10.6 %collective-permute-start.15 = (bf16[128,2048]{1,0:T(8,128)(2,1)S(1)}, bf16[128,2048]{1,0:T(8,128)(2,1)S(1)}, u32[]{:S(2)}, u32[]{:S(2)}) collective-permute-start(bf16[128,2048]{1,0:T(8,128)(2,1)S(1)} %collective-permute-done.7), channel_id=1, source_target_pairs={{8,16},{12,20},{16,24},{20,28},{9,17},{13,21},{17,25},{21,29},{10,... | collective-permute-start | bytes 1572872 | tf_op jit(solution)/shard_map/ppermute | solution.py:146
  58.7 15.7 %collective-permute-start.16 = (bf16[128,2048]{1,0:T(8,128)(2,1)S(1)}, bf16[128,2048]{1,0:T(8,128)(2,1)S(1)}, u32[]{:S(2)}, u32[]{:S(2)}) collective-permute-start(bf16[128,2048]{1,0:T(8,128)(2,1)S(1)} %collective-permute-done.11), channel_id=1, source_target_pairs={{8,0},{12,4},{16,8},{20,12},{9,1},{13,5},{17,9},{21,13},{10,2},{14... | collective-permute-start | bytes 1572872 | tf_op jit(solution)/shard_map/ppermute | solution.py:146
  60.0 15.8 %collective-permute-start.28 = (bf16[128,2048]{1,0:T(8,128)(2,1)S(1)}, bf16[128,2048]{1,0:T(8,128)(2,1)S(1)}, u32[]{:S(2)}, u32[]{:S(2)}) collective-permute-start(bf16[128,2048]{1,0:T(8,128)(2,1)S(1)} %collective-permute-done.7), channel_id=1, source_target_pairs={{8,12},{12,8},{16,20},{20,16},{24,28},{28,24},{9,13},{13,9},{17,21... | collective-permute-start | bytes 1572872 | tf_op jit(solution)/shard_map/ppermute | solution.py:149
  65.6 36.4 %collective-permute-start.5 = (bf16[128,1024]{1,0:T(8,128)(2,1)S(1)}, bf16[128,1024]{1,0:T(8,128)(2,1)S(1)}, u32[]{:S(2)}, u32[]{:S(2)}) collective-permute-start(bf16[128,1024]{1,0:T(8,128)(2,1)S(1)} %add_convert_fusion.9), channel_id=1, source_target_pairs={{0,0},{4,4},{9,9},{13,13},{18,18},{22,22},{27,27},{31,31}} | collective-permute-start | bytes 786440 | tf_op jit(solution)/shard_map/ppermute | solution.py:203
  66.4 15.0 %collective-permute-start.32 = (bf16[128,2048]{1,0:T(8,128)(2,1)S(1)}, bf16[128,2048]{1,0:T(8,128)(2,1)S(1)}, u32[]{:S(2)}, u32[]{:S(2)}) collective-permute-start(bf16[128,2048]{1,0:T(8,128)(2,1)S(1)} %collective-permute-done.11), channel_id=1, source_target_pairs={{0,4},{4,0},{8,12},{12,8},{16,20},{20,16},{1,5},{5,1},{9,13},{13,9... | collective-permute-start | bytes 1572872 | tf_op jit(solution)/shard_map/ppermute | solution.py:149
  68.7 34.0 %collective-permute-start.6 = (bf16[128,1024]{1,0:T(8,128)(2,1)S(1)}, bf16[128,1024]{1,0:T(8,128)(2,1)S(1)}, u32[]{:S(2)}, u32[]{:S(2)}) collective-permute-start(bf16[128,1024]{1,0:T(8,128)(2,1)S(1)} %add_convert_fusion.9), channel_id=1, source_target_pairs={{2,0},{6,4},{11,9},{15,13},{16,18},{20,22},{25,27},{29,31}} | collective-permute-start | bytes 786440 | tf_op jit(solution)/shard_map/ppermute | solution.py:203
  74.5 15.2 %collective-permute-start.20 = (bf16[128,2048]{1,0:T(8,128)(2,1)S(1)}, bf16[128,2048]{1,0:T(8,128)(2,1)S(1)}, u32[]{:S(2)}, u32[]{:S(2)}) collective-permute-start(bf16[128,2048]{1,0:T(8,128)(2,1)S(1)} %add.116), channel_id=1, source_target_pairs={{8,0},{12,4},{16,24},{20,28},{9,1},{13,5},{17,25},{21,29},{10,2},{... | collective-permute-start | bytes 1572872 | tf_op jit(solution)/shard_map/ppermute | solution.py:146
  76.6 9.5 %collective-permute-start.29 = (bf16[128,1024]{1,0:T(8,128)(2,1)S(1)}, bf16[128,1024]{1,0:T(8,128)(2,1)S(1)}, u32[]{:S(2)}, u32[]{:S(2)}) collective-permute-start(bf16[128,1024]{1,0:T(8,128)(2,1)S(1)} %get-tuple-element.24), channel_id=1, source_target_pairs={{8,9},{10,11},{12,13},{14,15},{17,16},{19,18},{21,20},{23,22},{24,... | collective-permute-start | bytes 786440 | tf_op jit(solution)/shard_map/ppermute | solution.py:193
  82.2 4.6 %collective-permute-start.33 = (bf16[128,1024]{1,0:T(8,128)(2,1)S(1)}, bf16[128,1024]{1,0:T(8,128)(2,1)S(1)}, u32[]{:S(2)}, u32[]{:S(2)}) collective-permute-start(bf16[128,1024]{1,0:T(8,128)(2,1)S(1)} %get-tuple-element.22), channel_id=1, source_target_pairs={{1,0},{3,2},{5,4},{7,6},{8,9},{10,11},{12,13},{14,15},{17,16},{19,... | collective-permute-start | bytes 786440 | tf_op jit(solution)/shard_map/ppermute | solution.py:193
  86.1 17.3 %collective-permute-start.10 = (bf16[128,1024]{1,0:T(8,128)(2,1)S(1)}, bf16[128,1024]{1,0:T(8,128)(2,1)S(1)}, u32[]{:S(2)}, u32[]{:S(2)}) collective-permute-start(bf16[128,1024]{1,0:T(8,128)(2,1)S(1)} %add_convert_fusion.8), channel_id=1, source_target_pairs={{11,1},{15,5},{16,10},{20,14},{25,19},{29,23}} | collective-permute-start | bytes 786440 | tf_op jit(solution)/shard_map/ppermute | solution.py:203
  86.8 13.7 %collective-permute-start.36 = (bf16[128,2048]{1,0:T(8,128)(2,1)S(1)}, bf16[128,2048]{1,0:T(8,128)(2,1)S(1)}, u32[]{:S(2)}, u32[]{:S(2)}) collective-permute-start(bf16[128,2048]{1,0:T(8,128)(2,1)S(1)} %add.116), channel_id=1, source_target_pairs={{0,4},{4,0},{8,12},{12,8},{16,20},{20,16},{24,28},{28,24},{1,5},{5... | collective-permute-start | bytes 1572872 | tf_op jit(solution)/shard_map/ppermute | solution.py:149
  89.7 31.1 %collective-permute-start.40 = (bf16[128,2048]{1,0:T(8,128)(2,1)S(1)}, bf16[128,2048]{1,0:T(8,128)(2,1)S(1)}, u32[]{:S(2)}, u32[]{:S(2)}) collective-permute-start(bf16[128,2048]{1,0:T(8,128)(2,1)S(1)} %collective-permute-done.20), channel_id=1, source_target_pairs={{0,4},{4,0},{24,28},{28,24},{1,5},{5,1},{25,29},{29,25},{2,6},{6,2... | collective-permute-start | bytes 1572872 | tf_op jit(solution)/shard_map/ppermute | solution.py:149
  100.6 3.5 %collective-permute-start.13 = (bf16[128,1024]{1,0:T(8,128)(2,1)S(1)}, bf16[128,1024]{1,0:T(8,128)(2,1)S(1)}, u32[]{:S(2)}, u32[]{:S(2)}) collective-permute-start(bf16[128,1024]{1,0:T(8,128)(2,1)S(1)} %add_convert_fusion.7), channel_id=1, source_target_pairs={{0,8},{4,12},{9,17},{13,21},{18,26},{22,30}} | collective-permute-start | bytes 786440 | tf_op jit(solution)/shard_map/ppermute | solution.py:203
  102.0 20.9 %collective-permute-start.14 = (bf16[128,1024]{1,0:T(8,128)(2,1)S(1)}, bf16[128,1024]{1,0:T(8,128)(2,1)S(1)}, u32[]{:S(2)}, u32[]{:S(2)}) collective-permute-start(bf16[128,1024]{1,0:T(8,128)(2,1)S(1)} %add_convert_fusion.7), channel_id=1, source_target_pairs={{2,8},{6,12},{11,17},{15,21},{16,26},{20,30}} | collective-permute-start | bytes 786440 | tf_op jit(solution)/shard_map/ppermute | solution.py:203
  102.7 20.9 %collective-permute-start.26 = (bf16[128,1024]{1,0:T(8,128)(2,1)S(1)}, bf16[128,1024]{1,0:T(8,128)(2,1)S(1)}, u32[]{:S(2)}, u32[]{:S(2)}) collective-permute-start(bf16[128,1024]{1,0:T(8,128)(2,1)S(1)} %add_convert_fusion.4), channel_id=1, source_target_pairs={{0,4},{4,0},{9,13},{13,9},{18,22},{22,18},{27,31},{31,27}} | collective-permute-start | bytes 786440 | tf_op jit(solution)/shard_map/ppermute | solution.py:203
  103.4 20.9 %collective-permute-start.27 = (bf16[128,1024]{1,0:T(8,128)(2,1)S(1)}, bf16[128,1024]{1,0:T(8,128)(2,1)S(1)}, u32[]{:S(2)}, u32[]{:S(2)}) collective-permute-start(bf16[128,1024]{1,0:T(8,128)(2,1)S(1)} %add_convert_fusion.4), channel_id=1, source_target_pairs={{2,4},{6,0},{11,13},{15,9},{16,22},{20,18},{25,31},{29,27}} | collective-permute-start | bytes 786440 | tf_op jit(solution)/shard_map/ppermute | solution.py:203
  104.1 20.9 %collective-permute-start.17 = (bf16[128,1024]{1,0:T(8,128)(2,1)S(1)}, bf16[128,1024]{1,0:T(8,128)(2,1)S(1)}, u32[]{:S(2)}, u32[]{:S(2)}) collective-permute-start(bf16[128,1024]{1,0:T(8,128)(2,1)S(1)} %get-tuple-element.10), channel_id=1, source_target_pairs={{1,0},{3,2},{5,4},{7,6},{8,9},{10,11},{12,13},{14,15},{17,16},{19,... | collective-permute-start | bytes 786440 | tf_op jit(solution)/shard_map/ppermute | solution.py:193
  120.9 5.5 %collective-permute-start.37 = (bf16[128,1024]{1,0:T(8,128)(2,1)S(1)}, bf16[128,1024]{1,0:T(8,128)(2,1)S(1)}, u32[]{:S(2)}, u32[]{:S(2)}) collective-permute-start(bf16[128,1024]{1,0:T(8,128)(2,1)S(1)} %get-tuple-element.20), channel_id=1, source_target_pairs={{1,0},{3,2},{5,4},{7,6},{8,9},{10,11},{12,13},{14,15},{17,16},{19,... | collective-permute-start | bytes 786440 | tf_op jit(solution)/shard_map/ppermute | solution.py:193
  123.0 4.9 %collective-permute-start.9 = (bf16[128,1024]{1,0:T(8,128)(2,1)S(1)}, bf16[128,1024]{1,0:T(8,128)(2,1)S(1)}, u32[]{:S(2)}, u32[]{:S(2)}) collective-permute-start(bf16[128,1024]{1,0:T(8,128)(2,1)S(1)} %add_convert_fusion.8), channel_id=1, source_target_pairs={{9,1},{13,5},{18,10},{22,14},{27,19},{31,23}} | collective-permute-start | bytes 786440 | tf_op jit(solution)/shard_map/ppermute | solution.py:203
  123.7 4.9 %collective-permute-start.30 = (bf16[128,1024]{1,0:T(8,128)(2,1)S(1)}, bf16[128,1024]{1,0:T(8,128)(2,1)S(1)}, u32[]{:S(2)}, u32[]{:S(2)}) collective-permute-start(bf16[128,1024]{1,0:T(8,128)(2,1)S(1)} %add_convert_fusion.3), channel_id=1, source_target_pairs={{9,5},{13,1},{18,14},{22,10},{27,23},{31,19}} | collective-permute-start | bytes 786440 | tf_op jit(solution)/shard_map/ppermute | solution.py:203
  124.3 4.9 %collective-permute-start.31 = (bf16[128,1024]{1,0:T(8,128)(2,1)S(1)}, bf16[128,1024]{1,0:T(8,128)(2,1)S(1)}, u32[]{:S(2)}, u32[]{:S(2)}) collective-permute-start(bf16[128,1024]{1,0:T(8,128)(2,1)S(1)} %add_convert_fusion.3), channel_id=1, source_target_pairs={{11,5},{15,1},{16,14},{20,10},{25,23},{29,19}} | collective-permute-start | bytes 786440 | tf_op jit(solution)/shard_map/ppermute | solution.py:203
  125.0 4.9 %collective-permute-start.21 = (bf16[128,1024]{1,0:T(8,128)(2,1)S(1)}, bf16[128,1024]{1,0:T(8,128)(2,1)S(1)}, u32[]{:S(2)}, u32[]{:S(2)}) collective-permute-start(bf16[128,1024]{1,0:T(8,128)(2,1)S(1)} %get-tuple-element.8), channel_id=1, source_target_pairs={{1,0},{3,2},{5,4},{7,6},{24,25},{26,27},{28,29},{30,31}} | collective-permute-start | bytes 786440 | tf_op jit(solution)/shard_map/ppermute | solution.py:193
  126.4 4.2 %collective-permute-start.41 = (bf16[128,1024]{1,0:T(8,128)(2,1)S(1)}, bf16[128,1024]{1,0:T(8,128)(2,1)S(1)}, u32[]{:S(2)}, u32[]{:S(2)}) collective-permute-start(bf16[128,1024]{1,0:T(8,128)(2,1)S(1)} %get-tuple-element.18), channel_id=1, source_target_pairs={{1,0},{3,2},{5,4},{7,6},{24,25},{26,27},{28,29},{30,31}} | collective-permute-start | bytes 786440 | tf_op jit(solution)/shard_map/ppermute | solution.py:193
  127.8 3.6 %collective-permute-start.34 = (bf16[128,1024]{1,0:T(8,128)(2,1)S(1)}, bf16[128,1024]{1,0:T(8,128)(2,1)S(1)}, u32[]{:S(2)}, u32[]{:S(2)}) collective-permute-start(bf16[128,1024]{1,0:T(8,128)(2,1)S(1)} %add_convert_fusion.2), channel_id=1, source_target_pairs={{0,12},{4,8},{9,21},{13,17},{18,30},{22,26}} | collective-permute-start | bytes 786440 | tf_op jit(solution)/shard_map/ppermute | solution.py:203
  128.5 3.6 %collective-permute-start.35 = (bf16[128,1024]{1,0:T(8,128)(2,1)S(1)}, bf16[128,1024]{1,0:T(8,128)(2,1)S(1)}, u32[]{:S(2)}, u32[]{:S(2)}) collective-permute-start(bf16[128,1024]{1,0:T(8,128)(2,1)S(1)} %add_convert_fusion.2), channel_id=1, source_target_pairs={{2,12},{6,8},{11,21},{15,17},{16,30},{20,26}} | collective-permute-start | bytes 786440 | tf_op jit(solution)/shard_map/ppermute | solution.py:203
  129.2 4.2 %collective-permute-start.18 = (bf16[128,1024]{1,0:T(8,128)(2,1)S(1)}, bf16[128,1024]{1,0:T(8,128)(2,1)S(1)}, u32[]{:S(2)}, u32[]{:S(2)}) collective-permute-start(bf16[128,1024]{1,0:T(8,128)(2,1)S(1)} %add_convert_fusion.6), channel_id=1, source_target_pairs={{0,16},{4,20},{9,25},{13,29},{18,2},{22,6},{27,11},{31,15}} | collective-permute-start | bytes 786440 | tf_op jit(solution)/shard_map/ppermute | solution.py:203
  129.9 4.8 %collective-permute-start.19 = (bf16[128,1024]{1,0:T(8,128)(2,1)S(1)}, bf16[128,1024]{1,0:T(8,128)(2,1)S(1)}, u32[]{:S(2)}, u32[]{:S(2)}) collective-permute-start(bf16[128,1024]{1,0:T(8,128)(2,1)S(1)} %add_convert_fusion.6), channel_id=1, source_target_pairs={{2,16},{6,20},{11,25},{15,29},{16,2},{20,6},{25,11},{29,15}} | collective-permute-start | bytes 786440 | tf_op jit(solution)/shard_map/ppermute | solution.py:203
  130.6 5.4 %collective-permute-start.38 = (bf16[128,1024]{1,0:T(8,128)(2,1)S(1)}, bf16[128,1024]{1,0:T(8,128)(2,1)S(1)}, u32[]{:S(2)}, u32[]{:S(2)}) collective-permute-start(bf16[128,1024]{1,0:T(8,128)(2,1)S(1)} %add_convert_fusion.1), channel_id=1, source_target_pairs={{0,20},{4,16},{9,29},{13,25},{18,6},{22,2},{27,15},{31,11}} | collective-permute-start | bytes 786440 | tf_op jit(solution)/shard_map/ppermute | solution.py:203
  131.4 5.9 %collective-permute-start.39 = (bf16[128,1024]{1,0:T(8,128)(2,1)S(1)}, bf16[128,1024]{1,0:T(8,128)(2,1)S(1)}, u32[]{:S(2)}, u32[]{:S(2)}) collective-permute-start(bf16[128,1024]{1,0:T(8,128)(2,1)S(1)} %add_convert_fusion.1), channel_id=1, source_target_pairs={{2,20},{6,16},{11,29},{15,25},{16,6},{20,2},{25,15},{29,11}} | collective-permute-start | bytes 786440 | tf_op jit(solution)/shard_map/ppermute | solution.py:203
  132.1 16.6 %collective-permute-start.22 = (bf16[128,1024]{1,0:T(8,128)(2,1)S(1)}, bf16[128,1024]{1,0:T(8,128)(2,1)S(1)}, u32[]{:S(2)}, u32[]{:S(2)}) collective-permute-start(bf16[128,1024]{1,0:T(8,128)(2,1)S(1)} %add_convert_fusion.5), channel_id=1, source_target_pairs={{0,24},{4,28},{27,3},{31,7}} | collective-permute-start | bytes 786440 | tf_op jit(solution)/shard_map/ppermute | solution.py:203
  133.4 18.0 %collective-permute-start.23 = (bf16[128,1024]{1,0:T(8,128)(2,1)S(1)}, bf16[128,1024]{1,0:T(8,128)(2,1)S(1)}, u32[]{:S(2)}, u32[]{:S(2)}) collective-permute-start(bf16[128,1024]{1,0:T(8,128)(2,1)S(1)} %add_convert_fusion.5), channel_id=1, source_target_pairs={{2,24},{6,28},{25,3},{29,7}} | collective-permute-start | bytes 786440 | tf_op jit(solution)/shard_map/ppermute | solution.py:203
  134.7 17.0 %collective-permute-start.42 = (bf16[128,1024]{1,0:T(8,128)(2,1)S(1)}, bf16[128,1024]{1,0:T(8,128)(2,1)S(1)}, u32[]{:S(2)}, u32[]{:S(2)}) collective-permute-start(bf16[128,1024]{1,0:T(8,128)(2,1)S(1)} %add_convert_fusion), channel_id=1, source_target_pairs={{0,28},{4,24},{27,7},{31,3}} | collective-permute-start | bytes 786440 | tf_op jit(solution)/shard_map/ppermute | solution.py:203
  136.0 30.0 %collective-permute-start.43 = (bf16[128,1024]{1,0:T(8,128)(2,1)S(1)}, bf16[128,1024]{1,0:T(8,128)(2,1)S(1)}, u32[]{:S(2)}, u32[]{:S(2)}) collective-permute-start(bf16[128,1024]{1,0:T(8,128)(2,1)S(1)} %add_convert_fusion), channel_id=1, source_target_pairs={{2,28},{6,24},{25,7},{29,3}} | collective-permute-start | bytes 786440 | tf_op jit(solution)/shard_map/ppermute | solution.py:203
  (6 other events, 5.5 us)

commit v2 on v1

--- a/solution.py
+++ b/solution.py
@@ -109,13 +109,15 @@
 
 def run(kernel, out, scratch, ops, *args):
     rows, width = args[0].shape
+    part = min(width, 4 * LANES)
     return pl.pallas_call(
         kernel,
+        grid=(width // part,),
         out_shape=out,
-        in_specs=[pl.BlockSpec(memory_space=pltpu.VMEM)] * len(args),
-        out_specs=pl.BlockSpec(memory_space=pltpu.VMEM),
+        in_specs=[pl.BlockSpec((arg.shape[0], part), lambda i: (0, i)) for arg in args],
+        out_specs=pl.BlockSpec((out.shape[0], part), lambda i: (0, i)),
         scratch_shapes=[pltpu.VMEM((rows, LANES), F32)] * scratch,
-        compiler_params=pltpu.CompilerParams(vmem_limit_bytes=32 * 1024 * 1024),
+        compiler_params=pltpu.CompilerParams(vmem_limit_bytes=16 * 1024 * 1024),
         cost_estimate=pl.CostEstimate(
             flops=ops * rows * width, bytes_accessed=6 * rows * width, transcendentals=0
         ),
@@ -163,47 +165,52 @@
     entering = jnp.where(y == 0, entering, entering * fade(rows) + first)
     hidden = hidden_of(entering)
 
+    chan = lax.axis_index("chan")
+    side, core = chan // 2, chan % 2
     up1 = along(hidden, shift(1))
     down1 = along(hidden, shift(-1))
-    far2 = along(up1, [(1, 2), (2, 3)]) + along(down1, [(1, 0), (2, 1)])
-    far3 = along(far2, [(1, 0), (2, 3)])
-    swap = {0: 2, 1: 3, 2: 0, 3: 1}
-    slots = [
-        (hidden, [(a, a) for a in every]),
-        (up1, shift(-1)),
-        (down1, shift(1)),
-        (far2, list(swap.items())),
-        (far3, [(0, 3), (3, 0)]),
-    ]
-    gathered = []
-    for block, moves in slots:
-        gathered.append((block, moves, 0))
-        gathered.append((across(block, [a for a, c in moves]), moves, 1))
-
-    root = (lax.axis_index("chan") % 2) == (z % 2)
-    sums = [0.0, 0.0]
-    for block, moves, dy in gathered:
-        part = matmul(block, w_out)
-        pairs = [
-            ((a * 2 + b) * 4 + x * 2 + 1 - a % 2, (a * 2 + b) * 4 + x * 2 + a % 2)
-            for a, c in moves
-            for b in range(2)
-            for x in range(2)
-        ]
-        pair_sum = (part + lax.ppermute(part.astype(BF16), BOTH, pairs).astype(F32)).astype(BF16)
-        for side in range(2):
+    near_y = across(hidden, every)
+    one = jnp.where(z % 2 == 1, up1, down1)
+    up2 = along(up1, [(1, 2), (2, 3)])
+    down2 = along(down1, [(1, 0), (2, 1)])
+    one_y = across(one, every)
+    two = jnp.where(z >= 2, up2, down2)
+    far3 = along(two, [(1, 0), (2, 3)])
+    two_y = across(two, every)
+    three = jnp.where(z % 3 == 0, far3, jnp.where(z == 1, down1, up1))
+    three_y = across(three, every)
+
+    flip = [(c, c ^ 1) for c in range(4)]
+    turn = [(c, c ^ 2) for c in range(4)]
+
+    def reduced(group, even, odd):
+        even = [matmul(block, w_out) for block in even]
+        odd = [matmul(block, w_out) for block in odd]
+        keep = jnp.stack([jnp.where(core == 0, a, b) for a, b in zip(even, odd)])
+        send = jnp.stack([jnp.where(core == 0, b, a).astype(BF16) for a, b in zip(even, odd)])
+        keep = keep + lax.ppermute(send, "chan", flip).astype(F32)
+        send = jnp.where(side == 0, keep[1], keep[0]).astype(BF16)
+        keep = jnp.where(side == 0, keep[0], keep[1])
+        tile = (keep + lax.ppermute(send, "chan", turn).astype(F32)).astype(BF16)
+        arrived = []
+        for x in range(2):
             pairs = [
-                (
-                    (a * 2 + b) * 4 + ((a // 2) ^ side) * 2 + a % 2,
-                    (c * 2 + (b ^ dy)) * 4 + a,
-                )
-                for a, c in moves
+                ((a * 2 + b) * 4 + x * 2 + k, ((a ^ (group + k)) * 2 + (b ^ x)) * 4 + a)
+                for a in every
                 for b in range(2)
+                for k in range(2)
             ]
-            sums[dy] = sums[dy] + lax.ppermute(pair_sum, BOTH, pairs).astype(F32)
-    low = jnp.where(y == 0, sums[0], sums[1])
-    high = jnp.where(y == 0, sums[1], sums[0])
-    return jnp.concatenate([low, high], axis=1).astype(BF16)
+            arrived.append(lax.ppermute(tile, BOTH, pairs))
+        return arrived
+
+    close = reduced(0, [hidden, near_y], [one, one_y])
+    remote = reduced(2, [two, two_y], [three, three_y])
+    close_here = (z ^ chan) < 2
+    same = jnp.where(close_here, close[0], remote[0])
+    cross = jnp.where(close_here, close[1], remote[1])
+    low = jnp.where(y == 0, same, cross)
+    high = jnp.where(y == 0, cross, same)
+    return jnp.concatenate([low, high], axis=1)
 
 
 def local(q_proj, k_proj, v_proj, residues, rates, skip_gain, w_out):

time: 169 us -> 129 us (0.76)
  the two profiles are of different devices: /device:TPU:7 before, /device:TPU:2 now
where the time goes in v2:
time: 129 us
  waiting for transfers between devices  59.8 us (46%)
  starting transfers between devices  38.6 us (30%)
  Pallas kernels  9.67 us (7%)
  local copies, waits for them, and re-layouts  8.61 us (7%)
  matrix products  7.95 us (6%)
  other arithmetic  3.31 us (3%)
    ppermute x8, waiting for transfers between devices, along(): lax.ppermute(x, 'seq', [(a * 2 + b, c * 2 + b) for a, c in moves for b in...  21.9 us
    ppermute x5, waiting for transfers between devices, across(): lax.ppermute(x, 'seq', [(a * 2 + b, a * 2 + 1 - b) for a in planes for b...  19.8 us
    ppermute x8, starting transfers between devices, along(): lax.ppermute(x, 'seq', [(a * 2 + b, c * 2 + b) for a, c in moves for b in...  18.4 us
    ppermute x4, starting transfers between devices, reduced(): arrived.append(lax.ppermute(tile, BOTH, pairs))  11.9 us
    ppermute x4, waiting for transfers between devices, reduced(): arrived.append(lax.ppermute(tile, BOTH, pairs))  10.4 us
    pallas_call x3, Pallas kernels, run(): pl.pallas_call(kernel, grid=(width // part,), out_shape=out, in_specs=[pl...  9.67 us
    unnamed x20, local copies, waits for them, and re-layouts  8.61 us
    dot_general x8, matrix products, matmul(): return jnp.dot(x, w, preferred_element_type=F32)  7.95 us
  transfers between devices with their start and end apart: 21, of which 10 were waited for; matrix products, arithmetic and copies ran while one was open for 7% of the time, Pallas kernels for 4%

profile of v2, /device:TPU:2, one launch (start us, length us, event | category | flops | bytes accessed | tf_op | source)
XLA Modules:
  0.0 128.6 jit_solution(18021327507106867729)
XLA Ops:
  0.0 0.9 copy-done
  0.9 1.0 copy-done.3
  1.9 1.0 copy-done.5
  3.0 2.3 %shard_map.74 = f32[16,2048]{1,0:T(8,128)S(1)} custom-call(bf16[128,2048]{1,0:T(8,128)(2,1)S(1)} %copy-done.3, bf16[128,2048]{1,0:T(8,128)(2,1)S(1)} %copy-done.5, f32[16,2048]{1,0:T(8,128)S(1)} %bitcast.49), custom_call_target="tpu_custom_call" | custom-call | flops 12582912 | bytes 1572864 | tf_op jit(solution)/shard_map/pallas_call | solution.py:113
  5.3 1.6 %collective-permute-start = (bf16[16,2048]{1,0:T(8,128)(2,1)S(1)}, bf16[16,2048]{1,0:T(8,128)(2,1)S(1)}, u32[]{:S(2)}, u32[]{:S(2)}) collective-permute-start(bf16[16,2048]{1,0:T(8,128)(2,1)S(1)} %convert_element_type.63), channel_id=1, source_target_pairs={{0,4},{4,0},{8,12},{12,8},{16,20},{20,16},{24,28},{28,24},{1,5},{5... | collective-permute-start | bytes 196616 | tf_op jit(solution)/shard_map/ppermute | solution.py:151
  6.9 2.7 %collective-permute-done = bf16[16,2048]{1,0:T(8,128)(2,1)S(1)} collective-permute-done((bf16[16,2048]{1,0:T(8,128)(2,1)S(1)}, bf16[16,2048]{1,0:T(8,128)(2,1)S(1)}, u32[]{:S(2)}, u32[]{:S(2)}) %collective-permute-start) | collective-permute-done | bytes 65568 | tf_op jit(solution)/shard_map/ppermute | solution.py:151
  9.6 0.9 fusion.9
  10.6 5.5 %collective-permute-start.3 = (bf16[16,2048]{1,0:T(8,128)(2,1)S(1)}, bf16[16,2048]{1,0:T(8,128)(2,1)S(1)}, u32[]{:S(2)}, u32[]{:S(2)}) collective-permute-start(bf16[16,2048]{1,0:T(8,128)(2,1)S(1)} %fusion.9), channel_id=1, source_target_pairs={{0,24},{4,28},{1,25},{5,29},{2,26},{6,30},{3,27},{7,31}} | collective-permute-start | bytes 196616 | tf_op jit(solution)/shard_map/ppermute | solution.py:148
  16.1 1.3 %collective-permute-start.2 = (bf16[16,2048]{1,0:T(8,128)(2,1)S(1)}, bf16[16,2048]{1,0:T(8,128)(2,1)S(1)}, u32[]{:S(2)}, u32[]{:S(2)}) collective-permute-start(bf16[16,2048]{1,0:T(8,128)(2,1)S(1)} %fusion.9), channel_id=1, source_target_pairs={{0,16},{4,20},{8,24},{12,28},{1,17},{5,21},{9,25},{13,29},{2,18},{... | collective-permute-start | bytes 196616 | tf_op jit(solution)/shard_map/ppermute | solution.py:148
  17.4 2.5 %collective-permute-start.1 = (bf16[16,2048]{1,0:T(8,128)(2,1)S(1)}, bf16[16,2048]{1,0:T(8,128)(2,1)S(1)}, u32[]{:S(2)}, u32[]{:S(2)}) collective-permute-start(bf16[16,2048]{1,0:T(8,128)(2,1)S(1)} %fusion.9), channel_id=1, source_target_pairs={{0,8},{4,12},{8,16},{12,20},{16,24},{20,28},{1,9},{5,13},{9,17},{1... | collective-permute-start | bytes 196616 | tf_op jit(solution)/shard_map/ppermute | solution.py:148
  19.9 0.9 copy-done.1
  20.8 1.0 copy-done.2
  21.8 1.0 copy-done.4
  22.9 1.0 copy-done.6
  23.9 0.9 copy-done.7
  24.8 0.7 copy-done.8
  25.5 5.3 %shard_map.73.base_ref = f32[128,2048]{1,0:T(8,128)S(1)} custom-call(bf16[128,2048]{1,0:T(8,128)(2,1)S(1)} %copy-done.2, bf16[128,2048]{1,0:T(8,128)(2,1)S(1)} %copy-done.4, bf16[128,2048]{1,0:T(8,128)(2,1)S(1)} %copy-done.6, f32[16,2048]{1,0:T(8,128)S(1)} %bitcast.52, f32[16,2048]{1,0:T(8,128)S(1)} %bitcast.50, f32[1,2048]{1,0:T(1,128)S(1)} %bitcast.54), custom_call_target="tpu_custom_call" | custom-call | flops 26214400 | bytes 1572864 | tf_op jit(solution)/shard_map/pallas_call | solution.py:113
  31.0 2.1 %shard_map.75 = bf16[128,2048]{1,0:T(8,128)(2,1)S(1)} custom-call(bf16[128,2048]{1,0:T(8,128)(2,1)S(1)} %copy-done.2, f32[128,2048]{1,0:T(8,128)S(1)} %shard_map.73.base_ref, f32[16,2048]{1,0:T(8,128)S(1)} %fusion.10.state_ref, f32[16,2048]{1,0:T(8,128)S(1)} %bitcast.53, f32[16,2048]{1,0:T(8,128)S(1)} %bitcast.51), custom_call_target="tpu_custom_call" | custom-call | flops 8388608 | bytes 1572864 | tf_op jit(solution)/shard_map/pallas_call | solution.py:113
  33.1 1.3 %collective-permute-start.5 = (bf16[128,2048]{1,0:T(8,128)(2,1)S(1)}, bf16[128,2048]{1,0:T(8,128)(2,1)S(1)}, u32[]{:S(2)}, u32[]{:S(2)}) collective-permute-start(bf16[128,2048]{1,0:T(8,128)(2,1)S(1)} %shard_map.75), channel_id=1, source_target_pairs={{8,0},{12,4},{16,8},{20,12},{24,16},{28,20},{9,1},{13,5},{17,9},{2... | collective-permute-start | bytes 1572872 | tf_op jit(solution)/shard_map/ppermute | solution.py:148
  34.4 4.6 %collective-permute-start.4 = (bf16[128,2048]{1,0:T(8,128)(2,1)S(1)}, bf16[128,2048]{1,0:T(8,128)(2,1)S(1)}, u32[]{:S(2)}, u32[]{:S(2)}) collective-permute-start(bf16[128,2048]{1,0:T(8,128)(2,1)S(1)} %shard_map.75), channel_id=1, source_target_pairs={{0,8},{4,12},{8,16},{12,20},{16,24},{20,28},{1,9},{5,13},{9,17},{1... | collective-permute-start | bytes 1572872 | tf_op jit(solution)/shard_map/ppermute | solution.py:148
  39.0 8.0 %collective-permute-done.5 = bf16[128,2048]{1,0:T(8,128)(2,1)S(1)} collective-permute-done((bf16[128,2048]{1,0:T(8,128)(2,1)S(1)}, bf16[128,2048]{1,0:T(8,128)(2,1)S(1)}, u32[]{:S(2)}, u32[]{:S(2)}) %collective-permute-start.5) | collective-permute-done | bytes 524320 | tf_op jit(solution)/shard_map/ppermute | solution.py:148
  46.9 1.3 collective-permute-start.12
  48.2 0.7 collective-permute-start.11
  49.0 1.6 %collective-permute-start.6 = (bf16[128,2048]{1,0:T(8,128)(2,1)S(1)}, bf16[128,2048]{1,0:T(8,128)(2,1)S(1)}, u32[]{:S(2)}, u32[]{:S(2)}) collective-permute-start(bf16[128,2048]{1,0:T(8,128)(2,1)S(1)} %shard_map.75), channel_id=1, source_target_pairs={{0,4},{4,0},{8,12},{12,8},{16,20},{20,16},{24,28},{28,24},{1,5},{5... | collective-permute-start | bytes 1572872 | tf_op jit(solution)/shard_map/ppermute | solution.py:151
  50.6 2.9 %fusion.11 = f32[128,1024]{1,0:T(8,128)S(1)} fusion(bf16[128,2048]{1,0:T(8,128)(2,1)S(1)} %shard_map.75, bf16[2048,1024]{1,0:T(8,128)(2,1)} %param.13), kind=kOutput, calls=%fused_computation.39 | convolution fusion | flops 536870912 | bytes 5242880 | tf_op jit(solution)/shard_map/dot_general | solution.py:128
  53.5 6.3 %collective-permute-done.12 = bf16[128,2048]{1,0:T(8,128)(2,1)S(1)} collective-permute-done((bf16[128,2048]{1,0:T(8,128)(2,1)S(1)}, bf16[128,2048]{1,0:T(8,128)(2,1)S(1)}, u32[]{:S(2)}, u32[]{:S(2)}) %collective-permute-start.12) | collective-permute-done | bytes 524320 | tf_op jit(solution)/shard_map/ppermute | solution.py:148
  59.9 1.3 %collective-permute-start.13 = (bf16[128,2048]{1,0:T(8,128)(2,1)S(1)}, bf16[128,2048]{1,0:T(8,128)(2,1)S(1)}, u32[]{:S(2)}, u32[]{:S(2)}) collective-permute-start(bf16[128,2048]{1,0:T(8,128)(2,1)S(1)} %broadcast_select_fusion), channel_id=1, source_target_pairs={{8,0},{12,4},{16,24},{20,28},{9,1},{13,5},{17,25},{21,29},{10,2},{... | collective-permute-start | bytes 1572872 | tf_op jit(solution)/shard_map/ppermute | solution.py:148
  61.2 0.7 fusion.13
  62.0 1.6 %collective-permute-start.14 = (bf16[128,2048]{1,0:T(8,128)(2,1)S(1)}, bf16[128,2048]{1,0:T(8,128)(2,1)S(1)}, u32[]{:S(2)}, u32[]{:S(2)}) collective-permute-start(bf16[128,2048]{1,0:T(8,128)(2,1)S(1)} %broadcast_select_fusion), channel_id=1, source_target_pairs={{0,4},{4,0},{8,12},{12,8},{16,20},{20,16},{24,28},{28,24},{1,5},{5... | collective-permute-start | bytes 1572872 | tf_op jit(solution)/shard_map/ppermute | solution.py:151
  63.5 0.7 fusion.15
  64.3 7.6 %collective-permute-done.13 = bf16[128,2048]{1,0:T(8,128)(2,1)S(1)} collective-permute-done((bf16[128,2048]{1,0:T(8,128)(2,1)S(1)}, bf16[128,2048]{1,0:T(8,128)(2,1)S(1)}, u32[]{:S(2)}, u32[]{:S(2)}) %collective-permute-start.13) | collective-permute-done | bytes 524320 | tf_op jit(solution)/shard_map/ppermute | solution.py:148
  72.0 0.7 fusion.16
  72.7 1.6 %collective-permute-start.15 = (bf16[128,2048]{1,0:T(8,128)(2,1)S(1)}, bf16[128,2048]{1,0:T(8,128)(2,1)S(1)}, u32[]{:S(2)}, u32[]{:S(2)}) collective-permute-start(bf16[128,2048]{1,0:T(8,128)(2,1)S(1)} %get-tuple-element.7), channel_id=1, source_target_pairs={{0,4},{4,0},{8,12},{12,8},{16,20},{20,16},{24,28},{28,24},{1,5},{5... | collective-permute-start | bytes 1572872 | tf_op jit(solution)/shard_map/ppermute | solution.py:151
  74.3 0.7 fusion.12
  75.9 0.7 fusion.17
  76.7 11.0 %collective-permute-done.15 = bf16[128,2048]{1,0:T(8,128)(2,1)S(1)} collective-permute-done((bf16[128,2048]{1,0:T(8,128)(2,1)S(1)}, bf16[128,2048]{1,0:T(8,128)(2,1)S(1)}, u32[]{:S(2)}, u32[]{:S(2)}) %collective-permute-start.15) | collective-permute-done | bytes 524320 | tf_op jit(solution)/shard_map/ppermute | solution.py:151
  87.7 0.7 fusion.18
  88.6 6.0 %collective-permute-done.7 = bf16[128,2048]{1,0:T(8,128)(2,1)S(1)} collective-permute-done((bf16[128,2048]{1,0:T(8,128)(2,1)S(1)}, bf16[128,2048]{1,0:T(8,128)(2,1)S(1)}, u32[]{:S(2)}, u32[]{:S(2)}) %collective-permute-start.7) | collective-permute-done | bytes 524320 | tf_op jit(solution)/shard_map/ppermute | solution.py:151
  94.6 0.7 fusion.14
  96.5 0.9 collective-permute-done.8
  98.2 6.8 %collective-permute-done.17 = bf16[128,1024]{1,0:T(8,128)(2,1)S(1)} collective-permute-done((bf16[128,1024]{1,0:T(8,128)(2,1)S(1)}, bf16[128,1024]{1,0:T(8,128)(2,1)S(1)}, u32[]{:S(2)}, u32[]{:S(2)}) %collective-permute-start.17) | collective-permute-done | bytes 262176 | tf_op jit(solution)/shard_map/ppermute | solution.py:194
  105.2 7.5 %collective-permute-start.20 = (bf16[128,1024]{1,0:T(8,128)(2,1)S(1)}, bf16[128,1024]{1,0:T(8,128)(2,1)S(1)}, u32[]{:S(2)}, u32[]{:S(2)}) collective-permute-start(bf16[128,1024]{1,0:T(8,128)(2,1)S(1)} %fusion), channel_id=1, source_target_pairs={{2,20},{3,28},{6,16},{7,24},{10,29},{11,21},{14,25},{15,17},{18,6}... | collective-permute-start | bytes 786440 | tf_op jit(solution)/shard_map/ppermute | solution.py:203
  112.6 1.3 %collective-permute-start.18 = (bf16[128,1024]{1,0:T(8,128)(2,1)S(1)}, bf16[128,1024]{1,0:T(8,128)(2,1)S(1)}, u32[]{:S(2)}, u32[]{:S(2)}) collective-permute-start(bf16[128,1024]{1,0:T(8,128)(2,1)S(1)} %fusion), channel_id=1, source_target_pairs={{0,16},{1,24},{4,20},{5,28},{8,25},{9,17},{12,29},{13,21},{16,2},{... | collective-permute-start | bytes 786440 | tf_op jit(solution)/shard_map/ppermute | solution.py:203
  114.1 2.5 %collective-permute-start.19 = (bf16[128,1024]{1,0:T(8,128)(2,1)S(1)}, bf16[128,1024]{1,0:T(8,128)(2,1)S(1)}, u32[]{:S(2)}, u32[]{:S(2)}) collective-permute-start(bf16[128,1024]{1,0:T(8,128)(2,1)S(1)} %fusion.1), channel_id=1, source_target_pairs={{2,4},{3,12},{6,0},{7,8},{10,13},{11,5},{14,9},{15,1},{18,22},{19,... | collective-permute-start | bytes 786440 | tf_op jit(solution)/shard_map/ppermute | solution.py:203
  116.6 0.7 collective-permute-start.10
  117.3 5.6 %collective-permute-done.20 = bf16[128,1024]{1,0:T(8,128)(2,1)S(1)} collective-permute-done((bf16[128,1024]{1,0:T(8,128)(2,1)S(1)}, bf16[128,1024]{1,0:T(8,128)(2,1)S(1)}, u32[]{:S(2)}, u32[]{:S(2)}) %collective-permute-start.20) | collective-permute-done | bytes 262176 | tf_op jit(solution)/shard_map/ppermute | solution.py:203
  122.9 4.8 %collective-permute-done.18 = bf16[128,1024]{1,0:T(8,128)(2,1)S(1)} collective-permute-done((bf16[128,1024]{1,0:T(8,128)(2,1)S(1)}, bf16[128,1024]{1,0:T(8,128)(2,1)S(1)}, u32[]{:S(2)}, u32[]{:S(2)}) %collective-permute-start.18) | collective-permute-done | bytes 262176 | tf_op jit(solution)/shard_map/ppermute | solution.py:203
  127.7 0.8 pad_maximum_fusion.2
  (47 shorter events, 3.5 us)
Async XLA Ops:
  0.0 0.9 copy-start
  0.9 1.0 copy-start.3
  1.9 1.0 copy-start.5
  5.3 4.3 %collective-permute-start = (bf16[16,2048]{1,0:T(8,128)(2,1)S(1)}, bf16[16,2048]{1,0:T(8,128)(2,1)S(1)}, u32[]{:S(2)}, u32[]{:S(2)}) collective-permute-start(bf16[16,2048]{1,0:T(8,128)(2,1)S(1)} %convert_element_type.63), channel_id=1, source_target_pairs={{0,4},{4,0},{8,12},{12,8},{16,20},{20,16},{24,28},{28,24},{1,5},{5... | collective-permute-start | bytes 196616 | tf_op jit(solution)/shard_map/ppermute | solution.py:151
  10.6 20.3 %collective-permute-start.3 = (bf16[16,2048]{1,0:T(8,128)(2,1)S(1)}, bf16[16,2048]{1,0:T(8,128)(2,1)S(1)}, u32[]{:S(2)}, u32[]{:S(2)}) collective-permute-start(bf16[16,2048]{1,0:T(8,128)(2,1)S(1)} %fusion.9), channel_id=1, source_target_pairs={{0,24},{4,28},{1,25},{5,29},{2,26},{6,30},{3,27},{7,31}} | collective-permute-start | bytes 196616 | tf_op jit(solution)/shard_map/ppermute | solution.py:148
  16.1 14.8 %collective-permute-start.2 = (bf16[16,2048]{1,0:T(8,128)(2,1)S(1)}, bf16[16,2048]{1,0:T(8,128)(2,1)S(1)}, u32[]{:S(2)}, u32[]{:S(2)}) collective-permute-start(bf16[16,2048]{1,0:T(8,128)(2,1)S(1)} %fusion.9), channel_id=1, source_target_pairs={{0,16},{4,20},{8,24},{12,28},{1,17},{5,21},{9,25},{13,29},{2,18},{... | collective-permute-start | bytes 196616 | tf_op jit(solution)/shard_map/ppermute | solution.py:148
  17.4 13.5 %collective-permute-start.1 = (bf16[16,2048]{1,0:T(8,128)(2,1)S(1)}, bf16[16,2048]{1,0:T(8,128)(2,1)S(1)}, u32[]{:S(2)}, u32[]{:S(2)}) collective-permute-start(bf16[16,2048]{1,0:T(8,128)(2,1)S(1)} %fusion.9), channel_id=1, source_target_pairs={{0,8},{4,12},{8,16},{12,20},{16,24},{20,28},{1,9},{5,13},{9,17},{1... | collective-permute-start | bytes 196616 | tf_op jit(solution)/shard_map/ppermute | solution.py:148
  19.9 0.9 copy-start.1
  20.8 1.0 copy-start.2
  21.8 1.0 copy-start.4
  22.9 1.0 copy-start.6
  23.9 0.9 copy-start.7
  24.8 0.7 copy-start.8
  33.1 13.8 %collective-permute-start.5 = (bf16[128,2048]{1,0:T(8,128)(2,1)S(1)}, bf16[128,2048]{1,0:T(8,128)(2,1)S(1)}, u32[]{:S(2)}, u32[]{:S(2)}) collective-permute-start(bf16[128,2048]{1,0:T(8,128)(2,1)S(1)} %shard_map.75), channel_id=1, source_target_pairs={{8,0},{12,4},{16,8},{20,12},{24,16},{28,20},{9,1},{13,5},{17,9},{2... | collective-permute-start | bytes 1572872 | tf_op jit(solution)/shard_map/ppermute | solution.py:148
  34.4 13.8 %collective-permute-start.4 = (bf16[128,2048]{1,0:T(8,128)(2,1)S(1)}, bf16[128,2048]{1,0:T(8,128)(2,1)S(1)}, u32[]{:S(2)}, u32[]{:S(2)}) collective-permute-start(bf16[128,2048]{1,0:T(8,128)(2,1)S(1)} %shard_map.75), channel_id=1, source_target_pairs={{0,8},{4,12},{8,16},{12,20},{16,24},{20,28},{1,9},{5,13},{9,17},{1... | collective-permute-start | bytes 1572872 | tf_op jit(solution)/shard_map/ppermute | solution.py:148
  46.9 12.9 %collective-permute-start.12 = (bf16[128,2048]{1,0:T(8,128)(2,1)S(1)}, bf16[128,2048]{1,0:T(8,128)(2,1)S(1)}, u32[]{:S(2)}, u32[]{:S(2)}) collective-permute-start(bf16[128,2048]{1,0:T(8,128)(2,1)S(1)} %collective-permute-done.5), channel_id=1, source_target_pairs={{8,0},{12,4},{16,8},{20,12},{9,1},{13,5},{17,9},{21,13},{10,2},{14... | collective-permute-start | bytes 1572872 | tf_op jit(solution)/shard_map/ppermute | solution.py:148
  48.2 11.6 %collective-permute-start.11 = (bf16[128,2048]{1,0:T(8,128)(2,1)S(1)}, bf16[128,2048]{1,0:T(8,128)(2,1)S(1)}, u32[]{:S(2)}, u32[]{:S(2)}) collective-permute-start(bf16[128,2048]{1,0:T(8,128)(2,1)S(1)} %collective-permute-done.4), channel_id=1, source_target_pairs={{8,16},{12,20},{16,24},{20,28},{9,17},{13,21},{17,25},{21,29},{10,... | collective-permute-start | bytes 1572872 | tf_op jit(solution)/shard_map/ppermute | solution.py:148
  49.0 12.2 %copy-start.9 = (bf16[2048,1024]{1,0:T(8,128)(2,1)S(1)}, bf16[2048,1024]{1,0:T(8,128)(2,1)}, u32[]{:S(2)}) copy-start(bf16[2048,1024]{1,0:T(8,128)(2,1)} %param.13) | copy-start | bytes 12582916
  49.0 12.2 %collective-permute-start.6 = (bf16[128,2048]{1,0:T(8,128)(2,1)S(1)}, bf16[128,2048]{1,0:T(8,128)(2,1)S(1)}, u32[]{:S(2)}, u32[]{:S(2)}) collective-permute-start(bf16[128,2048]{1,0:T(8,128)(2,1)S(1)} %shard_map.75), channel_id=1, source_target_pairs={{0,4},{4,0},{8,12},{12,8},{16,20},{20,16},{24,28},{28,24},{1,5},{5... | collective-permute-start | bytes 1572872 | tf_op jit(solution)/shard_map/ppermute | solution.py:151
  59.9 12.0 %collective-permute-start.13 = (bf16[128,2048]{1,0:T(8,128)(2,1)S(1)}, bf16[128,2048]{1,0:T(8,128)(2,1)S(1)}, u32[]{:S(2)}, u32[]{:S(2)}) collective-permute-start(bf16[128,2048]{1,0:T(8,128)(2,1)S(1)} %broadcast_select_fusion), channel_id=1, source_target_pairs={{8,0},{12,4},{16,24},{20,28},{9,1},{13,5},{17,25},{21,29},{10,2},{... | collective-permute-start | bytes 1572872 | tf_op jit(solution)/shard_map/ppermute | solution.py:148
  62.0 14.0 %collective-permute-start.14 = (bf16[128,2048]{1,0:T(8,128)(2,1)S(1)}, bf16[128,2048]{1,0:T(8,128)(2,1)S(1)}, u32[]{:S(2)}, u32[]{:S(2)}) collective-permute-start(bf16[128,2048]{1,0:T(8,128)(2,1)S(1)} %broadcast_select_fusion), channel_id=1, source_target_pairs={{0,4},{4,0},{8,12},{12,8},{16,20},{20,16},{24,28},{28,24},{1,5},{5... | collective-permute-start | bytes 1572872 | tf_op jit(solution)/shard_map/ppermute | solution.py:151
  72.7 14.9 %collective-permute-start.15 = (bf16[128,2048]{1,0:T(8,128)(2,1)S(1)}, bf16[128,2048]{1,0:T(8,128)(2,1)S(1)}, u32[]{:S(2)}, u32[]{:S(2)}) collective-permute-start(bf16[128,2048]{1,0:T(8,128)(2,1)S(1)} %get-tuple-element.7), channel_id=1, source_target_pairs={{0,4},{4,0},{8,12},{12,8},{16,20},{20,16},{24,28},{28,24},{1,5},{5... | collective-permute-start | bytes 1572872 | tf_op jit(solution)/shard_map/ppermute | solution.py:151
  75.0 19.6 %collective-permute-start.7 = (bf16[128,2048]{1,0:T(8,128)(2,1)S(1)}, bf16[128,2048]{1,0:T(8,128)(2,1)S(1)}, u32[]{:S(2)}, u32[]{:S(2)}) collective-permute-start(bf16[128,2048]{1,0:T(8,128)(2,1)S(1)} %get-tuple-element.8), channel_id=1, source_target_pairs={{0,4},{4,0},{8,12},{12,8},{16,20},{20,16},{24,28},{28,24},{1,5},{5... | collective-permute-start | bytes 1572872 | tf_op jit(solution)/shard_map/ppermute | solution.py:151
  88.5 7.2 %collective-permute-start.16 = (bf16[2,128,1024]{2,1,0:T(8,128)(2,1)S(1)}, bf16[2,128,1024]{2,1,0:T(8,128)(2,1)S(1)}, u32[]{:S(2)}, u32[]{:S(2)}) collective-permute-start(bf16[2,128,1024]{2,1,0:T(8,128)(2,1)S(1)} %pad_maximum_fusion.1), channel_id=1, source_target_pairs={{0,1},{1,0},{2,3},{3,2},{4,5},{5,4},{6,7},{7,6},{8,9},{9,8},{10,11... | collective-permute-start | bytes 1572872 | tf_op jit(solution)/shard_map/ppermute | solution.py:191
  95.4 2.0 %collective-permute-start.8 = (bf16[2,128,1024]{2,1,0:T(8,128)(2,1)S(1)}, bf16[2,128,1024]{2,1,0:T(8,128)(2,1)S(1)}, u32[]{:S(2)}, u32[]{:S(2)}) collective-permute-start(bf16[2,128,1024]{2,1,0:T(8,128)(2,1)S(1)} %pad_maximum_fusion), channel_id=1, source_target_pairs={{0,1},{1,0},{2,3},{3,2},{4,5},{5,4},{6,7},{7,6},{8,9},{9,8},{10,11... | collective-permute-start | bytes 1572872 | tf_op jit(solution)/shard_map/ppermute | solution.py:191
  95.9 9.2 %collective-permute-start.17 = (bf16[128,1024]{1,0:T(8,128)(2,1)S(1)}, bf16[128,1024]{1,0:T(8,128)(2,1)S(1)}, u32[]{:S(2)}, u32[]{:S(2)}) collective-permute-start(bf16[128,1024]{1,0:T(8,128)(2,1)S(1)} %fusion.7), channel_id=1, source_target_pairs={{0,2},{1,3},{2,0},{3,1},{4,6},{5,7},{6,4},{7,5},{8,10},{9,11},{10,... | collective-permute-start | bytes 786440 | tf_op jit(solution)/shard_map/ppermute | solution.py:194
  97.6 16.3 %collective-permute-start.9 = (bf16[128,1024]{1,0:T(8,128)(2,1)S(1)}, bf16[128,1024]{1,0:T(8,128)(2,1)S(1)}, u32[]{:S(2)}, u32[]{:S(2)}) collective-permute-start(bf16[128,1024]{1,0:T(8,128)(2,1)S(1)} %fusion.4), channel_id=1, source_target_pairs={{0,2},{1,3},{2,0},{3,1},{4,6},{5,7},{6,4},{7,5},{8,10},{9,11},{10,... | collective-permute-start | bytes 786440 | tf_op jit(solution)/shard_map/ppermute | solution.py:194
  105.2 17.7 %collective-permute-start.20 = (bf16[128,1024]{1,0:T(8,128)(2,1)S(1)}, bf16[128,1024]{1,0:T(8,128)(2,1)S(1)}, u32[]{:S(2)}, u32[]{:S(2)}) collective-permute-start(bf16[128,1024]{1,0:T(8,128)(2,1)S(1)} %fusion), channel_id=1, source_target_pairs={{2,20},{3,28},{6,16},{7,24},{10,29},{11,21},{14,25},{15,17},{18,6}... | collective-permute-start | bytes 786440 | tf_op jit(solution)/shard_map/ppermute | solution.py:203
  112.6 15.0 %collective-permute-start.18 = (bf16[128,1024]{1,0:T(8,128)(2,1)S(1)}, bf16[128,1024]{1,0:T(8,128)(2,1)S(1)}, u32[]{:S(2)}, u32[]{:S(2)}) collective-permute-start(bf16[128,1024]{1,0:T(8,128)(2,1)S(1)} %fusion), channel_id=1, source_target_pairs={{0,16},{1,24},{4,20},{5,28},{8,25},{9,17},{12,29},{13,21},{16,2},{... | collective-permute-start | bytes 786440 | tf_op jit(solution)/shard_map/ppermute | solution.py:203
  114.1 13.6 %collective-permute-start.19 = (bf16[128,1024]{1,0:T(8,128)(2,1)S(1)}, bf16[128,1024]{1,0:T(8,128)(2,1)S(1)}, u32[]{:S(2)}, u32[]{:S(2)}) collective-permute-start(bf16[128,1024]{1,0:T(8,128)(2,1)S(1)} %fusion.1), channel_id=1, source_target_pairs={{2,4},{3,12},{6,0},{7,8},{10,13},{11,5},{14,9},{15,1},{18,22},{19,... | collective-permute-start | bytes 786440 | tf_op jit(solution)/shard_map/ppermute | solution.py:203
  116.6 11.1 %collective-permute-start.10 = (bf16[128,1024]{1,0:T(8,128)(2,1)S(1)}, bf16[128,1024]{1,0:T(8,128)(2,1)S(1)}, u32[]{:S(2)}, u32[]{:S(2)}) collective-permute-start(bf16[128,1024]{1,0:T(8,128)(2,1)S(1)} %fusion.1), channel_id=1, source_target_pairs={{0,0},{1,8},{4,4},{5,12},{8,9},{9,1},{12,13},{13,5},{16,18},{17,26... | collective-permute-start | bytes 786440 | tf_op jit(solution)/shard_map/ppermute | solution.py:203

commit v3 on v2

v3 whole, which is shorter than its diff:
```python
import functools

import jax
import jax.numpy as jnp
from jax import lax
from jax.experimental import pallas as pl
from jax.experimental.pallas import tpu as pltpu
from jax.sharding import PartitionSpec as P

BF16 = jnp.bfloat16
F32 = jnp.float32
SUB = 8
LANES = 128
BOTH = ("seq", "chan")


def spread_rows(row):
    return jnp.broadcast_to(row, (SUB, row.shape[-1]))


def source_rows(k_ref, v_ref, x_ref, lanes):
    x_ref[...] = k_ref[:, lanes].astype(F32) * v_ref[:, lanes].astype(F32)
    length = x_ref.shape[0] // SUB
    return [x_ref[pl.ds(i, SUB, stride=length), :] for i in range(length)]


def state_kernel(total, k_ref, v_ref, rate_ref, state_ref, x_ref):
    modes, width = rate_ref.shape
    length = x_ref.shape[0] // SUB
    block = lax.broadcasted_iota(jnp.int32, (SUB, LANES), 0).astype(F32)

    @pl.loop(0, width // LANES)
    def _(chunk):
        lanes = pl.ds(pl.multiple_of(chunk * LANES, LANES), LANES)
        x = source_rows(k_ref, v_ref, x_ref, lanes)
        rate = rate_ref[:, lanes] * (-1.0 / total)
        decay = jnp.exp(rate)
        rows = []
        for m in range(modes):
            d = spread_rows(decay[m : m + 1])
            state = x[0]
            for i in range(1, length):
                state = state * d + x[i]
            weight = jnp.exp(spread_rows(rate[m : m + 1]) * ((SUB - 1.0 - block) * length))
            rows.append(jnp.sum(state * weight, axis=0, keepdims=True))
        state_ref[:, lanes] = jnp.concatenate(rows, axis=0).astype(BF16)


def local_kernel(total, q_ref, k_ref, v_ref, res_ref, rate_ref, skip_ref, *rest):
    base_ref, x_ref, y_ref = rest[-3:]
    modes, width = rate_ref.shape
    length = x_ref.shape[0] // SUB
    block = lax.broadcasted_iota(jnp.int32, (SUB, LANES), 0)

    @pl.loop(0, width // LANES)
    def _(chunk):
        lanes = pl.ds(pl.multiple_of(chunk * LANES, LANES), LANES)
        x = source_rows(k_ref, v_ref, x_ref, lanes)
        rate = rate_ref[:, lanes] * (-1.0 / total)
        gain = res_ref[:, lanes] * jnp.sqrt(rate_ref[:, lanes] * (2.0 / total))
        decay = jnp.exp(rate)
        y = [spread_rows(skip_ref[:, lanes]) * x[i] for i in range(length)]
        power = gain
        for j in range(length):
            tap = spread_rows(jnp.sum(power, axis=0, keepdims=True))
            for i in range(j, length):
                y[i] = y[i] + tap * x[i - j]
            power = power * decay
        for m in range(modes):
            d = spread_rows(decay[m : m + 1])
            state = x[0]
            for i in range(1, length):
                state = state * d + x[i]
            step = spread_rows(rate[m : m + 1]) * length
            state = jnp.where(block >= 1, pltpu.roll(state, 1, 0), 0.0)
            for shift in (1, 2, 4):
                moved = jnp.where(block >= shift, pltpu.roll(state, shift, 0), 0.0)
                state = state + jnp.exp(step * shift) * moved
            state = state * spread_rows(gain[m : m + 1])
            for i in range(length):
                state = state * d
                y[i] = y[i] + state
        for i in range(length):
            y_ref[pl.ds(i, SUB, stride=length), :] = y[i]
        base_ref[:, lanes] = y_ref[...] * q_ref[:, lanes].astype(F32)


def carry_kernel(total, odd_ref, q_ref, base_ref, below_ref, further_ref, first_ref, res_ref, rate_ref, out_ref, y_ref):
    modes, width = rate_ref.shape
    length = y_ref.shape[0] // SUB
    block = lax.broadcasted_iota(jnp.int32, (SUB, LANES), 0).astype(F32)

    @pl.loop(0, width // LANES)
    def _(chunk):
        lanes = pl.ds(pl.multiple_of(chunk * LANES, LANES), LANES)
        rate = rate_ref[:, lanes] * (-1.0 / total)
        rows = SUB * length
        start = below_ref[:, lanes].astype(F32) + further_ref[:, lanes].astype(F32) * jnp.exp(rate * (2 * rows))
        later = start * jnp.exp(rate * rows) + first_ref[:, lanes].astype(F32)
        start = jnp.where(odd_ref[0] == 1, later, start)
        start = start * res_ref[:, lanes] * jnp.sqrt(rate_ref[:, lanes] * (2.0 / total))
        decay = jnp.exp(rate)
        y = [jnp.zeros((SUB, LANES), F32) for i in range(length)]
        for m in range(modes):
            d = spread_rows(decay[m : m + 1])
            state = spread_rows(start[m : m + 1]) * jnp.exp(spread_rows(rate[m : m + 1]) * (block * length))
            for i in range(length):
                state = state * d
                y[i] = y[i] + state
        for i in range(length):
            y_ref[pl.ds(i, SUB, stride=length), :] = y[i]
        out_ref[:, lanes] = (base_ref[:, lanes] + y_ref[...] * q_ref[:, lanes].astype(F32)).astype(BF16)


def run(kernel, out, scratch, ops, mib, args, window=None, filled=None, scalars=()):
    rows, width = args[0].shape
    part = min(width // 4, 4 * LANES)
    steps = width // part
    first = 0
    if window is not None:
        first, steps = window[0] * steps // 4, (window[1] - window[0]) * steps // 4
    specs = [pl.BlockSpec(memory_space=pltpu.SMEM)] * len(scalars)
    specs += [pl.BlockSpec((arg.shape[0], part), lambda i: (0, i + first)) for arg in args]
    if filled is not None:
        specs.append(pl.BlockSpec(memory_space=pl.ANY))
    return pl.pallas_call(
        kernel,
        grid=(steps,),
        out_shape=out,
        in_specs=specs,
        out_specs=pl.BlockSpec((out.shape[0], part), lambda i: (0, i + first)),
        scratch_shapes=[pltpu.VMEM((rows, LANES), F32)] * scratch,
        input_output_aliases={} if filled is None else {len(specs) - 1: 0},
        compiler_params=pltpu.CompilerParams(vmem_limit_bytes=mib * 1024 * 1024),
        cost_estimate=pl.CostEstimate(
            flops=ops * rows * part * steps, bytes_accessed=6 * rows * part * steps, transcendentals=0
        ),
    )(*scalars, *args, *(() if filled is None else (filled,)))


def matmul(x, w):
    return jnp.dot(x, w, preferred_element_type=F32)


def moved(x, axes, pairs, name):
    with jax.named_scope(name):
        return lax.ppermute(x, axes, pairs)


def fence(*xs):
    return lax.optimization_barrier(xs)


def general(base_of, hidden_of, state, w_out, fade, rows, index, parts):
    states = lax.all_gather(state, "seq", axis=0)
    entering = jnp.zeros(state.shape, F32)
    for b in range(parts):
        entering = jnp.where(b < index, entering * fade(rows) + states[b].astype(F32), entering)
    nothing = jnp.zeros_like(state)
    hidden = hidden_of(base_of((0, 4)), entering, nothing, nothing, jnp.int32(0))
    spread = matmul(lax.all_gather(hidden, "seq", axis=0, tiled=True), w_out)
    partial_value = lax.all_to_all(spread, "seq", split_axis=0, concat_axis=1, tiled=True)
    summed = lax.psum_scatter(partial_value, "chan", scatter_dimension=1, tiled=True)
    return summed.astype(BF16)


def lined(base_of, hidden_of, state, w_out, fade, rows, index):
    depth = 4
    z, y = index // 2, index % 2

    def along(x, moves, name):
        return moved(x, "seq", [(a * 2 + b, c * 2 + b) for a, c in moves for b in range(2)], name)

    def across(x, planes, name):
        return moved(x, "seq", [(a * 2 + b, a * 2 + 1 - b) for a in planes for b in range(2)], name)

    def shift(by):
        return [(a, a + by) for a in range(depth) if 0 <= a + by < depth]

    every = range(depth)
    other = across(state, every, "state_y")
    other, base = fence(other, base_of((0, 2)))
    first = jnp.where(y == 0, state, other)
    second = jnp.where(y == 0, other, state)
    plane = first.astype(F32) * fade(rows) + second.astype(F32)
    below = along(plane.astype(BF16), shift(1), "state_1")
    below, base = fence(below, base_of((2, 3), base))
    two_below = (plane + below.astype(F32) * fade(2 * rows)).astype(BF16)
    further = along(two_below, shift(2), "state_2")
    base = base_of((3, 4), base)
    hidden = hidden_of(base, below, further, first, y)

    chan = lax.axis_index("chan")
    side, core = chan // 2, chan % 2
    pairwise = [(0, 1), (1, 0), (2, 3), (3, 2)]
    inner, outward = [(1, 2), (2, 1)], [(1, 0), (2, 3)]
    near_y = across(hidden, every, "near_y")
    one = along(hidden, pairwise, "one")
    middle = along(hidden, inner, "middle")
    one, middle, near_y = fence(one, middle, near_y)

    one_y = across(one, every, "one_y")
    given = along(one, inner, "given")
    out2 = along(middle, outward, "out2")
    given, out2, one_y, late_y = fence(given, out2, one_y, near_y[:, hidden.shape[1] // 2 :])

    at_end = z % 3 == 0
    two = jnp.where(at_end, out2, given)
    two_y = across(two, every, "two_y")
    out3 = along(given, outward, "out3")
    split = hidden.shape[1] // 2
    middle_y = along(late_y, inner, "middle_y")

    flip = [(c, c ^ 1) for c in range(4)]
    turn = [(c, c ^ 2) for c in range(4)]

    def root(group, a):
        return (a // 2) ^ (group % 2)

    def owners(group):
        return [
            [
                (
                    (a * 2 + b) * 4 + ((d ^ k) if group == 0 else root(group + g, a)) * 2 + (k if group == 0 else d),
                    ((a ^ (group + (k if group == 0 else g))) * 2 + (b ^ d)) * 4 + a,
                )
                for a in every
                for b in range(2)
                for k, g in (((0, 0), (1, 0)) if group == 0 else ((0, 0), (0, 1)))
            ]
            for d in range(2)
        ]

    even = [matmul(block, w_out) for block in (hidden, near_y)]
    odd = [matmul(block, w_out) for block in (one, one_y)]
    keep = jnp.stack([jnp.where(core == 0, a, b) for a, b in zip(even, odd)])
    send = jnp.stack([jnp.where(core == 0, b, a).astype(BF16) for a, b in zip(even, odd)])
    close_core = moved(send, "chan", flip, "core_0")
    keep = keep + close_core.astype(F32)
    send = jnp.where(side == core, keep[1], keep[0]).astype(BF16)
    keep = jnp.where(side == core, keep[0], keep[1])
    close_side = moved(send, "chan", turn, "side_0")

    def remote(group, parts, before):
        first, second = parts
        keep = jnp.where(core == 0, first, second)
        send = fence(jnp.where(core == 0, second, first).astype(BF16), *before)[0]
        keep = keep + moved(send, "chan", flip, f"core_{group}").astype(F32)
        pairs = [
            ((a * 2 + b) * 4 + (1 - root(group, a)) * 2 + k, (a * 2 + b) * 4 + root(group, a) * 2 + k)
            for a in every
            for b in range(2)
            for k in range(2)
        ]
        turned = moved(keep.astype(BF16), BOTH, pairs, f"side_{group}")
        return (keep + turned.astype(F32)).astype(BF16)

    out3, two_y, close_side, middle_y = fence(out3, two_y, close_side, middle_y)
    three = jnp.where(at_end, out3, middle)
    three_y = across(three[:, :split], every, "three_y")
    out_y = along(two_y[:, split:], outward, "out_y")
    with_three = matmul(three, w_out)
    tile = (keep + close_side.astype(F32)).astype(BF16)
    three_y, out_y, tile = fence(three_y, out_y, tile)
    close = [moved(tile, BOTH, pairs, "own_0") for pairs in owners(0)]
    with_three_y = matmul(three_y, w_out[:split]) + matmul(jnp.where(at_end, out_y, middle_y), w_out[split:])
    tile2 = remote(2, [matmul(two, w_out), matmul(two_y, w_out)], [with_three])
    with_three_y, tile2 = fence(with_three_y, tile2)
    tile3 = remote(3, [with_three, with_three_y], [])
    tile = jnp.where(side == root(2, z), tile2, tile3)
    far = [moved(tile, BOTH, pairs, "own_2") for pairs in owners(2)]
    near_here = (z ^ chan) < 2
    same = jnp.where(near_here, close[0], far[0])
    cross = jnp.where(near_here, close[1], far[1])
    low = jnp.where(y == 0, same, cross)
    high = jnp.where(y == 0, cross, same)
    return jnp.concatenate([low, high], axis=1)


def local(q_proj, k_proj, v_proj, residues, rates, skip_gain, w_out):
    rows, width = q_proj.shape
    parts = lax.axis_size("seq")
    index = lax.axis_index("seq")
    total = rows * parts
    modes = rates.shape[1]
    res_t, rate_t = residues.T, rates.T
    state = run(
        functools.partial(state_kernel, total),
        jax.ShapeDtypeStruct((modes, width), BF16),
        1,
        48,
        60,
        [k_proj, v_proj, rate_t],
    )

    def base_of(window, filled=None):
        return run(
            functools.partial(local_kernel, total),
            jax.ShapeDtypeStruct((rows, width), F32),
            2,
            100,
            60,
            [q_proj, k_proj, v_proj, res_t, rate_t, skip_gain[None, :]],
            window,
            filled,
        )

    def hidden_of(base, below, further, first, odd):
        return run(
            functools.partial(carry_kernel, total),
            jax.ShapeDtypeStruct((rows, width), BF16),
            1,
            32,
            16,
            [q_proj, base, below, further, first, res_t, rate_t],
            scalars=(odd.astype(jnp.int32)[None],),
        )

    def fade(steps):
        return jnp.exp(rate_t * (-float(steps) / total))

    if parts == 8 and lax.axis_size("chan") == 4:
        return lined(base_of, hidden_of, state, w_out, fade, rows, index)
    return general(base_of, hidden_of, state, w_out, fade, rows, index, parts)


def solution(mesh):
    return jax.shard_map(
        local,
        mesh=mesh,
        in_specs=(
            P("seq", "chan"),
            P("seq", "chan"),
            P("seq", "chan"),
            P("chan", None),
            P("chan", None),
            P("chan"),
            P("chan", "seq"),
        ),
        out_specs=P("seq", "chan"),
        check_vma=False,
    )
```

time: 129 us -> 122 us (0.946)
  the two profiles are of different devices: /device:TPU:2 before, /device:TPU:10 now
where the time goes in v3:
time: 122 us
  waiting for transfers between devices  48.1 us (39%)
  starting transfers between devices  43.2 us (35%)
  Pallas kernels  16.9 us (14%)
  matrix products  8.35 us (7%)
  other arithmetic  3.18 us (3%)
  local copies, waits for them, and re-layouts  1.31 us (1%)
    ppermute x24, waiting for transfers between devices, moved(): return lax.ppermute(x, axes, pairs)  48.1 us
    ppermute x24, starting transfers between devices, moved(): return lax.ppermute(x, axes, pairs)  43.2 us
    pallas_call x5, Pallas kernels, run(): pl.pallas_call(kernel, grid=(steps,), out_shape=out, in_specs=specs, out_...  16.9 us
    dot_general x9, matrix products, matmul(): return jnp.dot(x, w, preferred_element_type=F32)  8.35 us
  transfers between devices with their start and end apart: 24, of which 12 were waited for; matrix products, arithmetic and copies ran while one was open for 6% of the time, Pallas kernels for 9%

profile of v3, /device:TPU:10, one launch (start us, length us, event | category | flops | bytes accessed | tf_op | source)
XLA Modules:
  0.0 121.6 jit_solution(1339763663959779263)
XLA Ops:
  0.0 4.3 %shard_map.73 = bf16[16,2048]{1,0:T(8,128)(2,1)} custom-call(bf16[128,2048]{1,0:T(8,128)(2,1)} %k_ref.7, bf16[128,2048]{1,0:T(8,128)(2,1)} %v_ref.7, f32[16,2048]{1,0:T(8,128)} %bitcast.35), custom_call_target="tpu_custom_call" | custom-call | flops 12582912 | bytes 1572864 | tf_op jit(solution)/shard_map/pallas_call | solution.py:126
  4.3 1.5 %collective-permute-start = (bf16[16,2048]{1,0:T(8,128)(2,1)}, bf16[16,2048]{1,0:T(8,128)(2,1)S(1)}, u32[]{:S(2)}, u32[]{:S(2)}) collective-permute-start(bf16[16,2048]{1,0:T(8,128)(2,1)} %shard_map.73), channel_id=1, source_target_pairs={{0,4},{4,0},{8,12},{12,8},{16,20},{20,16},{24,28},{28,24},{1,5},{5... | collective-permute-start | bytes 196616 | tf_op jit(solution)/shard_map/state_y/ppermute | solution.py:147
  5.8 4.3 %shard_map.74.rest_0_ = f32[128,2048]{1,0:T(8,128)} custom-call(bf16[128,2048]{1,0:T(8,128)(2,1)} %q_ref.7, bf16[128,2048]{1,0:T(8,128)(2,1)} %k_ref.7, bf16[128,2048]{1,0:T(8,128)(2,1)} %v_ref.7, f32[16,2048]{1,0:T(8,128)} %bitcast.40, f32[16,2048]{1,0:T(8,128)} %bitcast.36, f32[1,2048]{1,0:T(1,128)} %bitcast.44), custom_call_target="tpu_custom_call" | custom-call | flops 13107200 | bytes 786432 | tf_op jit(solution)/shard_map/pallas_call | solution.py:126
  10.2 0.9 fusion.14
  11.1 3.6 %collective-permute-start.1 = (bf16[16,2048]{1,0:T(8,128)(2,1)S(1)}, bf16[16,2048]{1,0:T(8,128)(2,1)S(1)}, u32[]{:S(2)}, u32[]{:S(2)}) collective-permute-start(bf16[16,2048]{1,0:T(8,128)(2,1)S(1)} %get-tuple-element.47), channel_id=1, source_target_pairs={{0,8},{4,12},{8,16},{12,20},{16,24},{20,28},{1,9},{5,13},{9,17},{1... | collective-permute-start | bytes 196616 | tf_op jit(solution)/shard_map/state_1/ppermute | solution.py:147
  14.7 3.0 %shard_map.75.rest_0_ = f32[128,2048]{1,0:T(8,128)} custom-call(bf16[128,2048]{1,0:T(8,128)(2,1)} %q_ref.7, bf16[128,2048]{1,0:T(8,128)(2,1)} %k_ref.7, bf16[128,2048]{1,0:T(8,128)(2,1)} %v_ref.7, f32[16,2048]{1,0:T(8,128)} %bitcast.41, f32[16,2048]{1,0:T(8,128)} %bitcast.37, f32[1,2048]{1,0:T(1,128)} %bitcast.45, ...), custom_call_target="tpu_custom_call", output_to_operand_aliasing={{}: (6, {})} | custom-call | flops 6553600 | bytes 393216 | tf_op jit(solution)/shard_map/pallas_call | solution.py:126
  17.8 4.1 %collective-permute-start.2 = (bf16[16,2048]{1,0:T(8,128)(2,1)S(1)}, bf16[16,2048]{1,0:T(8,128)(2,1)S(1)}, u32[]{:S(2)}, u32[]{:S(2)}) collective-permute-start(bf16[16,2048]{1,0:T(8,128)(2,1)S(1)} %add_convert_fusion.2), channel_id=1, source_target_pairs={{0,16},{4,20},{8,24},{12,28},{1,17},{5,21},{9,25},{13,29},{2,18},{... | collective-permute-start | bytes 196616 | tf_op jit(solution)/shard_map/state_2/ppermute | solution.py:147
  22.0 3.0 %shard_map.76.base_ref = f32[128,2048]{1,0:T(8,128)} custom-call(bf16[128,2048]{1,0:T(8,128)(2,1)} %q_ref.7, bf16[128,2048]{1,0:T(8,128)(2,1)} %k_ref.7, bf16[128,2048]{1,0:T(8,128)(2,1)} %v_ref.7, f32[16,2048]{1,0:T(8,128)} %bitcast.42, f32[16,2048]{1,0:T(8,128)} %bitcast.38, f32[1,2048]{1,0:T(1,128)} %bitcast.46, ...), custom_call_target="tpu_custom_call", output_to_operand_aliasing={{}: (6, {})} | custom-call | flops 6553600 | bytes 393216 | tf_op jit(solution)/shard_map/pallas_call | solution.py:126
  25.0 1.2 copy-done
  26.3 2.2 %shard_map.77 = bf16[128,2048]{1,0:T(8,128)(2,1)S(1)} custom-call(s32[1]{0:T(128)} %bitcast.odd_ref, bf16[128,2048]{1,0:T(8,128)(2,1)S(1)} %copy-done.1, f32[128,2048]{1,0:T(8,128)S(1)} %copy-done, bf16[16,2048]{1,0:T(8,128)(2,1)S(1)} %collective-permute-done.1.below_ref, bf16[16,2048]{1,0:T(8,128)(2,1)S(1)} %collective-permute-done.2.further_ref, ...), custom_call_target="tpu_custom_call" | custom-call | flops 8388608 | bytes 1572864 | tf_op jit(solution)/shard_map/pallas_call | solution.py:126
  28.5 0.6 collective-permute-start.5
  29.1 3.5 %collective-permute-start.4 = (bf16[128,2048]{1,0:T(8,128)(2,1)S(1)}, bf16[128,2048]{1,0:T(8,128)(2,1)S(1)}, u32[]{:S(2)}, u32[]{:S(2)}) collective-permute-start(bf16[128,2048]{1,0:T(8,128)(2,1)S(1)} %shard_map.77), channel_id=1, source_target_pairs={{8,16},{12,20},{16,8},{20,12},{9,17},{13,21},{17,9},{21,13},{10,18... | collective-permute-start | bytes 1572872 | tf_op jit(solution)/shard_map/middle/ppermute | solution.py:147
  32.7 3.0 %fusion.17 = f32[128,1024]{1,0:T(8,128)S(1)} fusion(bf16[128,2048]{1,0:T(8,128)(2,1)S(1)} %shard_map.77, bf16[2048,1024]{1,0:T(8,128)(2,1)} %param.13), kind=kOutput, calls=%fused_computation.40 | convolution fusion | flops 536870912 | bytes 5242880 | tf_op jit(solution)/shard_map/dot_general | solution.py:142
  35.8 4.8 %collective-permute-done.5 = bf16[128,2048]{1,0:T(8,128)(2,1)S(1)} collective-permute-done((bf16[128,2048]{1,0:T(8,128)(2,1)S(1)}, bf16[128,2048]{1,0:T(8,128)(2,1)S(1)}, u32[]{:S(2)}, u32[]{:S(2)}) %collective-permute-start.5) | collective-permute-done | bytes 524320 | tf_op jit(solution)/shard_map/near_y/ppermute | solution.py:147
  40.5 2.1 %collective-permute-done.4 = bf16[128,2048]{1,0:T(8,128)(2,1)S(1)} collective-permute-done((bf16[128,2048]{1,0:T(8,128)(2,1)S(1)}, bf16[128,2048]{1,0:T(8,128)(2,1)S(1)}, u32[]{:S(2)}, u32[]{:S(2)}) %collective-permute-start.4) | collective-permute-done | bytes 524320 | tf_op jit(solution)/shard_map/middle/ppermute | solution.py:147
  42.6 1.3 %collective-permute-done.3 = bf16[128,2048]{1,0:T(8,128)(2,1)S(1)} collective-permute-done((bf16[128,2048]{1,0:T(8,128)(2,1)S(1)}, bf16[128,2048]{1,0:T(8,128)(2,1)S(1)}, u32[]{:S(2)}, u32[]{:S(2)}) %collective-permute-start.3) | collective-permute-done | bytes 524320 | tf_op jit(solution)/shard_map/one/ppermute | solution.py:147
  43.9 0.7 fusion.18
  44.7 1.6 %collective-permute-start.8 = (bf16[128,2048]{1,0:T(8,128)(2,1)S(1)}, bf16[128,2048]{1,0:T(8,128)(2,1)S(1)}, u32[]{:S(2)}, u32[]{:S(2)}) collective-permute-start(bf16[128,2048]{1,0:T(8,128)(2,1)S(1)} %collective-permute-done.3), channel_id=1, source_target_pairs={{0,4},{4,0},{8,12},{12,8},{16,20},{20,16},{24,28},{28,24},{1,5},{5... | collective-permute-start | bytes 1572872 | tf_op jit(solution)/shard_map/one_y/ppermute | solution.py:147
  46.2 2.5 %collective-permute-start.6 = (bf16[128,2048]{1,0:T(8,128)(2,1)S(1)}, bf16[128,2048]{1,0:T(8,128)(2,1)S(1)}, u32[]{:S(2)}, u32[]{:S(2)}) collective-permute-start(bf16[128,2048]{1,0:T(8,128)(2,1)S(1)} %collective-permute-done.3), channel_id=1, source_target_pairs={{8,16},{12,20},{16,8},{20,12},{9,17},{13,21},{17,9},{21,13},{10,18... | collective-permute-start | bytes 1572872 | tf_op jit(solution)/shard_map/given/ppermute | solution.py:147
  48.7 1.3 %collective-permute-start.7 = (bf16[128,2048]{1,0:T(8,128)(2,1)S(1)}, bf16[128,2048]{1,0:T(8,128)(2,1)S(1)}, u32[]{:S(2)}, u32[]{:S(2)}) collective-permute-start(bf16[128,2048]{1,0:T(8,128)(2,1)S(1)} %collective-permute-done.4), channel_id=1, source_target_pairs={{8,0},{12,4},{16,24},{20,28},{9,1},{13,5},{17,25},{21,29},{10,2},{... | collective-permute-start | bytes 1572872 | tf_op jit(solution)/shard_map/out2/ppermute | solution.py:147
  50.2 0.7 fusion.19
  51.0 6.8 %collective-permute-done.7 = bf16[128,2048]{1,0:T(8,128)(2,1)S(1)} collective-permute-done((bf16[128,2048]{1,0:T(8,128)(2,1)S(1)}, bf16[128,2048]{1,0:T(8,128)(2,1)S(1)}, u32[]{:S(2)}, u32[]{:S(2)}) %collective-permute-start.7) | collective-permute-done | bytes 524320 | tf_op jit(solution)/shard_map/out2/ppermute | solution.py:147
  57.7 0.6 collective-permute-done.6
  58.3 2.7 %collective-permute-start.13 = (bf16[128,1024]{1,0:T(8,128)(2,1)S(1)}, bf16[128,1024]{1,0:T(8,128)(2,1)S(1)}, u32[]{:S(2)}, u32[]{:S(2)}) collective-permute-start(bf16[128,1024]{1,0:T(8,128)(2,1)S(1)} %slice.23), channel_id=1, source_target_pairs={{8,16},{12,20},{16,8},{20,12},{9,17},{13,21},{17,9},{21,13},{10,18... | collective-permute-start | bytes 786440 | tf_op jit(solution)/shard_map/middle_y/ppermute | solution.py:147
  61.0 0.7 fusion.20
  62.0 1.8 %collective-permute-start.9 = (bf16[128,2048]{1,0:T(8,128)(2,1)S(1)}, bf16[128,2048]{1,0:T(8,128)(2,1)S(1)}, u32[]{:S(2)}, u32[]{:S(2)}) collective-permute-start(bf16[128,2048]{1,0:T(8,128)(2,1)S(1)} %collective-permute-done.6), channel_id=1, source_target_pairs={{8,0},{12,4},{16,24},{20,28},{9,1},{13,5},{17,25},{21,29},{10,2},{... | collective-permute-start | bytes 1572872 | tf_op jit(solution)/shard_map/out3/ppermute | solution.py:147
  63.9 0.6 collective-permute-start.10
  64.7 0.6 collective-permute-start.12
  65.3 0.7 fusion.21
  66.0 0.5 collective-permute-done.13
  66.6 11.4 %collective-permute-done.10 = bf16[128,2048]{1,0:T(8,128)(2,1)S(1)} collective-permute-done((bf16[128,2048]{1,0:T(8,128)(2,1)S(1)}, bf16[128,2048]{1,0:T(8,128)(2,1)S(1)}, u32[]{:S(2)}, u32[]{:S(2)}) %collective-permute-start.10) | collective-permute-done | bytes 524320 | tf_op jit(solution)/shard_map/two_y/ppermute | solution.py:147
  78.0 0.7 fusion.22
  78.8 0.7 select_convert_fusion.1
  79.7 2.0 %collective-permute-start.15 = (bf16[128,1024]{1,0:T(8,128)(2,1)S(1)}, bf16[128,1024]{1,0:T(8,128)(2,1)S(1)}, u32[]{:S(2)}, u32[]{:S(2)}) collective-permute-start(bf16[128,1024]{1,0:T(8,128)(2,1)S(1)} %slice.27), channel_id=1, source_target_pairs={{8,0},{12,4},{16,24},{20,28},{9,1},{13,5},{17,25},{21,29},{10,2},{... | collective-permute-start | bytes 786440 | tf_op jit(solution)/shard_map/out_y/ppermute | solution.py:147
  81.7 0.6 collective-permute-start.14
  82.5 2.5 %collective-permute-start.18 = (bf16[128,1024]{1,0:T(8,128)(2,1)S(1)}, bf16[128,1024]{1,0:T(8,128)(2,1)S(1)}, u32[]{:S(2)}, u32[]{:S(2)}) collective-permute-start(bf16[128,1024]{1,0:T(8,128)(2,1)S(1)} %fusion.15), channel_id=1, source_target_pairs={{2,0},{3,1},{6,4},{7,5},{10,8},{11,9},{14,12},{15,13},{16,18},{17,... | collective-permute-start | bytes 786440 | tf_op jit(solution)/shard_map/side_2/ppermute | solution.py:147
  84.9 2.9 %collective-permute-done.15 = bf16[128,1024]{1,0:T(8,128)(2,1)S(1)} collective-permute-done((bf16[128,1024]{1,0:T(8,128)(2,1)S(1)}, bf16[128,1024]{1,0:T(8,128)(2,1)S(1)}, u32[]{:S(2)}, u32[]{:S(2)}) %collective-permute-start.15) | collective-permute-done | bytes 262176 | tf_op jit(solution)/shard_map/out_y/ppermute | solution.py:147
  87.9 2.3 %collective-permute-done.14 = bf16[128,1024]{1,0:T(8,128)(2,1)S(1)} collective-permute-done((bf16[128,1024]{1,0:T(8,128)(2,1)S(1)}, bf16[128,1024]{1,0:T(8,128)(2,1)S(1)}, u32[]{:S(2)}, u32[]{:S(2)}) %collective-permute-start.14) | collective-permute-done | bytes 262176 | tf_op jit(solution)/shard_map/three_y/ppermute | solution.py:147
  90.6 0.5 fusion.4
  91.4 1.5 %collective-permute-done.19 = bf16[128,1024]{1,0:T(8,128)(2,1)S(1)} collective-permute-done((bf16[128,1024]{1,0:T(8,128)(2,1)S(1)}, bf16[128,1024]{1,0:T(8,128)(2,1)S(1)}, u32[]{:S(2)}, u32[]{:S(2)}) %collective-permute-start.19) | collective-permute-done | bytes 262176 | tf_op jit(solution)/shard_map/core_3/ppermute | solution.py:147
  93.0 1.3 %collective-permute-start.20 = (bf16[128,1024]{1,0:T(8,128)(2,1)S(1)}, bf16[128,1024]{1,0:T(8,128)(2,1)S(1)}, u32[]{:S(2)}, u32[]{:S(2)}) collective-permute-start(bf16[128,1024]{1,0:T(8,128)(2,1)S(1)} %fusion.16), channel_id=1, source_target_pairs={{0,2},{1,3},{4,6},{5,7},{8,10},{9,11},{12,14},{13,15},{18,16},{19,... | collective-permute-start | bytes 786440 | tf_op jit(solution)/shard_map/side_3/ppermute | solution.py:147
  94.3 4.6 %collective-permute-start.22 = (bf16[128,1024]{1,0:T(8,128)(2,1)S(1)}, bf16[128,1024]{1,0:T(8,128)(2,1)S(1)}, u32[]{:S(2)}, u32[]{:S(2)}) collective-permute-start(bf16[128,1024]{1,0:T(8,128)(2,1)S(1)} %fusion.7), channel_id=1, source_target_pairs={{2,4},{1,12},{6,0},{5,8},{10,13},{9,5},{14,9},{13,1},{18,22},{17,3... | collective-permute-start | bytes 786440 | tf_op jit(solution)/shard_map/own_0/ppermute | solution.py:147
  98.9 0.7 collective-permute-start.16
  99.6 3.6 %collective-permute-done.20 = bf16[128,1024]{1,0:T(8,128)(2,1)S(1)} collective-permute-done((bf16[128,1024]{1,0:T(8,128)(2,1)S(1)}, bf16[128,1024]{1,0:T(8,128)(2,1)S(1)}, u32[]{:S(2)}, u32[]{:S(2)}) %collective-permute-start.20) | collective-permute-done | bytes 262176 | tf_op jit(solution)/shard_map/side_3/ppermute | solution.py:147
  103.4 1.3 %collective-permute-start.23 = (bf16[128,1024]{1,0:T(8,128)(2,1)S(1)}, bf16[128,1024]{1,0:T(8,128)(2,1)S(1)}, u32[]{:S(2)}, u32[]{:S(2)}) collective-permute-start(bf16[128,1024]{1,0:T(8,128)(2,1)S(1)} %fusion.11), channel_id=1, source_target_pairs={{1,20},{3,28},{5,16},{7,24},{9,29},{11,21},{13,25},{15,17},{19,6},... | collective-permute-start | bytes 786440 | tf_op jit(solution)/shard_map/own_2/ppermute | solution.py:147
  104.7 5.7 %collective-permute-start.21 = (bf16[128,1024]{1,0:T(8,128)(2,1)S(1)}, bf16[128,1024]{1,0:T(8,128)(2,1)S(1)}, u32[]{:S(2)}, u32[]{:S(2)}) collective-permute-start(bf16[128,1024]{1,0:T(8,128)(2,1)S(1)} %fusion.11), channel_id=1, source_target_pairs={{0,16},{2,24},{4,20},{6,28},{8,25},{10,17},{12,29},{14,21},{18,2},... | collective-permute-start | bytes 786440 | tf_op jit(solution)/shard_map/own_2/ppermute | solution.py:147
  110.5 10.2 %collective-permute-done.23 = bf16[128,1024]{1,0:T(8,128)(2,1)S(1)} collective-permute-done((bf16[128,1024]{1,0:T(8,128)(2,1)S(1)}, bf16[128,1024]{1,0:T(8,128)(2,1)S(1)}, u32[]{:S(2)}, u32[]{:S(2)}) %collective-permute-start.23) | collective-permute-done | bytes 262176 | tf_op jit(solution)/shard_map/own_2/ppermute | solution.py:147
  120.8 0.8 pad_maximum_fusion.1
  (52 shorter events, 2.3 us)
Async XLA Ops:
  0.0 10.2 %copy-start.2 = (f32[2048,16]{0,1:T(8,128)S(1)}, f32[2048,16]{0,1:T(8,128)}, u32[]{:S(2)}) copy-start(f32[2048,16]{0,1:T(8,128)} %param.11) | copy-start | bytes 393220
  0.0 17.8 %copy-start.3 = (f32[2048,16]{0,1:T(8,128)S(1)}, f32[2048,16]{0,1:T(8,128)}, u32[]{:S(2)}) copy-start(f32[2048,16]{0,1:T(8,128)} %param.11) | copy-start | bytes 393220
  4.3 13.5 %copy-start.7 = (bf16[16,2048]{1,0:T(8,128)(2,1)S(1)}, bf16[16,2048]{1,0:T(8,128)(2,1)}, u32[]{:S(2)}) copy-start(bf16[16,2048]{1,0:T(8,128)(2,1)} %shard_map.73) | copy-start | bytes 196612
  4.3 5.9 %collective-permute-start = (bf16[16,2048]{1,0:T(8,128)(2,1)}, bf16[16,2048]{1,0:T(8,128)(2,1)S(1)}, u32[]{:S(2)}, u32[]{:S(2)}) collective-permute-start(bf16[16,2048]{1,0:T(8,128)(2,1)} %shard_map.73), channel_id=1, source_target_pairs={{0,4},{4,0},{8,12},{12,8},{16,20},{20,16},{24,28},{28,24},{1,5},{5... | collective-permute-start | bytes 196616 | tf_op jit(solution)/shard_map/state_y/ppermute | solution.py:147
  11.1 13.9 %copy-start.1 = (bf16[128,2048]{1,0:T(8,128)(2,1)S(1)}, bf16[128,2048]{1,0:T(8,128)(2,1)}, u32[]{:S(2)}) copy-start(bf16[128,2048]{1,0:T(8,128)(2,1)} %q_ref.7) | copy-start | bytes 1572868
  11.1 13.9 %copy-start.4 = (f32[2048,16]{0,1:T(8,128)S(1)}, f32[2048,16]{0,1:T(8,128)}, u32[]{:S(2)}) copy-start(f32[2048,16]{0,1:T(8,128)} %param.11) | copy-start | bytes 393220
  11.1 13.9 %copy-start.5 = (f32[2048,16]{0,1:T(8,128)S(1)}, f32[2048,16]{0,1:T(8,128)}, u32[]{:S(2)}) copy-start(f32[2048,16]{0,1:T(8,128)} %param.10) | copy-start | bytes 393220
  11.1 6.7 %collective-permute-start.1 = (bf16[16,2048]{1,0:T(8,128)(2,1)S(1)}, bf16[16,2048]{1,0:T(8,128)(2,1)S(1)}, u32[]{:S(2)}, u32[]{:S(2)}) collective-permute-start(bf16[16,2048]{1,0:T(8,128)(2,1)S(1)} %get-tuple-element.47), channel_id=1, source_target_pairs={{0,8},{4,12},{8,16},{12,20},{16,24},{20,28},{1,9},{5,13},{9,17},{1... | collective-permute-start | bytes 196616 | tf_op jit(solution)/shard_map/state_1/ppermute | solution.py:147
  17.8 7.2 %collective-permute-start.2 = (bf16[16,2048]{1,0:T(8,128)(2,1)S(1)}, bf16[16,2048]{1,0:T(8,128)(2,1)S(1)}, u32[]{:S(2)}, u32[]{:S(2)}) collective-permute-start(bf16[16,2048]{1,0:T(8,128)(2,1)S(1)} %add_convert_fusion.2), channel_id=1, source_target_pairs={{0,16},{4,20},{8,24},{12,28},{1,17},{5,21},{9,25},{13,29},{2,18},{... | collective-permute-start | bytes 196616 | tf_op jit(solution)/shard_map/state_2/ppermute | solution.py:147
  25.0 1.2 %copy-start = (f32[128,2048]{1,0:T(8,128)S(1)}, f32[128,2048]{1,0:T(8,128)}, u32[]{:S(2)}) copy-start(f32[128,2048]{1,0:T(8,128)} %shard_map.76.base_ref) | copy-start | bytes 3145732
  28.5 12.0 %collective-permute-start.5 = (bf16[128,2048]{1,0:T(8,128)(2,1)S(1)}, bf16[128,2048]{1,0:T(8,128)(2,1)S(1)}, u32[]{:S(2)}, u32[]{:S(2)}) collective-permute-start(bf16[128,2048]{1,0:T(8,128)(2,1)S(1)} %shard_map.77), channel_id=1, source_target_pairs={{0,4},{4,0},{8,12},{12,8},{16,20},{20,16},{24,28},{28,24},{1,5},{5... | collective-permute-start | bytes 1572872 | tf_op jit(solution)/shard_map/near_y/ppermute | solution.py:147
  29.1 13.6 %collective-permute-start.4 = (bf16[128,2048]{1,0:T(8,128)(2,1)S(1)}, bf16[128,2048]{1,0:T(8,128)(2,1)S(1)}, u32[]{:S(2)}, u32[]{:S(2)}) collective-permute-start(bf16[128,2048]{1,0:T(8,128)(2,1)S(1)} %shard_map.77), channel_id=1, source_target_pairs={{8,16},{12,20},{16,8},{20,12},{9,17},{13,21},{17,9},{21,13},{10,18... | collective-permute-start | bytes 1572872 | tf_op jit(solution)/shard_map/middle/ppermute | solution.py:147
  32.6 11.4 %collective-permute-start.3 = (bf16[128,2048]{1,0:T(8,128)(2,1)S(1)}, bf16[128,2048]{1,0:T(8,128)(2,1)S(1)}, u32[]{:S(2)}, u32[]{:S(2)}) collective-permute-start(bf16[128,2048]{1,0:T(8,128)(2,1)S(1)} %shard_map.77), channel_id=1, source_target_pairs={{0,8},{4,12},{8,0},{12,4},{16,24},{20,28},{24,16},{28,20},{1,9},{5... | collective-permute-start | bytes 1572872 | tf_op jit(solution)/shard_map/one/ppermute | solution.py:147
  32.7 11.2 %copy-start.6 = (bf16[2048,1024]{1,0:T(8,128)(2,1)S(1)}, bf16[2048,1024]{1,0:T(8,128)(2,1)}, u32[]{:S(2)}) copy-start(bf16[2048,1024]{1,0:T(8,128)(2,1)} %param.13) | copy-start | bytes 12582916
  44.7 13.1 %collective-permute-start.8 = (bf16[128,2048]{1,0:T(8,128)(2,1)S(1)}, bf16[128,2048]{1,0:T(8,128)(2,1)S(1)}, u32[]{:S(2)}, u32[]{:S(2)}) collective-permute-start(bf16[128,2048]{1,0:T(8,128)(2,1)S(1)} %collective-permute-done.3), channel_id=1, source_target_pairs={{0,4},{4,0},{8,12},{12,8},{16,20},{20,16},{24,28},{28,24},{1,5},{5... | collective-permute-start | bytes 1572872 | tf_op jit(solution)/shard_map/one_y/ppermute | solution.py:147
  46.2 12.1 %collective-permute-start.6 = (bf16[128,2048]{1,0:T(8,128)(2,1)S(1)}, bf16[128,2048]{1,0:T(8,128)(2,1)S(1)}, u32[]{:S(2)}, u32[]{:S(2)}) collective-permute-start(bf16[128,2048]{1,0:T(8,128)(2,1)S(1)} %collective-permute-done.3), channel_id=1, source_target_pairs={{8,16},{12,20},{16,8},{20,12},{9,17},{13,21},{17,9},{21,13},{10,18... | collective-permute-start | bytes 1572872 | tf_op jit(solution)/shard_map/given/ppermute | solution.py:147
  48.7 9.0 %collective-permute-start.7 = (bf16[128,2048]{1,0:T(8,128)(2,1)S(1)}, bf16[128,2048]{1,0:T(8,128)(2,1)S(1)}, u32[]{:S(2)}, u32[]{:S(2)}) collective-permute-start(bf16[128,2048]{1,0:T(8,128)(2,1)S(1)} %collective-permute-done.4), channel_id=1, source_target_pairs={{8,0},{12,4},{16,24},{20,28},{9,1},{13,5},{17,25},{21,29},{10,2},{... | collective-permute-start | bytes 1572872 | tf_op jit(solution)/shard_map/out2/ppermute | solution.py:147
  58.3 8.3 %collective-permute-start.13 = (bf16[128,1024]{1,0:T(8,128)(2,1)S(1)}, bf16[128,1024]{1,0:T(8,128)(2,1)S(1)}, u32[]{:S(2)}, u32[]{:S(2)}) collective-permute-start(bf16[128,1024]{1,0:T(8,128)(2,1)S(1)} %slice.23), channel_id=1, source_target_pairs={{8,16},{12,20},{16,8},{20,12},{9,17},{13,21},{17,9},{21,13},{10,18... | collective-permute-start | bytes 786440 | tf_op jit(solution)/shard_map/middle_y/ppermute | solution.py:147
  61.9 2.6 %collective-permute-start.11 = (bf16[2,128,1024]{2,1,0:T(8,128)(2,1)S(1)}, bf16[2,128,1024]{2,1,0:T(8,128)(2,1)S(1)}, u32[]{:S(2)}, u32[]{:S(2)}) collective-permute-start(bf16[2,128,1024]{2,1,0:T(8,128)(2,1)S(1)} %pad_maximum_fusion), channel_id=1, source_target_pairs={{0,1},{1,0},{2,3},{3,2},{4,5},{5,4},{6,7},{7,6},{8,9},{9,8},{10,11... | collective-permute-start | bytes 1572872 | tf_op jit(solution)/shard_map/core_0/ppermute | solution.py:147
  62.0 16.0 %collective-permute-start.9 = (bf16[128,2048]{1,0:T(8,128)(2,1)S(1)}, bf16[128,2048]{1,0:T(8,128)(2,1)S(1)}, u32[]{:S(2)}, u32[]{:S(2)}) collective-permute-start(bf16[128,2048]{1,0:T(8,128)(2,1)S(1)} %collective-permute-done.6), channel_id=1, source_target_pairs={{8,0},{12,4},{16,24},{20,28},{9,1},{13,5},{17,25},{21,29},{10,2},{... | collective-permute-start | bytes 1572872 | tf_op jit(solution)/shard_map/out3/ppermute | solution.py:147
  63.9 14.1 %collective-permute-start.10 = (bf16[128,2048]{1,0:T(8,128)(2,1)S(1)}, bf16[128,2048]{1,0:T(8,128)(2,1)S(1)}, u32[]{:S(2)}, u32[]{:S(2)}) collective-permute-start(bf16[128,2048]{1,0:T(8,128)(2,1)S(1)} %broadcast_select_fusion.1), channel_id=1, source_target_pairs={{0,4},{4,0},{8,12},{12,8},{16,20},{20,16},{24,28},{28,24},{1,5},{5... | collective-permute-start | bytes 1572872 | tf_op jit(solution)/shard_map/two_y/ppermute | solution.py:147
  64.7 13.2 %collective-permute-start.12 = (bf16[128,1024]{1,0:T(8,128)(2,1)S(1)}, bf16[128,1024]{1,0:T(8,128)(2,1)S(1)}, u32[]{:S(2)}, u32[]{:S(2)}) collective-permute-start(bf16[128,1024]{1,0:T(8,128)(2,1)S(1)} %fusion.10), channel_id=1, source_target_pairs={{0,2},{1,3},{2,0},{3,1},{4,6},{5,7},{6,4},{7,5},{8,10},{9,11},{10,... | collective-permute-start | bytes 786440 | tf_op jit(solution)/shard_map/side_0/ppermute | solution.py:147
  79.5 2.8 %collective-permute-start.17 = (bf16[128,1024]{1,0:T(8,128)(2,1)S(1)}, bf16[128,1024]{1,0:T(8,128)(2,1)S(1)}, u32[]{:S(2)}, u32[]{:S(2)}) collective-permute-start(bf16[128,1024]{1,0:T(8,128)(2,1)S(1)} %get-tuple-element.44), channel_id=1, source_target_pairs={{0,1},{1,0},{2,3},{3,2},{4,5},{5,4},{6,7},{7,6},{8,9},{9,8},{10,11... | collective-permute-start | bytes 786440 | tf_op jit(solution)/shard_map/core_2/ppermute | solution.py:147
  79.7 8.2 %collective-permute-start.15 = (bf16[128,1024]{1,0:T(8,128)(2,1)S(1)}, bf16[128,1024]{1,0:T(8,128)(2,1)S(1)}, u32[]{:S(2)}, u32[]{:S(2)}) collective-permute-start(bf16[128,1024]{1,0:T(8,128)(2,1)S(1)} %slice.27), channel_id=1, source_target_pairs={{8,0},{12,4},{16,24},{20,28},{9,1},{13,5},{17,25},{21,29},{10,2},{... | collective-permute-start | bytes 786440 | tf_op jit(solution)/shard_map/out_y/ppermute | solution.py:147
  81.7 8.5 %collective-permute-start.14 = (bf16[128,1024]{1,0:T(8,128)(2,1)S(1)}, bf16[128,1024]{1,0:T(8,128)(2,1)S(1)}, u32[]{:S(2)}, u32[]{:S(2)}) collective-permute-start(bf16[128,1024]{1,0:T(8,128)(2,1)S(1)} %slice.32), channel_id=1, source_target_pairs={{0,4},{4,0},{8,12},{12,8},{16,20},{20,16},{24,28},{28,24},{1,5},{5... | collective-permute-start | bytes 786440 | tf_op jit(solution)/shard_map/three_y/ppermute | solution.py:147
  82.5 8.6 %collective-permute-start.18 = (bf16[128,1024]{1,0:T(8,128)(2,1)S(1)}, bf16[128,1024]{1,0:T(8,128)(2,1)S(1)}, u32[]{:S(2)}, u32[]{:S(2)}) collective-permute-start(bf16[128,1024]{1,0:T(8,128)(2,1)S(1)} %fusion.15), channel_id=1, source_target_pairs={{2,0},{3,1},{6,4},{7,5},{10,8},{11,9},{14,12},{15,13},{16,18},{17,... | collective-permute-start | bytes 786440 | tf_op jit(solution)/shard_map/side_2/ppermute | solution.py:147
  91.3 1.6 %collective-permute-start.19 = (bf16[128,1024]{1,0:T(8,128)(2,1)S(1)}, bf16[128,1024]{1,0:T(8,128)(2,1)S(1)}, u32[]{:S(2)}, u32[]{:S(2)}) collective-permute-start(bf16[128,1024]{1,0:T(8,128)(2,1)S(1)} %select_convert_fusion), channel_id=1, source_target_pairs={{0,1},{1,0},{2,3},{3,2},{4,5},{5,4},{6,7},{7,6},{8,9},{9,8},{10,11... | collective-permute-start | bytes 786440 | tf_op jit(solution)/shard_map/core_3/ppermute | solution.py:147
  93.0 10.2 %collective-permute-start.20 = (bf16[128,1024]{1,0:T(8,128)(2,1)S(1)}, bf16[128,1024]{1,0:T(8,128)(2,1)S(1)}, u32[]{:S(2)}, u32[]{:S(2)}) collective-permute-start(bf16[128,1024]{1,0:T(8,128)(2,1)S(1)} %fusion.16), channel_id=1, source_target_pairs={{0,2},{1,3},{4,6},{5,7},{8,10},{9,11},{12,14},{13,15},{18,16},{19,... | collective-permute-start | bytes 786440 | tf_op jit(solution)/shard_map/side_3/ppermute | solution.py:147
  94.3 16.1 %collective-permute-start.22 = (bf16[128,1024]{1,0:T(8,128)(2,1)S(1)}, bf16[128,1024]{1,0:T(8,128)(2,1)S(1)}, u32[]{:S(2)}, u32[]{:S(2)}) collective-permute-start(bf16[128,1024]{1,0:T(8,128)(2,1)S(1)} %fusion.7), channel_id=1, source_target_pairs={{2,4},{1,12},{6,0},{5,8},{10,13},{9,5},{14,9},{13,1},{18,22},{17,3... | collective-permute-start | bytes 786440 | tf_op jit(solution)/shard_map/own_0/ppermute | solution.py:147
  98.9 11.5 %collective-permute-start.16 = (bf16[128,1024]{1,0:T(8,128)(2,1)S(1)}, bf16[128,1024]{1,0:T(8,128)(2,1)S(1)}, u32[]{:S(2)}, u32[]{:S(2)}) collective-permute-start(bf16[128,1024]{1,0:T(8,128)(2,1)S(1)} %fusion.7), channel_id=1, source_target_pairs={{0,0},{3,8},{4,4},{7,12},{8,9},{11,1},{12,13},{15,5},{16,18},{19,2... | collective-permute-start | bytes 786440 | tf_op jit(solution)/shard_map/own_0/ppermute | solution.py:147
  103.4 17.3 %collective-permute-start.23 = (bf16[128,1024]{1,0:T(8,128)(2,1)S(1)}, bf16[128,1024]{1,0:T(8,128)(2,1)S(1)}, u32[]{:S(2)}, u32[]{:S(2)}) collective-permute-start(bf16[128,1024]{1,0:T(8,128)(2,1)S(1)} %fusion.11), channel_id=1, source_target_pairs={{1,20},{3,28},{5,16},{7,24},{9,29},{11,21},{13,25},{15,17},{19,6},... | collective-permute-start | bytes 786440 | tf_op jit(solution)/shard_map/own_2/ppermute | solution.py:147
  104.7 16.0 %collective-permute-start.21 = (bf16[128,1024]{1,0:T(8,128)(2,1)S(1)}, bf16[128,1024]{1,0:T(8,128)(2,1)S(1)}, u32[]{:S(2)}, u32[]{:S(2)}) collective-permute-start(bf16[128,1024]{1,0:T(8,128)(2,1)S(1)} %fusion.11), channel_id=1, source_target_pairs={{0,16},{2,24},{4,20},{6,28},{8,25},{10,17},{12,29},{14,21},{18,2},... | collective-permute-start | bytes 786440 | tf_op jit(solution)/shard_map/own_2/ppermute | solution.py:147

commit v4 on v3

--- a/solution.py
+++ b/solution.py
@@ -255,13 +255,13 @@
         turned = moved(keep.astype(BF16), BOTH, pairs, f"side_{group}")
         return (keep + turned.astype(F32)).astype(BF16)
 
-    out3, two_y, close_side, middle_y = fence(out3, two_y, close_side, middle_y)
+    out3, two_y, middle_y = fence(out3, two_y, middle_y)
     three = jnp.where(at_end, out3, middle)
     three_y = across(three[:, :split], every, "three_y")
     out_y = along(two_y[:, split:], outward, "out_y")
     with_three = matmul(three, w_out)
+    three_y, out_y, close_side = fence(three_y, out_y, close_side)
     tile = (keep + close_side.astype(F32)).astype(BF16)
-    three_y, out_y, tile = fence(three_y, out_y, tile)
     close = [moved(tile, BOTH, pairs, "own_0") for pairs in owners(0)]
     with_three_y = matmul(three_y, w_out[:split]) + matmul(jnp.where(at_end, out_y, middle_y), w_out[split:])
     tile2 = remote(2, [matmul(two, w_out), matmul(two_y, w_out)], [with_three])

time: 122 us -> 119 us (0.975)
  waiting for transfers between devices: 48.1 us -> 43 us
  starting transfers between devices: 43.2 us -> 44.5 us
    ppermute x24, waiting for transfers between devices: 48.1 us -> 43 us  [moved(): return lax.ppermute(x, axes, pairs)]
    ppermute x24, starting transfers between devices: 43.2 us -> 44.5 us  [moved(): return lax.ppermute(x, axes, pairs)]
  transfers between devices with their start and end apart: 24 -> 24, of which waited for: 12 -> 13; matrix products, arithmetic and copies ran while one was open for 6% -> 7% of each run, Pallas kernels for 9% -> 9%
where the time goes in v4:
time: 119 us
  starting transfers between devices  44.5 us (37%)
  waiting for transfers between devices  43 us (36%)
  Pallas kernels  16.9 us (14%)
  matrix products  8.34 us (7%)
  other arithmetic  4.1 us (3%)
  local copies, waits for them, and re-layouts  1.31 us (1%)
    ppermute x24, starting transfers between devices, moved(): return lax.ppermute(x, axes, pairs)  44.5 us
    ppermute x24, waiting for transfers between devices, moved(): return lax.ppermute(x, axes, pairs)  43 us
    pallas_call x5, Pallas kernels, run(): pl.pallas_call(kernel, grid=(steps,), out_shape=out, in_specs=specs, out_...  16.9 us
    dot_general x9, matrix products, matmul(): return jnp.dot(x, w, preferred_element_type=F32)  8.34 us
  transfers between devices with their start and end apart: 24, of which 13 were waited for; matrix products, arithmetic and copies ran while one was open for 7% of the time, Pallas kernels for 9%

profile of v4, /device:TPU:10, one launch (start us, length us, event | category | flops | bytes accessed | tf_op | source)
XLA Modules:
  0.0 118.7 jit_solution(16051133075907808129)
XLA Ops:
  0.0 4.3 %shard_map.73 = bf16[16,2048]{1,0:T(8,128)(2,1)} custom-call(bf16[128,2048]{1,0:T(8,128)(2,1)} %k_ref.7, bf16[128,2048]{1,0:T(8,128)(2,1)} %v_ref.7, f32[16,2048]{1,0:T(8,128)} %bitcast.35), custom_call_target="tpu_custom_call" | custom-call | flops 12582912 | bytes 1572864 | tf_op jit(solution)/shard_map/pallas_call | solution.py:126
  4.3 1.5 %collective-permute-start = (bf16[16,2048]{1,0:T(8,128)(2,1)}, bf16[16,2048]{1,0:T(8,128)(2,1)S(1)}, u32[]{:S(2)}, u32[]{:S(2)}) collective-permute-start(bf16[16,2048]{1,0:T(8,128)(2,1)} %shard_map.73), channel_id=1, source_target_pairs={{0,4},{4,0},{8,12},{12,8},{16,20},{20,16},{24,28},{28,24},{1,5},{5... | collective-permute-start | bytes 196616 | tf_op jit(solution)/shard_map/state_y/ppermute | solution.py:147
  5.8 4.3 %shard_map.74.rest_0_ = f32[128,2048]{1,0:T(8,128)} custom-call(bf16[128,2048]{1,0:T(8,128)(2,1)} %q_ref.7, bf16[128,2048]{1,0:T(8,128)(2,1)} %k_ref.7, bf16[128,2048]{1,0:T(8,128)(2,1)} %v_ref.7, f32[16,2048]{1,0:T(8,128)} %bitcast.40, f32[16,2048]{1,0:T(8,128)} %bitcast.36, f32[1,2048]{1,0:T(1,128)} %bitcast.44), custom_call_target="tpu_custom_call" | custom-call | flops 13107200 | bytes 786432 | tf_op jit(solution)/shard_map/pallas_call | solution.py:126
  10.2 0.9 fusion.14
  11.1 3.6 %collective-permute-start.1 = (bf16[16,2048]{1,0:T(8,128)(2,1)S(1)}, bf16[16,2048]{1,0:T(8,128)(2,1)S(1)}, u32[]{:S(2)}, u32[]{:S(2)}) collective-permute-start(bf16[16,2048]{1,0:T(8,128)(2,1)S(1)} %get-tuple-element.45), channel_id=1, source_target_pairs={{0,8},{4,12},{8,16},{12,20},{16,24},{20,28},{1,9},{5,13},{9,17},{1... | collective-permute-start | bytes 196616 | tf_op jit(solution)/shard_map/state_1/ppermute | solution.py:147
  14.7 3.0 %shard_map.75.rest_0_ = f32[128,2048]{1,0:T(8,128)} custom-call(bf16[128,2048]{1,0:T(8,128)(2,1)} %q_ref.7, bf16[128,2048]{1,0:T(8,128)(2,1)} %k_ref.7, bf16[128,2048]{1,0:T(8,128)(2,1)} %v_ref.7, f32[16,2048]{1,0:T(8,128)} %bitcast.41, f32[16,2048]{1,0:T(8,128)} %bitcast.37, f32[1,2048]{1,0:T(1,128)} %bitcast.45, ...), custom_call_target="tpu_custom_call", output_to_operand_aliasing={{}: (6, {})} | custom-call | flops 6553600 | bytes 393216 | tf_op jit(solution)/shard_map/pallas_call | solution.py:126
  17.8 4.1 %collective-permute-start.2 = (bf16[16,2048]{1,0:T(8,128)(2,1)S(1)}, bf16[16,2048]{1,0:T(8,128)(2,1)S(1)}, u32[]{:S(2)}, u32[]{:S(2)}) collective-permute-start(bf16[16,2048]{1,0:T(8,128)(2,1)S(1)} %add_convert_fusion.2), channel_id=1, source_target_pairs={{0,16},{4,20},{8,24},{12,28},{1,17},{5,21},{9,25},{13,29},{2,18},{... | collective-permute-start | bytes 196616 | tf_op jit(solution)/shard_map/state_2/ppermute | solution.py:147
  22.0 3.0 %shard_map.76.base_ref = f32[128,2048]{1,0:T(8,128)} custom-call(bf16[128,2048]{1,0:T(8,128)(2,1)} %q_ref.7, bf16[128,2048]{1,0:T(8,128)(2,1)} %k_ref.7, bf16[128,2048]{1,0:T(8,128)(2,1)} %v_ref.7, f32[16,2048]{1,0:T(8,128)} %bitcast.42, f32[16,2048]{1,0:T(8,128)} %bitcast.38, f32[1,2048]{1,0:T(1,128)} %bitcast.46, ...), custom_call_target="tpu_custom_call", output_to_operand_aliasing={{}: (6, {})} | custom-call | flops 6553600 | bytes 393216 | tf_op jit(solution)/shard_map/pallas_call | solution.py:126
  25.0 1.2 %copy-done = f32[128,2048]{1,0:T(8,128)S(1)} copy-done((f32[128,2048]{1,0:T(8,128)S(1)}, f32[128,2048]{1,0:T(8,128)}, u32[]{:S(2)}) %copy-start) | copy-done | bytes 1048600
  26.3 2.2 %shard_map.77 = bf16[128,2048]{1,0:T(8,128)(2,1)S(1)} custom-call(s32[1]{0:T(128)} %bitcast.odd_ref, bf16[128,2048]{1,0:T(8,128)(2,1)S(1)} %copy-done.1, f32[128,2048]{1,0:T(8,128)S(1)} %copy-done, bf16[16,2048]{1,0:T(8,128)(2,1)S(1)} %collective-permute-done.1.below_ref, bf16[16,2048]{1,0:T(8,128)(2,1)S(1)} %collective-permute-done.2.further_ref, ...), custom_call_target="tpu_custom_call" | custom-call | flops 8388608 | bytes 1572864 | tf_op jit(solution)/shard_map/pallas_call | solution.py:126
  28.5 0.6 collective-permute-start.5
  29.1 3.5 %collective-permute-start.4 = (bf16[128,2048]{1,0:T(8,128)(2,1)S(1)}, bf16[128,2048]{1,0:T(8,128)(2,1)S(1)}, u32[]{:S(2)}, u32[]{:S(2)}) collective-permute-start(bf16[128,2048]{1,0:T(8,128)(2,1)S(1)} %shard_map.77), channel_id=1, source_target_pairs={{8,16},{12,20},{16,8},{20,12},{9,17},{13,21},{17,9},{21,13},{10,18... | collective-permute-start | bytes 1572872 | tf_op jit(solution)/shard_map/middle/ppermute | solution.py:147
  32.7 3.0 %fusion.17 = f32[128,1024]{1,0:T(8,128)S(1)} fusion(bf16[128,2048]{1,0:T(8,128)(2,1)S(1)} %shard_map.77, bf16[2048,1024]{1,0:T(8,128)(2,1)} %param.13), kind=kOutput, calls=%fused_computation.40 | convolution fusion | flops 536870912 | bytes 5242880 | tf_op jit(solution)/shard_map/dot_general | solution.py:142
  35.8 4.8 %collective-permute-done.5 = bf16[128,2048]{1,0:T(8,128)(2,1)S(1)} collective-permute-done((bf16[128,2048]{1,0:T(8,128)(2,1)S(1)}, bf16[128,2048]{1,0:T(8,128)(2,1)S(1)}, u32[]{:S(2)}, u32[]{:S(2)}) %collective-permute-start.5) | collective-permute-done | bytes 524320 | tf_op jit(solution)/shard_map/near_y/ppermute | solution.py:147
  40.5 2.1 %collective-permute-done.4 = bf16[128,2048]{1,0:T(8,128)(2,1)S(1)} collective-permute-done((bf16[128,2048]{1,0:T(8,128)(2,1)S(1)}, bf16[128,2048]{1,0:T(8,128)(2,1)S(1)}, u32[]{:S(2)}, u32[]{:S(2)}) %collective-permute-start.4) | collective-permute-done | bytes 524320 | tf_op jit(solution)/shard_map/middle/ppermute | solution.py:147
  42.6 1.3 %collective-permute-done.3 = bf16[128,2048]{1,0:T(8,128)(2,1)S(1)} collective-permute-done((bf16[128,2048]{1,0:T(8,128)(2,1)S(1)}, bf16[128,2048]{1,0:T(8,128)(2,1)S(1)}, u32[]{:S(2)}, u32[]{:S(2)}) %collective-permute-start.3) | collective-permute-done | bytes 524320 | tf_op jit(solution)/shard_map/one/ppermute | solution.py:147
  43.9 0.7 fusion.18
  44.7 1.6 %collective-permute-start.8 = (bf16[128,2048]{1,0:T(8,128)(2,1)S(1)}, bf16[128,2048]{1,0:T(8,128)(2,1)S(1)}, u32[]{:S(2)}, u32[]{:S(2)}) collective-permute-start(bf16[128,2048]{1,0:T(8,128)(2,1)S(1)} %collective-permute-done.3), channel_id=1, source_target_pairs={{0,4},{4,0},{8,12},{12,8},{16,20},{20,16},{24,28},{28,24},{1,5},{5... | collective-permute-start | bytes 1572872 | tf_op jit(solution)/shard_map/one_y/ppermute | solution.py:147
  46.2 2.5 %collective-permute-start.6 = (bf16[128,2048]{1,0:T(8,128)(2,1)S(1)}, bf16[128,2048]{1,0:T(8,128)(2,1)S(1)}, u32[]{:S(2)}, u32[]{:S(2)}) collective-permute-start(bf16[128,2048]{1,0:T(8,128)(2,1)S(1)} %collective-permute-done.3), channel_id=1, source_target_pairs={{8,16},{12,20},{16,8},{20,12},{9,17},{13,21},{17,9},{21,13},{10,18... | collective-permute-start | bytes 1572872 | tf_op jit(solution)/shard_map/given/ppermute | solution.py:147
  48.7 1.3 %collective-permute-start.7 = (bf16[128,2048]{1,0:T(8,128)(2,1)S(1)}, bf16[128,2048]{1,0:T(8,128)(2,1)S(1)}, u32[]{:S(2)}, u32[]{:S(2)}) collective-permute-start(bf16[128,2048]{1,0:T(8,128)(2,1)S(1)} %collective-permute-done.4), channel_id=1, source_target_pairs={{8,0},{12,4},{16,24},{20,28},{9,1},{13,5},{17,25},{21,29},{10,2},{... | collective-permute-start | bytes 1572872 | tf_op jit(solution)/shard_map/out2/ppermute | solution.py:147
  50.2 0.7 fusion.19
  51.0 6.8 %collective-permute-done.7 = bf16[128,2048]{1,0:T(8,128)(2,1)S(1)} collective-permute-done((bf16[128,2048]{1,0:T(8,128)(2,1)S(1)}, bf16[128,2048]{1,0:T(8,128)(2,1)S(1)}, u32[]{:S(2)}, u32[]{:S(2)}) %collective-permute-start.7) | collective-permute-done | bytes 524320 | tf_op jit(solution)/shard_map/out2/ppermute | solution.py:147
  58.2 0.7 fusion.20
  59.0 2.8 %collective-permute-start.12 = (bf16[128,1024]{1,0:T(8,128)(2,1)S(1)}, bf16[128,1024]{1,0:T(8,128)(2,1)S(1)}, u32[]{:S(2)}, u32[]{:S(2)}) collective-permute-start(bf16[128,1024]{1,0:T(8,128)(2,1)S(1)} %slice.23), channel_id=1, source_target_pairs={{8,16},{12,20},{16,8},{20,12},{9,17},{13,21},{17,9},{21,13},{10,18... | collective-permute-start | bytes 786440 | tf_op jit(solution)/shard_map/middle_y/ppermute | solution.py:147
  61.7 1.8 %collective-permute-start.10 = (bf16[128,2048]{1,0:T(8,128)(2,1)S(1)}, bf16[128,2048]{1,0:T(8,128)(2,1)S(1)}, u32[]{:S(2)}, u32[]{:S(2)}) collective-permute-start(bf16[128,2048]{1,0:T(8,128)(2,1)S(1)} %collective-permute-done.6), channel_id=1, source_target_pairs={{8,0},{12,4},{16,24},{20,28},{9,1},{13,5},{17,25},{21,29},{10,2},{... | collective-permute-start | bytes 1572872 | tf_op jit(solution)/shard_map/out3/ppermute | solution.py:147
  63.7 0.6 collective-permute-start.11
  64.4 0.7 fusion.21
  65.2 2.0 %collective-permute-done.12 = bf16[128,1024]{1,0:T(8,128)(2,1)S(1)} collective-permute-done((bf16[128,1024]{1,0:T(8,128)(2,1)S(1)}, bf16[128,1024]{1,0:T(8,128)(2,1)S(1)}, u32[]{:S(2)}, u32[]{:S(2)}) %collective-permute-start.12) | collective-permute-done | bytes 262176 | tf_op jit(solution)/shard_map/middle_y/ppermute | solution.py:147
  67.2 5.7 %collective-permute-done.11 = bf16[128,2048]{1,0:T(8,128)(2,1)S(1)} collective-permute-done((bf16[128,2048]{1,0:T(8,128)(2,1)S(1)}, bf16[128,2048]{1,0:T(8,128)(2,1)S(1)}, u32[]{:S(2)}, u32[]{:S(2)}) %collective-permute-start.11) | collective-permute-done | bytes 524320 | tf_op jit(solution)/shard_map/two_y/ppermute | solution.py:147
  73.0 0.7 fusion.22
  73.7 0.7 select_convert_fusion.1
  74.8 0.6 collective-permute-start.15
  75.4 1.8 %collective-permute-start.14 = (bf16[128,1024]{1,0:T(8,128)(2,1)S(1)}, bf16[128,1024]{1,0:T(8,128)(2,1)S(1)}, u32[]{:S(2)}, u32[]{:S(2)}) collective-permute-start(bf16[128,1024]{1,0:T(8,128)(2,1)S(1)} %slice.27), channel_id=1, source_target_pairs={{8,0},{12,4},{16,24},{20,28},{9,1},{13,5},{17,25},{21,29},{10,2},{... | collective-permute-start | bytes 786440 | tf_op jit(solution)/shard_map/out_y/ppermute | solution.py:147
  77.2 0.6 collective-permute-start.13
  77.9 3.4 %collective-permute-start.18 = (bf16[128,1024]{1,0:T(8,128)(2,1)S(1)}, bf16[128,1024]{1,0:T(8,128)(2,1)S(1)}, u32[]{:S(2)}, u32[]{:S(2)}) collective-permute-start(bf16[128,1024]{1,0:T(8,128)(2,1)S(1)} %fusion.15), channel_id=1, source_target_pairs={{2,0},{3,1},{6,4},{7,5},{10,8},{11,9},{14,12},{15,13},{16,18},{17,... | collective-permute-start | bytes 786440 | tf_op jit(solution)/shard_map/side_2/ppermute | solution.py:147
  81.3 2.3 %collective-permute-done.15 = bf16[128,1024]{1,0:T(8,128)(2,1)S(1)} collective-permute-done((bf16[128,1024]{1,0:T(8,128)(2,1)S(1)}, bf16[128,1024]{1,0:T(8,128)(2,1)S(1)}, u32[]{:S(2)}, u32[]{:S(2)}) %collective-permute-start.15) | collective-permute-done | bytes 262176 | tf_op jit(solution)/shard_map/side_0/ppermute | solution.py:147
  83.6 1.8 %collective-permute-done.13 = bf16[128,1024]{1,0:T(8,128)(2,1)S(1)} collective-permute-done((bf16[128,1024]{1,0:T(8,128)(2,1)S(1)}, bf16[128,1024]{1,0:T(8,128)(2,1)S(1)}, u32[]{:S(2)}, u32[]{:S(2)}) %collective-permute-start.13) | collective-permute-done | bytes 262176 | tf_op jit(solution)/shard_map/three_y/ppermute | solution.py:147
  86.3 0.9 collective-permute-done.18
  87.5 1.5 %collective-permute-done.19 = bf16[128,1024]{1,0:T(8,128)(2,1)S(1)} collective-permute-done((bf16[128,1024]{1,0:T(8,128)(2,1)S(1)}, bf16[128,1024]{1,0:T(8,128)(2,1)S(1)}, u32[]{:S(2)}, u32[]{:S(2)}) %collective-permute-start.19) | collective-permute-done | bytes 262176 | tf_op jit(solution)/shard_map/core_3/ppermute | solution.py:147
  89.2 1.3 %collective-permute-start.20 = (bf16[128,1024]{1,0:T(8,128)(2,1)S(1)}, bf16[128,1024]{1,0:T(8,128)(2,1)}, u32[]{:S(2)}, u32[]{:S(2)}) collective-permute-start(bf16[128,1024]{1,0:T(8,128)(2,1)S(1)} %fusion.16), channel_id=1, source_target_pairs={{0,2},{1,3},{4,6},{5,7},{8,10},{9,11},{12,14},{13,15},{18,16},{19,... | collective-permute-start | bytes 786440 | tf_op jit(solution)/shard_map/side_3/ppermute | solution.py:147
  90.6 5.2 %collective-permute-start.22 = (bf16[128,1024]{1,0:T(8,128)(2,1)S(1)}, bf16[128,1024]{1,0:T(8,128)(2,1)S(1)}, u32[]{:S(2)}, u32[]{:S(2)}) collective-permute-start(bf16[128,1024]{1,0:T(8,128)(2,1)S(1)} %fusion.7), channel_id=1, source_target_pairs={{2,4},{1,12},{6,0},{5,8},{10,13},{9,5},{14,9},{13,1},{18,22},{17,3... | collective-permute-start | bytes 786440 | tf_op jit(solution)/shard_map/own_0/ppermute | solution.py:147
  95.8 0.7 collective-permute-start.16
  96.5 3.2 %collective-permute-done.20 = bf16[128,1024]{1,0:T(8,128)(2,1)} collective-permute-done((bf16[128,1024]{1,0:T(8,128)(2,1)S(1)}, bf16[128,1024]{1,0:T(8,128)(2,1)}, u32[]{:S(2)}, u32[]{:S(2)}) %collective-permute-start.20) | collective-permute-done | bytes 262176 | tf_op jit(solution)/shard_map/side_3/ppermute | solution.py:147
  99.6 1.1 fusion.11
  100.8 1.3 %collective-permute-start.23 = (bf16[128,1024]{1,0:T(8,128)(2,1)S(1)}, bf16[128,1024]{1,0:T(8,128)(2,1)S(1)}, u32[]{:S(2)}, u32[]{:S(2)}) collective-permute-start(bf16[128,1024]{1,0:T(8,128)(2,1)S(1)} %fusion.11), channel_id=1, source_target_pairs={{1,20},{3,28},{5,16},{7,24},{9,29},{11,21},{13,25},{15,17},{19,6},... | collective-permute-start | bytes 786440 | tf_op jit(solution)/shard_map/own_2/ppermute | solution.py:147
  102.0 5.6 %collective-permute-start.21 = (bf16[128,1024]{1,0:T(8,128)(2,1)S(1)}, bf16[128,1024]{1,0:T(8,128)(2,1)S(1)}, u32[]{:S(2)}, u32[]{:S(2)}) collective-permute-start(bf16[128,1024]{1,0:T(8,128)(2,1)S(1)} %fusion.11), channel_id=1, source_target_pairs={{0,16},{2,24},{4,20},{6,28},{8,25},{10,17},{12,29},{14,21},{18,2},... | collective-permute-start | bytes 786440 | tf_op jit(solution)/shard_map/own_2/ppermute | solution.py:147
  107.6 10.2 %collective-permute-done.23 = bf16[128,1024]{1,0:T(8,128)(2,1)S(1)} collective-permute-done((bf16[128,1024]{1,0:T(8,128)(2,1)S(1)}, bf16[128,1024]{1,0:T(8,128)(2,1)S(1)}, u32[]{:S(2)}, u32[]{:S(2)}) %collective-permute-start.23) | collective-permute-done | bytes 262176 | tf_op jit(solution)/shard_map/own_2/ppermute | solution.py:147
  117.9 0.8 pad_maximum_fusion.1
  (52 shorter events, 3.0 us)
Async XLA Ops:
  0.0 10.2 %copy-start.2 = (f32[2048,16]{0,1:T(8,128)S(1)}, f32[2048,16]{0,1:T(8,128)}, u32[]{:S(2)}) copy-start(f32[2048,16]{0,1:T(8,128)} %param.11) | copy-start | bytes 393220
  0.0 17.8 %copy-start.3 = (f32[2048,16]{0,1:T(8,128)S(1)}, f32[2048,16]{0,1:T(8,128)}, u32[]{:S(2)}) copy-start(f32[2048,16]{0,1:T(8,128)} %param.11) | copy-start | bytes 393220
  4.3 13.5 %copy-start.7 = (bf16[16,2048]{1,0:T(8,128)(2,1)S(1)}, bf16[16,2048]{1,0:T(8,128)(2,1)}, u32[]{:S(2)}) copy-start(bf16[16,2048]{1,0:T(8,128)(2,1)} %shard_map.73) | copy-start | bytes 196612
  4.3 5.9 %collective-permute-start = (bf16[16,2048]{1,0:T(8,128)(2,1)}, bf16[16,2048]{1,0:T(8,128)(2,1)S(1)}, u32[]{:S(2)}, u32[]{:S(2)}) collective-permute-start(bf16[16,2048]{1,0:T(8,128)(2,1)} %shard_map.73), channel_id=1, source_target_pairs={{0,4},{4,0},{8,12},{12,8},{16,20},{20,16},{24,28},{28,24},{1,5},{5... | collective-permute-start | bytes 196616 | tf_op jit(solution)/shard_map/state_y/ppermute | solution.py:147
  11.1 13.9 %copy-start.1 = (bf16[128,2048]{1,0:T(8,128)(2,1)S(1)}, bf16[128,2048]{1,0:T(8,128)(2,1)}, u32[]{:S(2)}) copy-start(bf16[128,2048]{1,0:T(8,128)(2,1)} %q_ref.7) | copy-start | bytes 1572868
  11.1 13.9 %copy-start.4 = (f32[2048,16]{0,1:T(8,128)S(1)}, f32[2048,16]{0,1:T(8,128)}, u32[]{:S(2)}) copy-start(f32[2048,16]{0,1:T(8,128)} %param.11) | copy-start | bytes 393220
  11.1 13.9 %copy-start.5 = (f32[2048,16]{0,1:T(8,128)S(1)}, f32[2048,16]{0,1:T(8,128)}, u32[]{:S(2)}) copy-start(f32[2048,16]{0,1:T(8,128)} %param.10) | copy-start | bytes 393220
  11.1 6.7 %collective-permute-start.1 = (bf16[16,2048]{1,0:T(8,128)(2,1)S(1)}, bf16[16,2048]{1,0:T(8,128)(2,1)S(1)}, u32[]{:S(2)}, u32[]{:S(2)}) collective-permute-start(bf16[16,2048]{1,0:T(8,128)(2,1)S(1)} %get-tuple-element.45), channel_id=1, source_target_pairs={{0,8},{4,12},{8,16},{12,20},{16,24},{20,28},{1,9},{5,13},{9,17},{1... | collective-permute-start | bytes 196616 | tf_op jit(solution)/shard_map/state_1/ppermute | solution.py:147
  17.8 7.2 %collective-permute-start.2 = (bf16[16,2048]{1,0:T(8,128)(2,1)S(1)}, bf16[16,2048]{1,0:T(8,128)(2,1)S(1)}, u32[]{:S(2)}, u32[]{:S(2)}) collective-permute-start(bf16[16,2048]{1,0:T(8,128)(2,1)S(1)} %add_convert_fusion.2), channel_id=1, source_target_pairs={{0,16},{4,20},{8,24},{12,28},{1,17},{5,21},{9,25},{13,29},{2,18},{... | collective-permute-start | bytes 196616 | tf_op jit(solution)/shard_map/state_2/ppermute | solution.py:147
  25.0 1.2 %copy-start = (f32[128,2048]{1,0:T(8,128)S(1)}, f32[128,2048]{1,0:T(8,128)}, u32[]{:S(2)}) copy-start(f32[128,2048]{1,0:T(8,128)} %shard_map.76.base_ref) | copy-start | bytes 3145732
  28.5 12.0 %collective-permute-start.5 = (bf16[128,2048]{1,0:T(8,128)(2,1)S(1)}, bf16[128,2048]{1,0:T(8,128)(2,1)S(1)}, u32[]{:S(2)}, u32[]{:S(2)}) collective-permute-start(bf16[128,2048]{1,0:T(8,128)(2,1)S(1)} %shard_map.77), channel_id=1, source_target_pairs={{0,4},{4,0},{8,12},{12,8},{16,20},{20,16},{24,28},{28,24},{1,5},{5... | collective-permute-start | bytes 1572872 | tf_op jit(solution)/shard_map/near_y/ppermute | solution.py:147
  29.1 13.6 %collective-permute-start.4 = (bf16[128,2048]{1,0:T(8,128)(2,1)S(1)}, bf16[128,2048]{1,0:T(8,128)(2,1)S(1)}, u32[]{:S(2)}, u32[]{:S(2)}) collective-permute-start(bf16[128,2048]{1,0:T(8,128)(2,1)S(1)} %shard_map.77), channel_id=1, source_target_pairs={{8,16},{12,20},{16,8},{20,12},{9,17},{13,21},{17,9},{21,13},{10,18... | collective-permute-start | bytes 1572872 | tf_op jit(solution)/shard_map/middle/ppermute | solution.py:147
  32.6 11.4 %collective-permute-start.3 = (bf16[128,2048]{1,0:T(8,128)(2,1)S(1)}, bf16[128,2048]{1,0:T(8,128)(2,1)S(1)}, u32[]{:S(2)}, u32[]{:S(2)}) collective-permute-start(bf16[128,2048]{1,0:T(8,128)(2,1)S(1)} %shard_map.77), channel_id=1, source_target_pairs={{0,8},{4,12},{8,0},{12,4},{16,24},{20,28},{24,16},{28,20},{1,9},{5... | collective-permute-start | bytes 1572872 | tf_op jit(solution)/shard_map/one/ppermute | solution.py:147
  32.7 11.2 %copy-start.6 = (bf16[2048,1024]{1,0:T(8,128)(2,1)S(1)}, bf16[2048,1024]{1,0:T(8,128)(2,1)}, u32[]{:S(2)}) copy-start(bf16[2048,1024]{1,0:T(8,128)(2,1)} %param.13) | copy-start | bytes 12582916
  44.7 13.1 %collective-permute-start.8 = (bf16[128,2048]{1,0:T(8,128)(2,1)S(1)}, bf16[128,2048]{1,0:T(8,128)(2,1)S(1)}, u32[]{:S(2)}, u32[]{:S(2)}) collective-permute-start(bf16[128,2048]{1,0:T(8,128)(2,1)S(1)} %collective-permute-done.3), channel_id=1, source_target_pairs={{0,4},{4,0},{8,12},{12,8},{16,20},{20,16},{24,28},{28,24},{1,5},{5... | collective-permute-start | bytes 1572872 | tf_op jit(solution)/shard_map/one_y/ppermute | solution.py:147
  46.2 12.0 %collective-permute-start.6 = (bf16[128,2048]{1,0:T(8,128)(2,1)S(1)}, bf16[128,2048]{1,0:T(8,128)(2,1)S(1)}, u32[]{:S(2)}, u32[]{:S(2)}) collective-permute-start(bf16[128,2048]{1,0:T(8,128)(2,1)S(1)} %collective-permute-done.3), channel_id=1, source_target_pairs={{8,16},{12,20},{16,8},{20,12},{9,17},{13,21},{17,9},{21,13},{10,18... | collective-permute-start | bytes 1572872 | tf_op jit(solution)/shard_map/given/ppermute | solution.py:147
  48.7 9.0 %collective-permute-start.7 = (bf16[128,2048]{1,0:T(8,128)(2,1)S(1)}, bf16[128,2048]{1,0:T(8,128)(2,1)S(1)}, u32[]{:S(2)}, u32[]{:S(2)}) collective-permute-start(bf16[128,2048]{1,0:T(8,128)(2,1)S(1)} %collective-permute-done.4), channel_id=1, source_target_pairs={{8,0},{12,4},{16,24},{20,28},{9,1},{13,5},{17,25},{21,29},{10,2},{... | collective-permute-start | bytes 1572872 | tf_op jit(solution)/shard_map/out2/ppermute | solution.py:147
  59.0 8.3 %collective-permute-start.12 = (bf16[128,1024]{1,0:T(8,128)(2,1)S(1)}, bf16[128,1024]{1,0:T(8,128)(2,1)S(1)}, u32[]{:S(2)}, u32[]{:S(2)}) collective-permute-start(bf16[128,1024]{1,0:T(8,128)(2,1)S(1)} %slice.23), channel_id=1, source_target_pairs={{8,16},{12,20},{16,8},{20,12},{9,17},{13,21},{17,9},{21,13},{10,18... | collective-permute-start | bytes 786440 | tf_op jit(solution)/shard_map/middle_y/ppermute | solution.py:147
  61.7 11.2 %collective-permute-start.10 = (bf16[128,2048]{1,0:T(8,128)(2,1)S(1)}, bf16[128,2048]{1,0:T(8,128)(2,1)S(1)}, u32[]{:S(2)}, u32[]{:S(2)}) collective-permute-start(bf16[128,2048]{1,0:T(8,128)(2,1)S(1)} %collective-permute-done.6), channel_id=1, source_target_pairs={{8,0},{12,4},{16,24},{20,28},{9,1},{13,5},{17,25},{21,29},{10,2},{... | collective-permute-start | bytes 1572872 | tf_op jit(solution)/shard_map/out3/ppermute | solution.py:147
  63.7 9.2 %collective-permute-start.11 = (bf16[128,2048]{1,0:T(8,128)(2,1)S(1)}, bf16[128,2048]{1,0:T(8,128)(2,1)S(1)}, u32[]{:S(2)}, u32[]{:S(2)}) collective-permute-start(bf16[128,2048]{1,0:T(8,128)(2,1)S(1)} %broadcast_select_fusion.1), channel_id=1, source_target_pairs={{0,4},{4,0},{8,12},{12,8},{16,20},{20,16},{24,28},{28,24},{1,5},{5... | collective-permute-start | bytes 1572872 | tf_op jit(solution)/shard_map/two_y/ppermute | solution.py:147
  64.3 10.2 %collective-permute-start.9 = (bf16[2,128,1024]{2,1,0:T(8,128)(2,1)S(1)}, bf16[2,128,1024]{2,1,0:T(8,128)(2,1)S(1)}, u32[]{:S(2)}, u32[]{:S(2)}) collective-permute-start(bf16[2,128,1024]{2,1,0:T(8,128)(2,1)S(1)} %pad_maximum_fusion), channel_id=1, source_target_pairs={{0,1},{1,0},{2,3},{3,2},{4,5},{5,4},{6,7},{7,6},{8,9},{9,8},{10,11... | collective-permute-start | bytes 1572872 | tf_op jit(solution)/shard_map/core_0/ppermute | solution.py:147
  74.5 3.3 %collective-permute-start.17 = (bf16[128,1024]{1,0:T(8,128)(2,1)S(1)}, bf16[128,1024]{1,0:T(8,128)(2,1)S(1)}, u32[]{:S(2)}, u32[]{:S(2)}) collective-permute-start(bf16[128,1024]{1,0:T(8,128)(2,1)S(1)} %get-tuple-element.42), channel_id=1, source_target_pairs={{0,1},{1,0},{2,3},{3,2},{4,5},{5,4},{6,7},{7,6},{8,9},{9,8},{10,11... | collective-permute-start | bytes 786440 | tf_op jit(solution)/shard_map/core_2/ppermute | solution.py:147
  74.8 8.8 %collective-permute-start.15 = (bf16[128,1024]{1,0:T(8,128)(2,1)S(1)}, bf16[128,1024]{1,0:T(8,128)(2,1)S(1)}, u32[]{:S(2)}, u32[]{:S(2)}) collective-permute-start(bf16[128,1024]{1,0:T(8,128)(2,1)S(1)} %fusion.10), channel_id=1, source_target_pairs={{0,2},{1,3},{2,0},{3,1},{4,6},{5,7},{6,4},{7,5},{8,10},{9,11},{10,... | collective-permute-start | bytes 786440 | tf_op jit(solution)/shard_map/side_0/ppermute | solution.py:147
  75.4 8.2 %collective-permute-start.14 = (bf16[128,1024]{1,0:T(8,128)(2,1)S(1)}, bf16[128,1024]{1,0:T(8,128)(2,1)S(1)}, u32[]{:S(2)}, u32[]{:S(2)}) collective-permute-start(bf16[128,1024]{1,0:T(8,128)(2,1)S(1)} %slice.27), channel_id=1, source_target_pairs={{8,0},{12,4},{16,24},{20,28},{9,1},{13,5},{17,25},{21,29},{10,2},{... | collective-permute-start | bytes 786440 | tf_op jit(solution)/shard_map/out_y/ppermute | solution.py:147
  77.2 8.2 %collective-permute-start.13 = (bf16[128,1024]{1,0:T(8,128)(2,1)S(1)}, bf16[128,1024]{1,0:T(8,128)(2,1)S(1)}, u32[]{:S(2)}, u32[]{:S(2)}) collective-permute-start(bf16[128,1024]{1,0:T(8,128)(2,1)S(1)} %slice.32), channel_id=1, source_target_pairs={{0,4},{4,0},{8,12},{12,8},{16,20},{20,16},{24,28},{28,24},{1,5},{5... | collective-permute-start | bytes 786440 | tf_op jit(solution)/shard_map/three_y/ppermute | solution.py:147
  77.9 9.3 %collective-permute-start.18 = (bf16[128,1024]{1,0:T(8,128)(2,1)S(1)}, bf16[128,1024]{1,0:T(8,128)(2,1)S(1)}, u32[]{:S(2)}, u32[]{:S(2)}) collective-permute-start(bf16[128,1024]{1,0:T(8,128)(2,1)S(1)} %fusion.15), channel_id=1, source_target_pairs={{2,0},{3,1},{6,4},{7,5},{10,8},{11,9},{14,12},{15,13},{16,18},{17,... | collective-permute-start | bytes 786440 | tf_op jit(solution)/shard_map/side_2/ppermute | solution.py:147
  87.5 1.6 %collective-permute-start.19 = (bf16[128,1024]{1,0:T(8,128)(2,1)S(1)}, bf16[128,1024]{1,0:T(8,128)(2,1)S(1)}, u32[]{:S(2)}, u32[]{:S(2)}) collective-permute-start(bf16[128,1024]{1,0:T(8,128)(2,1)S(1)} %select_convert_fusion), channel_id=1, source_target_pairs={{0,1},{1,0},{2,3},{3,2},{4,5},{5,4},{6,7},{7,6},{8,9},{9,8},{10,11... | collective-permute-start | bytes 786440 | tf_op jit(solution)/shard_map/core_3/ppermute | solution.py:147
  89.2 10.5 %collective-permute-start.20 = (bf16[128,1024]{1,0:T(8,128)(2,1)S(1)}, bf16[128,1024]{1,0:T(8,128)(2,1)}, u32[]{:S(2)}, u32[]{:S(2)}) collective-permute-start(bf16[128,1024]{1,0:T(8,128)(2,1)S(1)} %fusion.16), channel_id=1, source_target_pairs={{0,2},{1,3},{4,6},{5,7},{8,10},{9,11},{12,14},{13,15},{18,16},{19,... | collective-permute-start | bytes 786440 | tf_op jit(solution)/shard_map/side_3/ppermute | solution.py:147
  90.6 17.0 %collective-permute-start.22 = (bf16[128,1024]{1,0:T(8,128)(2,1)S(1)}, bf16[128,1024]{1,0:T(8,128)(2,1)S(1)}, u32[]{:S(2)}, u32[]{:S(2)}) collective-permute-start(bf16[128,1024]{1,0:T(8,128)(2,1)S(1)} %fusion.7), channel_id=1, source_target_pairs={{2,4},{1,12},{6,0},{5,8},{10,13},{9,5},{14,9},{13,1},{18,22},{17,3... | collective-permute-start | bytes 786440 | tf_op jit(solution)/shard_map/own_0/ppermute | solution.py:147
  95.8 11.9 %collective-permute-start.16 = (bf16[128,1024]{1,0:T(8,128)(2,1)S(1)}, bf16[128,1024]{1,0:T(8,128)(2,1)S(1)}, u32[]{:S(2)}, u32[]{:S(2)}) collective-permute-start(bf16[128,1024]{1,0:T(8,128)(2,1)S(1)} %fusion.7), channel_id=1, source_target_pairs={{0,0},{3,8},{4,4},{7,12},{8,9},{11,1},{12,13},{15,5},{16,18},{19,2... | collective-permute-start | bytes 786440 | tf_op jit(solution)/shard_map/own_0/ppermute | solution.py:147
  100.8 17.1 %collective-permute-start.23 = (bf16[128,1024]{1,0:T(8,128)(2,1)S(1)}, bf16[128,1024]{1,0:T(8,128)(2,1)S(1)}, u32[]{:S(2)}, u32[]{:S(2)}) collective-permute-start(bf16[128,1024]{1,0:T(8,128)(2,1)S(1)} %fusion.11), channel_id=1, source_target_pairs={{1,20},{3,28},{5,16},{7,24},{9,29},{11,21},{13,25},{15,17},{19,6},... | collective-permute-start | bytes 786440 | tf_op jit(solution)/shard_map/own_2/ppermute | solution.py:147
  102.0 15.8 %collective-permute-start.21 = (bf16[128,1024]{1,0:T(8,128)(2,1)S(1)}, bf16[128,1024]{1,0:T(8,128)(2,1)S(1)}, u32[]{:S(2)}, u32[]{:S(2)}) collective-permute-start(bf16[128,1024]{1,0:T(8,128)(2,1)S(1)} %fusion.11), channel_id=1, source_target_pairs={{0,16},{2,24},{4,20},{6,28},{8,25},{10,17},{12,29},{14,21},{18,2},... | collective-permute-start | bytes 786440 | tf_op jit(solution)/shard_map/own_2/ppermute | solution.py:147

commit v5 on v4

--- a/solution.py
+++ b/solution.py
@@ -1,4 +1,5 @@
 import functools
+import itertools
 
 import jax
 import jax.numpy as jnp
@@ -214,64 +215,43 @@
     flip = [(c, c ^ 1) for c in range(4)]
     turn = [(c, c ^ 2) for c in range(4)]
 
-    def root(group, a):
-        return (a // 2) ^ (group % 2)
-
-    def owners(group):
-        return [
-            [
-                (
-                    (a * 2 + b) * 4 + ((d ^ k) if group == 0 else root(group + g, a)) * 2 + (k if group == 0 else d),
-                    ((a ^ (group + (k if group == 0 else g))) * 2 + (b ^ d)) * 4 + a,
-                )
-                for a in every
-                for b in range(2)
-                for k, g in (((0, 0), (1, 0)) if group == 0 else ((0, 0), (0, 1)))
-            ]
-            for d in range(2)
-        ]
-
-    even = [matmul(block, w_out) for block in (hidden, near_y)]
-    odd = [matmul(block, w_out) for block in (one, one_y)]
-    keep = jnp.stack([jnp.where(core == 0, a, b) for a, b in zip(even, odd)])
-    send = jnp.stack([jnp.where(core == 0, b, a).astype(BF16) for a, b in zip(even, odd)])
-    close_core = moved(send, "chan", flip, "core_0")
-    keep = keep + close_core.astype(F32)
-    send = jnp.where(side == core, keep[1], keep[0]).astype(BF16)
-    keep = jnp.where(side == core, keep[0], keep[1])
-    close_side = moved(send, "chan", turn, "side_0")
-
-    def remote(group, parts, before):
-        first, second = parts
-        keep = jnp.where(core == 0, first, second)
-        send = fence(jnp.where(core == 0, second, first).astype(BF16), *before)[0]
-        keep = keep + moved(send, "chan", flip, f"core_{group}").astype(F32)
-        pairs = [
-            ((a * 2 + b) * 4 + (1 - root(group, a)) * 2 + k, (a * 2 + b) * 4 + root(group, a) * 2 + k)
-            for a in every
-            for b in range(2)
-            for k in range(2)
-        ]
-        turned = moved(keep.astype(BF16), BOTH, pairs, f"side_{group}")
-        return (keep + turned.astype(F32)).astype(BF16)
+    def owned(dy):
+        pairs = []
+        for a, b, x in itertools.product(every, range(2), range(2)):
+            for k in range(2):
+                apart = 2 + (x ^ (a // 2)) if k == dy else x
+                pairs.append(((a * 2 + b) * 4 + x * 2 + k, ((a ^ apart) * 2 + (b ^ dy)) * 4 + a))
+        return pairs
+
+    def turned(here, first, second, pairs, name):
+        keep = jnp.where(here, first, second)
+        return keep, moved(jnp.where(here, second, first).astype(BF16), "chan", pairs, name)
+
+    def far(first, second, dy):
+        parts = jnp.stack([first, second])
+        parts = parts + moved(parts.astype(BF16), "chan", [(1 - dy, dy), (3 - dy, 2 + dy)], f"core_far{dy}").astype(F32)
+        return turned(side == z // 2, parts[0], parts[1], [(dy, 2 + dy), (2 + dy, dy)], f"side_far{dy}")
+
+    ready = [[matmul(x, w_out) for x in (hidden, near_y)], [matmul(x, w_out) for x in (one, one_y)]]
+    keep = jnp.stack([jnp.where(core == 0, second, first) for first, second in ready])
+    send = jnp.stack([jnp.where(core == 0, first, second).astype(BF16) for first, second in ready])
+    close = keep + moved(send, "chan", flip, "core_close").astype(F32)
+    close_keep, close_side = turned(side == 0, close[0], close[1], turn, "side_close")
 
     out3, two_y, middle_y = fence(out3, two_y, middle_y)
     three = jnp.where(at_end, out3, middle)
     three_y = across(three[:, :split], every, "three_y")
     out_y = along(two_y[:, split:], outward, "out_y")
     with_three = matmul(three, w_out)
-    three_y, out_y, close_side = fence(three_y, out_y, close_side)
-    tile = (keep + close_side.astype(F32)).astype(BF16)
-    close = [moved(tile, BOTH, pairs, "own_0") for pairs in owners(0)]
+    far_keep, far_side = far(matmul(two, w_out), with_three, 0)
+    three_y, out_y, close_side, far_side = fence(three_y, out_y, close_side, far_side)
+    close_tile = (close_keep + close_side.astype(F32)).astype(BF16)
+    tile = (far_keep + far_side.astype(F32)).astype(BF16)
+    same = moved(jnp.where(core == 0, tile, close_tile), BOTH, owned(0), "own_0")
     with_three_y = matmul(three_y, w_out[:split]) + matmul(jnp.where(at_end, out_y, middle_y), w_out[split:])
-    tile2 = remote(2, [matmul(two, w_out), matmul(two_y, w_out)], [with_three])
-    with_three_y, tile2 = fence(with_three_y, tile2)
-    tile3 = remote(3, [with_three, with_three_y], [])
-    tile = jnp.where(side == root(2, z), tile2, tile3)
-    far = [moved(tile, BOTH, pairs, "own_2") for pairs in owners(2)]
-    near_here = (z ^ chan) < 2
-    same = jnp.where(near_here, close[0], far[0])
-    cross = jnp.where(near_here, close[1], far[1])
+    far_keep, far_side = far(matmul(two_y, w_out), with_three_y, 1)
+    tile = (far_keep + far_side.astype(F32)).astype(BF16)
+    cross = moved(jnp.where(core == 1, tile, close_tile), BOTH, owned(1), "own_1")
     low = jnp.where(y == 0, same, cross)
     high = jnp.where(y == 0, cross, same)
     return jnp.concatenate([low, high], axis=1)

time: 119 us -> 116 us (0.975)
  starting transfers between devices: 44.5 us -> 40.4 us
  other arithmetic: 4.1 us -> 6.27 us
  waiting for transfers between devices: 43 us -> 41.5 us
    ppermute x24 -> x22, starting transfers between devices: 44.5 us -> 40.4 us  [moved(): return lax.ppermute(x, axes, pairs)]
    ppermute x24 -> x22, waiting for transfers between devices: 43 us -> 41.5 us  [moved(): return lax.ppermute(x, axes, pairs)]
    add x1 -> x3, other arithmetic: 0.13 us -> 1.47 us  [the longest x2 1.32 us: far(): parts + moved(parts.astype(BF16), 'chan', [(1 - dy, dy), (3 - dy, 2 + dy)...]
  transfers between devices with their start and end apart: 24 -> 22, of which waited for: 13 -> 13; matrix products, arithmetic and copies ran while one was open for 7% -> 9% of each run, Pallas kernels for 9% -> 9%
where the time goes in v5:
time: 116 us; the launch traced here: 115 us
  waiting for transfers between devices  41.5 us (36%)
  starting transfers between devices  40.4 us (35%)
  Pallas kernels  16.9 us (15%)
  matrix products  8.32 us (7%)
  other arithmetic  6.27 us (5%)
  local copies, waits for them, and re-layouts  1.31 us (1%)
    ppermute x22, waiting for transfers between devices, moved(): return lax.ppermute(x, axes, pairs)  41.5 us
    ppermute x22, starting transfers between devices, moved(): return lax.ppermute(x, axes, pairs)  40.4 us
    pallas_call x5, Pallas kernels, run(): pl.pallas_call(kernel, grid=(steps,), out_shape=out, in_specs=specs, out_...  16.9 us
    dot_general x9, matrix products, matmul(): return jnp.dot(x, w, preferred_element_type=F32)  8.32 us
  transfers between devices with their start and end apart: 22, of which 13 were waited for; matrix products, arithmetic and copies ran while one was open for 9% of the time, Pallas kernels for 9%

profile of v5, /device:TPU:10, one launch (start us, length us, event | category | flops | bytes accessed | tf_op | source)
XLA Modules:
  0.0 115.2 jit_solution(1122963451514047687)
XLA Ops:
  0.0 4.3 %shard_map.73 = bf16[16,2048]{1,0:T(8,128)(2,1)} custom-call(bf16[128,2048]{1,0:T(8,128)(2,1)} %k_ref.7, bf16[128,2048]{1,0:T(8,128)(2,1)} %v_ref.7, f32[16,2048]{1,0:T(8,128)} %bitcast.60), custom_call_target="tpu_custom_call" | custom-call | flops 12582912 | bytes 1572864 | tf_op jit(solution)/shard_map/pallas_call | solution.py:127
  4.3 1.5 %collective-permute-start = (bf16[16,2048]{1,0:T(8,128)(2,1)}, bf16[16,2048]{1,0:T(8,128)(2,1)S(1)}, u32[]{:S(2)}, u32[]{:S(2)}) collective-permute-start(bf16[16,2048]{1,0:T(8,128)(2,1)} %shard_map.73), channel_id=1, source_target_pairs={{0,4},{4,0},{8,12},{12,8},{16,20},{20,16},{24,28},{28,24},{1,5},{5... | collective-permute-start | bytes 196616 | tf_op jit(solution)/shard_map/state_y/ppermute | solution.py:148
  5.8 4.3 %shard_map.74.rest_0_ = f32[128,2048]{1,0:T(8,128)} custom-call(bf16[128,2048]{1,0:T(8,128)(2,1)} %q_ref.7, bf16[128,2048]{1,0:T(8,128)(2,1)} %k_ref.7, bf16[128,2048]{1,0:T(8,128)(2,1)} %v_ref.7, f32[16,2048]{1,0:T(8,128)} %bitcast.65, f32[16,2048]{1,0:T(8,128)} %bitcast.61, f32[1,2048]{1,0:T(1,128)} %bitcast.69), custom_call_target="tpu_custom_call" | custom-call | flops 13107200 | bytes 786432 | tf_op jit(solution)/shard_map/pallas_call | solution.py:127
  10.1 0.9 fusion.24
  11.1 3.6 %collective-permute-start.1 = (bf16[16,2048]{1,0:T(8,128)(2,1)S(1)}, bf16[16,2048]{1,0:T(8,128)(2,1)S(1)}, u32[]{:S(2)}, u32[]{:S(2)}) collective-permute-start(bf16[16,2048]{1,0:T(8,128)(2,1)S(1)} %get-tuple-element.43), channel_id=1, source_target_pairs={{0,8},{4,12},{8,16},{12,20},{16,24},{20,28},{1,9},{5,13},{9,17},{1... | collective-permute-start | bytes 196616 | tf_op jit(solution)/shard_map/state_1/ppermute | solution.py:148
  14.7 3.0 %shard_map.75.rest_0_ = f32[128,2048]{1,0:T(8,128)} custom-call(bf16[128,2048]{1,0:T(8,128)(2,1)} %q_ref.7, bf16[128,2048]{1,0:T(8,128)(2,1)} %k_ref.7, bf16[128,2048]{1,0:T(8,128)(2,1)} %v_ref.7, f32[16,2048]{1,0:T(8,128)} %bitcast.66, f32[16,2048]{1,0:T(8,128)} %bitcast.62, f32[1,2048]{1,0:T(1,128)} %bitcast.70, ...), custom_call_target="tpu_custom_call", output_to_operand_aliasing={{}: (6, {})} | custom-call | flops 6553600 | bytes 393216 | tf_op jit(solution)/shard_map/pallas_call | solution.py:127
  17.8 4.1 %collective-permute-start.2 = (bf16[16,2048]{1,0:T(8,128)(2,1)S(1)}, bf16[16,2048]{1,0:T(8,128)(2,1)S(1)}, u32[]{:S(2)}, u32[]{:S(2)}) collective-permute-start(bf16[16,2048]{1,0:T(8,128)(2,1)S(1)} %add_convert_fusion), channel_id=1, source_target_pairs={{0,16},{4,20},{8,24},{12,28},{1,17},{5,21},{9,25},{13,29},{2,18},{... | collective-permute-start | bytes 196616 | tf_op jit(solution)/shard_map/state_2/ppermute | solution.py:148
  22.0 3.0 %shard_map.76.base_ref = f32[128,2048]{1,0:T(8,128)} custom-call(bf16[128,2048]{1,0:T(8,128)(2,1)} %q_ref.7, bf16[128,2048]{1,0:T(8,128)(2,1)} %k_ref.7, bf16[128,2048]{1,0:T(8,128)(2,1)} %v_ref.7, f32[16,2048]{1,0:T(8,128)} %bitcast.67, f32[16,2048]{1,0:T(8,128)} %bitcast.63, f32[1,2048]{1,0:T(1,128)} %bitcast.71, ...), custom_call_target="tpu_custom_call", output_to_operand_aliasing={{}: (6, {})} | custom-call | flops 6553600 | bytes 393216 | tf_op jit(solution)/shard_map/pallas_call | solution.py:127
  25.0 1.2 %copy-done = f32[128,2048]{1,0:T(8,128)S(1)} copy-done((f32[128,2048]{1,0:T(8,128)S(1)}, f32[128,2048]{1,0:T(8,128)}, u32[]{:S(2)}) %copy-start) | copy-done | bytes 1048600
  26.3 2.2 %shard_map.77 = bf16[128,2048]{1,0:T(8,128)(2,1)S(1)} custom-call(s32[1]{0:T(128)} %bitcast.odd_ref, bf16[128,2048]{1,0:T(8,128)(2,1)S(1)} %copy-done.1, f32[128,2048]{1,0:T(8,128)S(1)} %copy-done, bf16[16,2048]{1,0:T(8,128)(2,1)S(1)} %collective-permute-done.1.below_ref, bf16[16,2048]{1,0:T(8,128)(2,1)S(1)} %collective-permute-done.2.further_ref, ...), custom_call_target="tpu_custom_call" | custom-call | flops 8388608 | bytes 1572864 | tf_op jit(solution)/shard_map/pallas_call | solution.py:127
  28.5 0.6 collective-permute-start.5
  29.1 3.4 %collective-permute-start.4 = (bf16[128,2048]{1,0:T(8,128)(2,1)S(1)}, bf16[128,2048]{1,0:T(8,128)(2,1)S(1)}, u32[]{:S(2)}, u32[]{:S(2)}) collective-permute-start(bf16[128,2048]{1,0:T(8,128)(2,1)S(1)} %shard_map.77), channel_id=1, source_target_pairs={{8,16},{12,20},{16,8},{20,12},{9,17},{13,21},{17,9},{21,13},{10,18... | collective-permute-start | bytes 1572872 | tf_op jit(solution)/shard_map/middle/ppermute | solution.py:148
  32.7 3.0 %fusion.27 = f32[128,1024]{1,0:T(8,128)S(1)} fusion(bf16[128,2048]{1,0:T(8,128)(2,1)S(1)} %shard_map.77, bf16[2048,1024]{1,0:T(8,128)(2,1)} %param.13), kind=kOutput, calls=%fused_computation.50 | convolution fusion | flops 536870912 | bytes 5242880 | tf_op jit(solution)/shard_map/dot_general | solution.py:143
  35.8 4.8 %collective-permute-done.5 = bf16[128,2048]{1,0:T(8,128)(2,1)S(1)} collective-permute-done((bf16[128,2048]{1,0:T(8,128)(2,1)S(1)}, bf16[128,2048]{1,0:T(8,128)(2,1)S(1)}, u32[]{:S(2)}, u32[]{:S(2)}) %collective-permute-start.5) | collective-permute-done | bytes 524320 | tf_op jit(solution)/shard_map/near_y/ppermute | solution.py:148
  40.5 2.1 %collective-permute-done.4 = bf16[128,2048]{1,0:T(8,128)(2,1)S(1)} collective-permute-done((bf16[128,2048]{1,0:T(8,128)(2,1)S(1)}, bf16[128,2048]{1,0:T(8,128)(2,1)S(1)}, u32[]{:S(2)}, u32[]{:S(2)}) %collective-permute-start.4) | collective-permute-done | bytes 524320 | tf_op jit(solution)/shard_map/middle/ppermute | solution.py:148
  42.6 1.3 %collective-permute-done.3 = bf16[128,2048]{1,0:T(8,128)(2,1)S(1)} collective-permute-done((bf16[128,2048]{1,0:T(8,128)(2,1)S(1)}, bf16[128,2048]{1,0:T(8,128)(2,1)S(1)}, u32[]{:S(2)}, u32[]{:S(2)}) %collective-permute-start.3) | collective-permute-done | bytes 524320 | tf_op jit(solution)/shard_map/one/ppermute | solution.py:148
  43.9 1.5 %collective-permute-start.8 = (bf16[128,2048]{1,0:T(8,128)(2,1)S(1)}, bf16[128,2048]{1,0:T(8,128)(2,1)S(1)}, u32[]{:S(2)}, u32[]{:S(2)}) collective-permute-start(bf16[128,2048]{1,0:T(8,128)(2,1)S(1)} %collective-permute-done.3), channel_id=1, source_target_pairs={{0,4},{4,0},{8,12},{12,8},{16,20},{20,16},{24,28},{28,24},{1,5},{5... | collective-permute-start | bytes 1572872 | tf_op jit(solution)/shard_map/one_y/ppermute | solution.py:148
  45.4 2.5 %collective-permute-start.6 = (bf16[128,2048]{1,0:T(8,128)(2,1)S(1)}, bf16[128,2048]{1,0:T(8,128)(2,1)S(1)}, u32[]{:S(2)}, u32[]{:S(2)}) collective-permute-start(bf16[128,2048]{1,0:T(8,128)(2,1)S(1)} %collective-permute-done.3), channel_id=1, source_target_pairs={{8,16},{12,20},{16,8},{20,12},{9,17},{13,21},{17,9},{21,13},{10,18... | collective-permute-start | bytes 1572872 | tf_op jit(solution)/shard_map/given/ppermute | solution.py:148
  47.9 1.3 %collective-permute-start.7 = (bf16[128,2048]{1,0:T(8,128)(2,1)S(1)}, bf16[128,2048]{1,0:T(8,128)(2,1)S(1)}, u32[]{:S(2)}, u32[]{:S(2)}) collective-permute-start(bf16[128,2048]{1,0:T(8,128)(2,1)S(1)} %collective-permute-done.4), channel_id=1, source_target_pairs={{8,0},{12,4},{16,24},{20,28},{9,1},{13,5},{17,25},{21,29},{10,2},{... | collective-permute-start | bytes 1572872 | tf_op jit(solution)/shard_map/out2/ppermute | solution.py:148
  49.2 0.7 fusion.26
  50.0 0.7 fusion.29
  50.8 6.1 %collective-permute-done.7 = bf16[128,2048]{1,0:T(8,128)(2,1)S(1)} collective-permute-done((bf16[128,2048]{1,0:T(8,128)(2,1)S(1)}, bf16[128,2048]{1,0:T(8,128)(2,1)S(1)}, u32[]{:S(2)}, u32[]{:S(2)}) %collective-permute-start.7) | collective-permute-done | bytes 524320 | tf_op jit(solution)/shard_map/out2/ppermute | solution.py:148
  56.9 0.6 collective-permute-done.6
  57.5 2.6 %collective-permute-start.11 = (bf16[128,1024]{1,0:T(8,128)(2,1)S(1)}, bf16[128,1024]{1,0:T(8,128)(2,1)S(1)}, u32[]{:S(2)}, u32[]{:S(2)}) collective-permute-start(bf16[128,1024]{1,0:T(8,128)(2,1)S(1)} %slice.33), channel_id=1, source_target_pairs={{8,16},{12,20},{16,8},{20,12},{9,17},{13,21},{17,9},{21,13},{10,18... | collective-permute-start | bytes 786440 | tf_op jit(solution)/shard_map/middle_y/ppermute | solution.py:148
  60.1 0.7 fusion.28
  60.9 1.8 %collective-permute-start.9 = (bf16[128,2048]{1,0:T(8,128)(2,1)S(1)}, bf16[128,2048]{1,0:T(8,128)(2,1)S(1)}, u32[]{:S(2)}, u32[]{:S(2)}) collective-permute-start(bf16[128,2048]{1,0:T(8,128)(2,1)S(1)} %collective-permute-done.6), channel_id=1, source_target_pairs={{8,0},{12,4},{16,24},{20,28},{9,1},{13,5},{17,25},{21,29},{10,2},{... | collective-permute-start | bytes 1572872 | tf_op jit(solution)/shard_map/out3/ppermute | solution.py:148
  63.7 0.7 convolution_bitcast_fusion.2
  64.4 1.3 %collective-permute-done.11 = bf16[128,1024]{1,0:T(8,128)(2,1)S(1)} collective-permute-done((bf16[128,1024]{1,0:T(8,128)(2,1)S(1)}, bf16[128,1024]{1,0:T(8,128)(2,1)S(1)}, u32[]{:S(2)}, u32[]{:S(2)}) %collective-permute-start.11) | collective-permute-done | bytes 262176 | tf_op jit(solution)/shard_map/middle_y/ppermute | solution.py:148
  65.8 6.3 %collective-permute-done.10 = bf16[128,2048]{1,0:T(8,128)(2,1)S(1)} collective-permute-done((bf16[128,2048]{1,0:T(8,128)(2,1)S(1)}, bf16[128,2048]{1,0:T(8,128)(2,1)S(1)}, u32[]{:S(2)}, u32[]{:S(2)}) %collective-permute-start.10) | collective-permute-done | bytes 524320 | tf_op jit(solution)/shard_map/two_y/ppermute | solution.py:148
  72.1 0.7 convolution_bitcast_fusion.1
  72.9 1.3 %collective-permute-start.12 = (bf16[2,128,1024]{2,1,0:T(8,128)(2,1)S(1)}, bf16[2,128,1024]{2,1,0:T(8,128)(2,1)S(1)}, u32[]{:S(2)}, u32[]{:S(2)}) collective-permute-start(bf16[2,128,1024]{2,1,0:T(8,128)(2,1)S(1)} %fusion.11), channel_id=1, source_target_pairs={{1,0},{3,2},{5,4},{7,6},{9,8},{11,10},{13,12},{15,14},{17,16},{19,... | collective-permute-start | bytes 1572872 | tf_op jit(solution)/shard_map/core_far0/ppermute | solution.py:148
  74.6 0.6 collective-permute-start.16
  75.3 1.8 %collective-permute-start.14 = (bf16[128,1024]{1,0:T(8,128)(2,1)S(1)}, bf16[128,1024]{1,0:T(8,128)(2,1)S(1)}, u32[]{:S(2)}, u32[]{:S(2)}) collective-permute-start(bf16[128,1024]{1,0:T(8,128)(2,1)S(1)} %slice.37), channel_id=1, source_target_pairs={{8,0},{12,4},{16,24},{20,28},{9,1},{13,5},{17,25},{21,29},{10,2},{... | collective-permute-start | bytes 786440 | tf_op jit(solution)/shard_map/out_y/ppermute | solution.py:148
  77.9 3.4 %collective-permute-start.17 = (bf16[128,1024]{1,0:T(8,128)(2,1)S(1)}, bf16[128,1024]{1,0:T(8,128)(2,1)S(1)}, u32[]{:S(2)}, u32[]{:S(2)}) collective-permute-start(bf16[128,1024]{1,0:T(8,128)(2,1)S(1)} %fusion.18), channel_id=1, source_target_pairs={{0,2},{2,0},{4,6},{6,4},{8,10},{10,8},{12,14},{14,12},{16,18},{18,... | collective-permute-start | bytes 786440 | tf_op jit(solution)/shard_map/side_far0/ppermute | solution.py:148
  81.3 0.7 convolution_bitcast_fusion
  82.0 1.7 %collective-permute-done.16 = bf16[128,1024]{1,0:T(8,128)(2,1)S(1)} collective-permute-done((bf16[128,1024]{1,0:T(8,128)(2,1)S(1)}, bf16[128,1024]{1,0:T(8,128)(2,1)S(1)}, u32[]{:S(2)}, u32[]{:S(2)}) %collective-permute-start.16) | collective-permute-done | bytes 262176 | tf_op jit(solution)/shard_map/side_close/ppermute | solution.py:148
  83.7 2.3 %collective-permute-done.13 = bf16[128,1024]{1,0:T(8,128)(2,1)S(1)} collective-permute-done((bf16[128,1024]{1,0:T(8,128)(2,1)S(1)}, bf16[128,1024]{1,0:T(8,128)(2,1)S(1)}, u32[]{:S(2)}, u32[]{:S(2)}) %collective-permute-start.13) | collective-permute-done | bytes 262176 | tf_op jit(solution)/shard_map/three_y/ppermute | solution.py:148
  86.0 0.7 collective-permute-done.17
  87.6 0.9 fusion.10
  88.5 2.1 %collective-permute-start.19 = (bf16[2,128,1024]{2,1,0:T(8,128)(2,1)}, bf16[2,128,1024]{2,1,0:T(8,128)(2,1)}, u32[]{:S(2)}, u32[]{:S(2)}) collective-permute-start(bf16[2,128,1024]{2,1,0:T(8,128)(2,1)} %fusion.10), channel_id=1, source_target_pairs={{0,1},{2,3},{4,5},{6,7},{8,9},{10,11},{12,13},{14,15},{16,17},{18,... | collective-permute-start | bytes 1572872 | tf_op jit(solution)/shard_map/core_far1/ppermute | solution.py:148
  90.5 1.1 collective-permute-done.19
  91.6 1.2 %convert_add_fusion = f32[2,128,1024]{2,1,0:T(8,128)S(1)} fusion(bf16[2,128,1024]{2,1,0:T(8,128)(2,1)} %collective-permute-done.19, f32[1,128,1024]{2,1,0:T(8,128)S(1)} %fusion.7, f32[1,128,1024]{2,1,0:T(8,128)S(1)} %convolution_bitcast_fusion), kind=kLoop, calls=%fused_computation.12 | loop fusion | flops 786432 | bytes 2621440 | tf_op jit(solution)/shard_map/add | solution.py:232
  92.9 0.7 collective-permute-start.20
  93.5 1.2 %fusion.20 = (bf16[128,1024]{1,0:T(8,128)(2,1)S(1)}, bf16[128,1024]{1,0:T(8,128)(2,1)S(1)}) fusion(bf16[128,1024]{1,0:T(8,128)(2,1)} %copy-done.8, f32[2,128,1024]{2,1,0:T(8,128)S(1)} %convert_add_fusion.1, pred[]{:T(512)S(6)} %eq.32, pred[]{:T(512)S(6)} %eq.31, bf16[128,1024]{1,0:T(8,128)(2,1)S(1)} %collective-permute-done.16, ...), kind=kLoop, calls=%fused_computation.38 | loop fusion | flops 1179648 | bytes 3145731 | tf_op jit(solution)/shard_map/jit(_where)/select_n | solution.py:250
  94.8 5.6 %collective-permute-start.18 = (bf16[128,1024]{1,0:T(8,128)(2,1)S(1)}, bf16[128,1024]{1,0:T(8,128)(2,1)S(1)}, u32[]{:S(2)}, u32[]{:S(2)}) collective-permute-start(bf16[128,1024]{1,0:T(8,128)(2,1)S(1)} %get-tuple-element.41), channel_id=1, source_target_pairs={{0,16},{1,0},{2,24},{3,8},{4,20},{5,4},{6,28},{7,12},{8,25},{9,9},... | collective-permute-start | bytes 786440 | tf_op jit(solution)/shard_map/own_0/ppermute | solution.py:148
  101.1 10.1 %collective-permute-done.18 = bf16[128,1024]{1,0:T(8,128)(2,1)S(1)} collective-permute-done((bf16[128,1024]{1,0:T(8,128)(2,1)S(1)}, bf16[128,1024]{1,0:T(8,128)(2,1)S(1)}, u32[]{:S(2)}, u32[]{:S(2)}) %collective-permute-start.18) | collective-permute-done | bytes 262176 | tf_op jit(solution)/shard_map/own_0/ppermute | solution.py:148
  111.2 3.1 %collective-permute-done.21 = bf16[128,1024]{1,0:T(8,128)(2,1)S(1)} collective-permute-done((bf16[128,1024]{1,0:T(8,128)(2,1)S(1)}, bf16[128,1024]{1,0:T(8,128)(2,1)S(1)}, u32[]{:S(2)}, u32[]{:S(2)}) %collective-permute-start.21) | collective-permute-done | bytes 262176 | tf_op jit(solution)/shard_map/own_1/ppermute | solution.py:148
  114.4 0.8 pad_maximum_fusion.3
  (50 shorter events, 4.1 us)
Async XLA Ops:
  0.0 10.1 %copy-start.2 = (f32[2048,16]{0,1:T(8,128)S(1)}, f32[2048,16]{0,1:T(8,128)}, u32[]{:S(2)}) copy-start(f32[2048,16]{0,1:T(8,128)} %param.11) | copy-start | bytes 393220
  0.0 17.7 %copy-start.3 = (f32[2048,16]{0,1:T(8,128)S(1)}, f32[2048,16]{0,1:T(8,128)}, u32[]{:S(2)}) copy-start(f32[2048,16]{0,1:T(8,128)} %param.11) | copy-start | bytes 393220
  4.3 13.4 %copy-start.7 = (bf16[16,2048]{1,0:T(8,128)(2,1)S(1)}, bf16[16,2048]{1,0:T(8,128)(2,1)}, u32[]{:S(2)}) copy-start(bf16[16,2048]{1,0:T(8,128)(2,1)} %shard_map.73) | copy-start | bytes 196612
  4.3 5.8 %collective-permute-start = (bf16[16,2048]{1,0:T(8,128)(2,1)}, bf16[16,2048]{1,0:T(8,128)(2,1)S(1)}, u32[]{:S(2)}, u32[]{:S(2)}) collective-permute-start(bf16[16,2048]{1,0:T(8,128)(2,1)} %shard_map.73), channel_id=1, source_target_pairs={{0,4},{4,0},{8,12},{12,8},{16,20},{20,16},{24,28},{28,24},{1,5},{5... | collective-permute-start | bytes 196616 | tf_op jit(solution)/shard_map/state_y/ppermute | solution.py:148
  11.0 14.0 %copy-start.1 = (bf16[128,2048]{1,0:T(8,128)(2,1)S(1)}, bf16[128,2048]{1,0:T(8,128)(2,1)}, u32[]{:S(2)}) copy-start(bf16[128,2048]{1,0:T(8,128)(2,1)} %q_ref.7) | copy-start | bytes 1572868
  11.1 14.0 %copy-start.4 = (f32[2048,16]{0,1:T(8,128)S(1)}, f32[2048,16]{0,1:T(8,128)}, u32[]{:S(2)}) copy-start(f32[2048,16]{0,1:T(8,128)} %param.11) | copy-start | bytes 393220
  11.1 14.0 %copy-start.5 = (f32[2048,16]{0,1:T(8,128)S(1)}, f32[2048,16]{0,1:T(8,128)}, u32[]{:S(2)}) copy-start(f32[2048,16]{0,1:T(8,128)} %param.10) | copy-start | bytes 393220
  11.1 6.7 %collective-permute-start.1 = (bf16[16,2048]{1,0:T(8,128)(2,1)S(1)}, bf16[16,2048]{1,0:T(8,128)(2,1)S(1)}, u32[]{:S(2)}, u32[]{:S(2)}) collective-permute-start(bf16[16,2048]{1,0:T(8,128)(2,1)S(1)} %get-tuple-element.43), channel_id=1, source_target_pairs={{0,8},{4,12},{8,16},{12,20},{16,24},{20,28},{1,9},{5,13},{9,17},{1... | collective-permute-start | bytes 196616 | tf_op jit(solution)/shard_map/state_1/ppermute | solution.py:148
  17.8 7.2 %collective-permute-start.2 = (bf16[16,2048]{1,0:T(8,128)(2,1)S(1)}, bf16[16,2048]{1,0:T(8,128)(2,1)S(1)}, u32[]{:S(2)}, u32[]{:S(2)}) collective-permute-start(bf16[16,2048]{1,0:T(8,128)(2,1)S(1)} %add_convert_fusion), channel_id=1, source_target_pairs={{0,16},{4,20},{8,24},{12,28},{1,17},{5,21},{9,25},{13,29},{2,18},{... | collective-permute-start | bytes 196616 | tf_op jit(solution)/shard_map/state_2/ppermute | solution.py:148
  25.0 1.2 %copy-start = (f32[128,2048]{1,0:T(8,128)S(1)}, f32[128,2048]{1,0:T(8,128)}, u32[]{:S(2)}) copy-start(f32[128,2048]{1,0:T(8,128)} %shard_map.76.base_ref) | copy-start | bytes 3145732
  28.5 12.0 %collective-permute-start.5 = (bf16[128,2048]{1,0:T(8,128)(2,1)S(1)}, bf16[128,2048]{1,0:T(8,128)(2,1)S(1)}, u32[]{:S(2)}, u32[]{:S(2)}) collective-permute-start(bf16[128,2048]{1,0:T(8,128)(2,1)S(1)} %shard_map.77), channel_id=1, source_target_pairs={{0,4},{4,0},{8,12},{12,8},{16,20},{20,16},{24,28},{28,24},{1,5},{5... | collective-permute-start | bytes 1572872 | tf_op jit(solution)/shard_map/near_y/ppermute | solution.py:148
  29.1 13.6 %collective-permute-start.4 = (bf16[128,2048]{1,0:T(8,128)(2,1)S(1)}, bf16[128,2048]{1,0:T(8,128)(2,1)S(1)}, u32[]{:S(2)}, u32[]{:S(2)}) collective-permute-start(bf16[128,2048]{1,0:T(8,128)(2,1)S(1)} %shard_map.77), channel_id=1, source_target_pairs={{8,16},{12,20},{16,8},{20,12},{9,17},{13,21},{17,9},{21,13},{10,18... | collective-permute-start | bytes 1572872 | tf_op jit(solution)/shard_map/middle/ppermute | solution.py:148
  32.5 11.4 %collective-permute-start.3 = (bf16[128,2048]{1,0:T(8,128)(2,1)S(1)}, bf16[128,2048]{1,0:T(8,128)(2,1)S(1)}, u32[]{:S(2)}, u32[]{:S(2)}) collective-permute-start(bf16[128,2048]{1,0:T(8,128)(2,1)S(1)} %shard_map.77), channel_id=1, source_target_pairs={{0,8},{4,12},{8,0},{12,4},{16,24},{20,28},{24,16},{28,20},{1,9},{5... | collective-permute-start | bytes 1572872 | tf_op jit(solution)/shard_map/one/ppermute | solution.py:148
  32.7 16.5 %copy-start.6 = (bf16[2048,1024]{1,0:T(8,128)(2,1)S(1)}, bf16[2048,1024]{1,0:T(8,128)(2,1)}, u32[]{:S(2)}) copy-start(bf16[2048,1024]{1,0:T(8,128)(2,1)} %param.13) | copy-start | bytes 12582916
  43.9 13.0 %collective-permute-start.8 = (bf16[128,2048]{1,0:T(8,128)(2,1)S(1)}, bf16[128,2048]{1,0:T(8,128)(2,1)S(1)}, u32[]{:S(2)}, u32[]{:S(2)}) collective-permute-start(bf16[128,2048]{1,0:T(8,128)(2,1)S(1)} %collective-permute-done.3), channel_id=1, source_target_pairs={{0,4},{4,0},{8,12},{12,8},{16,20},{20,16},{24,28},{28,24},{1,5},{5... | collective-permute-start | bytes 1572872 | tf_op jit(solution)/shard_map/one_y/ppermute | solution.py:148
  45.4 12.1 %collective-permute-start.6 = (bf16[128,2048]{1,0:T(8,128)(2,1)S(1)}, bf16[128,2048]{1,0:T(8,128)(2,1)S(1)}, u32[]{:S(2)}, u32[]{:S(2)}) collective-permute-start(bf16[128,2048]{1,0:T(8,128)(2,1)S(1)} %collective-permute-done.3), channel_id=1, source_target_pairs={{8,16},{12,20},{16,8},{20,12},{9,17},{13,21},{17,9},{21,13},{10,18... | collective-permute-start | bytes 1572872 | tf_op jit(solution)/shard_map/given/ppermute | solution.py:148
  47.9 9.0 %collective-permute-start.7 = (bf16[128,2048]{1,0:T(8,128)(2,1)S(1)}, bf16[128,2048]{1,0:T(8,128)(2,1)S(1)}, u32[]{:S(2)}, u32[]{:S(2)}) collective-permute-start(bf16[128,2048]{1,0:T(8,128)(2,1)S(1)} %collective-permute-done.4), channel_id=1, source_target_pairs={{8,0},{12,4},{16,24},{20,28},{9,1},{13,5},{17,25},{21,29},{10,2},{... | collective-permute-start | bytes 1572872 | tf_op jit(solution)/shard_map/out2/ppermute | solution.py:148
  57.5 8.3 %collective-permute-start.11 = (bf16[128,1024]{1,0:T(8,128)(2,1)S(1)}, bf16[128,1024]{1,0:T(8,128)(2,1)S(1)}, u32[]{:S(2)}, u32[]{:S(2)}) collective-permute-start(bf16[128,1024]{1,0:T(8,128)(2,1)S(1)} %slice.33), channel_id=1, source_target_pairs={{8,16},{12,20},{16,8},{20,12},{9,17},{13,21},{17,9},{21,13},{10,18... | collective-permute-start | bytes 786440 | tf_op jit(solution)/shard_map/middle_y/ppermute | solution.py:148
  60.9 11.2 %collective-permute-start.9 = (bf16[128,2048]{1,0:T(8,128)(2,1)S(1)}, bf16[128,2048]{1,0:T(8,128)(2,1)S(1)}, u32[]{:S(2)}, u32[]{:S(2)}) collective-permute-start(bf16[128,2048]{1,0:T(8,128)(2,1)S(1)} %collective-permute-done.6), channel_id=1, source_target_pairs={{8,0},{12,4},{16,24},{20,28},{9,1},{13,5},{17,25},{21,29},{10,2},{... | collective-permute-start | bytes 1572872 | tf_op jit(solution)/shard_map/out3/ppermute | solution.py:148
  62.8 9.2 %collective-permute-start.10 = (bf16[128,2048]{1,0:T(8,128)(2,1)S(1)}, bf16[128,2048]{1,0:T(8,128)(2,1)S(1)}, u32[]{:S(2)}, u32[]{:S(2)}) collective-permute-start(bf16[128,2048]{1,0:T(8,128)(2,1)S(1)} %broadcast_select_fusion.1), channel_id=1, source_target_pairs={{0,4},{4,0},{8,12},{12,8},{16,20},{20,16},{24,28},{28,24},{1,5},{5... | collective-permute-start | bytes 1572872 | tf_op jit(solution)/shard_map/two_y/ppermute | solution.py:148
  63.6 10.8 %collective-permute-start.15 = (bf16[2,128,1024]{2,1,0:T(8,128)(2,1)S(1)}, bf16[2,128,1024]{2,1,0:T(8,128)(2,1)S(1)}, u32[]{:S(2)}, u32[]{:S(2)}) collective-permute-start(bf16[2,128,1024]{2,1,0:T(8,128)(2,1)S(1)} %pad_maximum_fusion.2), channel_id=1, source_target_pairs={{0,1},{1,0},{2,3},{3,2},{4,5},{5,4},{6,7},{7,6},{8,9},{9,8},{10,11... | collective-permute-start | bytes 1572872 | tf_op jit(solution)/shard_map/core_close/ppermute | solution.py:148
  72.9 4.7 %collective-permute-start.12 = (bf16[2,128,1024]{2,1,0:T(8,128)(2,1)S(1)}, bf16[2,128,1024]{2,1,0:T(8,128)(2,1)S(1)}, u32[]{:S(2)}, u32[]{:S(2)}) collective-permute-start(bf16[2,128,1024]{2,1,0:T(8,128)(2,1)S(1)} %fusion.11), channel_id=1, source_target_pairs={{1,0},{3,2},{5,4},{7,6},{9,8},{11,10},{13,12},{15,14},{17,16},{19,... | collective-permute-start | bytes 1572872 | tf_op jit(solution)/shard_map/core_far0/ppermute | solution.py:148
  74.6 9.1 %collective-permute-start.16 = (bf16[128,1024]{1,0:T(8,128)(2,1)S(1)}, bf16[128,1024]{1,0:T(8,128)(2,1)S(1)}, u32[]{:S(2)}, u32[]{:S(2)}) collective-permute-start(bf16[128,1024]{1,0:T(8,128)(2,1)S(1)} %fusion.17), channel_id=1, source_target_pairs={{0,2},{1,3},{2,0},{3,1},{4,6},{5,7},{6,4},{7,5},{8,10},{9,11},{10,... | collective-permute-start | bytes 786440 | tf_op jit(solution)/shard_map/side_close/ppermute | solution.py:148
  75.3 8.4 %collective-permute-start.14 = (bf16[128,1024]{1,0:T(8,128)(2,1)S(1)}, bf16[128,1024]{1,0:T(8,128)(2,1)S(1)}, u32[]{:S(2)}, u32[]{:S(2)}) collective-permute-start(bf16[128,1024]{1,0:T(8,128)(2,1)S(1)} %slice.37), channel_id=1, source_target_pairs={{8,0},{12,4},{16,24},{20,28},{9,1},{13,5},{17,25},{21,29},{10,2},{... | collective-permute-start | bytes 786440 | tf_op jit(solution)/shard_map/out_y/ppermute | solution.py:148
  77.1 8.9 %collective-permute-start.13 = (bf16[128,1024]{1,0:T(8,128)(2,1)S(1)}, bf16[128,1024]{1,0:T(8,128)(2,1)S(1)}, u32[]{:S(2)}, u32[]{:S(2)}) collective-permute-start(bf16[128,1024]{1,0:T(8,128)(2,1)S(1)} %slice.46), channel_id=1, source_target_pairs={{0,4},{4,0},{8,12},{12,8},{16,20},{20,16},{24,28},{28,24},{1,5},{5... | collective-permute-start | bytes 786440 | tf_op jit(solution)/shard_map/three_y/ppermute | solution.py:148
  77.9 8.8 %collective-permute-start.17 = (bf16[128,1024]{1,0:T(8,128)(2,1)S(1)}, bf16[128,1024]{1,0:T(8,128)(2,1)S(1)}, u32[]{:S(2)}, u32[]{:S(2)}) collective-permute-start(bf16[128,1024]{1,0:T(8,128)(2,1)S(1)} %fusion.18), channel_id=1, source_target_pairs={{0,2},{2,0},{4,6},{6,4},{8,10},{10,8},{12,14},{14,12},{16,18},{18,... | collective-permute-start | bytes 786440 | tf_op jit(solution)/shard_map/side_far0/ppermute | solution.py:148
  86.7 1.8 %copy-start.8 = (bf16[128,1024]{1,0:T(8,128)(2,1)}, bf16[128,1024]{1,0:T(8,128)(2,1)S(1)}, u32[]{:S(2)}) copy-start(bf16[128,1024]{1,0:T(8,128)(2,1)S(1)} %collective-permute-done.17) | copy-start | bytes 786436
  88.5 3.1 %collective-permute-start.19 = (bf16[2,128,1024]{2,1,0:T(8,128)(2,1)}, bf16[2,128,1024]{2,1,0:T(8,128)(2,1)}, u32[]{:S(2)}, u32[]{:S(2)}) collective-permute-start(bf16[2,128,1024]{2,1,0:T(8,128)(2,1)} %fusion.10), channel_id=1, source_target_pairs={{0,1},{2,3},{4,5},{6,7},{8,9},{10,11},{12,13},{14,15},{16,17},{18,... | collective-permute-start | bytes 1572872 | tf_op jit(solution)/shard_map/core_far1/ppermute | solution.py:148
  92.9 7.6 %collective-permute-start.20 = (bf16[128,1024]{1,0:T(8,128)(2,1)S(1)}, bf16[128,1024]{1,0:T(8,128)(2,1)S(1)}, u32[]{:S(2)}, u32[]{:S(2)}) collective-permute-start(bf16[128,1024]{1,0:T(8,128)(2,1)S(1)} %fusion.19), channel_id=1, source_target_pairs={{1,3},{3,1},{5,7},{7,5},{9,11},{11,9},{13,15},{15,13},{17,19},{19,... | collective-permute-start | bytes 786440 | tf_op jit(solution)/shard_map/side_far1/ppermute | solution.py:148
  94.8 16.4 %collective-permute-start.18 = (bf16[128,1024]{1,0:T(8,128)(2,1)S(1)}, bf16[128,1024]{1,0:T(8,128)(2,1)S(1)}, u32[]{:S(2)}, u32[]{:S(2)}) collective-permute-start(bf16[128,1024]{1,0:T(8,128)(2,1)S(1)} %get-tuple-element.41), channel_id=1, source_target_pairs={{0,16},{1,0},{2,24},{3,8},{4,20},{5,4},{6,28},{7,12},{8,25},{9,9},... | collective-permute-start | bytes 786440 | tf_op jit(solution)/shard_map/own_0/ppermute | solution.py:148
  100.6 13.7 %collective-permute-start.21 = (bf16[128,1024]{1,0:T(8,128)(2,1)S(1)}, bf16[128,1024]{1,0:T(8,128)(2,1)S(1)}, u32[]{:S(2)}, u32[]{:S(2)}) collective-permute-start(bf16[128,1024]{1,0:T(8,128)(2,1)S(1)} %fusion.21), channel_id=1, source_target_pairs={{0,4},{1,20},{2,12},{3,28},{4,0},{5,16},{6,8},{7,24},{8,13},{9,29}... | collective-permute-start | bytes 786440 | tf_op jit(solution)/shard_map/own_1/ppermute | solution.py:148

commit v6 on v5

--- a/solution.py
+++ b/solution.py
@@ -19,47 +19,86 @@
     return jnp.broadcast_to(row, (SUB, row.shape[-1]))
 
 
-def source_rows(k_ref, v_ref, x_ref, lanes):
-    x_ref[...] = k_ref[:, lanes].astype(F32) * v_ref[:, lanes].astype(F32)
-    length = x_ref.shape[0] // SUB
-    return [x_ref[pl.ds(i, SUB, stride=length), :] for i in range(length)]
-
-
-def state_kernel(total, k_ref, v_ref, rate_ref, state_ref, x_ref):
+def runs(ref, chunk):
+    length = ref.shape[1] // SUB
+    return [ref[chunk, pl.ds(i, SUB, stride=length), :] for i in range(length)]
+
+
+def powers(rate, length):
+    once = jnp.exp(rate * length)
+    twice = once * once
+    return once, twice, twice * twice
+
+
+def raised(steps, pows, m):
+    result = jnp.where(steps % 2 == 1, spread_rows(pows[0][m : m + 1]), 1.0)
+    result = result * jnp.where(steps // 2 % 2 == 1, spread_rows(pows[1][m : m + 1]), 1.0)
+    return result * jnp.where(steps >= 4, spread_rows(pows[2][m : m + 1]), 1.0)
+
+
+def state_kernel(total, pieces, *refs):
+    hbm, (state_ref, *near, k_ref, v_ref, sems) = refs[:6], refs[6:]
+    x_ref, rate_ref, gain_ref, q_ref, skip_ref = near
     modes, width = rate_ref.shape
-    length = x_ref.shape[0] // SUB
-    block = lax.broadcasted_iota(jnp.int32, (SUB, LANES), 0).astype(F32)
-
-    @pl.loop(0, width // LANES)
+    length = x_ref.shape[1] // SUB
+    part = width // pieces
+
+    def copies(piece):
+        lanes = pl.ds(piece * part, part)
+        pairs = zip(hbm[:4], (k_ref, v_ref, rate_ref, gain_ref))
+        return [
+            pltpu.make_async_copy(src.at[:, lanes], dst.at[:, lanes], sems.at[piece, j])
+            for j, (src, dst) in enumerate(pairs)
+        ]
+
+    whole = [pltpu.make_async_copy(src, dst, sems.at[pieces, j]) for j, (src, dst) in enumerate(zip(hbm[4:6], (q_ref, skip_ref)))]
+    for piece in range(pieces):
+        for copy in copies(piece):
+            copy.start()
+    for copy in whole:
+        copy.start()
+    left = SUB - 1 - lax.broadcasted_iota(jnp.int32, (SUB, LANES), 0)
+    for piece in range(pieces):
+        for copy in copies(piece):
+            copy.wait()
+
+        @pl.loop(0, part // LANES)
+        def _(chunk):
+            chunk = piece * (part // LANES) + chunk
+            lanes = pl.ds(pl.multiple_of(chunk * LANES, LANES), LANES)
+            x_ref[chunk] = k_ref[:, lanes].astype(F32) * v_ref[:, lanes].astype(F32)
+            gain_ref[:, lanes] = gain_ref[:, lanes] * jnp.sqrt(rate_ref[:, lanes] * (2.0 / total))
+            x = runs(x_ref, chunk)
+            rate = rate_ref[:, lanes] * (-1.0 / total)
+            decay = jnp.exp(rate)
+            pows = powers(rate, length)
+            rows = []
+            for m in range(modes):
+                d = spread_rows(decay[m : m + 1])
+                state = x[0]
+                for i in range(1, length):
+                    state = state * d + x[i]
+                rows.append(jnp.sum(state * raised(left, pows, m), axis=0, keepdims=True))
+            state_ref[:, lanes] = jnp.concatenate(rows, axis=0).astype(BF16)
+
+    for copy in whole:
+        copy.wait()
+
+
+def local_kernel(total, window, x_ref, rate_ref, gain_ref, skip_ref, *rest):
+    base_ref = rest[-1]
+    modes, width = rate_ref.shape
+    length = x_ref.shape[1] // SUB
+    block = lax.broadcasted_iota(jnp.int32, (SUB, LANES), 0)
+
+    @pl.loop(window[0], window[1])
     def _(chunk):
         lanes = pl.ds(pl.multiple_of(chunk * LANES, LANES), LANES)
-        x = source_rows(k_ref, v_ref, x_ref, lanes)
+        x = runs(x_ref, chunk)
         rate = rate_ref[:, lanes] * (-1.0 / total)
+        gain = gain_ref[:, lanes]
         decay = jnp.exp(rate)
-        rows = []
-        for m in range(modes):
-            d = spread_rows(decay[m : m + 1])
-            state = x[0]
-            for i in range(1, length):
-                state = state * d + x[i]
-            weight = jnp.exp(spread_rows(rate[m : m + 1]) * ((SUB - 1.0 - block) * length))
-            rows.append(jnp.sum(state * weight, axis=0, keepdims=True))
-        state_ref[:, lanes] = jnp.concatenate(rows, axis=0).astype(BF16)
-
-
-def local_kernel(total, q_ref, k_ref, v_ref, res_ref, rate_ref, skip_ref, *rest):
-    base_ref, x_ref, y_ref = rest[-3:]
-    modes, width = rate_ref.shape
-    length = x_ref.shape[0] // SUB
-    block = lax.broadcasted_iota(jnp.int32, (SUB, LANES), 0)
-
-    @pl.loop(0, width // LANES)
-    def _(chunk):
-        lanes = pl.ds(pl.multiple_of(chunk * LANES, LANES), LANES)
-        x = source_rows(k_ref, v_ref, x_ref, lanes)
-        rate = rate_ref[:, lanes] * (-1.0 / total)
-        gain = res_ref[:, lanes] * jnp.sqrt(rate_ref[:, lanes] * (2.0 / total))
-        decay = jnp.exp(rate)
+        pows = powers(rate, length)
         y = [spread_rows(skip_ref[:, lanes]) * x[i] for i in range(length)]
         power = gain
         for j in range(length):
@@ -72,71 +111,60 @@
             state = x[0]
             for i in range(1, length):
                 state = state * d + x[i]
-            step = spread_rows(rate[m : m + 1]) * length
             state = jnp.where(block >= 1, pltpu.roll(state, 1, 0), 0.0)
-            for shift in (1, 2, 4):
-                moved = jnp.where(block >= shift, pltpu.roll(state, shift, 0), 0.0)
-                state = state + jnp.exp(step * shift) * moved
+            for shift, step in zip((1, 2, 4), pows):
+                moved_on = jnp.where(block >= shift, pltpu.roll(state, shift, 0), 0.0)
+                state = state + spread_rows(step[m : m + 1]) * moved_on
             state = state * spread_rows(gain[m : m + 1])
             for i in range(length):
                 state = state * d
                 y[i] = y[i] + state
         for i in range(length):
-            y_ref[pl.ds(i, SUB, stride=length), :] = y[i]
-        base_ref[:, lanes] = y_ref[...] * q_ref[:, lanes].astype(F32)
-
-
-def carry_kernel(total, odd_ref, q_ref, base_ref, below_ref, further_ref, first_ref, res_ref, rate_ref, out_ref, y_ref):
+            base_ref[chunk, pl.ds(i, SUB, stride=length), :] = y[i]
+
+
+def carry_kernel(total, odd_ref, q_ref, base_ref, below_ref, further_ref, first_ref, rate_ref, gain_ref, out_ref, y_ref):
     modes, width = rate_ref.shape
     length = y_ref.shape[0] // SUB
-    block = lax.broadcasted_iota(jnp.int32, (SUB, LANES), 0).astype(F32)
+    rows = y_ref.shape[0]
+    block = lax.broadcasted_iota(jnp.int32, (SUB, LANES), 0)
 
     @pl.loop(0, width // LANES)
     def _(chunk):
         lanes = pl.ds(pl.multiple_of(chunk * LANES, LANES), LANES)
         rate = rate_ref[:, lanes] * (-1.0 / total)
-        rows = SUB * length
+        pows = powers(rate, length)
         start = below_ref[:, lanes].astype(F32) + further_ref[:, lanes].astype(F32) * jnp.exp(rate * (2 * rows))
         later = start * jnp.exp(rate * rows) + first_ref[:, lanes].astype(F32)
-        start = jnp.where(odd_ref[0] == 1, later, start)
-        start = start * res_ref[:, lanes] * jnp.sqrt(rate_ref[:, lanes] * (2.0 / total))
+        start = jnp.where(odd_ref[0] == 1, later, start) * gain_ref[:, lanes]
         decay = jnp.exp(rate)
-        y = [jnp.zeros((SUB, LANES), F32) for i in range(length)]
+        y = runs(base_ref, chunk)
         for m in range(modes):
             d = spread_rows(decay[m : m + 1])
-            state = spread_rows(start[m : m + 1]) * jnp.exp(spread_rows(rate[m : m + 1]) * (block * length))
+            state = spread_rows(start[m : m + 1]) * raised(block, pows, m)
             for i in range(length):
                 state = state * d
                 y[i] = y[i] + state
         for i in range(length):
             y_ref[pl.ds(i, SUB, stride=length), :] = y[i]
-        out_ref[:, lanes] = (base_ref[:, lanes] + y_ref[...] * q_ref[:, lanes].astype(F32)).astype(BF16)
-
-
-def run(kernel, out, scratch, ops, mib, args, window=None, filled=None, scalars=()):
-    rows, width = args[0].shape
-    part = min(width // 4, 4 * LANES)
-    steps = width // part
-    first = 0
-    if window is not None:
-        first, steps = window[0] * steps // 4, (window[1] - window[0]) * steps // 4
-    specs = [pl.BlockSpec(memory_space=pltpu.SMEM)] * len(scalars)
-    specs += [pl.BlockSpec((arg.shape[0], part), lambda i: (0, i + first)) for arg in args]
-    if filled is not None:
-        specs.append(pl.BlockSpec(memory_space=pl.ANY))
+        out_ref[:, lanes] = (y_ref[...] * q_ref[:, lanes].astype(F32)).astype(BF16)
+
+
+def run(kernel, outs, ops, mib, args, scratch=(), scalars=(), near=True, aliases={}):
+    space = pltpu.VMEM if near else pl.ANY
     return pl.pallas_call(
         kernel,
-        grid=(steps,),
-        out_shape=out,
-        in_specs=specs,
-        out_specs=pl.BlockSpec((out.shape[0], part), lambda i: (0, i + first)),
-        scratch_shapes=[pltpu.VMEM((rows, LANES), F32)] * scratch,
-        input_output_aliases={} if filled is None else {len(specs) - 1: 0},
+        out_shape=[jax.ShapeDtypeStruct(shape, kind) for shape, kind in outs],
+        in_specs=[pl.BlockSpec(memory_space=pltpu.SMEM)] * len(scalars)
+        + [pl.BlockSpec(memory_space=space)] * len(args),
+        out_specs=[pl.BlockSpec(memory_space=pltpu.VMEM)] * len(outs),
+        scratch_shapes=scratch,
+        input_output_aliases=aliases,
         compiler_params=pltpu.CompilerParams(vmem_limit_bytes=mib * 1024 * 1024),
         cost_estimate=pl.CostEstimate(
-            flops=ops * rows * part * steps, bytes_accessed=6 * rows * part * steps, transcendentals=0
+            flops=int(ops * args[0].size), bytes_accessed=4 * args[0].size, transcendentals=0
         ),
-    )(*scalars, *args, *(() if filled is None else (filled,)))
+    )(*scalars, *args)
 
 
 def matmul(x, w):
@@ -158,7 +186,7 @@
     for b in range(parts):
         entering = jnp.where(b < index, entering * fade(rows) + states[b].astype(F32), entering)
     nothing = jnp.zeros_like(state)
-    hidden = hidden_of(base_of((0, 4)), entering, nothing, nothing, jnp.int32(0))
+    hidden = hidden_of(base_of((0, 16)), entering, nothing, nothing, jnp.int32(0))
     spread = matmul(lax.all_gather(hidden, "seq", axis=0, tiled=True), w_out)
     partial_value = lax.all_to_all(spread, "seq", split_axis=0, concat_axis=1, tiled=True)
     summed = lax.psum_scatter(partial_value, "chan", scatter_dimension=1, tiled=True)
@@ -180,15 +208,15 @@
 
     every = range(depth)
     other = across(state, every, "state_y")
-    other, base = fence(other, base_of((0, 2)))
+    other, *base = fence(other, *base_of((0, 2)))
     first = jnp.where(y == 0, state, other)
     second = jnp.where(y == 0, other, state)
     plane = first.astype(F32) * fade(rows) + second.astype(F32)
     below = along(plane.astype(BF16), shift(1), "state_1")
-    below, base = fence(below, base_of((2, 3), base))
+    below, *base = fence(below, *base_of((2, 9), base))
     two_below = (plane + below.astype(F32) * fade(2 * rows)).astype(BF16)
     further = along(two_below, shift(2), "state_2")
-    base = base_of((3, 4), base)
+    base = base_of((9, 16), base)
     hidden = hidden_of(base, below, further, first, y)
 
     chan = lax.axis_index("chan")
@@ -264,37 +292,41 @@
     total = rows * parts
     modes = rates.shape[1]
     res_t, rate_t = residues.T, rates.T
-    state = run(
-        functools.partial(state_kernel, total),
-        jax.ShapeDtypeStruct((modes, width), BF16),
-        1,
+    pieces = 4
+    tall, thin = (rows, width), (modes, width)
+    chunks = (width // LANES, rows, LANES)
+    state, x, rate_near, gain, q_near, skip = run(
+        functools.partial(state_kernel, total, pieces),
+        [(thin, BF16), (chunks, F32), (thin, F32), (thin, F32), (tall, BF16), ((1, width), F32)],
         48,
         60,
-        [k_proj, v_proj, rate_t],
+        [k_proj, v_proj, rate_t, res_t, q_proj, skip_gain[None, :]],
+        [pltpu.VMEM(tall, BF16), pltpu.VMEM(tall, BF16), pltpu.SemaphoreType.DMA((pieces + 1, 4))],
+        near=False,
     )
 
-    def base_of(window, filled=None):
+    def base_of(window, filled=()):
+        count = width // LANES
+        window = (window[0] * count // 16, window[1] * count // 16)
         return run(
-            functools.partial(local_kernel, total),
-            jax.ShapeDtypeStruct((rows, width), F32),
-            2,
-            100,
-            60,
-            [q_proj, k_proj, v_proj, res_t, rate_t, skip_gain[None, :]],
-            window,
-            filled,
+            functools.partial(local_kernel, total, window),
+            [(chunks, F32)],
+            100 * (window[1] - window[0]) / count,
+            16,
+            [x, rate_near, gain, skip, *filled],
+            aliases={4: 0} if filled else {},
         )
 
     def hidden_of(base, below, further, first, odd):
         return run(
             functools.partial(carry_kernel, total),
-            jax.ShapeDtypeStruct((rows, width), BF16),
-            1,
+            [(tall, BF16)],
             32,
             16,
-            [q_proj, base, below, further, first, res_t, rate_t],
+            [q_near, *base, below, further, first, rate_near, gain],
+            [pltpu.VMEM((rows, LANES), F32)],
             scalars=(odd.astype(jnp.int32)[None],),
-        )
+        )[0]
 
     def fade(steps):
         return jnp.exp(rate_t * (-float(steps) / total))

time: 116 us -> 114 us (0.983)
  Pallas kernels: 16.9 us -> 11.5 us
  local copies, waits for them, and re-layouts: 1.31 us -> 3.8 us
    pallas_call x5, Pallas kernels: 16.9 us -> 11.5 us  [run(): pl.pallas_call(kernel, out_shape=[jax.ShapeDtypeStruct(shape, kind) for s...]
    unnamed x18, local copies, waits for them, and re-layouts: 1.26 us -> 3.75 us
  transfers between devices with their start and end apart: 22 -> 22, of which waited for: 13 -> 15; matrix products, arithmetic and copies ran while one was open for 9% -> 9% of each run, Pallas kernels for 9% -> 4%
where the time goes in v6:
time: 114 us; the launch traced here: 113 us
  waiting for transfers between devices  42.2 us (37%)
  starting transfers between devices  40.2 us (35%)
  Pallas kernels  11.5 us (10%)
  matrix products  8.32 us (7%)
  other arithmetic  6.32 us (6%)
  local copies, waits for them, and re-layouts  3.8 us (3%)
    ppermute x22, waiting for transfers between devices, moved(): return lax.ppermute(x, axes, pairs)  42.2 us
    ppermute x22, starting transfers between devices, moved(): return lax.ppermute(x, axes, pairs)  40.2 us
    pallas_call x5, Pallas kernels, run(): pl.pallas_call(kernel, out_shape=[jax.ShapeDtypeStruct(shape, kind) for s...  11.5 us
    dot_general x9, matrix products, matmul(): return jnp.dot(x, w, preferred_element_type=F32)  8.32 us
    unnamed x18, local copies, waits for them, and re-layouts  3.75 us
  transfers between devices with their start and end apart: 22, of which 15 were waited for; matrix products, arithmetic and copies ran while one was open for 9% of the time, Pallas kernels for 4%

profile of v6, /device:TPU:10, one launch (start us, length us, event | category | flops | bytes accessed | tf_op | source)
XLA Modules:
  0.0 112.8 jit_solution(906968329174257187)
XLA Ops:
  0.0 4.9 %shard_map.73 = (bf16[16,2048]{1,0:T(8,128)(2,1)}, f32[16,128,128]{2,1,0:T(8,128)}, f32[16,2048]{1,0:T(8,128)}, f32[16,2048]{1,0:T(8,128)}, bf16[128,2048]{1,0:T(8,128)(2,1)}, /*index=5*/f32[1,2048]{1,0:T(1,128)}) custom-call(bf16[128,2048]{1,0:T(8,128)(2,1)} %refs_0_.1, bf16[128,2048]{1,0:T(8,128)(2,1)} %refs_1_.1, f32[16,2048]{1,0:T(8,128)} %bitcast.60, ...), custom_call_target="tpu_custom_call" | custom-call | flops 12582912 | bytes 1048576 | tf_op jit(solution)/shard_map/pallas_call | solution.py:155
  5.0 1.6 %collective-permute-start = (bf16[16,2048]{1,0:T(8,128)(2,1)}, bf16[16,2048]{1,0:T(8,128)(2,1)S(1)}, u32[]{:S(2)}, u32[]{:S(2)}) collective-permute-start(bf16[16,2048]{1,0:T(8,128)(2,1)} %get-tuple-element.34), channel_id=1, source_target_pairs={{0,4},{4,0},{8,12},{12,8},{16,20},{20,16},{24,28},{28,24},{1,5},{5... | collective-permute-start | bytes 196616 | tf_op jit(solution)/shard_map/state_y/ppermute | solution.py:176
  6.5 1.2 %copy-done = f32[16,128,128]{2,1,0:T(8,128)S(1)} copy-done((f32[16,128,128]{2,1,0:T(8,128)S(1)}, f32[16,128,128]{2,1,0:T(8,128)}, u32[]{:S(2)}) %copy-start) | copy-done | bytes 1048600
  7.8 0.9 copy-done.1
  8.7 0.9 copy-done.2
  9.6 0.7 copy-done.4
  10.9 0.9 fusion.24
  11.8 3.5 %collective-permute-start.1 = (bf16[16,2048]{1,0:T(8,128)(2,1)S(1)}, bf16[16,2048]{1,0:T(8,128)(2,1)S(1)}, u32[]{:S(2)}, u32[]{:S(2)}) collective-permute-start(bf16[16,2048]{1,0:T(8,128)(2,1)S(1)} %get-tuple-element.55), channel_id=1, source_target_pairs={{0,8},{4,12},{8,16},{12,20},{16,24},{20,28},{1,9},{5,13},{9,17},{1... | collective-permute-start | bytes 196616 | tf_op jit(solution)/shard_map/state_1/ppermute | solution.py:176
  15.3 1.9 %shard_map.75.rest_0_ = f32[16,128,128]{2,1,0:T(8,128)S(1)} custom-call(f32[16,128,128]{2,1,0:T(8,128)S(1)} %copy-done, f32[16,2048]{1,0:T(8,128)S(1)} %copy-done.1, f32[16,2048]{1,0:T(8,128)S(1)} %copy-done.2, f32[1,2048]{1,0:T(1,128)S(1)} %copy-done.4, f32[16,128,128]{2,1,0:T(8,128)S(1)} %shard_map.74.rest_0_), custom_call_target="tpu_custom_call", output_to_operand_aliasing={{}: (4, {})} | custom-call | flops 11468800 | bytes 1048576 | tf_op jit(solution)/shard_map/pallas_call | solution.py:155
  17.2 0.8 collective-permute-done.1.below_ref
  18.0 4.5 %collective-permute-start.2 = (bf16[16,2048]{1,0:T(8,128)(2,1)S(1)}, bf16[16,2048]{1,0:T(8,128)(2,1)S(1)}, u32[]{:S(2)}, u32[]{:S(2)}) collective-permute-start(bf16[16,2048]{1,0:T(8,128)(2,1)S(1)} %add_convert_fusion), channel_id=1, source_target_pairs={{0,16},{4,20},{8,24},{12,28},{1,17},{5,21},{9,25},{13,29},{2,18},{... | collective-permute-start | bytes 196616 | tf_op jit(solution)/shard_map/state_2/ppermute | solution.py:176
  22.5 1.9 %shard_map.76.base_ref = f32[16,128,128]{2,1,0:T(8,128)S(1)} custom-call(f32[16,128,128]{2,1,0:T(8,128)S(1)} %copy-done, f32[16,2048]{1,0:T(8,128)S(1)} %copy-done.1, f32[16,2048]{1,0:T(8,128)S(1)} %copy-done.2, f32[1,2048]{1,0:T(1,128)S(1)} %copy-done.4, f32[16,128,128]{2,1,0:T(8,128)S(1)} %shard_map.75.rest_0_), custom_call_target="tpu_custom_call", output_to_operand_aliasing={{}: (4, {})} | custom-call | flops 11468800 | bytes 1048576 | tf_op jit(solution)/shard_map/pallas_call | solution.py:155
  24.9 2.2 %shard_map.77 = bf16[128,2048]{1,0:T(8,128)(2,1)S(1)} custom-call(s32[1]{0:T(128)} %bitcast.odd_ref, bf16[128,2048]{1,0:T(8,128)(2,1)S(1)} %copy-done.3, f32[16,128,128]{2,1,0:T(8,128)S(1)} %shard_map.76.base_ref, bf16[16,2048]{1,0:T(8,128)(2,1)S(1)} %collective-permute-done.1.below_ref, bf16[16,2048]{1,0:T(8,128)(2,1)S(1)} %collective-permute-done.2.further_ref, ...), custom_call_target="tpu_custom_call" | custom-call | flops 8388608 | bytes 1048576 | tf_op jit(solution)/shard_map/pallas_call | solution.py:155
  27.7 3.7 %collective-permute-start.4 = (bf16[128,2048]{1,0:T(8,128)(2,1)S(1)}, bf16[128,2048]{1,0:T(8,128)(2,1)S(1)}, u32[]{:S(2)}, u32[]{:S(2)}) collective-permute-start(bf16[128,2048]{1,0:T(8,128)(2,1)S(1)} %shard_map.77), channel_id=1, source_target_pairs={{8,16},{12,20},{16,8},{20,12},{9,17},{13,21},{17,9},{21,13},{10,18... | collective-permute-start | bytes 1572872 | tf_op jit(solution)/shard_map/middle/ppermute | solution.py:176
  31.6 3.0 %fusion.27 = f32[128,1024]{1,0:T(8,128)S(1)} fusion(bf16[128,2048]{1,0:T(8,128)(2,1)S(1)} %shard_map.77, bf16[2048,1024]{1,0:T(8,128)(2,1)} %param.13), kind=kOutput, calls=%fused_computation.50 | convolution fusion | flops 536870912 | bytes 5242880 | tf_op jit(solution)/shard_map/dot_general | solution.py:171
  34.7 4.0 %collective-permute-done.5 = bf16[128,2048]{1,0:T(8,128)(2,1)S(1)} collective-permute-done((bf16[128,2048]{1,0:T(8,128)(2,1)S(1)}, bf16[128,2048]{1,0:T(8,128)(2,1)S(1)}, u32[]{:S(2)}, u32[]{:S(2)}) %collective-permute-start.5) | collective-permute-done | bytes 524320 | tf_op jit(solution)/shard_map/near_y/ppermute | solution.py:176
  38.7 2.1 %collective-permute-done.4 = bf16[128,2048]{1,0:T(8,128)(2,1)S(1)} collective-permute-done((bf16[128,2048]{1,0:T(8,128)(2,1)S(1)}, bf16[128,2048]{1,0:T(8,128)(2,1)S(1)}, u32[]{:S(2)}, u32[]{:S(2)}) %collective-permute-start.4) | collective-permute-done | bytes 524320 | tf_op jit(solution)/shard_map/middle/ppermute | solution.py:176
  40.8 1.3 %collective-permute-done.3 = bf16[128,2048]{1,0:T(8,128)(2,1)S(1)} collective-permute-done((bf16[128,2048]{1,0:T(8,128)(2,1)S(1)}, bf16[128,2048]{1,0:T(8,128)(2,1)S(1)}, u32[]{:S(2)}, u32[]{:S(2)}) %collective-permute-start.3) | collective-permute-done | bytes 524320 | tf_op jit(solution)/shard_map/one/ppermute | solution.py:176
  42.1 1.5 %collective-permute-start.8 = (bf16[128,2048]{1,0:T(8,128)(2,1)S(1)}, bf16[128,2048]{1,0:T(8,128)(2,1)S(1)}, u32[]{:S(2)}, u32[]{:S(2)}) collective-permute-start(bf16[128,2048]{1,0:T(8,128)(2,1)S(1)} %collective-permute-done.3), channel_id=1, source_target_pairs={{0,4},{4,0},{8,12},{12,8},{16,20},{20,16},{24,28},{28,24},{1,5},{5... | collective-permute-start | bytes 1572872 | tf_op jit(solution)/shard_map/one_y/ppermute | solution.py:176
  43.7 2.4 %collective-permute-start.6 = (bf16[128,2048]{1,0:T(8,128)(2,1)S(1)}, bf16[128,2048]{1,0:T(8,128)(2,1)S(1)}, u32[]{:S(2)}, u32[]{:S(2)}) collective-permute-start(bf16[128,2048]{1,0:T(8,128)(2,1)S(1)} %collective-permute-done.3), channel_id=1, source_target_pairs={{8,16},{12,20},{16,8},{20,12},{9,17},{13,21},{17,9},{21,13},{10,18... | collective-permute-start | bytes 1572872 | tf_op jit(solution)/shard_map/given/ppermute | solution.py:176
  46.1 1.3 %collective-permute-start.7 = (bf16[128,2048]{1,0:T(8,128)(2,1)S(1)}, bf16[128,2048]{1,0:T(8,128)(2,1)S(1)}, u32[]{:S(2)}, u32[]{:S(2)}) collective-permute-start(bf16[128,2048]{1,0:T(8,128)(2,1)S(1)} %collective-permute-done.4), channel_id=1, source_target_pairs={{8,0},{12,4},{16,24},{20,28},{9,1},{13,5},{17,25},{21,29},{10,2},{... | collective-permute-start | bytes 1572872 | tf_op jit(solution)/shard_map/out2/ppermute | solution.py:176
  47.4 0.7 fusion.26
  48.2 0.7 fusion.29
  48.9 5.7 %collective-permute-done.7 = bf16[128,2048]{1,0:T(8,128)(2,1)S(1)} collective-permute-done((bf16[128,2048]{1,0:T(8,128)(2,1)S(1)}, bf16[128,2048]{1,0:T(8,128)(2,1)S(1)}, u32[]{:S(2)}, u32[]{:S(2)}) %collective-permute-start.7) | collective-permute-done | bytes 524320 | tf_op jit(solution)/shard_map/out2/ppermute | solution.py:176
  54.6 1.1 %collective-permute-done.6 = bf16[128,2048]{1,0:T(8,128)(2,1)S(1)} collective-permute-done((bf16[128,2048]{1,0:T(8,128)(2,1)S(1)}, bf16[128,2048]{1,0:T(8,128)(2,1)S(1)}, u32[]{:S(2)}, u32[]{:S(2)}) %collective-permute-start.6) | collective-permute-done | bytes 524320 | tf_op jit(solution)/shard_map/given/ppermute | solution.py:176
  55.8 2.4 %collective-permute-start.11 = (bf16[128,1024]{1,0:T(8,128)(2,1)S(1)}, bf16[128,1024]{1,0:T(8,128)(2,1)S(1)}, u32[]{:S(2)}, u32[]{:S(2)}) collective-permute-start(bf16[128,1024]{1,0:T(8,128)(2,1)S(1)} %slice.33), channel_id=1, source_target_pairs={{8,16},{12,20},{16,8},{20,12},{9,17},{13,21},{17,9},{21,13},{10,18... | collective-permute-start | bytes 786440 | tf_op jit(solution)/shard_map/middle_y/ppermute | solution.py:176
  58.1 0.7 fusion.28
  58.9 1.6 %collective-permute-start.9 = (bf16[128,2048]{1,0:T(8,128)(2,1)S(1)}, bf16[128,2048]{1,0:T(8,128)(2,1)S(1)}, u32[]{:S(2)}, u32[]{:S(2)}) collective-permute-start(bf16[128,2048]{1,0:T(8,128)(2,1)S(1)} %collective-permute-done.6), channel_id=1, source_target_pairs={{8,0},{12,4},{16,24},{20,28},{9,1},{13,5},{17,25},{21,29},{10,2},{... | collective-permute-start | bytes 1572872 | tf_op jit(solution)/shard_map/out3/ppermute | solution.py:176
  61.4 0.7 convolution_bitcast_fusion.2
  62.1 1.9 %collective-permute-done.11 = bf16[128,1024]{1,0:T(8,128)(2,1)S(1)} collective-permute-done((bf16[128,1024]{1,0:T(8,128)(2,1)S(1)}, bf16[128,1024]{1,0:T(8,128)(2,1)S(1)}, u32[]{:S(2)}, u32[]{:S(2)}) %collective-permute-start.11) | collective-permute-done | bytes 262176 | tf_op jit(solution)/shard_map/middle_y/ppermute | solution.py:176
  64.0 5.7 %collective-permute-done.10 = bf16[128,2048]{1,0:T(8,128)(2,1)S(1)} collective-permute-done((bf16[128,2048]{1,0:T(8,128)(2,1)S(1)}, bf16[128,2048]{1,0:T(8,128)(2,1)S(1)}, u32[]{:S(2)}, u32[]{:S(2)}) %collective-permute-start.10) | collective-permute-done | bytes 524320 | tf_op jit(solution)/shard_map/two_y/ppermute | solution.py:176
  69.8 0.7 convolution_bitcast_fusion.1
  70.6 1.3 %collective-permute-start.12 = (bf16[2,128,1024]{2,1,0:T(8,128)(2,1)S(1)}, bf16[2,128,1024]{2,1,0:T(8,128)(2,1)S(1)}, u32[]{:S(2)}, u32[]{:S(2)}) collective-permute-start(bf16[2,128,1024]{2,1,0:T(8,128)(2,1)S(1)} %fusion.11), channel_id=1, source_target_pairs={{1,0},{3,2},{5,4},{7,6},{9,8},{11,10},{13,12},{15,14},{17,16},{19,... | collective-permute-start | bytes 1572872 | tf_op jit(solution)/shard_map/core_far0/ppermute | solution.py:176
  73.0 1.7 %collective-permute-start.14 = (bf16[128,1024]{1,0:T(8,128)(2,1)S(1)}, bf16[128,1024]{1,0:T(8,128)(2,1)S(1)}, u32[]{:S(2)}, u32[]{:S(2)}) collective-permute-start(bf16[128,1024]{1,0:T(8,128)(2,1)S(1)} %slice.37), channel_id=1, source_target_pairs={{8,0},{12,4},{16,24},{20,28},{9,1},{13,5},{17,25},{21,29},{10,2},{... | collective-permute-start | bytes 786440 | tf_op jit(solution)/shard_map/out_y/ppermute | solution.py:176
  75.5 3.4 %collective-permute-start.17 = (bf16[128,1024]{1,0:T(8,128)(2,1)S(1)}, bf16[128,1024]{1,0:T(8,128)(2,1)S(1)}, u32[]{:S(2)}, u32[]{:S(2)}) collective-permute-start(bf16[128,1024]{1,0:T(8,128)(2,1)S(1)} %fusion.18), channel_id=1, source_target_pairs={{0,2},{2,0},{4,6},{6,4},{8,10},{10,8},{12,14},{14,12},{16,18},{18,... | collective-permute-start | bytes 786440 | tf_op jit(solution)/shard_map/side_far0/ppermute | solution.py:176
  78.9 0.7 convolution_bitcast_fusion
  79.6 1.8 %collective-permute-done.16 = bf16[128,1024]{1,0:T(8,128)(2,1)S(1)} collective-permute-done((bf16[128,1024]{1,0:T(8,128)(2,1)S(1)}, bf16[128,1024]{1,0:T(8,128)(2,1)S(1)}, u32[]{:S(2)}, u32[]{:S(2)}) %collective-permute-start.16) | collective-permute-done | bytes 262176 | tf_op jit(solution)/shard_map/side_close/ppermute | solution.py:176
  81.4 2.2 %collective-permute-done.13 = bf16[128,1024]{1,0:T(8,128)(2,1)S(1)} collective-permute-done((bf16[128,1024]{1,0:T(8,128)(2,1)S(1)}, bf16[128,1024]{1,0:T(8,128)(2,1)S(1)}, u32[]{:S(2)}, u32[]{:S(2)}) %collective-permute-start.13) | collective-permute-done | bytes 262176 | tf_op jit(solution)/shard_map/three_y/ppermute | solution.py:176
  83.6 0.8 collective-permute-done.17
  85.3 0.9 fusion.10
  86.2 2.1 %collective-permute-start.19 = (bf16[2,128,1024]{2,1,0:T(8,128)(2,1)}, bf16[2,128,1024]{2,1,0:T(8,128)(2,1)}, u32[]{:S(2)}, u32[]{:S(2)}) collective-permute-start(bf16[2,128,1024]{2,1,0:T(8,128)(2,1)} %fusion.10), channel_id=1, source_target_pairs={{0,1},{2,3},{4,5},{6,7},{8,9},{10,11},{12,13},{14,15},{16,17},{18,... | collective-permute-start | bytes 1572872 | tf_op jit(solution)/shard_map/core_far1/ppermute | solution.py:176
  88.3 1.1 collective-permute-done.19
  89.3 1.2 %convert_add_fusion = f32[2,128,1024]{2,1,0:T(8,128)S(1)} fusion(bf16[2,128,1024]{2,1,0:T(8,128)(2,1)} %collective-permute-done.19, f32[1,128,1024]{2,1,0:T(8,128)S(1)} %fusion.7, f32[1,128,1024]{2,1,0:T(8,128)S(1)} %convolution_bitcast_fusion), kind=kLoop, calls=%fused_computation.12 | loop fusion | flops 786432 | bytes 2621440 | tf_op jit(solution)/shard_map/add | solution.py:260
  91.3 1.2 %fusion.20 = (bf16[128,1024]{1,0:T(8,128)(2,1)S(1)}, bf16[128,1024]{1,0:T(8,128)(2,1)S(1)}) fusion(bf16[128,1024]{1,0:T(8,128)(2,1)} %copy-done.7, f32[2,128,1024]{2,1,0:T(8,128)S(1)} %convert_add_fusion.1, pred[]{:T(512)S(6)} %eq.32, pred[]{:T(512)S(6)} %eq.31, bf16[128,1024]{1,0:T(8,128)(2,1)S(1)} %collective-permute-done.16, ...), kind=kLoop, calls=%fused_computation.38 | loop fusion | flops 1179648 | bytes 3145731 | tf_op jit(solution)/shard_map/jit(_where)/select_n | solution.py:278
  92.5 5.6 %collective-permute-start.18 = (bf16[128,1024]{1,0:T(8,128)(2,1)S(1)}, bf16[128,1024]{1,0:T(8,128)(2,1)S(1)}, u32[]{:S(2)}, u32[]{:S(2)}) collective-permute-start(bf16[128,1024]{1,0:T(8,128)(2,1)S(1)} %get-tuple-element.53), channel_id=1, source_target_pairs={{0,16},{1,0},{2,24},{3,8},{4,20},{5,4},{6,28},{7,12},{8,25},{9,9},... | collective-permute-start | bytes 786440 | tf_op jit(solution)/shard_map/own_0/ppermute | solution.py:176
  98.7 10.1 %collective-permute-done.18 = bf16[128,1024]{1,0:T(8,128)(2,1)S(1)} collective-permute-done((bf16[128,1024]{1,0:T(8,128)(2,1)S(1)}, bf16[128,1024]{1,0:T(8,128)(2,1)S(1)}, u32[]{:S(2)}, u32[]{:S(2)}) %collective-permute-start.18) | collective-permute-done | bytes 262176 | tf_op jit(solution)/shard_map/own_0/ppermute | solution.py:176
  108.9 3.0 %collective-permute-done.21 = bf16[128,1024]{1,0:T(8,128)(2,1)S(1)} collective-permute-done((bf16[128,1024]{1,0:T(8,128)(2,1)S(1)}, bf16[128,1024]{1,0:T(8,128)(2,1)S(1)}, u32[]{:S(2)}, u32[]{:S(2)}) %collective-permute-start.21) | collective-permute-done | bytes 262176 | tf_op jit(solution)/shard_map/own_1/ppermute | solution.py:176
  112.0 0.8 pad_maximum_fusion.3
  (50 shorter events, 6.9 us)
Async XLA Ops:
  0.0 10.8 %copy-start.6 = (f32[2048,16]{0,1:T(8,128)S(1)}, f32[2048,16]{0,1:T(8,128)}, u32[]{:S(2)}) copy-start(f32[2048,16]{0,1:T(8,128)} %param.11) | copy-start | bytes 393220
  5.0 5.9 %collective-permute-start = (bf16[16,2048]{1,0:T(8,128)(2,1)}, bf16[16,2048]{1,0:T(8,128)(2,1)S(1)}, u32[]{:S(2)}, u32[]{:S(2)}) collective-permute-start(bf16[16,2048]{1,0:T(8,128)(2,1)} %get-tuple-element.34), channel_id=1, source_target_pairs={{0,4},{4,0},{8,12},{12,8},{16,20},{20,16},{24,28},{28,24},{1,5},{5... | collective-permute-start | bytes 196616 | tf_op jit(solution)/shard_map/state_y/ppermute | solution.py:176
  6.5 1.2 %copy-start = (f32[16,128,128]{2,1,0:T(8,128)S(1)}, f32[16,128,128]{2,1,0:T(8,128)}, u32[]{:S(2)}) copy-start(f32[16,128,128]{2,1,0:T(8,128)} %get-tuple-element.30.x_ref) | copy-start | bytes 3145732
  7.8 0.9 copy-start.1
  8.7 0.9 copy-start.2
  9.6 0.7 copy-start.4
  10.3 7.7 %copy-start.8 = (bf16[16,2048]{1,0:T(8,128)(2,1)S(1)}, bf16[16,2048]{1,0:T(8,128)(2,1)}, u32[]{:S(2)}) copy-start(bf16[16,2048]{1,0:T(8,128)(2,1)} %get-tuple-element.34) | copy-start | bytes 196612
  10.8 14.1 %copy-start.3 = (bf16[128,2048]{1,0:T(8,128)(2,1)S(1)}, bf16[128,2048]{1,0:T(8,128)(2,1)}, u32[]{:S(2)}) copy-start(bf16[128,2048]{1,0:T(8,128)(2,1)} %get-tuple-element.29.q_ref) | copy-start | bytes 1572868
  11.8 6.2 %collective-permute-start.1 = (bf16[16,2048]{1,0:T(8,128)(2,1)S(1)}, bf16[16,2048]{1,0:T(8,128)(2,1)S(1)}, u32[]{:S(2)}, u32[]{:S(2)}) collective-permute-start(bf16[16,2048]{1,0:T(8,128)(2,1)S(1)} %get-tuple-element.55), channel_id=1, source_target_pairs={{0,8},{4,12},{8,16},{12,20},{16,24},{20,28},{1,9},{5,13},{9,17},{1... | collective-permute-start | bytes 196616 | tf_op jit(solution)/shard_map/state_1/ppermute | solution.py:176
  18.0 6.9 %collective-permute-start.2 = (bf16[16,2048]{1,0:T(8,128)(2,1)S(1)}, bf16[16,2048]{1,0:T(8,128)(2,1)S(1)}, u32[]{:S(2)}, u32[]{:S(2)}) collective-permute-start(bf16[16,2048]{1,0:T(8,128)(2,1)S(1)} %add_convert_fusion), channel_id=1, source_target_pairs={{0,16},{4,20},{8,24},{12,28},{1,17},{5,21},{9,25},{13,29},{2,18},{... | collective-permute-start | bytes 196616 | tf_op jit(solution)/shard_map/state_2/ppermute | solution.py:176
  27.1 11.6 %collective-permute-start.5 = (bf16[128,2048]{1,0:T(8,128)(2,1)S(1)}, bf16[128,2048]{1,0:T(8,128)(2,1)S(1)}, u32[]{:S(2)}, u32[]{:S(2)}) collective-permute-start(bf16[128,2048]{1,0:T(8,128)(2,1)S(1)} %shard_map.77), channel_id=1, source_target_pairs={{0,4},{4,0},{8,12},{12,8},{16,20},{20,16},{24,28},{28,24},{1,5},{5... | collective-permute-start | bytes 1572872 | tf_op jit(solution)/shard_map/near_y/ppermute | solution.py:176
  27.7 13.1 %collective-permute-start.4 = (bf16[128,2048]{1,0:T(8,128)(2,1)S(1)}, bf16[128,2048]{1,0:T(8,128)(2,1)S(1)}, u32[]{:S(2)}, u32[]{:S(2)}) collective-permute-start(bf16[128,2048]{1,0:T(8,128)(2,1)S(1)} %shard_map.77), channel_id=1, source_target_pairs={{8,16},{12,20},{16,8},{20,12},{9,17},{13,21},{17,9},{21,13},{10,18... | collective-permute-start | bytes 1572872 | tf_op jit(solution)/shard_map/middle/ppermute | solution.py:176
  31.4 10.7 %collective-permute-start.3 = (bf16[128,2048]{1,0:T(8,128)(2,1)S(1)}, bf16[128,2048]{1,0:T(8,128)(2,1)S(1)}, u32[]{:S(2)}, u32[]{:S(2)}) collective-permute-start(bf16[128,2048]{1,0:T(8,128)(2,1)S(1)} %shard_map.77), channel_id=1, source_target_pairs={{0,8},{4,12},{8,0},{12,4},{16,24},{20,28},{24,16},{28,20},{1,9},{5... | collective-permute-start | bytes 1572872 | tf_op jit(solution)/shard_map/one/ppermute | solution.py:176
  31.6 15.8 %copy-start.5 = (bf16[2048,1024]{1,0:T(8,128)(2,1)S(1)}, bf16[2048,1024]{1,0:T(8,128)(2,1)}, u32[]{:S(2)}) copy-start(bf16[2048,1024]{1,0:T(8,128)(2,1)} %param.13) | copy-start | bytes 12582916
  42.1 12.5 %collective-permute-start.8 = (bf16[128,2048]{1,0:T(8,128)(2,1)S(1)}, bf16[128,2048]{1,0:T(8,128)(2,1)S(1)}, u32[]{:S(2)}, u32[]{:S(2)}) collective-permute-start(bf16[128,2048]{1,0:T(8,128)(2,1)S(1)} %collective-permute-done.3), channel_id=1, source_target_pairs={{0,4},{4,0},{8,12},{12,8},{16,20},{20,16},{24,28},{28,24},{1,5},{5... | collective-permute-start | bytes 1572872 | tf_op jit(solution)/shard_map/one_y/ppermute | solution.py:176
  43.7 12.1 %collective-permute-start.6 = (bf16[128,2048]{1,0:T(8,128)(2,1)S(1)}, bf16[128,2048]{1,0:T(8,128)(2,1)S(1)}, u32[]{:S(2)}, u32[]{:S(2)}) collective-permute-start(bf16[128,2048]{1,0:T(8,128)(2,1)S(1)} %collective-permute-done.3), channel_id=1, source_target_pairs={{8,16},{12,20},{16,8},{20,12},{9,17},{13,21},{17,9},{21,13},{10,18... | collective-permute-start | bytes 1572872 | tf_op jit(solution)/shard_map/given/ppermute | solution.py:176
  46.1 8.5 %collective-permute-start.7 = (bf16[128,2048]{1,0:T(8,128)(2,1)S(1)}, bf16[128,2048]{1,0:T(8,128)(2,1)S(1)}, u32[]{:S(2)}, u32[]{:S(2)}) collective-permute-start(bf16[128,2048]{1,0:T(8,128)(2,1)S(1)} %collective-permute-done.4), channel_id=1, source_target_pairs={{8,0},{12,4},{16,24},{20,28},{9,1},{13,5},{17,25},{21,29},{10,2},{... | collective-permute-start | bytes 1572872 | tf_op jit(solution)/shard_map/out2/ppermute | solution.py:176
  55.8 8.3 %collective-permute-start.11 = (bf16[128,1024]{1,0:T(8,128)(2,1)S(1)}, bf16[128,1024]{1,0:T(8,128)(2,1)S(1)}, u32[]{:S(2)}, u32[]{:S(2)}) collective-permute-start(bf16[128,1024]{1,0:T(8,128)(2,1)S(1)} %slice.33), channel_id=1, source_target_pairs={{8,16},{12,20},{16,8},{20,12},{9,17},{13,21},{17,9},{21,13},{10,18... | collective-permute-start | bytes 786440 | tf_op jit(solution)/shard_map/middle_y/ppermute | solution.py:176
  58.9 10.9 %collective-permute-start.9 = (bf16[128,2048]{1,0:T(8,128)(2,1)S(1)}, bf16[128,2048]{1,0:T(8,128)(2,1)S(1)}, u32[]{:S(2)}, u32[]{:S(2)}) collective-permute-start(bf16[128,2048]{1,0:T(8,128)(2,1)S(1)} %collective-permute-done.6), channel_id=1, source_target_pairs={{8,0},{12,4},{16,24},{20,28},{9,1},{13,5},{17,25},{21,29},{10,2},{... | collective-permute-start | bytes 1572872 | tf_op jit(solution)/shard_map/out3/ppermute | solution.py:176
  60.5 9.2 %collective-permute-start.10 = (bf16[128,2048]{1,0:T(8,128)(2,1)S(1)}, bf16[128,2048]{1,0:T(8,128)(2,1)S(1)}, u32[]{:S(2)}, u32[]{:S(2)}) collective-permute-start(bf16[128,2048]{1,0:T(8,128)(2,1)S(1)} %broadcast_select_fusion.1), channel_id=1, source_target_pairs={{0,4},{4,0},{8,12},{12,8},{16,20},{20,16},{24,28},{28,24},{1,5},{5... | collective-permute-start | bytes 1572872 | tf_op jit(solution)/shard_map/two_y/ppermute | solution.py:176
  61.3 10.8 %collective-permute-start.15 = (bf16[2,128,1024]{2,1,0:T(8,128)(2,1)S(1)}, bf16[2,128,1024]{2,1,0:T(8,128)(2,1)S(1)}, u32[]{:S(2)}, u32[]{:S(2)}) collective-permute-start(bf16[2,128,1024]{2,1,0:T(8,128)(2,1)S(1)} %pad_maximum_fusion.2), channel_id=1, source_target_pairs={{0,1},{1,0},{2,3},{3,2},{4,5},{5,4},{6,7},{7,6},{8,9},{9,8},{10,11... | collective-permute-start | bytes 1572872 | tf_op jit(solution)/shard_map/core_close/ppermute | solution.py:176
  70.6 4.7 %collective-permute-start.12 = (bf16[2,128,1024]{2,1,0:T(8,128)(2,1)S(1)}, bf16[2,128,1024]{2,1,0:T(8,128)(2,1)S(1)}, u32[]{:S(2)}, u32[]{:S(2)}) collective-permute-start(bf16[2,128,1024]{2,1,0:T(8,128)(2,1)S(1)} %fusion.11), channel_id=1, source_target_pairs={{1,0},{3,2},{5,4},{7,6},{9,8},{11,10},{13,12},{15,14},{17,16},{19,... | collective-permute-start | bytes 1572872 | tf_op jit(solution)/shard_map/core_far0/ppermute | solution.py:176
  72.3 9.1 %collective-permute-start.16 = (bf16[128,1024]{1,0:T(8,128)(2,1)S(1)}, bf16[128,1024]{1,0:T(8,128)(2,1)S(1)}, u32[]{:S(2)}, u32[]{:S(2)}) collective-permute-start(bf16[128,1024]{1,0:T(8,128)(2,1)S(1)} %fusion.17), channel_id=1, source_target_pairs={{0,2},{1,3},{2,0},{3,1},{4,6},{5,7},{6,4},{7,5},{8,10},{9,11},{10,... | collective-permute-start | bytes 786440 | tf_op jit(solution)/shard_map/side_close/ppermute | solution.py:176
  73.0 8.4 %collective-permute-start.14 = (bf16[128,1024]{1,0:T(8,128)(2,1)S(1)}, bf16[128,1024]{1,0:T(8,128)(2,1)S(1)}, u32[]{:S(2)}, u32[]{:S(2)}) collective-permute-start(bf16[128,1024]{1,0:T(8,128)(2,1)S(1)} %slice.37), channel_id=1, source_target_pairs={{8,0},{12,4},{16,24},{20,28},{9,1},{13,5},{17,25},{21,29},{10,2},{... | collective-permute-start | bytes 786440 | tf_op jit(solution)/shard_map/out_y/ppermute | solution.py:176
  74.7 8.9 %collective-permute-start.13 = (bf16[128,1024]{1,0:T(8,128)(2,1)S(1)}, bf16[128,1024]{1,0:T(8,128)(2,1)S(1)}, u32[]{:S(2)}, u32[]{:S(2)}) collective-permute-start(bf16[128,1024]{1,0:T(8,128)(2,1)S(1)} %slice.46), channel_id=1, source_target_pairs={{0,4},{4,0},{8,12},{12,8},{16,20},{20,16},{24,28},{28,24},{1,5},{5... | collective-permute-start | bytes 786440 | tf_op jit(solution)/shard_map/three_y/ppermute | solution.py:176
  75.5 8.9 %collective-permute-start.17 = (bf16[128,1024]{1,0:T(8,128)(2,1)S(1)}, bf16[128,1024]{1,0:T(8,128)(2,1)S(1)}, u32[]{:S(2)}, u32[]{:S(2)}) collective-permute-start(bf16[128,1024]{1,0:T(8,128)(2,1)S(1)} %fusion.18), channel_id=1, source_target_pairs={{0,2},{2,0},{4,6},{6,4},{8,10},{10,8},{12,14},{14,12},{16,18},{18,... | collective-permute-start | bytes 786440 | tf_op jit(solution)/shard_map/side_far0/ppermute | solution.py:176
  84.4 0.9 copy-start.7
  86.2 3.1 %collective-permute-start.19 = (bf16[2,128,1024]{2,1,0:T(8,128)(2,1)}, bf16[2,128,1024]{2,1,0:T(8,128)(2,1)}, u32[]{:S(2)}, u32[]{:S(2)}) collective-permute-start(bf16[2,128,1024]{2,1,0:T(8,128)(2,1)} %fusion.10), channel_id=1, source_target_pairs={{0,1},{2,3},{4,5},{6,7},{8,9},{10,11},{12,13},{14,15},{16,17},{18,... | collective-permute-start | bytes 1572872 | tf_op jit(solution)/shard_map/core_far1/ppermute | solution.py:176
  90.6 7.5 %collective-permute-start.20 = (bf16[128,1024]{1,0:T(8,128)(2,1)S(1)}, bf16[128,1024]{1,0:T(8,128)(2,1)S(1)}, u32[]{:S(2)}, u32[]{:S(2)}) collective-permute-start(bf16[128,1024]{1,0:T(8,128)(2,1)S(1)} %fusion.19), channel_id=1, source_target_pairs={{1,3},{3,1},{5,7},{7,5},{9,11},{11,9},{13,15},{15,13},{17,19},{19,... | collective-permute-start | bytes 786440 | tf_op jit(solution)/shard_map/side_far1/ppermute | solution.py:176
  92.5 16.4 %collective-permute-start.18 = (bf16[128,1024]{1,0:T(8,128)(2,1)S(1)}, bf16[128,1024]{1,0:T(8,128)(2,1)S(1)}, u32[]{:S(2)}, u32[]{:S(2)}) collective-permute-start(bf16[128,1024]{1,0:T(8,128)(2,1)S(1)} %get-tuple-element.53), channel_id=1, source_target_pairs={{0,16},{1,0},{2,24},{3,8},{4,20},{5,4},{6,28},{7,12},{8,25},{9,9},... | collective-permute-start | bytes 786440 | tf_op jit(solution)/shard_map/own_0/ppermute | solution.py:176
  98.3 13.7 %collective-permute-start.21 = (bf16[128,1024]{1,0:T(8,128)(2,1)S(1)}, bf16[128,1024]{1,0:T(8,128)(2,1)S(1)}, u32[]{:S(2)}, u32[]{:S(2)}) collective-permute-start(bf16[128,1024]{1,0:T(8,128)(2,1)S(1)} %fusion.21), channel_id=1, source_target_pairs={{0,4},{1,20},{2,12},{3,28},{4,0},{5,16},{6,8},{7,24},{8,13},{9,29}... | collective-permute-start | bytes 786440 | tf_op jit(solution)/shard_map/own_1/ppermute | solution.py:176

commit v7 on v6

--- a/solution.py
+++ b/solution.py
@@ -256,8 +256,9 @@
         return keep, moved(jnp.where(here, second, first).astype(BF16), "chan", pairs, name)
 
     def far(first, second, dy):
-        parts = jnp.stack([first, second])
-        parts = parts + moved(parts.astype(BF16), "chan", [(1 - dy, dy), (3 - dy, 2 + dy)], f"core_far{dy}").astype(F32)
+        parts = jnp.stack([first.astype(BF16), second.astype(BF16)])
+        given = moved(parts, "chan", [(1 - dy, dy), (3 - dy, 2 + dy)], f"core_far{dy}")
+        parts = (parts.astype(F32) + given.astype(F32)).astype(BF16)
         return turned(side == z // 2, parts[0], parts[1], [(dy, 2 + dy), (2 + dy, dy)], f"side_far{dy}")
 
     ready = [[matmul(x, w_out) for x in (hidden, near_y)], [matmul(x, w_out) for x in (one, one_y)]]
@@ -274,11 +275,11 @@
     far_keep, far_side = far(matmul(two, w_out), with_three, 0)
     three_y, out_y, close_side, far_side = fence(three_y, out_y, close_side, far_side)
     close_tile = (close_keep + close_side.astype(F32)).astype(BF16)
-    tile = (far_keep + far_side.astype(F32)).astype(BF16)
+    tile = (far_keep.astype(F32) + far_side.astype(F32)).astype(BF16)
     same = moved(jnp.where(core == 0, tile, close_tile), BOTH, owned(0), "own_0")
     with_three_y = matmul(three_y, w_out[:split]) + matmul(jnp.where(at_end, out_y, middle_y), w_out[split:])
     far_keep, far_side = far(matmul(two_y, w_out), with_three_y, 1)
-    tile = (far_keep + far_side.astype(F32)).astype(BF16)
+    tile = (far_keep.astype(F32) + far_side.astype(F32)).astype(BF16)
     cross = moved(jnp.where(core == 1, tile, close_tile), BOTH, owned(1), "own_1")
     low = jnp.where(y == 0, same, cross)
     high = jnp.where(y == 0, cross, same)

time: 114 us -> 111 us (0.974)
  other arithmetic: 6.32 us -> 4.49 us
    add x2 -> x0, other arithmetic: 1.32 us -> none  [far(): parts + moved(parts.astype(BF16), 'chan', [(1 - dy, dy), (3 - dy, 2 + dy)...]
where the time goes in v7:
time: 111 us
  waiting for transfers between devices  42.5 us (38%)
  starting transfers between devices  39.5 us (36%)
  Pallas kernels  11.5 us (10%)
  matrix products  8.33 us (8%)
  other arithmetic  4.49 us (4%)
  local copies, waits for them, and re-layouts  3.8 us (3%)
    ppermute x22, waiting for transfers between devices, moved(): return lax.ppermute(x, axes, pairs)  42.5 us
    ppermute x22, starting transfers between devices, moved(): return lax.ppermute(x, axes, pairs)  39.5 us
    pallas_call x5, Pallas kernels, run(): pl.pallas_call(kernel, out_shape=[jax.ShapeDtypeStruct(shape, kind) for s...  11.5 us
    dot_general x9, matrix products, matmul(): return jnp.dot(x, w, preferred_element_type=F32)  8.33 us
    unnamed x18, local copies, waits for them, and re-layouts  3.75 us
  transfers between devices with their start and end apart: 22, of which 15 were waited for; matrix products, arithmetic and copies ran while one was open for 9% of the time, Pallas kernels for 4%

profile of v7, /device:TPU:10, one launch (start us, length us, event | category | flops | bytes accessed | tf_op | source)
XLA Modules:
  0.0 110.6 jit_solution(8427541781404590194)
XLA Ops:
  0.0 4.9 %shard_map.73 = (bf16[16,2048]{1,0:T(8,128)(2,1)}, f32[16,128,128]{2,1,0:T(8,128)}, f32[16,2048]{1,0:T(8,128)}, f32[16,2048]{1,0:T(8,128)}, bf16[128,2048]{1,0:T(8,128)(2,1)}, /*index=5*/f32[1,2048]{1,0:T(1,128)}) custom-call(bf16[128,2048]{1,0:T(8,128)(2,1)} %refs_0_.1, bf16[128,2048]{1,0:T(8,128)(2,1)} %refs_1_.1, f32[16,2048]{1,0:T(8,128)} %bitcast.54, ...), custom_call_target="tpu_custom_call" | custom-call | flops 12582912 | bytes 1048576 | tf_op jit(solution)/shard_map/pallas_call | solution.py:155
  5.0 1.6 %collective-permute-start = (bf16[16,2048]{1,0:T(8,128)(2,1)}, bf16[16,2048]{1,0:T(8,128)(2,1)S(1)}, u32[]{:S(2)}, u32[]{:S(2)}) collective-permute-start(bf16[16,2048]{1,0:T(8,128)(2,1)} %get-tuple-element.34), channel_id=1, source_target_pairs={{0,4},{4,0},{8,12},{12,8},{16,20},{20,16},{24,28},{28,24},{1,5},{5... | collective-permute-start | bytes 196616 | tf_op jit(solution)/shard_map/state_y/ppermute | solution.py:176
  6.5 1.2 %copy-done = f32[16,128,128]{2,1,0:T(8,128)S(1)} copy-done((f32[16,128,128]{2,1,0:T(8,128)S(1)}, f32[16,128,128]{2,1,0:T(8,128)}, u32[]{:S(2)}) %copy-start) | copy-done | bytes 1048600
  7.8 0.9 copy-done.1
  8.7 0.9 copy-done.2
  9.6 0.7 copy-done.4
  10.9 0.9 fusion.26
  11.8 3.5 %collective-permute-start.1 = (bf16[16,2048]{1,0:T(8,128)(2,1)S(1)}, bf16[16,2048]{1,0:T(8,128)(2,1)S(1)}, u32[]{:S(2)}, u32[]{:S(2)}) collective-permute-start(bf16[16,2048]{1,0:T(8,128)(2,1)S(1)} %get-tuple-element.55), channel_id=1, source_target_pairs={{0,8},{4,12},{8,16},{12,20},{16,24},{20,28},{1,9},{5,13},{9,17},{1... | collective-permute-start | bytes 196616 | tf_op jit(solution)/shard_map/state_1/ppermute | solution.py:176
  15.3 1.9 %shard_map.75.rest_0_ = f32[16,128,128]{2,1,0:T(8,128)S(1)} custom-call(f32[16,128,128]{2,1,0:T(8,128)S(1)} %copy-done, f32[16,2048]{1,0:T(8,128)S(1)} %copy-done.1, f32[16,2048]{1,0:T(8,128)S(1)} %copy-done.2, f32[1,2048]{1,0:T(1,128)S(1)} %copy-done.4, f32[16,128,128]{2,1,0:T(8,128)S(1)} %shard_map.74.rest_0_), custom_call_target="tpu_custom_call", output_to_operand_aliasing={{}: (4, {})} | custom-call | flops 11468800 | bytes 1048576 | tf_op jit(solution)/shard_map/pallas_call | solution.py:155
  17.2 0.8 collective-permute-done.1.below_ref
  18.0 4.5 %collective-permute-start.2 = (bf16[16,2048]{1,0:T(8,128)(2,1)S(1)}, bf16[16,2048]{1,0:T(8,128)(2,1)S(1)}, u32[]{:S(2)}, u32[]{:S(2)}) collective-permute-start(bf16[16,2048]{1,0:T(8,128)(2,1)S(1)} %add_convert_fusion.2), channel_id=1, source_target_pairs={{0,16},{4,20},{8,24},{12,28},{1,17},{5,21},{9,25},{13,29},{2,18},{... | collective-permute-start | bytes 196616 | tf_op jit(solution)/shard_map/state_2/ppermute | solution.py:176
  22.5 1.9 %shard_map.76.base_ref = f32[16,128,128]{2,1,0:T(8,128)S(1)} custom-call(f32[16,128,128]{2,1,0:T(8,128)S(1)} %copy-done, f32[16,2048]{1,0:T(8,128)S(1)} %copy-done.1, f32[16,2048]{1,0:T(8,128)S(1)} %copy-done.2, f32[1,2048]{1,0:T(1,128)S(1)} %copy-done.4, f32[16,128,128]{2,1,0:T(8,128)S(1)} %shard_map.75.rest_0_), custom_call_target="tpu_custom_call", output_to_operand_aliasing={{}: (4, {})} | custom-call | flops 11468800 | bytes 1048576 | tf_op jit(solution)/shard_map/pallas_call | solution.py:155
  24.9 2.2 %shard_map.77 = bf16[128,2048]{1,0:T(8,128)(2,1)S(1)} custom-call(s32[1]{0:T(128)} %bitcast.odd_ref, bf16[128,2048]{1,0:T(8,128)(2,1)S(1)} %copy-done.3, f32[16,128,128]{2,1,0:T(8,128)S(1)} %shard_map.76.base_ref, bf16[16,2048]{1,0:T(8,128)(2,1)S(1)} %collective-permute-done.1.below_ref, bf16[16,2048]{1,0:T(8,128)(2,1)S(1)} %collective-permute-done.2.further_ref, ...), custom_call_target="tpu_custom_call" | custom-call | flops 8388608 | bytes 1048576 | tf_op jit(solution)/shard_map/pallas_call | solution.py:155
  27.7 3.7 %collective-permute-start.4 = (bf16[128,2048]{1,0:T(8,128)(2,1)S(1)}, bf16[128,2048]{1,0:T(8,128)(2,1)S(1)}, u32[]{:S(2)}, u32[]{:S(2)}) collective-permute-start(bf16[128,2048]{1,0:T(8,128)(2,1)S(1)} %shard_map.77), channel_id=1, source_target_pairs={{8,16},{12,20},{16,8},{20,12},{9,17},{13,21},{17,9},{21,13},{10,18... | collective-permute-start | bytes 1572872 | tf_op jit(solution)/shard_map/middle/ppermute | solution.py:176
  31.6 3.0 %fusion.29 = f32[128,1024]{1,0:T(8,128)S(1)} fusion(bf16[128,2048]{1,0:T(8,128)(2,1)S(1)} %shard_map.77, bf16[2048,1024]{1,0:T(8,128)(2,1)} %param.13), kind=kOutput, calls=%fused_computation.50 | convolution fusion | flops 536870912 | bytes 5242880 | tf_op jit(solution)/shard_map/dot_general | solution.py:171
  34.7 4.0 %collective-permute-done.5 = bf16[128,2048]{1,0:T(8,128)(2,1)S(1)} collective-permute-done((bf16[128,2048]{1,0:T(8,128)(2,1)S(1)}, bf16[128,2048]{1,0:T(8,128)(2,1)S(1)}, u32[]{:S(2)}, u32[]{:S(2)}) %collective-permute-start.5) | collective-permute-done | bytes 524320 | tf_op jit(solution)/shard_map/near_y/ppermute | solution.py:176
  38.7 2.1 %collective-permute-done.4 = bf16[128,2048]{1,0:T(8,128)(2,1)S(1)} collective-permute-done((bf16[128,2048]{1,0:T(8,128)(2,1)S(1)}, bf16[128,2048]{1,0:T(8,128)(2,1)S(1)}, u32[]{:S(2)}, u32[]{:S(2)}) %collective-permute-start.4) | collective-permute-done | bytes 524320 | tf_op jit(solution)/shard_map/middle/ppermute | solution.py:176
  40.8 1.3 %collective-permute-done.3 = bf16[128,2048]{1,0:T(8,128)(2,1)S(1)} collective-permute-done((bf16[128,2048]{1,0:T(8,128)(2,1)S(1)}, bf16[128,2048]{1,0:T(8,128)(2,1)S(1)}, u32[]{:S(2)}, u32[]{:S(2)}) %collective-permute-start.3) | collective-permute-done | bytes 524320 | tf_op jit(solution)/shard_map/one/ppermute | solution.py:176
  42.1 1.5 %collective-permute-start.8 = (bf16[128,2048]{1,0:T(8,128)(2,1)S(1)}, bf16[128,2048]{1,0:T(8,128)(2,1)S(1)}, u32[]{:S(2)}, u32[]{:S(2)}) collective-permute-start(bf16[128,2048]{1,0:T(8,128)(2,1)S(1)} %collective-permute-done.3), channel_id=1, source_target_pairs={{0,4},{4,0},{8,12},{12,8},{16,20},{20,16},{24,28},{28,24},{1,5},{5... | collective-permute-start | bytes 1572872 | tf_op jit(solution)/shard_map/one_y/ppermute | solution.py:176
  43.7 2.4 %collective-permute-start.6 = (bf16[128,2048]{1,0:T(8,128)(2,1)S(1)}, bf16[128,2048]{1,0:T(8,128)(2,1)S(1)}, u32[]{:S(2)}, u32[]{:S(2)}) collective-permute-start(bf16[128,2048]{1,0:T(8,128)(2,1)S(1)} %collective-permute-done.3), channel_id=1, source_target_pairs={{8,16},{12,20},{16,8},{20,12},{9,17},{13,21},{17,9},{21,13},{10,18... | collective-permute-start | bytes 1572872 | tf_op jit(solution)/shard_map/given/ppermute | solution.py:176
  46.1 1.3 %collective-permute-start.7 = (bf16[128,2048]{1,0:T(8,128)(2,1)S(1)}, bf16[128,2048]{1,0:T(8,128)(2,1)S(1)}, u32[]{:S(2)}, u32[]{:S(2)}) collective-permute-start(bf16[128,2048]{1,0:T(8,128)(2,1)S(1)} %collective-permute-done.4), channel_id=1, source_target_pairs={{8,0},{12,4},{16,24},{20,28},{9,1},{13,5},{17,25},{21,29},{10,2},{... | collective-permute-start | bytes 1572872 | tf_op jit(solution)/shard_map/out2/ppermute | solution.py:176
  47.4 0.7 fusion.28
  48.2 0.7 fusion.31
  48.9 5.7 %collective-permute-done.7 = bf16[128,2048]{1,0:T(8,128)(2,1)S(1)} collective-permute-done((bf16[128,2048]{1,0:T(8,128)(2,1)S(1)}, bf16[128,2048]{1,0:T(8,128)(2,1)S(1)}, u32[]{:S(2)}, u32[]{:S(2)}) %collective-permute-start.7) | collective-permute-done | bytes 524320 | tf_op jit(solution)/shard_map/out2/ppermute | solution.py:176
  54.6 1.1 %collective-permute-done.6 = bf16[128,2048]{1,0:T(8,128)(2,1)S(1)} collective-permute-done((bf16[128,2048]{1,0:T(8,128)(2,1)S(1)}, bf16[128,2048]{1,0:T(8,128)(2,1)S(1)}, u32[]{:S(2)}, u32[]{:S(2)}) %collective-permute-start.6) | collective-permute-done | bytes 524320 | tf_op jit(solution)/shard_map/given/ppermute | solution.py:176
  55.8 2.4 %collective-permute-start.11 = (bf16[128,1024]{1,0:T(8,128)(2,1)S(1)}, bf16[128,1024]{1,0:T(8,128)(2,1)S(1)}, u32[]{:S(2)}, u32[]{:S(2)}) collective-permute-start(bf16[128,1024]{1,0:T(8,128)(2,1)S(1)} %slice.33), channel_id=1, source_target_pairs={{8,16},{12,20},{16,8},{20,12},{9,17},{13,21},{17,9},{21,13},{10,18... | collective-permute-start | bytes 786440 | tf_op jit(solution)/shard_map/middle_y/ppermute | solution.py:176
  58.1 0.7 fusion.30
  58.9 1.6 %collective-permute-start.9 = (bf16[128,2048]{1,0:T(8,128)(2,1)S(1)}, bf16[128,2048]{1,0:T(8,128)(2,1)S(1)}, u32[]{:S(2)}, u32[]{:S(2)}) collective-permute-start(bf16[128,2048]{1,0:T(8,128)(2,1)S(1)} %collective-permute-done.6), channel_id=1, source_target_pairs={{8,0},{12,4},{16,24},{20,28},{9,1},{13,5},{17,25},{21,29},{10,2},{... | collective-permute-start | bytes 1572872 | tf_op jit(solution)/shard_map/out3/ppermute | solution.py:176
  61.4 0.7 fusion.10
  62.1 1.9 %collective-permute-done.11 = bf16[128,1024]{1,0:T(8,128)(2,1)S(1)} collective-permute-done((bf16[128,1024]{1,0:T(8,128)(2,1)S(1)}, bf16[128,1024]{1,0:T(8,128)(2,1)S(1)}, u32[]{:S(2)}, u32[]{:S(2)}) %collective-permute-start.11) | collective-permute-done | bytes 262176 | tf_op jit(solution)/shard_map/middle_y/ppermute | solution.py:176
  64.0 5.7 %collective-permute-done.10 = bf16[128,2048]{1,0:T(8,128)(2,1)S(1)} collective-permute-done((bf16[128,2048]{1,0:T(8,128)(2,1)S(1)}, bf16[128,2048]{1,0:T(8,128)(2,1)S(1)}, u32[]{:S(2)}, u32[]{:S(2)}) %collective-permute-start.10) | collective-permute-done | bytes 524320 | tf_op jit(solution)/shard_map/two_y/ppermute | solution.py:176
  69.8 0.7 fusion.11
  70.6 1.3 %collective-permute-start.12 = (bf16[2,128,1024]{2,1,0:T(8,128)(2,1)S(1)}, bf16[2,128,1024]{2,1,0:T(8,128)(2,1)S(1)}, u32[]{:S(2)}, u32[]{:S(2)}) collective-permute-start(bf16[2,128,1024]{2,1,0:T(8,128)(2,1)S(1)} %pad_maximum_fusion), channel_id=1, source_target_pairs={{1,0},{3,2},{5,4},{7,6},{9,8},{11,10},{13,12},{15,14},{17,16},{19,... | collective-permute-start | bytes 1572872 | tf_op jit(solution)/shard_map/core_far0/ppermute | solution.py:176
  72.3 0.6 collective-permute-start.16
  73.0 1.7 %collective-permute-start.14 = (bf16[128,1024]{1,0:T(8,128)(2,1)S(1)}, bf16[128,1024]{1,0:T(8,128)(2,1)S(1)}, u32[]{:S(2)}, u32[]{:S(2)}) collective-permute-start(bf16[128,1024]{1,0:T(8,128)(2,1)S(1)} %slice.37), channel_id=1, source_target_pairs={{8,0},{12,4},{16,24},{20,28},{9,1},{13,5},{17,25},{21,29},{10,2},{... | collective-permute-start | bytes 786440 | tf_op jit(solution)/shard_map/out_y/ppermute | solution.py:176
  75.5 3.4 %collective-permute-start.17 = (bf16[128,1024]{1,0:T(8,128)(2,1)S(1)}, bf16[128,1024]{1,0:T(8,128)(2,1)S(1)}, u32[]{:S(2)}, u32[]{:S(2)}) collective-permute-start(bf16[128,1024]{1,0:T(8,128)(2,1)S(1)} %select_bitcast_fusion.3), channel_id=1, source_target_pairs={{0,2},{2,0},{4,6},{6,4},{8,10},{10,8},{12,14},{14,12},{16,18},{18,... | collective-permute-start | bytes 786440 | tf_op jit(solution)/shard_map/side_far0/ppermute | solution.py:176
  78.9 0.7 fusion.12
  79.7 1.7 %collective-permute-done.16 = bf16[128,1024]{1,0:T(8,128)(2,1)S(1)} collective-permute-done((bf16[128,1024]{1,0:T(8,128)(2,1)S(1)}, bf16[128,1024]{1,0:T(8,128)(2,1)S(1)}, u32[]{:S(2)}, u32[]{:S(2)}) %collective-permute-start.16) | collective-permute-done | bytes 262176 | tf_op jit(solution)/shard_map/side_close/ppermute | solution.py:176
  81.4 2.2 %collective-permute-done.13 = bf16[128,1024]{1,0:T(8,128)(2,1)S(1)} collective-permute-done((bf16[128,1024]{1,0:T(8,128)(2,1)S(1)}, bf16[128,1024]{1,0:T(8,128)(2,1)S(1)}, u32[]{:S(2)}, u32[]{:S(2)}) %collective-permute-start.13) | collective-permute-done | bytes 262176 | tf_op jit(solution)/shard_map/three_y/ppermute | solution.py:176
  83.6 0.8 collective-permute-done.17
  85.4 1.3 %collective-permute-start.19 = (bf16[2,128,1024]{2,1,0:T(8,128)(2,1)S(1)}, bf16[2,128,1024]{2,1,0:T(8,128)(2,1)S(1)}, u32[]{:S(2)}, u32[]{:S(2)}) collective-permute-start(bf16[2,128,1024]{2,1,0:T(8,128)(2,1)S(1)} %pad_maximum_fusion.2), channel_id=1, source_target_pairs={{0,1},{2,3},{4,5},{6,7},{8,9},{10,11},{12,13},{14,15},{16,17},{18,... | collective-permute-start | bytes 1572872 | tf_op jit(solution)/shard_map/core_far1/ppermute | solution.py:176
  86.7 1.5 %collective-permute-done.19 = bf16[2,128,1024]{2,1,0:T(8,128)(2,1)S(1)} collective-permute-done((bf16[2,128,1024]{2,1,0:T(8,128)(2,1)S(1)}, bf16[2,128,1024]{2,1,0:T(8,128)(2,1)S(1)}, u32[]{:S(2)}, u32[]{:S(2)}) %collective-permute-start.19) | collective-permute-done | bytes 524320 | tf_op jit(solution)/shard_map/core_far1/ppermute | solution.py:176
  88.4 0.7 collective-permute-start.20
  89.1 1.2 %fusion.22 = (bf16[128,1024]{1,0:T(8,128)(2,1)S(1)}, bf16[128,1024]{1,0:T(8,128)(2,1)S(1)}) fusion(bf16[128,1024]{1,0:T(8,128)(2,1)} %copy-done.8, pred[]{:T(512)S(6)} %eq.32, pred[]{:T(512)S(6)} %eq.31, bf16[2,128,1024]{2,1,0:T(8,128)(2,1)S(1)} %add_convert_fusion.1, bf16[128,1024]{1,0:T(8,128)(2,1)S(1)} %collective-permute-done.16, ...), kind=kLoop, calls=%fused_computation.36 | loop fusion | flops 1310720 | bytes 2621443 | tf_op jit(solution)/shard_map/jit(_where)/select_n | solution.py:279
  90.3 5.6 %collective-permute-start.18 = (bf16[128,1024]{1,0:T(8,128)(2,1)S(1)}, bf16[128,1024]{1,0:T(8,128)(2,1)S(1)}, u32[]{:S(2)}, u32[]{:S(2)}) collective-permute-start(bf16[128,1024]{1,0:T(8,128)(2,1)S(1)} %get-tuple-element.53), channel_id=1, source_target_pairs={{0,16},{1,0},{2,24},{3,8},{4,20},{5,4},{6,28},{7,12},{8,25},{9,9},... | collective-permute-start | bytes 786440 | tf_op jit(solution)/shard_map/own_0/ppermute | solution.py:176
  96.6 10.0 %collective-permute-done.18 = bf16[128,1024]{1,0:T(8,128)(2,1)S(1)} collective-permute-done((bf16[128,1024]{1,0:T(8,128)(2,1)S(1)}, bf16[128,1024]{1,0:T(8,128)(2,1)S(1)}, u32[]{:S(2)}, u32[]{:S(2)}) %collective-permute-start.18) | collective-permute-done | bytes 262176 | tf_op jit(solution)/shard_map/own_0/ppermute | solution.py:176
  106.7 3.1 %collective-permute-done.21 = bf16[128,1024]{1,0:T(8,128)(2,1)S(1)} collective-permute-done((bf16[128,1024]{1,0:T(8,128)(2,1)S(1)}, bf16[128,1024]{1,0:T(8,128)(2,1)S(1)}, u32[]{:S(2)}, u32[]{:S(2)}) %collective-permute-start.21) | collective-permute-done | bytes 262176 | tf_op jit(solution)/shard_map/own_1/ppermute | solution.py:176
  109.8 0.8 pad_maximum_fusion.3
  (50 shorter events, 5.9 us)
Async XLA Ops:
  0.0 10.8 %copy-start.6 = (f32[2048,16]{0,1:T(8,128)S(1)}, f32[2048,16]{0,1:T(8,128)}, u32[]{:S(2)}) copy-start(f32[2048,16]{0,1:T(8,128)} %param.11) | copy-start | bytes 393220
  5.0 5.9 %collective-permute-start = (bf16[16,2048]{1,0:T(8,128)(2,1)}, bf16[16,2048]{1,0:T(8,128)(2,1)S(1)}, u32[]{:S(2)}, u32[]{:S(2)}) collective-permute-start(bf16[16,2048]{1,0:T(8,128)(2,1)} %get-tuple-element.34), channel_id=1, source_target_pairs={{0,4},{4,0},{8,12},{12,8},{16,20},{20,16},{24,28},{28,24},{1,5},{5... | collective-permute-start | bytes 196616 | tf_op jit(solution)/shard_map/state_y/ppermute | solution.py:176
  6.5 1.2 %copy-start = (f32[16,128,128]{2,1,0:T(8,128)S(1)}, f32[16,128,128]{2,1,0:T(8,128)}, u32[]{:S(2)}) copy-start(f32[16,128,128]{2,1,0:T(8,128)} %get-tuple-element.30.x_ref) | copy-start | bytes 3145732
  7.8 0.9 copy-start.1
  8.7 0.9 copy-start.2
  9.6 0.7 copy-start.4
  10.3 7.7 %copy-start.7 = (bf16[16,2048]{1,0:T(8,128)(2,1)S(1)}, bf16[16,2048]{1,0:T(8,128)(2,1)}, u32[]{:S(2)}) copy-start(bf16[16,2048]{1,0:T(8,128)(2,1)} %get-tuple-element.34) | copy-start | bytes 196612
  10.8 14.1 %copy-start.3 = (bf16[128,2048]{1,0:T(8,128)(2,1)S(1)}, bf16[128,2048]{1,0:T(8,128)(2,1)}, u32[]{:S(2)}) copy-start(bf16[128,2048]{1,0:T(8,128)(2,1)} %get-tuple-element.29.q_ref) | copy-start | bytes 1572868
  11.8 6.2 %collective-permute-start.1 = (bf16[16,2048]{1,0:T(8,128)(2,1)S(1)}, bf16[16,2048]{1,0:T(8,128)(2,1)S(1)}, u32[]{:S(2)}, u32[]{:S(2)}) collective-permute-start(bf16[16,2048]{1,0:T(8,128)(2,1)S(1)} %get-tuple-element.55), channel_id=1, source_target_pairs={{0,8},{4,12},{8,16},{12,20},{16,24},{20,28},{1,9},{5,13},{9,17},{1... | collective-permute-start | bytes 196616 | tf_op jit(solution)/shard_map/state_1/ppermute | solution.py:176
  18.0 6.9 %collective-permute-start.2 = (bf16[16,2048]{1,0:T(8,128)(2,1)S(1)}, bf16[16,2048]{1,0:T(8,128)(2,1)S(1)}, u32[]{:S(2)}, u32[]{:S(2)}) collective-permute-start(bf16[16,2048]{1,0:T(8,128)(2,1)S(1)} %add_convert_fusion.2), channel_id=1, source_target_pairs={{0,16},{4,20},{8,24},{12,28},{1,17},{5,21},{9,25},{13,29},{2,18},{... | collective-permute-start | bytes 196616 | tf_op jit(solution)/shard_map/state_2/ppermute | solution.py:176
  27.1 11.6 %collective-permute-start.5 = (bf16[128,2048]{1,0:T(8,128)(2,1)S(1)}, bf16[128,2048]{1,0:T(8,128)(2,1)S(1)}, u32[]{:S(2)}, u32[]{:S(2)}) collective-permute-start(bf16[128,2048]{1,0:T(8,128)(2,1)S(1)} %shard_map.77), channel_id=1, source_target_pairs={{0,4},{4,0},{8,12},{12,8},{16,20},{20,16},{24,28},{28,24},{1,5},{5... | collective-permute-start | bytes 1572872 | tf_op jit(solution)/shard_map/near_y/ppermute | solution.py:176
  27.7 13.1 %collective-permute-start.4 = (bf16[128,2048]{1,0:T(8,128)(2,1)S(1)}, bf16[128,2048]{1,0:T(8,128)(2,1)S(1)}, u32[]{:S(2)}, u32[]{:S(2)}) collective-permute-start(bf16[128,2048]{1,0:T(8,128)(2,1)S(1)} %shard_map.77), channel_id=1, source_target_pairs={{8,16},{12,20},{16,8},{20,12},{9,17},{13,21},{17,9},{21,13},{10,18... | collective-permute-start | bytes 1572872 | tf_op jit(solution)/shard_map/middle/ppermute | solution.py:176
  31.4 10.7 %collective-permute-start.3 = (bf16[128,2048]{1,0:T(8,128)(2,1)S(1)}, bf16[128,2048]{1,0:T(8,128)(2,1)S(1)}, u32[]{:S(2)}, u32[]{:S(2)}) collective-permute-start(bf16[128,2048]{1,0:T(8,128)(2,1)S(1)} %shard_map.77), channel_id=1, source_target_pairs={{0,8},{4,12},{8,0},{12,4},{16,24},{20,28},{24,16},{28,20},{1,9},{5... | collective-permute-start | bytes 1572872 | tf_op jit(solution)/shard_map/one/ppermute | solution.py:176
  31.6 15.8 %copy-start.5 = (bf16[2048,1024]{1,0:T(8,128)(2,1)S(1)}, bf16[2048,1024]{1,0:T(8,128)(2,1)}, u32[]{:S(2)}) copy-start(bf16[2048,1024]{1,0:T(8,128)(2,1)} %param.13) | copy-start | bytes 12582916
  42.1 12.5 %collective-permute-start.8 = (bf16[128,2048]{1,0:T(8,128)(2,1)S(1)}, bf16[128,2048]{1,0:T(8,128)(2,1)S(1)}, u32[]{:S(2)}, u32[]{:S(2)}) collective-permute-start(bf16[128,2048]{1,0:T(8,128)(2,1)S(1)} %collective-permute-done.3), channel_id=1, source_target_pairs={{0,4},{4,0},{8,12},{12,8},{16,20},{20,16},{24,28},{28,24},{1,5},{5... | collective-permute-start | bytes 1572872 | tf_op jit(solution)/shard_map/one_y/ppermute | solution.py:176
  43.7 12.1 %collective-permute-start.6 = (bf16[128,2048]{1,0:T(8,128)(2,1)S(1)}, bf16[128,2048]{1,0:T(8,128)(2,1)S(1)}, u32[]{:S(2)}, u32[]{:S(2)}) collective-permute-start(bf16[128,2048]{1,0:T(8,128)(2,1)S(1)} %collective-permute-done.3), channel_id=1, source_target_pairs={{8,16},{12,20},{16,8},{20,12},{9,17},{13,21},{17,9},{21,13},{10,18... | collective-permute-start | bytes 1572872 | tf_op jit(solution)/shard_map/given/ppermute | solution.py:176
  46.1 8.5 %collective-permute-start.7 = (bf16[128,2048]{1,0:T(8,128)(2,1)S(1)}, bf16[128,2048]{1,0:T(8,128)(2,1)S(1)}, u32[]{:S(2)}, u32[]{:S(2)}) collective-permute-start(bf16[128,2048]{1,0:T(8,128)(2,1)S(1)} %collective-permute-done.4), channel_id=1, source_target_pairs={{8,0},{12,4},{16,24},{20,28},{9,1},{13,5},{17,25},{21,29},{10,2},{... | collective-permute-start | bytes 1572872 | tf_op jit(solution)/shard_map/out2/ppermute | solution.py:176
  55.8 8.3 %collective-permute-start.11 = (bf16[128,1024]{1,0:T(8,128)(2,1)S(1)}, bf16[128,1024]{1,0:T(8,128)(2,1)S(1)}, u32[]{:S(2)}, u32[]{:S(2)}) collective-permute-start(bf16[128,1024]{1,0:T(8,128)(2,1)S(1)} %slice.33), channel_id=1, source_target_pairs={{8,16},{12,20},{16,8},{20,12},{9,17},{13,21},{17,9},{21,13},{10,18... | collective-permute-start | bytes 786440 | tf_op jit(solution)/shard_map/middle_y/ppermute | solution.py:176
  58.9 10.9 %collective-permute-start.9 = (bf16[128,2048]{1,0:T(8,128)(2,1)S(1)}, bf16[128,2048]{1,0:T(8,128)(2,1)S(1)}, u32[]{:S(2)}, u32[]{:S(2)}) collective-permute-start(bf16[128,2048]{1,0:T(8,128)(2,1)S(1)} %collective-permute-done.6), channel_id=1, source_target_pairs={{8,0},{12,4},{16,24},{20,28},{9,1},{13,5},{17,25},{21,29},{10,2},{... | collective-permute-start | bytes 1572872 | tf_op jit(solution)/shard_map/out3/ppermute | solution.py:176
  60.5 9.2 %collective-permute-start.10 = (bf16[128,2048]{1,0:T(8,128)(2,1)S(1)}, bf16[128,2048]{1,0:T(8,128)(2,1)S(1)}, u32[]{:S(2)}, u32[]{:S(2)}) collective-permute-start(bf16[128,2048]{1,0:T(8,128)(2,1)S(1)} %broadcast_select_fusion.1), channel_id=1, source_target_pairs={{0,4},{4,0},{8,12},{12,8},{16,20},{20,16},{24,28},{28,24},{1,5},{5... | collective-permute-start | bytes 1572872 | tf_op jit(solution)/shard_map/two_y/ppermute | solution.py:176
  61.3 10.8 %collective-permute-start.15 = (bf16[2,128,1024]{2,1,0:T(8,128)(2,1)S(1)}, bf16[2,128,1024]{2,1,0:T(8,128)(2,1)S(1)}, u32[]{:S(2)}, u32[]{:S(2)}) collective-permute-start(bf16[2,128,1024]{2,1,0:T(8,128)(2,1)S(1)} %pad_maximum_fusion.1), channel_id=1, source_target_pairs={{0,1},{1,0},{2,3},{3,2},{4,5},{5,4},{6,7},{7,6},{8,9},{9,8},{10,11... | collective-permute-start | bytes 1572872 | tf_op jit(solution)/shard_map/core_close/ppermute | solution.py:176
  70.6 4.7 %collective-permute-start.12 = (bf16[2,128,1024]{2,1,0:T(8,128)(2,1)S(1)}, bf16[2,128,1024]{2,1,0:T(8,128)(2,1)S(1)}, u32[]{:S(2)}, u32[]{:S(2)}) collective-permute-start(bf16[2,128,1024]{2,1,0:T(8,128)(2,1)S(1)} %pad_maximum_fusion), channel_id=1, source_target_pairs={{1,0},{3,2},{5,4},{7,6},{9,8},{11,10},{13,12},{15,14},{17,16},{19,... | collective-permute-start | bytes 1572872 | tf_op jit(solution)/shard_map/core_far0/ppermute | solution.py:176
  72.3 9.1 %collective-permute-start.16 = (bf16[128,1024]{1,0:T(8,128)(2,1)S(1)}, bf16[128,1024]{1,0:T(8,128)(2,1)S(1)}, u32[]{:S(2)}, u32[]{:S(2)}) collective-permute-start(bf16[128,1024]{1,0:T(8,128)(2,1)S(1)} %fusion.21), channel_id=1, source_target_pairs={{0,2},{1,3},{2,0},{3,1},{4,6},{5,7},{6,4},{7,5},{8,10},{9,11},{10,... | collective-permute-start | bytes 786440 | tf_op jit(solution)/shard_map/side_close/ppermute | solution.py:176
  73.0 8.4 %collective-permute-start.14 = (bf16[128,1024]{1,0:T(8,128)(2,1)S(1)}, bf16[128,1024]{1,0:T(8,128)(2,1)S(1)}, u32[]{:S(2)}, u32[]{:S(2)}) collective-permute-start(bf16[128,1024]{1,0:T(8,128)(2,1)S(1)} %slice.37), channel_id=1, source_target_pairs={{8,0},{12,4},{16,24},{20,28},{9,1},{13,5},{17,25},{21,29},{10,2},{... | collective-permute-start | bytes 786440 | tf_op jit(solution)/shard_map/out_y/ppermute | solution.py:176
  74.7 8.9 %collective-permute-start.13 = (bf16[128,1024]{1,0:T(8,128)(2,1)S(1)}, bf16[128,1024]{1,0:T(8,128)(2,1)S(1)}, u32[]{:S(2)}, u32[]{:S(2)}) collective-permute-start(bf16[128,1024]{1,0:T(8,128)(2,1)S(1)} %slice.46), channel_id=1, source_target_pairs={{0,4},{4,0},{8,12},{12,8},{16,20},{20,16},{24,28},{28,24},{1,5},{5... | collective-permute-start | bytes 786440 | tf_op jit(solution)/shard_map/three_y/ppermute | solution.py:176
  75.5 8.9 %collective-permute-start.17 = (bf16[128,1024]{1,0:T(8,128)(2,1)S(1)}, bf16[128,1024]{1,0:T(8,128)(2,1)S(1)}, u32[]{:S(2)}, u32[]{:S(2)}) collective-permute-start(bf16[128,1024]{1,0:T(8,128)(2,1)S(1)} %select_bitcast_fusion.3), channel_id=1, source_target_pairs={{0,2},{2,0},{4,6},{6,4},{8,10},{10,8},{12,14},{14,12},{16,18},{18,... | collective-permute-start | bytes 786440 | tf_op jit(solution)/shard_map/side_far0/ppermute | solution.py:176
  84.4 0.9 copy-start.8
  85.4 2.8 %collective-permute-start.19 = (bf16[2,128,1024]{2,1,0:T(8,128)(2,1)S(1)}, bf16[2,128,1024]{2,1,0:T(8,128)(2,1)S(1)}, u32[]{:S(2)}, u32[]{:S(2)}) collective-permute-start(bf16[2,128,1024]{2,1,0:T(8,128)(2,1)S(1)} %pad_maximum_fusion.2), channel_id=1, source_target_pairs={{0,1},{2,3},{4,5},{6,7},{8,9},{10,11},{12,13},{14,15},{16,17},{18,... | collective-permute-start | bytes 1572872 | tf_op jit(solution)/shard_map/core_far1/ppermute | solution.py:176
  88.4 7.5 %collective-permute-start.20 = (bf16[128,1024]{1,0:T(8,128)(2,1)S(1)}, bf16[128,1024]{1,0:T(8,128)(2,1)S(1)}, u32[]{:S(2)}, u32[]{:S(2)}) collective-permute-start(bf16[128,1024]{1,0:T(8,128)(2,1)S(1)} %select_bitcast_fusion.2), channel_id=1, source_target_pairs={{1,3},{3,1},{5,7},{7,5},{9,11},{11,9},{13,15},{15,13},{17,19},{19,... | collective-permute-start | bytes 786440 | tf_op jit(solution)/shard_map/side_far1/ppermute | solution.py:176
  90.3 16.4 %collective-permute-start.18 = (bf16[128,1024]{1,0:T(8,128)(2,1)S(1)}, bf16[128,1024]{1,0:T(8,128)(2,1)S(1)}, u32[]{:S(2)}, u32[]{:S(2)}) collective-permute-start(bf16[128,1024]{1,0:T(8,128)(2,1)S(1)} %get-tuple-element.53), channel_id=1, source_target_pairs={{0,16},{1,0},{2,24},{3,8},{4,20},{5,4},{6,28},{7,12},{8,25},{9,9},... | collective-permute-start | bytes 786440 | tf_op jit(solution)/shard_map/own_0/ppermute | solution.py:176
  96.1 13.6 %collective-permute-start.21 = (bf16[128,1024]{1,0:T(8,128)(2,1)S(1)}, bf16[128,1024]{1,0:T(8,128)(2,1)S(1)}, u32[]{:S(2)}, u32[]{:S(2)}) collective-permute-start(bf16[128,1024]{1,0:T(8,128)(2,1)S(1)} %fusion.23), channel_id=1, source_target_pairs={{0,4},{1,20},{2,12},{3,28},{4,0},{5,16},{6,8},{7,24},{8,13},{9,29}... | collective-permute-start | bytes 786440 | tf_op jit(solution)/shard_map/own_1/ppermute | solution.py:176

commit v8 on v7

--- a/solution.py
+++ b/solution.py
@@ -273,10 +273,11 @@
     out_y = along(two_y[:, split:], outward, "out_y")
     with_three = matmul(three, w_out)
     far_keep, far_side = far(matmul(two, w_out), with_three, 0)
-    three_y, out_y, close_side, far_side = fence(three_y, out_y, close_side, far_side)
     close_tile = (close_keep + close_side.astype(F32)).astype(BF16)
     tile = (far_keep.astype(F32) + far_side.astype(F32)).astype(BF16)
-    same = moved(jnp.where(core == 0, tile, close_tile), BOTH, owned(0), "own_0")
+    mixed = jnp.where(core == 0, tile, close_tile)
+    three_y, out_y, mixed, close_tile = fence(three_y, out_y, mixed, close_tile)
+    same = moved(mixed, BOTH, owned(0), "own_0")
     with_three_y = matmul(three_y, w_out[:split]) + matmul(jnp.where(at_end, out_y, middle_y), w_out[split:])
     far_keep, far_side = far(matmul(two_y, w_out), with_three_y, 1)
     tile = (far_keep.astype(F32) + far_side.astype(F32)).astype(BF16)

time: 111 us -> 111 us (level)
    ppermute x22, waiting for transfers between devices: 42.5 us -> 41.4 us  [moved(): return lax.ppermute(x, axes, pairs)]
    unnamed x18 -> x16, local copies, waits for them, and re-layouts: 3.75 us -> 3.75 us
  transfers between devices with their start and end apart: 22 -> 22, of which waited for: 15 -> 14; matrix products, arithmetic and copies ran while one was open for 9% -> 8% of each run, Pallas kernels for 4% -> 4%
where the time goes in v8:
time: 111 us; the launch traced here: 110 us
  waiting for transfers between devices  41.4 us (37%)
  starting transfers between devices  40.4 us (36%)
  Pallas kernels  11.5 us (10%)
  matrix products  8.36 us (8%)
  local copies, waits for them, and re-layouts  3.8 us (3%)
  other arithmetic  3.54 us (3%)
    ppermute x22, waiting for transfers between devices, moved(): return lax.ppermute(x, axes, pairs)  41.4 us
    ppermute x22, starting transfers between devices, moved(): return lax.ppermute(x, axes, pairs)  40.4 us
    pallas_call x5, Pallas kernels, run(): pl.pallas_call(kernel, out_shape=[jax.ShapeDtypeStruct(shape, kind) for s...  11.5 us
    dot_general x9, matrix products, matmul(): return jnp.dot(x, w, preferred_element_type=F32)  8.36 us
    unnamed x16, local copies, waits for them, and re-layouts  3.75 us
  transfers between devices with their start and end apart: 22, of which 14 were waited for; matrix products, arithmetic and copies ran while one was open for 8% of the time, Pallas kernels for 4%

profile of v8, /device:TPU:10, one launch (start us, length us, event | category | flops | bytes accessed | tf_op | source)
XLA Modules:
  0.0 109.5 jit_solution(15124887935657885892)
XLA Ops:
  0.0 4.9 %shard_map.73 = (bf16[16,2048]{1,0:T(8,128)(2,1)}, f32[16,128,128]{2,1,0:T(8,128)}, f32[16,2048]{1,0:T(8,128)}, f32[16,2048]{1,0:T(8,128)}, bf16[128,2048]{1,0:T(8,128)(2,1)}, /*index=5*/f32[1,2048]{1,0:T(1,128)}) custom-call(bf16[128,2048]{1,0:T(8,128)(2,1)} %refs_0_.1, bf16[128,2048]{1,0:T(8,128)(2,1)} %refs_1_.1, f32[16,2048]{1,0:T(8,128)} %bitcast.54, ...), custom_call_target="tpu_custom_call" | custom-call | flops 12582912 | bytes 1048576 | tf_op jit(solution)/shard_map/pallas_call | solution.py:155
  5.0 1.6 %collective-permute-start = (bf16[16,2048]{1,0:T(8,128)(2,1)}, bf16[16,2048]{1,0:T(8,128)(2,1)S(1)}, u32[]{:S(2)}, u32[]{:S(2)}) collective-permute-start(bf16[16,2048]{1,0:T(8,128)(2,1)} %get-tuple-element.34), channel_id=1, source_target_pairs={{0,4},{4,0},{8,12},{12,8},{16,20},{20,16},{24,28},{28,24},{1,5},{5... | collective-permute-start | bytes 196616 | tf_op jit(solution)/shard_map/state_y/ppermute | solution.py:176
  6.5 1.2 %copy-done = f32[16,128,128]{2,1,0:T(8,128)S(1)} copy-done((f32[16,128,128]{2,1,0:T(8,128)S(1)}, f32[16,128,128]{2,1,0:T(8,128)}, u32[]{:S(2)}) %copy-start) | copy-done | bytes 1048600
  7.8 0.9 copy-done.1
  8.7 0.9 copy-done.2
  9.6 0.7 copy-done.4
  10.9 0.9 fusion.26
  11.8 3.5 %collective-permute-start.1 = (bf16[16,2048]{1,0:T(8,128)(2,1)S(1)}, bf16[16,2048]{1,0:T(8,128)(2,1)S(1)}, u32[]{:S(2)}, u32[]{:S(2)}) collective-permute-start(bf16[16,2048]{1,0:T(8,128)(2,1)S(1)} %get-tuple-element.55), channel_id=1, source_target_pairs={{0,8},{4,12},{8,16},{12,20},{16,24},{20,28},{1,9},{5,13},{9,17},{1... | collective-permute-start | bytes 196616 | tf_op jit(solution)/shard_map/state_1/ppermute | solution.py:176
  15.3 1.9 %shard_map.75.rest_0_ = f32[16,128,128]{2,1,0:T(8,128)S(1)} custom-call(f32[16,128,128]{2,1,0:T(8,128)S(1)} %copy-done, f32[16,2048]{1,0:T(8,128)S(1)} %copy-done.1, f32[16,2048]{1,0:T(8,128)S(1)} %copy-done.2, f32[1,2048]{1,0:T(1,128)S(1)} %copy-done.4, f32[16,128,128]{2,1,0:T(8,128)S(1)} %shard_map.74.rest_0_), custom_call_target="tpu_custom_call", output_to_operand_aliasing={{}: (4, {})} | custom-call | flops 11468800 | bytes 1048576 | tf_op jit(solution)/shard_map/pallas_call | solution.py:155
  17.2 0.8 collective-permute-done.1.below_ref
  18.0 4.5 %collective-permute-start.2 = (bf16[16,2048]{1,0:T(8,128)(2,1)S(1)}, bf16[16,2048]{1,0:T(8,128)(2,1)S(1)}, u32[]{:S(2)}, u32[]{:S(2)}) collective-permute-start(bf16[16,2048]{1,0:T(8,128)(2,1)S(1)} %add_convert_fusion.2), channel_id=1, source_target_pairs={{0,16},{4,20},{8,24},{12,28},{1,17},{5,21},{9,25},{13,29},{2,18},{... | collective-permute-start | bytes 196616 | tf_op jit(solution)/shard_map/state_2/ppermute | solution.py:176
  22.5 1.9 %shard_map.76.base_ref = f32[16,128,128]{2,1,0:T(8,128)S(1)} custom-call(f32[16,128,128]{2,1,0:T(8,128)S(1)} %copy-done, f32[16,2048]{1,0:T(8,128)S(1)} %copy-done.1, f32[16,2048]{1,0:T(8,128)S(1)} %copy-done.2, f32[1,2048]{1,0:T(1,128)S(1)} %copy-done.4, f32[16,128,128]{2,1,0:T(8,128)S(1)} %shard_map.75.rest_0_), custom_call_target="tpu_custom_call", output_to_operand_aliasing={{}: (4, {})} | custom-call | flops 11468800 | bytes 1048576 | tf_op jit(solution)/shard_map/pallas_call | solution.py:155
  24.9 2.2 %shard_map.77 = bf16[128,2048]{1,0:T(8,128)(2,1)S(1)} custom-call(s32[1]{0:T(128)} %bitcast.odd_ref, bf16[128,2048]{1,0:T(8,128)(2,1)S(1)} %copy-done.3, f32[16,128,128]{2,1,0:T(8,128)S(1)} %shard_map.76.base_ref, bf16[16,2048]{1,0:T(8,128)(2,1)S(1)} %collective-permute-done.1.below_ref, bf16[16,2048]{1,0:T(8,128)(2,1)S(1)} %collective-permute-done.2.further_ref, ...), custom_call_target="tpu_custom_call" | custom-call | flops 8388608 | bytes 1048576 | tf_op jit(solution)/shard_map/pallas_call | solution.py:155
  27.7 3.7 %collective-permute-start.4 = (bf16[128,2048]{1,0:T(8,128)(2,1)S(1)}, bf16[128,2048]{1,0:T(8,128)(2,1)S(1)}, u32[]{:S(2)}, u32[]{:S(2)}) collective-permute-start(bf16[128,2048]{1,0:T(8,128)(2,1)S(1)} %shard_map.77), channel_id=1, source_target_pairs={{8,16},{12,20},{16,8},{20,12},{9,17},{13,21},{17,9},{21,13},{10,18... | collective-permute-start | bytes 1572872 | tf_op jit(solution)/shard_map/middle/ppermute | solution.py:176
  31.6 3.0 %fusion.29 = f32[128,1024]{1,0:T(8,128)S(1)} fusion(bf16[128,2048]{1,0:T(8,128)(2,1)S(1)} %shard_map.77, bf16[2048,1024]{1,0:T(8,128)(2,1)} %param.13), kind=kOutput, calls=%fused_computation.50 | convolution fusion | flops 536870912 | bytes 5242880 | tf_op jit(solution)/shard_map/dot_general | solution.py:171
  34.7 4.0 %collective-permute-done.5 = bf16[128,2048]{1,0:T(8,128)(2,1)S(1)} collective-permute-done((bf16[128,2048]{1,0:T(8,128)(2,1)S(1)}, bf16[128,2048]{1,0:T(8,128)(2,1)S(1)}, u32[]{:S(2)}, u32[]{:S(2)}) %collective-permute-start.5) | collective-permute-done | bytes 524320 | tf_op jit(solution)/shard_map/near_y/ppermute | solution.py:176
  38.7 2.1 %collective-permute-done.4 = bf16[128,2048]{1,0:T(8,128)(2,1)S(1)} collective-permute-done((bf16[128,2048]{1,0:T(8,128)(2,1)S(1)}, bf16[128,2048]{1,0:T(8,128)(2,1)S(1)}, u32[]{:S(2)}, u32[]{:S(2)}) %collective-permute-start.4) | collective-permute-done | bytes 524320 | tf_op jit(solution)/shard_map/middle/ppermute | solution.py:176
  40.8 1.3 %collective-permute-done.3 = bf16[128,2048]{1,0:T(8,128)(2,1)S(1)} collective-permute-done((bf16[128,2048]{1,0:T(8,128)(2,1)S(1)}, bf16[128,2048]{1,0:T(8,128)(2,1)S(1)}, u32[]{:S(2)}, u32[]{:S(2)}) %collective-permute-start.3) | collective-permute-done | bytes 524320 | tf_op jit(solution)/shard_map/one/ppermute | solution.py:176
  42.1 1.5 %collective-permute-start.8 = (bf16[128,2048]{1,0:T(8,128)(2,1)S(1)}, bf16[128,2048]{1,0:T(8,128)(2,1)S(1)}, u32[]{:S(2)}, u32[]{:S(2)}) collective-permute-start(bf16[128,2048]{1,0:T(8,128)(2,1)S(1)} %collective-permute-done.3), channel_id=1, source_target_pairs={{0,4},{4,0},{8,12},{12,8},{16,20},{20,16},{24,28},{28,24},{1,5},{5... | collective-permute-start | bytes 1572872 | tf_op jit(solution)/shard_map/one_y/ppermute | solution.py:176
  43.7 2.4 %collective-permute-start.6 = (bf16[128,2048]{1,0:T(8,128)(2,1)S(1)}, bf16[128,2048]{1,0:T(8,128)(2,1)S(1)}, u32[]{:S(2)}, u32[]{:S(2)}) collective-permute-start(bf16[128,2048]{1,0:T(8,128)(2,1)S(1)} %collective-permute-done.3), channel_id=1, source_target_pairs={{8,16},{12,20},{16,8},{20,12},{9,17},{13,21},{17,9},{21,13},{10,18... | collective-permute-start | bytes 1572872 | tf_op jit(solution)/shard_map/given/ppermute | solution.py:176
  46.1 1.3 %collective-permute-start.7 = (bf16[128,2048]{1,0:T(8,128)(2,1)S(1)}, bf16[128,2048]{1,0:T(8,128)(2,1)S(1)}, u32[]{:S(2)}, u32[]{:S(2)}) collective-permute-start(bf16[128,2048]{1,0:T(8,128)(2,1)S(1)} %collective-permute-done.4), channel_id=1, source_target_pairs={{8,0},{12,4},{16,24},{20,28},{9,1},{13,5},{17,25},{21,29},{10,2},{... | collective-permute-start | bytes 1572872 | tf_op jit(solution)/shard_map/out2/ppermute | solution.py:176
  47.4 0.7 fusion.28
  48.2 0.7 fusion.31
  48.9 5.7 %collective-permute-done.7 = bf16[128,2048]{1,0:T(8,128)(2,1)S(1)} collective-permute-done((bf16[128,2048]{1,0:T(8,128)(2,1)S(1)}, bf16[128,2048]{1,0:T(8,128)(2,1)S(1)}, u32[]{:S(2)}, u32[]{:S(2)}) %collective-permute-start.7) | collective-permute-done | bytes 524320 | tf_op jit(solution)/shard_map/out2/ppermute | solution.py:176
  54.6 1.1 %collective-permute-done.6 = bf16[128,2048]{1,0:T(8,128)(2,1)S(1)} collective-permute-done((bf16[128,2048]{1,0:T(8,128)(2,1)S(1)}, bf16[128,2048]{1,0:T(8,128)(2,1)S(1)}, u32[]{:S(2)}, u32[]{:S(2)}) %collective-permute-start.6) | collective-permute-done | bytes 524320 | tf_op jit(solution)/shard_map/given/ppermute | solution.py:176
  55.8 2.4 %collective-permute-start.11 = (bf16[128,1024]{1,0:T(8,128)(2,1)S(1)}, bf16[128,1024]{1,0:T(8,128)(2,1)S(1)}, u32[]{:S(2)}, u32[]{:S(2)}) collective-permute-start(bf16[128,1024]{1,0:T(8,128)(2,1)S(1)} %slice.33), channel_id=1, source_target_pairs={{8,16},{12,20},{16,8},{20,12},{9,17},{13,21},{17,9},{21,13},{10,18... | collective-permute-start | bytes 786440 | tf_op jit(solution)/shard_map/middle_y/ppermute | solution.py:176
  58.1 0.7 fusion.30
  58.9 1.6 %collective-permute-start.9 = (bf16[128,2048]{1,0:T(8,128)(2,1)S(1)}, bf16[128,2048]{1,0:T(8,128)(2,1)S(1)}, u32[]{:S(2)}, u32[]{:S(2)}) collective-permute-start(bf16[128,2048]{1,0:T(8,128)(2,1)S(1)} %collective-permute-done.6), channel_id=1, source_target_pairs={{8,0},{12,4},{16,24},{20,28},{9,1},{13,5},{17,25},{21,29},{10,2},{... | collective-permute-start | bytes 1572872 | tf_op jit(solution)/shard_map/out3/ppermute | solution.py:176
  61.4 0.7 fusion.10
  62.1 1.9 %collective-permute-done.11 = bf16[128,1024]{1,0:T(8,128)(2,1)S(1)} collective-permute-done((bf16[128,1024]{1,0:T(8,128)(2,1)S(1)}, bf16[128,1024]{1,0:T(8,128)(2,1)S(1)}, u32[]{:S(2)}, u32[]{:S(2)}) %collective-permute-start.11) | collective-permute-done | bytes 262176 | tf_op jit(solution)/shard_map/middle_y/ppermute | solution.py:176
  64.0 5.7 %collective-permute-done.10 = bf16[128,2048]{1,0:T(8,128)(2,1)S(1)} collective-permute-done((bf16[128,2048]{1,0:T(8,128)(2,1)S(1)}, bf16[128,2048]{1,0:T(8,128)(2,1)S(1)}, u32[]{:S(2)}, u32[]{:S(2)}) %collective-permute-start.10) | collective-permute-done | bytes 524320 | tf_op jit(solution)/shard_map/two_y/ppermute | solution.py:176
  69.8 0.7 fusion.11
  70.6 1.3 %collective-permute-start.14 = (bf16[2,128,1024]{2,1,0:T(8,128)(2,1)S(1)}, bf16[2,128,1024]{2,1,0:T(8,128)(2,1)S(1)}, u32[]{:S(2)}, u32[]{:S(2)}) collective-permute-start(bf16[2,128,1024]{2,1,0:T(8,128)(2,1)S(1)} %pad_maximum_fusion), channel_id=1, source_target_pairs={{1,0},{3,2},{5,4},{7,6},{9,8},{11,10},{13,12},{15,14},{17,16},{19,... | collective-permute-start | bytes 1572872 | tf_op jit(solution)/shard_map/core_far0/ppermute | solution.py:176
  72.3 0.6 collective-permute-start.17
  72.9 1.7 %collective-permute-start.13 = (bf16[128,1024]{1,0:T(8,128)(2,1)S(1)}, bf16[128,1024]{1,0:T(8,128)(2,1)S(1)}, u32[]{:S(2)}, u32[]{:S(2)}) collective-permute-start(bf16[128,1024]{1,0:T(8,128)(2,1)S(1)} %slice.35), channel_id=1, source_target_pairs={{8,0},{12,4},{16,24},{20,28},{9,1},{13,5},{17,25},{21,29},{10,2},{... | collective-permute-start | bytes 786440 | tf_op jit(solution)/shard_map/out_y/ppermute | solution.py:176
  74.7 0.6 collective-permute-start.12
  75.5 3.4 %collective-permute-start.15 = (bf16[128,1024]{1,0:T(8,128)(2,1)S(1)}, bf16[128,1024]{1,0:T(8,128)(2,1)S(1)}, u32[]{:S(2)}, u32[]{:S(2)}) collective-permute-start(bf16[128,1024]{1,0:T(8,128)(2,1)S(1)} %select_bitcast_fusion.3), channel_id=1, source_target_pairs={{0,2},{2,0},{4,6},{6,4},{8,10},{10,8},{12,14},{14,12},{16,18},{18,... | collective-permute-start | bytes 786440 | tf_op jit(solution)/shard_map/side_far0/ppermute | solution.py:176
  78.9 0.7 fusion.12
  79.6 1.7 %collective-permute-done.17 = bf16[128,1024]{1,0:T(8,128)(2,1)S(1)} collective-permute-done((bf16[128,1024]{1,0:T(8,128)(2,1)S(1)}, bf16[128,1024]{1,0:T(8,128)(2,1)S(1)}, u32[]{:S(2)}, u32[]{:S(2)}) %collective-permute-start.17) | collective-permute-done | bytes 262176 | tf_op jit(solution)/shard_map/side_close/ppermute | solution.py:176
  81.4 3.0 %collective-permute-done.15 = bf16[128,1024]{1,0:T(8,128)(2,1)S(1)} collective-permute-done((bf16[128,1024]{1,0:T(8,128)(2,1)S(1)}, bf16[128,1024]{1,0:T(8,128)(2,1)S(1)}, u32[]{:S(2)}, u32[]{:S(2)}) %collective-permute-start.15) | collective-permute-done | bytes 262176 | tf_op jit(solution)/shard_map/side_far0/ppermute | solution.py:176
  85.7 1.3 %collective-permute-start.19 = (bf16[2,128,1024]{2,1,0:T(8,128)(2,1)S(1)}, bf16[2,128,1024]{2,1,0:T(8,128)(2,1)S(1)}, u32[]{:S(2)}, u32[]{:S(2)}) collective-permute-start(bf16[2,128,1024]{2,1,0:T(8,128)(2,1)S(1)} %pad_maximum_fusion.2), channel_id=1, source_target_pairs={{0,1},{2,3},{4,5},{6,7},{8,9},{10,11},{12,13},{14,15},{16,17},{18,... | collective-permute-start | bytes 1572872 | tf_op jit(solution)/shard_map/core_far1/ppermute | solution.py:176
  87.0 1.5 %collective-permute-done.19 = bf16[2,128,1024]{2,1,0:T(8,128)(2,1)S(1)} collective-permute-done((bf16[2,128,1024]{2,1,0:T(8,128)(2,1)S(1)}, bf16[2,128,1024]{2,1,0:T(8,128)(2,1)S(1)}, u32[]{:S(2)}, u32[]{:S(2)}) %collective-permute-start.19) | collective-permute-done | bytes 524320 | tf_op jit(solution)/shard_map/core_far1/ppermute | solution.py:176
  88.7 0.7 collective-permute-start.20
  89.4 5.6 %collective-permute-start.18 = (bf16[128,1024]{1,0:T(8,128)(2,1)S(1)}, bf16[128,1024]{1,0:T(8,128)(2,1)S(1)}, u32[]{:S(2)}, u32[]{:S(2)}) collective-permute-start(bf16[128,1024]{1,0:T(8,128)(2,1)S(1)} %get-tuple-element.48), channel_id=1, source_target_pairs={{0,16},{1,0},{2,24},{3,8},{4,20},{5,4},{6,28},{7,12},{8,25},{9,9},... | collective-permute-start | bytes 786440 | tf_op jit(solution)/shard_map/own_0/ppermute | solution.py:176
  95.2 1.5 %collective-permute-start.21 = (bf16[128,1024]{1,0:T(8,128)(2,1)S(1)}, bf16[128,1024]{1,0:T(8,128)(2,1)S(1)}, u32[]{:S(2)}, u32[]{:S(2)}) collective-permute-start(bf16[128,1024]{1,0:T(8,128)(2,1)S(1)} %fusion.23), channel_id=1, source_target_pairs={{0,4},{1,20},{2,12},{3,28},{4,0},{5,16},{6,8},{7,24},{8,13},{9,29}... | collective-permute-start | bytes 786440 | tf_op jit(solution)/shard_map/own_1/ppermute | solution.py:176
  96.7 8.6 %collective-permute-done.18 = bf16[128,1024]{1,0:T(8,128)(2,1)S(1)} collective-permute-done((bf16[128,1024]{1,0:T(8,128)(2,1)S(1)}, bf16[128,1024]{1,0:T(8,128)(2,1)S(1)}, u32[]{:S(2)}, u32[]{:S(2)}) %collective-permute-start.18) | collective-permute-done | bytes 262176 | tf_op jit(solution)/shard_map/own_0/ppermute | solution.py:176
  105.3 3.4 %collective-permute-done.21 = bf16[128,1024]{1,0:T(8,128)(2,1)S(1)} collective-permute-done((bf16[128,1024]{1,0:T(8,128)(2,1)S(1)}, bf16[128,1024]{1,0:T(8,128)(2,1)S(1)}, u32[]{:S(2)}, u32[]{:S(2)}) %collective-permute-start.21) | collective-permute-done | bytes 262176 | tf_op jit(solution)/shard_map/own_1/ppermute | solution.py:176
  108.7 0.8 pad_maximum_fusion.3
  (48 shorter events, 5.1 us)
Async XLA Ops:
  0.0 10.8 %copy-start.6 = (f32[2048,16]{0,1:T(8,128)S(1)}, f32[2048,16]{0,1:T(8,128)}, u32[]{:S(2)}) copy-start(f32[2048,16]{0,1:T(8,128)} %param.11) | copy-start | bytes 393220
  5.0 5.9 %collective-permute-start = (bf16[16,2048]{1,0:T(8,128)(2,1)}, bf16[16,2048]{1,0:T(8,128)(2,1)S(1)}, u32[]{:S(2)}, u32[]{:S(2)}) collective-permute-start(bf16[16,2048]{1,0:T(8,128)(2,1)} %get-tuple-element.34), channel_id=1, source_target_pairs={{0,4},{4,0},{8,12},{12,8},{16,20},{20,16},{24,28},{28,24},{1,5},{5... | collective-permute-start | bytes 196616 | tf_op jit(solution)/shard_map/state_y/ppermute | solution.py:176
  6.5 1.2 %copy-start = (f32[16,128,128]{2,1,0:T(8,128)S(1)}, f32[16,128,128]{2,1,0:T(8,128)}, u32[]{:S(2)}) copy-start(f32[16,128,128]{2,1,0:T(8,128)} %get-tuple-element.30.x_ref) | copy-start | bytes 3145732
  7.8 0.9 copy-start.1
  8.7 0.9 copy-start.2
  9.6 0.7 copy-start.4
  10.3 7.7 %copy-start.7 = (bf16[16,2048]{1,0:T(8,128)(2,1)S(1)}, bf16[16,2048]{1,0:T(8,128)(2,1)}, u32[]{:S(2)}) copy-start(bf16[16,2048]{1,0:T(8,128)(2,1)} %get-tuple-element.34) | copy-start | bytes 196612
  10.8 14.1 %copy-start.3 = (bf16[128,2048]{1,0:T(8,128)(2,1)S(1)}, bf16[128,2048]{1,0:T(8,128)(2,1)}, u32[]{:S(2)}) copy-start(bf16[128,2048]{1,0:T(8,128)(2,1)} %get-tuple-element.29.q_ref) | copy-start | bytes 1572868
  11.8 6.2 %collective-permute-start.1 = (bf16[16,2048]{1,0:T(8,128)(2,1)S(1)}, bf16[16,2048]{1,0:T(8,128)(2,1)S(1)}, u32[]{:S(2)}, u32[]{:S(2)}) collective-permute-start(bf16[16,2048]{1,0:T(8,128)(2,1)S(1)} %get-tuple-element.55), channel_id=1, source_target_pairs={{0,8},{4,12},{8,16},{12,20},{16,24},{20,28},{1,9},{5,13},{9,17},{1... | collective-permute-start | bytes 196616 | tf_op jit(solution)/shard_map/state_1/ppermute | solution.py:176
  18.0 6.9 %collective-permute-start.2 = (bf16[16,2048]{1,0:T(8,128)(2,1)S(1)}, bf16[16,2048]{1,0:T(8,128)(2,1)S(1)}, u32[]{:S(2)}, u32[]{:S(2)}) collective-permute-start(bf16[16,2048]{1,0:T(8,128)(2,1)S(1)} %add_convert_fusion.2), channel_id=1, source_target_pairs={{0,16},{4,20},{8,24},{12,28},{1,17},{5,21},{9,25},{13,29},{2,18},{... | collective-permute-start | bytes 196616 | tf_op jit(solution)/shard_map/state_2/ppermute | solution.py:176
  27.1 11.6 %collective-permute-start.5 = (bf16[128,2048]{1,0:T(8,128)(2,1)S(1)}, bf16[128,2048]{1,0:T(8,128)(2,1)S(1)}, u32[]{:S(2)}, u32[]{:S(2)}) collective-permute-start(bf16[128,2048]{1,0:T(8,128)(2,1)S(1)} %shard_map.77), channel_id=1, source_target_pairs={{0,4},{4,0},{8,12},{12,8},{16,20},{20,16},{24,28},{28,24},{1,5},{5... | collective-permute-start | bytes 1572872 | tf_op jit(solution)/shard_map/near_y/ppermute | solution.py:176
  27.7 13.1 %collective-permute-start.4 = (bf16[128,2048]{1,0:T(8,128)(2,1)S(1)}, bf16[128,2048]{1,0:T(8,128)(2,1)S(1)}, u32[]{:S(2)}, u32[]{:S(2)}) collective-permute-start(bf16[128,2048]{1,0:T(8,128)(2,1)S(1)} %shard_map.77), channel_id=1, source_target_pairs={{8,16},{12,20},{16,8},{20,12},{9,17},{13,21},{17,9},{21,13},{10,18... | collective-permute-start | bytes 1572872 | tf_op jit(solution)/shard_map/middle/ppermute | solution.py:176
  31.4 10.7 %collective-permute-start.3 = (bf16[128,2048]{1,0:T(8,128)(2,1)S(1)}, bf16[128,2048]{1,0:T(8,128)(2,1)S(1)}, u32[]{:S(2)}, u32[]{:S(2)}) collective-permute-start(bf16[128,2048]{1,0:T(8,128)(2,1)S(1)} %shard_map.77), channel_id=1, source_target_pairs={{0,8},{4,12},{8,0},{12,4},{16,24},{20,28},{24,16},{28,20},{1,9},{5... | collective-permute-start | bytes 1572872 | tf_op jit(solution)/shard_map/one/ppermute | solution.py:176
  31.6 15.8 %copy-start.5 = (bf16[2048,1024]{1,0:T(8,128)(2,1)S(1)}, bf16[2048,1024]{1,0:T(8,128)(2,1)}, u32[]{:S(2)}) copy-start(bf16[2048,1024]{1,0:T(8,128)(2,1)} %param.13) | copy-start | bytes 12582916
  42.1 12.5 %collective-permute-start.8 = (bf16[128,2048]{1,0:T(8,128)(2,1)S(1)}, bf16[128,2048]{1,0:T(8,128)(2,1)S(1)}, u32[]{:S(2)}, u32[]{:S(2)}) collective-permute-start(bf16[128,2048]{1,0:T(8,128)(2,1)S(1)} %collective-permute-done.3), channel_id=1, source_target_pairs={{0,4},{4,0},{8,12},{12,8},{16,20},{20,16},{24,28},{28,24},{1,5},{5... | collective-permute-start | bytes 1572872 | tf_op jit(solution)/shard_map/one_y/ppermute | solution.py:176
  43.7 12.1 %collective-permute-start.6 = (bf16[128,2048]{1,0:T(8,128)(2,1)S(1)}, bf16[128,2048]{1,0:T(8,128)(2,1)S(1)}, u32[]{:S(2)}, u32[]{:S(2)}) collective-permute-start(bf16[128,2048]{1,0:T(8,128)(2,1)S(1)} %collective-permute-done.3), channel_id=1, source_target_pairs={{8,16},{12,20},{16,8},{20,12},{9,17},{13,21},{17,9},{21,13},{10,18... | collective-permute-start | bytes 1572872 | tf_op jit(solution)/shard_map/given/ppermute | solution.py:176
  46.1 8.5 %collective-permute-start.7 = (bf16[128,2048]{1,0:T(8,128)(2,1)S(1)}, bf16[128,2048]{1,0:T(8,128)(2,1)S(1)}, u32[]{:S(2)}, u32[]{:S(2)}) collective-permute-start(bf16[128,2048]{1,0:T(8,128)(2,1)S(1)} %collective-permute-done.4), channel_id=1, source_target_pairs={{8,0},{12,4},{16,24},{20,28},{9,1},{13,5},{17,25},{21,29},{10,2},{... | collective-permute-start | bytes 1572872 | tf_op jit(solution)/shard_map/out2/ppermute | solution.py:176
  55.8 8.3 %collective-permute-start.11 = (bf16[128,1024]{1,0:T(8,128)(2,1)S(1)}, bf16[128,1024]{1,0:T(8,128)(2,1)S(1)}, u32[]{:S(2)}, u32[]{:S(2)}) collective-permute-start(bf16[128,1024]{1,0:T(8,128)(2,1)S(1)} %slice.33), channel_id=1, source_target_pairs={{8,16},{12,20},{16,8},{20,12},{9,17},{13,21},{17,9},{21,13},{10,18... | collective-permute-start | bytes 786440 | tf_op jit(solution)/shard_map/middle_y/ppermute | solution.py:176
  58.9 10.9 %collective-permute-start.9 = (bf16[128,2048]{1,0:T(8,128)(2,1)S(1)}, bf16[128,2048]{1,0:T(8,128)(2,1)S(1)}, u32[]{:S(2)}, u32[]{:S(2)}) collective-permute-start(bf16[128,2048]{1,0:T(8,128)(2,1)S(1)} %collective-permute-done.6), channel_id=1, source_target_pairs={{8,0},{12,4},{16,24},{20,28},{9,1},{13,5},{17,25},{21,29},{10,2},{... | collective-permute-start | bytes 1572872 | tf_op jit(solution)/shard_map/out3/ppermute | solution.py:176
  60.5 9.2 %collective-permute-start.10 = (bf16[128,2048]{1,0:T(8,128)(2,1)S(1)}, bf16[128,2048]{1,0:T(8,128)(2,1)S(1)}, u32[]{:S(2)}, u32[]{:S(2)}) collective-permute-start(bf16[128,2048]{1,0:T(8,128)(2,1)S(1)} %broadcast_select_fusion.1), channel_id=1, source_target_pairs={{0,4},{4,0},{8,12},{12,8},{16,20},{20,16},{24,28},{28,24},{1,5},{5... | collective-permute-start | bytes 1572872 | tf_op jit(solution)/shard_map/two_y/ppermute | solution.py:176
  61.3 10.8 %collective-permute-start.16 = (bf16[2,128,1024]{2,1,0:T(8,128)(2,1)S(1)}, bf16[2,128,1024]{2,1,0:T(8,128)(2,1)S(1)}, u32[]{:S(2)}, u32[]{:S(2)}) collective-permute-start(bf16[2,128,1024]{2,1,0:T(8,128)(2,1)S(1)} %pad_maximum_fusion.1), channel_id=1, source_target_pairs={{0,1},{1,0},{2,3},{3,2},{4,5},{5,4},{6,7},{7,6},{8,9},{9,8},{10,11... | collective-permute-start | bytes 1572872 | tf_op jit(solution)/shard_map/core_close/ppermute | solution.py:176
  70.6 4.6 %collective-permute-start.14 = (bf16[2,128,1024]{2,1,0:T(8,128)(2,1)S(1)}, bf16[2,128,1024]{2,1,0:T(8,128)(2,1)S(1)}, u32[]{:S(2)}, u32[]{:S(2)}) collective-permute-start(bf16[2,128,1024]{2,1,0:T(8,128)(2,1)S(1)} %pad_maximum_fusion), channel_id=1, source_target_pairs={{1,0},{3,2},{5,4},{7,6},{9,8},{11,10},{13,12},{15,14},{17,16},{19,... | collective-permute-start | bytes 1572872 | tf_op jit(solution)/shard_map/core_far0/ppermute | solution.py:176
  72.3 9.1 %collective-permute-start.17 = (bf16[128,1024]{1,0:T(8,128)(2,1)S(1)}, bf16[128,1024]{1,0:T(8,128)(2,1)S(1)}, u32[]{:S(2)}, u32[]{:S(2)}) collective-permute-start(bf16[128,1024]{1,0:T(8,128)(2,1)S(1)} %fusion.21), channel_id=1, source_target_pairs={{0,2},{1,3},{2,0},{3,1},{4,6},{5,7},{6,4},{7,5},{8,10},{9,11},{10,... | collective-permute-start | bytes 786440 | tf_op jit(solution)/shard_map/side_close/ppermute | solution.py:176
  72.9 11.7 %collective-permute-start.13 = (bf16[128,1024]{1,0:T(8,128)(2,1)S(1)}, bf16[128,1024]{1,0:T(8,128)(2,1)S(1)}, u32[]{:S(2)}, u32[]{:S(2)}) collective-permute-start(bf16[128,1024]{1,0:T(8,128)(2,1)S(1)} %slice.35), channel_id=1, source_target_pairs={{8,0},{12,4},{16,24},{20,28},{9,1},{13,5},{17,25},{21,29},{10,2},{... | collective-permute-start | bytes 786440 | tf_op jit(solution)/shard_map/out_y/ppermute | solution.py:176
  74.7 10.0 %collective-permute-start.12 = (bf16[128,1024]{1,0:T(8,128)(2,1)S(1)}, bf16[128,1024]{1,0:T(8,128)(2,1)S(1)}, u32[]{:S(2)}, u32[]{:S(2)}) collective-permute-start(bf16[128,1024]{1,0:T(8,128)(2,1)S(1)} %slice.44), channel_id=1, source_target_pairs={{0,4},{4,0},{8,12},{12,8},{16,20},{20,16},{24,28},{28,24},{1,5},{5... | collective-permute-start | bytes 786440 | tf_op jit(solution)/shard_map/three_y/ppermute | solution.py:176
  75.5 8.9 %collective-permute-start.15 = (bf16[128,1024]{1,0:T(8,128)(2,1)S(1)}, bf16[128,1024]{1,0:T(8,128)(2,1)S(1)}, u32[]{:S(2)}, u32[]{:S(2)}) collective-permute-start(bf16[128,1024]{1,0:T(8,128)(2,1)S(1)} %select_bitcast_fusion.3), channel_id=1, source_target_pairs={{0,2},{2,0},{4,6},{6,4},{8,10},{10,8},{12,14},{14,12},{16,18},{18,... | collective-permute-start | bytes 786440 | tf_op jit(solution)/shard_map/side_far0/ppermute | solution.py:176
  85.7 2.8 %collective-permute-start.19 = (bf16[2,128,1024]{2,1,0:T(8,128)(2,1)S(1)}, bf16[2,128,1024]{2,1,0:T(8,128)(2,1)S(1)}, u32[]{:S(2)}, u32[]{:S(2)}) collective-permute-start(bf16[2,128,1024]{2,1,0:T(8,128)(2,1)S(1)} %pad_maximum_fusion.2), channel_id=1, source_target_pairs={{0,1},{2,3},{4,5},{6,7},{8,9},{10,11},{12,13},{14,15},{16,17},{18,... | collective-permute-start | bytes 1572872 | tf_op jit(solution)/shard_map/core_far1/ppermute | solution.py:176
  88.7 6.3 %collective-permute-start.20 = (bf16[128,1024]{1,0:T(8,128)(2,1)S(1)}, bf16[128,1024]{1,0:T(8,128)(2,1)S(1)}, u32[]{:S(2)}, u32[]{:S(2)}) collective-permute-start(bf16[128,1024]{1,0:T(8,128)(2,1)S(1)} %select_bitcast_fusion.2), channel_id=1, source_target_pairs={{1,3},{3,1},{5,7},{7,5},{9,11},{11,9},{13,15},{15,13},{17,19},{19,... | collective-permute-start | bytes 786440 | tf_op jit(solution)/shard_map/side_far1/ppermute | solution.py:176
  89.4 15.9 %collective-permute-start.18 = (bf16[128,1024]{1,0:T(8,128)(2,1)S(1)}, bf16[128,1024]{1,0:T(8,128)(2,1)S(1)}, u32[]{:S(2)}, u32[]{:S(2)}) collective-permute-start(bf16[128,1024]{1,0:T(8,128)(2,1)S(1)} %get-tuple-element.48), channel_id=1, source_target_pairs={{0,16},{1,0},{2,24},{3,8},{4,20},{5,4},{6,28},{7,12},{8,25},{9,9},... | collective-permute-start | bytes 786440 | tf_op jit(solution)/shard_map/own_0/ppermute | solution.py:176
  95.2 13.5 %collective-permute-start.21 = (bf16[128,1024]{1,0:T(8,128)(2,1)S(1)}, bf16[128,1024]{1,0:T(8,128)(2,1)S(1)}, u32[]{:S(2)}, u32[]{:S(2)}) collective-permute-start(bf16[128,1024]{1,0:T(8,128)(2,1)S(1)} %fusion.23), channel_id=1, source_target_pairs={{0,4},{1,20},{2,12},{3,28},{4,0},{5,16},{6,8},{7,24},{8,13},{9,29}... | collective-permute-start | bytes 786440 | tf_op jit(solution)/shard_map/own_1/ppermute | solution.py:176

commit v9 on v8

--- a/solution.py
+++ b/solution.py
@@ -37,8 +37,8 @@
 
 
 def state_kernel(total, pieces, *refs):
-    hbm, (state_ref, *near, k_ref, v_ref, sems) = refs[:6], refs[6:]
-    x_ref, rate_ref, gain_ref, q_ref, skip_ref = near
+    hbm, (state_ref, *near, k_ref, v_ref, sems) = refs[:5], refs[5:]
+    x_ref, rate_ref, gain_ref, skip_ref = near
     modes, width = rate_ref.shape
     length = x_ref.shape[1] // SUB
     part = width // pieces
@@ -51,7 +51,7 @@
             for j, (src, dst) in enumerate(pairs)
         ]
 
-    whole = [pltpu.make_async_copy(src, dst, sems.at[pieces, j]) for j, (src, dst) in enumerate(zip(hbm[4:6], (q_ref, skip_ref)))]
+    whole = [pltpu.make_async_copy(hbm[4], skip_ref, sems.at[pieces, 0])]
     for piece in range(pieces):
         for copy in copies(piece):
             copy.start()
@@ -297,12 +297,12 @@
     pieces = 4
     tall, thin = (rows, width), (modes, width)
     chunks = (width // LANES, rows, LANES)
-    state, x, rate_near, gain, q_near, skip = run(
+    state, x, rate_near, gain, skip = run(
         functools.partial(state_kernel, total, pieces),
-        [(thin, BF16), (chunks, F32), (thin, F32), (thin, F32), (tall, BF16), ((1, width), F32)],
+        [(thin, BF16), (chunks, F32), (thin, F32), (thin, F32), ((1, width), F32)],
         48,
         60,
-        [k_proj, v_proj, rate_t, res_t, q_proj, skip_gain[None, :]],
+        [k_proj, v_proj, rate_t, res_t, skip_gain[None, :]],
         [pltpu.VMEM(tall, BF16), pltpu.VMEM(tall, BF16), pltpu.SemaphoreType.DMA((pieces + 1, 4))],
         near=False,
     )
@@ -325,7 +325,7 @@
             [(tall, BF16)],
             32,
             16,
-            [q_near, *base, below, further, first, rate_near, gain],
+            [q_proj, *base, below, further, first, rate_near, gain],
             [pltpu.VMEM((rows, LANES), F32)],
             scalars=(odd.astype(jnp.int32)[None],),
         )[0]

time: 111 us -> 111 us (level)
  no operation moved by 1% of the time
where the time goes in v9:
time: 111 us; the launch traced here: 109 us
  waiting for transfers between devices  41.5 us (37%)
  starting transfers between devices  40.4 us (36%)
  Pallas kernels  11.3 us (10%)
  matrix products  8.34 us (8%)
  local copies, waits for them, and re-layouts  3.8 us (3%)
  other arithmetic  3.64 us (3%)
    ppermute x22, waiting for transfers between devices, moved(): return lax.ppermute(x, axes, pairs)  41.5 us
    ppermute x22, starting transfers between devices, moved(): return lax.ppermute(x, axes, pairs)  40.4 us
    pallas_call x5, Pallas kernels, run(): pl.pallas_call(kernel, out_shape=[jax.ShapeDtypeStruct(shape, kind) for s...  11.3 us
    dot_general x9, matrix products, matmul(): return jnp.dot(x, w, preferred_element_type=F32)  8.34 us
    unnamed x16, local copies, waits for them, and re-layouts  3.75 us
  transfers between devices with their start and end apart: 22, of which 14 were waited for; matrix products, arithmetic and copies ran while one was open for 8% of the time, Pallas kernels for 4%

profile of v9, /device:TPU:10, one launch (start us, length us, event | category | flops | bytes accessed | tf_op | source)
XLA Modules:
  0.0 109.5 jit_solution(1939007825206380843)
XLA Ops:
  0.0 4.8 %shard_map.73 = (bf16[16,2048]{1,0:T(8,128)(2,1)}, f32[16,128,128]{2,1,0:T(8,128)}, f32[16,2048]{1,0:T(8,128)}, f32[16,2048]{1,0:T(8,128)}, f32[1,2048]{1,0:T(1,128)}) custom-call(bf16[128,2048]{1,0:T(8,128)(2,1)} %refs_0_.1, bf16[128,2048]{1,0:T(8,128)(2,1)} %refs_1_.1, f32[16,2048]{1,0:T(8,128)} %bitcast.54, f32[16,2048]{1,0:T(8,128)} %bitcast.55, ...), custom_call_target="tpu_custom_call" | custom-call | flops 12582912 | bytes 1048576 | tf_op jit(solution)/shard_map/pallas_call | solution.py:155
  4.8 1.6 %collective-permute-start = (bf16[16,2048]{1,0:T(8,128)(2,1)}, bf16[16,2048]{1,0:T(8,128)(2,1)S(1)}, u32[]{:S(2)}, u32[]{:S(2)}) collective-permute-start(bf16[16,2048]{1,0:T(8,128)(2,1)} %get-tuple-element.32), channel_id=1, source_target_pairs={{0,4},{4,0},{8,12},{12,8},{16,20},{20,16},{24,28},{28,24},{1,5},{5... | collective-permute-start | bytes 196616 | tf_op jit(solution)/shard_map/state_y/ppermute | solution.py:176
  6.4 1.2 %copy-done = f32[16,128,128]{2,1,0:T(8,128)S(1)} copy-done((f32[16,128,128]{2,1,0:T(8,128)S(1)}, f32[16,128,128]{2,1,0:T(8,128)}, u32[]{:S(2)}) %copy-start) | copy-done | bytes 1048600
  7.6 0.9 copy-done.1
  8.5 0.9 copy-done.2
  9.4 0.7 copy-done.4
  10.7 1.0 fusion.26
  11.7 3.5 %collective-permute-start.1 = (bf16[16,2048]{1,0:T(8,128)(2,1)S(1)}, bf16[16,2048]{1,0:T(8,128)(2,1)S(1)}, u32[]{:S(2)}, u32[]{:S(2)}) collective-permute-start(bf16[16,2048]{1,0:T(8,128)(2,1)S(1)} %get-tuple-element.53), channel_id=1, source_target_pairs={{0,8},{4,12},{8,16},{12,20},{16,24},{20,28},{1,9},{5,13},{9,17},{1... | collective-permute-start | bytes 196616 | tf_op jit(solution)/shard_map/state_1/ppermute | solution.py:176
  15.2 1.9 %shard_map.75.rest_0_ = f32[16,128,128]{2,1,0:T(8,128)S(1)} custom-call(f32[16,128,128]{2,1,0:T(8,128)S(1)} %copy-done, f32[16,2048]{1,0:T(8,128)S(1)} %copy-done.1, f32[16,2048]{1,0:T(8,128)S(1)} %copy-done.2, f32[1,2048]{1,0:T(1,128)S(1)} %copy-done.4, f32[16,128,128]{2,1,0:T(8,128)S(1)} %shard_map.74.rest_0_), custom_call_target="tpu_custom_call", output_to_operand_aliasing={{}: (4, {})} | custom-call | flops 11468800 | bytes 1048576 | tf_op jit(solution)/shard_map/pallas_call | solution.py:155
  17.1 0.8 collective-permute-done.1.below_ref
  18.0 4.5 %collective-permute-start.2 = (bf16[16,2048]{1,0:T(8,128)(2,1)S(1)}, bf16[16,2048]{1,0:T(8,128)(2,1)S(1)}, u32[]{:S(2)}, u32[]{:S(2)}) collective-permute-start(bf16[16,2048]{1,0:T(8,128)(2,1)S(1)} %add_convert_fusion.2), channel_id=1, source_target_pairs={{0,16},{4,20},{8,24},{12,28},{1,17},{5,21},{9,25},{13,29},{2,18},{... | collective-permute-start | bytes 196616 | tf_op jit(solution)/shard_map/state_2/ppermute | solution.py:176
  22.5 1.9 %shard_map.76.base_ref = f32[16,128,128]{2,1,0:T(8,128)S(1)} custom-call(f32[16,128,128]{2,1,0:T(8,128)S(1)} %copy-done, f32[16,2048]{1,0:T(8,128)S(1)} %copy-done.1, f32[16,2048]{1,0:T(8,128)S(1)} %copy-done.2, f32[1,2048]{1,0:T(1,128)S(1)} %copy-done.4, f32[16,128,128]{2,1,0:T(8,128)S(1)} %shard_map.75.rest_0_), custom_call_target="tpu_custom_call", output_to_operand_aliasing={{}: (4, {})} | custom-call | flops 11468800 | bytes 1048576 | tf_op jit(solution)/shard_map/pallas_call | solution.py:155
  24.8 2.2 %shard_map.77 = bf16[128,2048]{1,0:T(8,128)(2,1)S(1)} custom-call(s32[1]{0:T(128)} %bitcast.odd_ref, bf16[128,2048]{1,0:T(8,128)(2,1)S(1)} %copy-done.3, f32[16,128,128]{2,1,0:T(8,128)S(1)} %shard_map.76.base_ref, bf16[16,2048]{1,0:T(8,128)(2,1)S(1)} %collective-permute-done.1.below_ref, bf16[16,2048]{1,0:T(8,128)(2,1)S(1)} %collective-permute-done.2.further_ref, ...), custom_call_target="tpu_custom_call" | custom-call | flops 8388608 | bytes 1048576 | tf_op jit(solution)/shard_map/pallas_call | solution.py:155
  27.6 3.7 %collective-permute-start.4 = (bf16[128,2048]{1,0:T(8,128)(2,1)S(1)}, bf16[128,2048]{1,0:T(8,128)(2,1)S(1)}, u32[]{:S(2)}, u32[]{:S(2)}) collective-permute-start(bf16[128,2048]{1,0:T(8,128)(2,1)S(1)} %shard_map.77), channel_id=1, source_target_pairs={{8,16},{12,20},{16,8},{20,12},{9,17},{13,21},{17,9},{21,13},{10,18... | collective-permute-start | bytes 1572872 | tf_op jit(solution)/shard_map/middle/ppermute | solution.py:176
  31.5 3.0 %fusion.29 = f32[128,1024]{1,0:T(8,128)S(1)} fusion(bf16[128,2048]{1,0:T(8,128)(2,1)S(1)} %shard_map.77, bf16[2048,1024]{1,0:T(8,128)(2,1)} %param.13), kind=kOutput, calls=%fused_computation.50 | convolution fusion | flops 536870912 | bytes 5242880 | tf_op jit(solution)/shard_map/dot_general | solution.py:171
  34.6 4.0 %collective-permute-done.5 = bf16[128,2048]{1,0:T(8,128)(2,1)S(1)} collective-permute-done((bf16[128,2048]{1,0:T(8,128)(2,1)S(1)}, bf16[128,2048]{1,0:T(8,128)(2,1)S(1)}, u32[]{:S(2)}, u32[]{:S(2)}) %collective-permute-start.5) | collective-permute-done | bytes 524320 | tf_op jit(solution)/shard_map/near_y/ppermute | solution.py:176
  38.6 2.1 %collective-permute-done.4 = bf16[128,2048]{1,0:T(8,128)(2,1)S(1)} collective-permute-done((bf16[128,2048]{1,0:T(8,128)(2,1)S(1)}, bf16[128,2048]{1,0:T(8,128)(2,1)S(1)}, u32[]{:S(2)}, u32[]{:S(2)}) %collective-permute-start.4) | collective-permute-done | bytes 524320 | tf_op jit(solution)/shard_map/middle/ppermute | solution.py:176
  40.7 1.4 %collective-permute-done.3 = bf16[128,2048]{1,0:T(8,128)(2,1)S(1)} collective-permute-done((bf16[128,2048]{1,0:T(8,128)(2,1)S(1)}, bf16[128,2048]{1,0:T(8,128)(2,1)S(1)}, u32[]{:S(2)}, u32[]{:S(2)}) %collective-permute-start.3) | collective-permute-done | bytes 524320 | tf_op jit(solution)/shard_map/one/ppermute | solution.py:176
  42.1 1.5 %collective-permute-start.8 = (bf16[128,2048]{1,0:T(8,128)(2,1)S(1)}, bf16[128,2048]{1,0:T(8,128)(2,1)S(1)}, u32[]{:S(2)}, u32[]{:S(2)}) collective-permute-start(bf16[128,2048]{1,0:T(8,128)(2,1)S(1)} %collective-permute-done.3), channel_id=1, source_target_pairs={{0,4},{4,0},{8,12},{12,8},{16,20},{20,16},{24,28},{28,24},{1,5},{5... | collective-permute-start | bytes 1572872 | tf_op jit(solution)/shard_map/one_y/ppermute | solution.py:176
  43.6 2.4 %collective-permute-start.6 = (bf16[128,2048]{1,0:T(8,128)(2,1)S(1)}, bf16[128,2048]{1,0:T(8,128)(2,1)S(1)}, u32[]{:S(2)}, u32[]{:S(2)}) collective-permute-start(bf16[128,2048]{1,0:T(8,128)(2,1)S(1)} %collective-permute-done.3), channel_id=1, source_target_pairs={{8,16},{12,20},{16,8},{20,12},{9,17},{13,21},{17,9},{21,13},{10,18... | collective-permute-start | bytes 1572872 | tf_op jit(solution)/shard_map/given/ppermute | solution.py:176
  46.0 1.3 %collective-permute-start.7 = (bf16[128,2048]{1,0:T(8,128)(2,1)S(1)}, bf16[128,2048]{1,0:T(8,128)(2,1)S(1)}, u32[]{:S(2)}, u32[]{:S(2)}) collective-permute-start(bf16[128,2048]{1,0:T(8,128)(2,1)S(1)} %collective-permute-done.4), channel_id=1, source_target_pairs={{8,0},{12,4},{16,24},{20,28},{9,1},{13,5},{17,25},{21,29},{10,2},{... | collective-permute-start | bytes 1572872 | tf_op jit(solution)/shard_map/out2/ppermute | solution.py:176
  47.3 0.7 fusion.28
  48.1 0.7 fusion.31
  48.8 5.7 %collective-permute-done.7 = bf16[128,2048]{1,0:T(8,128)(2,1)S(1)} collective-permute-done((bf16[128,2048]{1,0:T(8,128)(2,1)S(1)}, bf16[128,2048]{1,0:T(8,128)(2,1)S(1)}, u32[]{:S(2)}, u32[]{:S(2)}) %collective-permute-start.7) | collective-permute-done | bytes 524320 | tf_op jit(solution)/shard_map/out2/ppermute | solution.py:176
  54.5 1.2 %collective-permute-done.6 = bf16[128,2048]{1,0:T(8,128)(2,1)S(1)} collective-permute-done((bf16[128,2048]{1,0:T(8,128)(2,1)S(1)}, bf16[128,2048]{1,0:T(8,128)(2,1)S(1)}, u32[]{:S(2)}, u32[]{:S(2)}) %collective-permute-start.6) | collective-permute-done | bytes 524320 | tf_op jit(solution)/shard_map/given/ppermute | solution.py:176
  55.7 2.4 %collective-permute-start.11 = (bf16[128,1024]{1,0:T(8,128)(2,1)S(1)}, bf16[128,1024]{1,0:T(8,128)(2,1)S(1)}, u32[]{:S(2)}, u32[]{:S(2)}) collective-permute-start(bf16[128,1024]{1,0:T(8,128)(2,1)S(1)} %slice.33), channel_id=1, source_target_pairs={{8,16},{12,20},{16,8},{20,12},{9,17},{13,21},{17,9},{21,13},{10,18... | collective-permute-start | bytes 786440 | tf_op jit(solution)/shard_map/middle_y/ppermute | solution.py:176
  58.1 0.7 fusion.30
  58.8 1.6 %collective-permute-start.9 = (bf16[128,2048]{1,0:T(8,128)(2,1)S(1)}, bf16[128,2048]{1,0:T(8,128)(2,1)S(1)}, u32[]{:S(2)}, u32[]{:S(2)}) collective-permute-start(bf16[128,2048]{1,0:T(8,128)(2,1)S(1)} %collective-permute-done.6), channel_id=1, source_target_pairs={{8,0},{12,4},{16,24},{20,28},{9,1},{13,5},{17,25},{21,29},{10,2},{... | collective-permute-start | bytes 1572872 | tf_op jit(solution)/shard_map/out3/ppermute | solution.py:176
  60.4 0.6 collective-permute-start.10
  61.3 0.7 fusion.10
  62.0 1.9 %collective-permute-done.11 = bf16[128,1024]{1,0:T(8,128)(2,1)S(1)} collective-permute-done((bf16[128,1024]{1,0:T(8,128)(2,1)S(1)}, bf16[128,1024]{1,0:T(8,128)(2,1)S(1)}, u32[]{:S(2)}, u32[]{:S(2)}) %collective-permute-start.11) | collective-permute-done | bytes 262176 | tf_op jit(solution)/shard_map/middle_y/ppermute | solution.py:176
  64.0 5.7 %collective-permute-done.10 = bf16[128,2048]{1,0:T(8,128)(2,1)S(1)} collective-permute-done((bf16[128,2048]{1,0:T(8,128)(2,1)S(1)}, bf16[128,2048]{1,0:T(8,128)(2,1)S(1)}, u32[]{:S(2)}, u32[]{:S(2)}) %collective-permute-start.10) | collective-permute-done | bytes 524320 | tf_op jit(solution)/shard_map/two_y/ppermute | solution.py:176
  69.7 0.7 fusion.11
  70.5 1.3 %collective-permute-start.14 = (bf16[2,128,1024]{2,1,0:T(8,128)(2,1)S(1)}, bf16[2,128,1024]{2,1,0:T(8,128)(2,1)S(1)}, u32[]{:S(2)}, u32[]{:S(2)}) collective-permute-start(bf16[2,128,1024]{2,1,0:T(8,128)(2,1)S(1)} %pad_maximum_fusion), channel_id=1, source_target_pairs={{1,0},{3,2},{5,4},{7,6},{9,8},{11,10},{13,12},{15,14},{17,16},{19,... | collective-permute-start | bytes 1572872 | tf_op jit(solution)/shard_map/core_far0/ppermute | solution.py:176
  72.2 0.6 collective-permute-start.17
  72.9 1.7 %collective-permute-start.13 = (bf16[128,1024]{1,0:T(8,128)(2,1)S(1)}, bf16[128,1024]{1,0:T(8,128)(2,1)S(1)}, u32[]{:S(2)}, u32[]{:S(2)}) collective-permute-start(bf16[128,1024]{1,0:T(8,128)(2,1)S(1)} %slice.35), channel_id=1, source_target_pairs={{8,0},{12,4},{16,24},{20,28},{9,1},{13,5},{17,25},{21,29},{10,2},{... | collective-permute-start | bytes 786440 | tf_op jit(solution)/shard_map/out_y/ppermute | solution.py:176
  75.4 3.4 %collective-permute-start.15 = (bf16[128,1024]{1,0:T(8,128)(2,1)S(1)}, bf16[128,1024]{1,0:T(8,128)(2,1)S(1)}, u32[]{:S(2)}, u32[]{:S(2)}) collective-permute-start(bf16[128,1024]{1,0:T(8,128)(2,1)S(1)} %select_bitcast_fusion.3), channel_id=1, source_target_pairs={{0,2},{2,0},{4,6},{6,4},{8,10},{10,8},{12,14},{14,12},{16,18},{18,... | collective-permute-start | bytes 786440 | tf_op jit(solution)/shard_map/side_far0/ppermute | solution.py:176
  78.8 0.7 fusion.12
  79.6 1.7 %collective-permute-done.17 = bf16[128,1024]{1,0:T(8,128)(2,1)S(1)} collective-permute-done((bf16[128,1024]{1,0:T(8,128)(2,1)S(1)}, bf16[128,1024]{1,0:T(8,128)(2,1)S(1)}, u32[]{:S(2)}, u32[]{:S(2)}) %collective-permute-start.17) | collective-permute-done | bytes 262176 | tf_op jit(solution)/shard_map/side_close/ppermute | solution.py:176
  81.3 3.0 %collective-permute-done.15 = bf16[128,1024]{1,0:T(8,128)(2,1)S(1)} collective-permute-done((bf16[128,1024]{1,0:T(8,128)(2,1)S(1)}, bf16[128,1024]{1,0:T(8,128)(2,1)S(1)}, u32[]{:S(2)}, u32[]{:S(2)}) %collective-permute-start.15) | collective-permute-done | bytes 262176 | tf_op jit(solution)/shard_map/side_far0/ppermute | solution.py:176
  85.6 1.3 %collective-permute-start.19 = (bf16[2,128,1024]{2,1,0:T(8,128)(2,1)S(1)}, bf16[2,128,1024]{2,1,0:T(8,128)(2,1)S(1)}, u32[]{:S(2)}, u32[]{:S(2)}) collective-permute-start(bf16[2,128,1024]{2,1,0:T(8,128)(2,1)S(1)} %pad_maximum_fusion.2), channel_id=1, source_target_pairs={{0,1},{2,3},{4,5},{6,7},{8,9},{10,11},{12,13},{14,15},{16,17},{18,... | collective-permute-start | bytes 1572872 | tf_op jit(solution)/shard_map/core_far1/ppermute | solution.py:176
  86.9 1.5 %collective-permute-done.19 = bf16[2,128,1024]{2,1,0:T(8,128)(2,1)S(1)} collective-permute-done((bf16[2,128,1024]{2,1,0:T(8,128)(2,1)S(1)}, bf16[2,128,1024]{2,1,0:T(8,128)(2,1)S(1)}, u32[]{:S(2)}, u32[]{:S(2)}) %collective-permute-start.19) | collective-permute-done | bytes 524320 | tf_op jit(solution)/shard_map/core_far1/ppermute | solution.py:176
  88.6 0.7 collective-permute-start.20
  89.3 5.6 %collective-permute-start.18 = (bf16[128,1024]{1,0:T(8,128)(2,1)S(1)}, bf16[128,1024]{1,0:T(8,128)(2,1)S(1)}, u32[]{:S(2)}, u32[]{:S(2)}) collective-permute-start(bf16[128,1024]{1,0:T(8,128)(2,1)S(1)} %get-tuple-element.46), channel_id=1, source_target_pairs={{0,16},{1,0},{2,24},{3,8},{4,20},{5,4},{6,28},{7,12},{8,25},{9,9},... | collective-permute-start | bytes 786440 | tf_op jit(solution)/shard_map/own_0/ppermute | solution.py:176
  95.1 1.5 %collective-permute-start.21 = (bf16[128,1024]{1,0:T(8,128)(2,1)S(1)}, bf16[128,1024]{1,0:T(8,128)(2,1)S(1)}, u32[]{:S(2)}, u32[]{:S(2)}) collective-permute-start(bf16[128,1024]{1,0:T(8,128)(2,1)S(1)} %fusion.23), channel_id=1, source_target_pairs={{0,4},{1,20},{2,12},{3,28},{4,0},{5,16},{6,8},{7,24},{8,13},{9,29}... | collective-permute-start | bytes 786440 | tf_op jit(solution)/shard_map/own_1/ppermute | solution.py:176
  96.6 8.7 %collective-permute-done.18 = bf16[128,1024]{1,0:T(8,128)(2,1)S(1)} collective-permute-done((bf16[128,1024]{1,0:T(8,128)(2,1)S(1)}, bf16[128,1024]{1,0:T(8,128)(2,1)S(1)}, u32[]{:S(2)}, u32[]{:S(2)}) %collective-permute-start.18) | collective-permute-done | bytes 262176 | tf_op jit(solution)/shard_map/own_0/ppermute | solution.py:176
  105.3 3.3 %collective-permute-done.21 = bf16[128,1024]{1,0:T(8,128)(2,1)S(1)} collective-permute-done((bf16[128,1024]{1,0:T(8,128)(2,1)S(1)}, bf16[128,1024]{1,0:T(8,128)(2,1)S(1)}, u32[]{:S(2)}, u32[]{:S(2)}) %collective-permute-start.21) | collective-permute-done | bytes 262176 | tf_op jit(solution)/shard_map/own_1/ppermute | solution.py:176
  108.6 0.8 pad_maximum_fusion.3
  (48 shorter events, 5.1 us)
Async XLA Ops:
  0.0 17.9 %copy-start.6 = (f32[2048,16]{0,1:T(8,128)S(1)}, f32[2048,16]{0,1:T(8,128)}, u32[]{:S(2)}) copy-start(f32[2048,16]{0,1:T(8,128)} %param.11) | copy-start | bytes 393220
  4.8 5.9 %collective-permute-start = (bf16[16,2048]{1,0:T(8,128)(2,1)}, bf16[16,2048]{1,0:T(8,128)(2,1)S(1)}, u32[]{:S(2)}, u32[]{:S(2)}) collective-permute-start(bf16[16,2048]{1,0:T(8,128)(2,1)} %get-tuple-element.32), channel_id=1, source_target_pairs={{0,4},{4,0},{8,12},{12,8},{16,20},{20,16},{24,28},{28,24},{1,5},{5... | collective-permute-start | bytes 196616 | tf_op jit(solution)/shard_map/state_y/ppermute | solution.py:176
  6.4 1.2 %copy-start = (f32[16,128,128]{2,1,0:T(8,128)S(1)}, f32[16,128,128]{2,1,0:T(8,128)}, u32[]{:S(2)}) copy-start(f32[16,128,128]{2,1,0:T(8,128)} %get-tuple-element.28.x_ref) | copy-start | bytes 3145732
  7.6 0.9 copy-start.1
  8.5 0.9 copy-start.2
  9.4 0.7 copy-start.4
  10.1 7.8 %copy-start.7 = (bf16[16,2048]{1,0:T(8,128)(2,1)S(1)}, bf16[16,2048]{1,0:T(8,128)(2,1)}, u32[]{:S(2)}) copy-start(bf16[16,2048]{1,0:T(8,128)(2,1)} %get-tuple-element.32) | copy-start | bytes 196612
  10.6 14.2 %copy-start.3 = (bf16[128,2048]{1,0:T(8,128)(2,1)S(1)}, bf16[128,2048]{1,0:T(8,128)(2,1)}, u32[]{:S(2)}) copy-start(bf16[128,2048]{1,0:T(8,128)(2,1)} %q_ref.1) | copy-start | bytes 1572868
  11.7 6.2 %collective-permute-start.1 = (bf16[16,2048]{1,0:T(8,128)(2,1)S(1)}, bf16[16,2048]{1,0:T(8,128)(2,1)S(1)}, u32[]{:S(2)}, u32[]{:S(2)}) collective-permute-start(bf16[16,2048]{1,0:T(8,128)(2,1)S(1)} %get-tuple-element.53), channel_id=1, source_target_pairs={{0,8},{4,12},{8,16},{12,20},{16,24},{20,28},{1,9},{5,13},{9,17},{1... | collective-permute-start | bytes 196616 | tf_op jit(solution)/shard_map/state_1/ppermute | solution.py:176
  18.0 6.9 %collective-permute-start.2 = (bf16[16,2048]{1,0:T(8,128)(2,1)S(1)}, bf16[16,2048]{1,0:T(8,128)(2,1)S(1)}, u32[]{:S(2)}, u32[]{:S(2)}) collective-permute-start(bf16[16,2048]{1,0:T(8,128)(2,1)S(1)} %add_convert_fusion.2), channel_id=1, source_target_pairs={{0,16},{4,20},{8,24},{12,28},{1,17},{5,21},{9,25},{13,29},{2,18},{... | collective-permute-start | bytes 196616 | tf_op jit(solution)/shard_map/state_2/ppermute | solution.py:176
  27.0 11.6 %collective-permute-start.5 = (bf16[128,2048]{1,0:T(8,128)(2,1)S(1)}, bf16[128,2048]{1,0:T(8,128)(2,1)S(1)}, u32[]{:S(2)}, u32[]{:S(2)}) collective-permute-start(bf16[128,2048]{1,0:T(8,128)(2,1)S(1)} %shard_map.77), channel_id=1, source_target_pairs={{0,4},{4,0},{8,12},{12,8},{16,20},{20,16},{24,28},{28,24},{1,5},{5... | collective-permute-start | bytes 1572872 | tf_op jit(solution)/shard_map/near_y/ppermute | solution.py:176
  27.6 13.1 %collective-permute-start.4 = (bf16[128,2048]{1,0:T(8,128)(2,1)S(1)}, bf16[128,2048]{1,0:T(8,128)(2,1)S(1)}, u32[]{:S(2)}, u32[]{:S(2)}) collective-permute-start(bf16[128,2048]{1,0:T(8,128)(2,1)S(1)} %shard_map.77), channel_id=1, source_target_pairs={{8,16},{12,20},{16,8},{20,12},{9,17},{13,21},{17,9},{21,13},{10,18... | collective-permute-start | bytes 1572872 | tf_op jit(solution)/shard_map/middle/ppermute | solution.py:176
  31.3 10.7 %collective-permute-start.3 = (bf16[128,2048]{1,0:T(8,128)(2,1)S(1)}, bf16[128,2048]{1,0:T(8,128)(2,1)S(1)}, u32[]{:S(2)}, u32[]{:S(2)}) collective-permute-start(bf16[128,2048]{1,0:T(8,128)(2,1)S(1)} %shard_map.77), channel_id=1, source_target_pairs={{0,8},{4,12},{8,0},{12,4},{16,24},{20,28},{24,16},{28,20},{1,9},{5... | collective-permute-start | bytes 1572872 | tf_op jit(solution)/shard_map/one/ppermute | solution.py:176
  31.5 15.8 %copy-start.5 = (bf16[2048,1024]{1,0:T(8,128)(2,1)S(1)}, bf16[2048,1024]{1,0:T(8,128)(2,1)}, u32[]{:S(2)}) copy-start(bf16[2048,1024]{1,0:T(8,128)(2,1)} %param.13) | copy-start | bytes 12582916
  42.1 12.4 %collective-permute-start.8 = (bf16[128,2048]{1,0:T(8,128)(2,1)S(1)}, bf16[128,2048]{1,0:T(8,128)(2,1)S(1)}, u32[]{:S(2)}, u32[]{:S(2)}) collective-permute-start(bf16[128,2048]{1,0:T(8,128)(2,1)S(1)} %collective-permute-done.3), channel_id=1, source_target_pairs={{0,4},{4,0},{8,12},{12,8},{16,20},{20,16},{24,28},{28,24},{1,5},{5... | collective-permute-start | bytes 1572872 | tf_op jit(solution)/shard_map/one_y/ppermute | solution.py:176
  43.6 12.1 %collective-permute-start.6 = (bf16[128,2048]{1,0:T(8,128)(2,1)S(1)}, bf16[128,2048]{1,0:T(8,128)(2,1)S(1)}, u32[]{:S(2)}, u32[]{:S(2)}) collective-permute-start(bf16[128,2048]{1,0:T(8,128)(2,1)S(1)} %collective-permute-done.3), channel_id=1, source_target_pairs={{8,16},{12,20},{16,8},{20,12},{9,17},{13,21},{17,9},{21,13},{10,18... | collective-permute-start | bytes 1572872 | tf_op jit(solution)/shard_map/given/ppermute | solution.py:176
  46.0 8.5 %collective-permute-start.7 = (bf16[128,2048]{1,0:T(8,128)(2,1)S(1)}, bf16[128,2048]{1,0:T(8,128)(2,1)S(1)}, u32[]{:S(2)}, u32[]{:S(2)}) collective-permute-start(bf16[128,2048]{1,0:T(8,128)(2,1)S(1)} %collective-permute-done.4), channel_id=1, source_target_pairs={{8,0},{12,4},{16,24},{20,28},{9,1},{13,5},{17,25},{21,29},{10,2},{... | collective-permute-start | bytes 1572872 | tf_op jit(solution)/shard_map/out2/ppermute | solution.py:176
  55.7 8.3 %collective-permute-start.11 = (bf16[128,1024]{1,0:T(8,128)(2,1)S(1)}, bf16[128,1024]{1,0:T(8,128)(2,1)S(1)}, u32[]{:S(2)}, u32[]{:S(2)}) collective-permute-start(bf16[128,1024]{1,0:T(8,128)(2,1)S(1)} %slice.33), channel_id=1, source_target_pairs={{8,16},{12,20},{16,8},{20,12},{9,17},{13,21},{17,9},{21,13},{10,18... | collective-permute-start | bytes 786440 | tf_op jit(solution)/shard_map/middle_y/ppermute | solution.py:176
  58.8 10.9 %collective-permute-start.9 = (bf16[128,2048]{1,0:T(8,128)(2,1)S(1)}, bf16[128,2048]{1,0:T(8,128)(2,1)S(1)}, u32[]{:S(2)}, u32[]{:S(2)}) collective-permute-start(bf16[128,2048]{1,0:T(8,128)(2,1)S(1)} %collective-permute-done.6), channel_id=1, source_target_pairs={{8,0},{12,4},{16,24},{20,28},{9,1},{13,5},{17,25},{21,29},{10,2},{... | collective-permute-start | bytes 1572872 | tf_op jit(solution)/shard_map/out3/ppermute | solution.py:176
  60.4 9.2 %collective-permute-start.10 = (bf16[128,2048]{1,0:T(8,128)(2,1)S(1)}, bf16[128,2048]{1,0:T(8,128)(2,1)S(1)}, u32[]{:S(2)}, u32[]{:S(2)}) collective-permute-start(bf16[128,2048]{1,0:T(8,128)(2,1)S(1)} %broadcast_select_fusion.1), channel_id=1, source_target_pairs={{0,4},{4,0},{8,12},{12,8},{16,20},{20,16},{24,28},{28,24},{1,5},{5... | collective-permute-start | bytes 1572872 | tf_op jit(solution)/shard_map/two_y/ppermute | solution.py:176
  61.2 10.8 %collective-permute-start.16 = (bf16[2,128,1024]{2,1,0:T(8,128)(2,1)S(1)}, bf16[2,128,1024]{2,1,0:T(8,128)(2,1)S(1)}, u32[]{:S(2)}, u32[]{:S(2)}) collective-permute-start(bf16[2,128,1024]{2,1,0:T(8,128)(2,1)S(1)} %pad_maximum_fusion.1), channel_id=1, source_target_pairs={{0,1},{1,0},{2,3},{3,2},{4,5},{5,4},{6,7},{7,6},{8,9},{9,8},{10,11... | collective-permute-start | bytes 1572872 | tf_op jit(solution)/shard_map/core_close/ppermute | solution.py:176
  70.5 4.6 %collective-permute-start.14 = (bf16[2,128,1024]{2,1,0:T(8,128)(2,1)S(1)}, bf16[2,128,1024]{2,1,0:T(8,128)(2,1)S(1)}, u32[]{:S(2)}, u32[]{:S(2)}) collective-permute-start(bf16[2,128,1024]{2,1,0:T(8,128)(2,1)S(1)} %pad_maximum_fusion), channel_id=1, source_target_pairs={{1,0},{3,2},{5,4},{7,6},{9,8},{11,10},{13,12},{15,14},{17,16},{19,... | collective-permute-start | bytes 1572872 | tf_op jit(solution)/shard_map/core_far0/ppermute | solution.py:176
  72.2 9.1 %collective-permute-start.17 = (bf16[128,1024]{1,0:T(8,128)(2,1)S(1)}, bf16[128,1024]{1,0:T(8,128)(2,1)S(1)}, u32[]{:S(2)}, u32[]{:S(2)}) collective-permute-start(bf16[128,1024]{1,0:T(8,128)(2,1)S(1)} %fusion.21), channel_id=1, source_target_pairs={{0,2},{1,3},{2,0},{3,1},{4,6},{5,7},{6,4},{7,5},{8,10},{9,11},{10,... | collective-permute-start | bytes 786440 | tf_op jit(solution)/shard_map/side_close/ppermute | solution.py:176
  72.9 11.7 %collective-permute-start.13 = (bf16[128,1024]{1,0:T(8,128)(2,1)S(1)}, bf16[128,1024]{1,0:T(8,128)(2,1)S(1)}, u32[]{:S(2)}, u32[]{:S(2)}) collective-permute-start(bf16[128,1024]{1,0:T(8,128)(2,1)S(1)} %slice.35), channel_id=1, source_target_pairs={{8,0},{12,4},{16,24},{20,28},{9,1},{13,5},{17,25},{21,29},{10,2},{... | collective-permute-start | bytes 786440 | tf_op jit(solution)/shard_map/out_y/ppermute | solution.py:176
  74.6 10.0 %collective-permute-start.12 = (bf16[128,1024]{1,0:T(8,128)(2,1)S(1)}, bf16[128,1024]{1,0:T(8,128)(2,1)S(1)}, u32[]{:S(2)}, u32[]{:S(2)}) collective-permute-start(bf16[128,1024]{1,0:T(8,128)(2,1)S(1)} %slice.44), channel_id=1, source_target_pairs={{0,4},{4,0},{8,12},{12,8},{16,20},{20,16},{24,28},{28,24},{1,5},{5... | collective-permute-start | bytes 786440 | tf_op jit(solution)/shard_map/three_y/ppermute | solution.py:176
  75.4 8.9 %collective-permute-start.15 = (bf16[128,1024]{1,0:T(8,128)(2,1)S(1)}, bf16[128,1024]{1,0:T(8,128)(2,1)S(1)}, u32[]{:S(2)}, u32[]{:S(2)}) collective-permute-start(bf16[128,1024]{1,0:T(8,128)(2,1)S(1)} %select_bitcast_fusion.3), channel_id=1, source_target_pairs={{0,2},{2,0},{4,6},{6,4},{8,10},{10,8},{12,14},{14,12},{16,18},{18,... | collective-permute-start | bytes 786440 | tf_op jit(solution)/shard_map/side_far0/ppermute | solution.py:176
  85.6 2.8 %collective-permute-start.19 = (bf16[2,128,1024]{2,1,0:T(8,128)(2,1)S(1)}, bf16[2,128,1024]{2,1,0:T(8,128)(2,1)S(1)}, u32[]{:S(2)}, u32[]{:S(2)}) collective-permute-start(bf16[2,128,1024]{2,1,0:T(8,128)(2,1)S(1)} %pad_maximum_fusion.2), channel_id=1, source_target_pairs={{0,1},{2,3},{4,5},{6,7},{8,9},{10,11},{12,13},{14,15},{16,17},{18,... | collective-permute-start | bytes 1572872 | tf_op jit(solution)/shard_map/core_far1/ppermute | solution.py:176
  88.6 6.3 %collective-permute-start.20 = (bf16[128,1024]{1,0:T(8,128)(2,1)S(1)}, bf16[128,1024]{1,0:T(8,128)(2,1)S(1)}, u32[]{:S(2)}, u32[]{:S(2)}) collective-permute-start(bf16[128,1024]{1,0:T(8,128)(2,1)S(1)} %select_bitcast_fusion.2), channel_id=1, source_target_pairs={{1,3},{3,1},{5,7},{7,5},{9,11},{11,9},{13,15},{15,13},{17,19},{19,... | collective-permute-start | bytes 786440 | tf_op jit(solution)/shard_map/side_far1/ppermute | solution.py:176
  89.3 16.0 %collective-permute-start.18 = (bf16[128,1024]{1,0:T(8,128)(2,1)S(1)}, bf16[128,1024]{1,0:T(8,128)(2,1)S(1)}, u32[]{:S(2)}, u32[]{:S(2)}) collective-permute-start(bf16[128,1024]{1,0:T(8,128)(2,1)S(1)} %get-tuple-element.46), channel_id=1, source_target_pairs={{0,16},{1,0},{2,24},{3,8},{4,20},{5,4},{6,28},{7,12},{8,25},{9,9},... | collective-permute-start | bytes 786440 | tf_op jit(solution)/shard_map/own_0/ppermute | solution.py:176
  95.1 13.4 %collective-permute-start.21 = (bf16[128,1024]{1,0:T(8,128)(2,1)S(1)}, bf16[128,1024]{1,0:T(8,128)(2,1)S(1)}, u32[]{:S(2)}, u32[]{:S(2)}) collective-permute-start(bf16[128,1024]{1,0:T(8,128)(2,1)S(1)} %fusion.23), channel_id=1, source_target_pairs={{0,4},{1,20},{2,12},{3,28},{4,0},{5,16},{6,8},{7,24},{8,13},{9,29}... | collective-permute-start | bytes 786440 | tf_op jit(solution)/shard_map/own_1/ppermute | solution.py:176
